TPU v7x, 32 devices: a whole 2x2x4 slice. The times are simulated.
32 devices in a mesh: ctx: 4 (over y, x), ffn: 8 (over z, core).
Axes of the slice: x: 2, y: 2, z: 4, core: 2. Of those that a mesh axis runs over, the one named last changes fastest.
Arguments:
- resid_in: bfloat16 [512, 4096], P(('ctx', 'ffn')), may hold values from -6 to 6
- queries: bfloat16 [512, 4096], P('ctx', 'ffn'), may hold values from -6 to 6
- keys_in: bfloat16 [512, 1024], P('ctx'), may hold values from -6 to 6
- value_rows_input: bfloat16 [512, 1024], P('ctx'), may hold values from -6 to 6
- w_out: bfloat16 [4096, 4096], P('ffn'), may hold values from -0.09375 to 0.09375
- norm_gain: float32 [4096], replicated, may hold values from 0.5 to 1.5
- w_gate: bfloat16 [4096, 7168], P(None, 'ffn'), may hold values from -0.09375 to 0.09375
- w_up: bfloat16 [4096, 7168], P(None, 'ffn'), may hold values from -0.09375 to 0.09375
- w_down: bfloat16 [7168, 4096], P('ffn'), may hold values from -0.0625 to 0.0625
- cotangent: bfloat16 [512, 4096], P(('ctx', 'ffn')), may hold values from -6 to 6
- positions: int32 [512], P('ctx'), may hold values from 0 to 511, as said below
- doc_ids: int32 [512], replicated, may hold values from 0 to 3, never falling along the last dimension, each value on 1 to 256 neighbouring positions
Outputs:
- mixed: bfloat16 [512, 4096], P(('ctx', 'ffn'))
- grad_resid: bfloat16 [512, 4096], P(('ctx', 'ffn'))
- grad_queries: bfloat16 [512, 4096], P('ctx', 'ffn')
- key_gradient_rows: float32 [512, 1024], P(('ctx', 'ffn'))
- value_gradient_rows: float32 [512, 1024], P(('ctx', 'ffn'))
- grad_gain: float32 [4096], replicated
- grad_w_out: float32 [4096, 4096], P('ffn', 'ctx')
- grad_w_gate: float32 [4096, 7168], P('ctx', 'ffn')
- grad_w_up: float32 [4096, 7168], P('ctx', 'ffn')
- grad_w_down: float32 [7168, 4096], P('ffn', 'ctx')
Inputs may be any that keep to these rules, and one draw needn't show every extreme that they name: Each aligned block of 64 rows holds 64 consecutive positions in rising order, and every position occurs once.
All inputs are finite; a program needn't handle non-finite values.
Results may differ from a plain program's by a relative error of at most 0.033.
Values may be sent and summed in bfloat16 or wider, within the bound.
No kernel may reach another device: no remote copies, remote signals or barrier semaphores. Data moves between devices by JAX's collectives and lax.ppermute only.
A program may use at most 128 MiB of HBM per device.

v0:
```python
import math

import jax
import jax.numpy as jnp
from jax import lax
from jax.sharding import PartitionSpec as P

QUERY_HEADS = 32
KEY_VALUE_HEADS = 8
HEAD_WIDTH = 128


masked_fill = -1e30
norm_eps = 1e-05


def passed_along(value, axis, by):
    count = lax.axis_size(axis)
    return lax.ppermute(value, axis, [(i, (i + by) % count) for i in range(count)])


def tile_visible(query_pos, query_seg, key_pos, key_seg):
    return (key_pos[None, :] <= query_pos[:, None]) & (key_seg[None, :] == query_seg[:, None])


def forward_tile(folded, q_heads, key_piece, value_piece, visible, score_scale):
    row_max, row_total, accumulated = folded
    scores = (
        jnp.einsum("rhd,kd->hrk", q_heads, key_piece, preferred_element_type=jnp.float32)
        * score_scale
    )
    scores = jnp.where(visible[None], scores, masked_fill)
    new_max = jnp.maximum(row_max, jnp.max(scores, axis=2))
    weights = jnp.where(visible[None], jnp.exp(scores - new_max[:, :, None]), 0.0)
    shrink = jnp.exp(row_max - new_max)
    new_total = row_total * shrink + jnp.sum(weights, axis=2)
    product = jnp.einsum(
        "hrk,kd->hrd", weights.astype(jnp.bfloat16), value_piece, preferred_element_type=jnp.float32
    )
    return (new_max, new_total, accumulated * shrink[:, :, None] + product)


def row_contract(left_rows, right_rows):
    return jnp.einsum("rd,rf->df", left_rows, right_rows, preferred_element_type=jnp.float32)


def body(
    resid_in,
    queries,
    keys_in,
    value_rows_input,
    w_out,
    norm_gain,
    w_gate,
    w_up,
    w_down,
    cotangent,
    positions,
    doc_ids,
):
    row_count = queries.shape[0]
    resident_heads = queries.shape[1] // HEAD_WIDTH
    ctx_size = lax.axis_size("ctx")
    ctx_index = lax.axis_index("ctx")
    key_value_group = lax.axis_index("ffn") * resident_heads // (QUERY_HEADS // KEY_VALUE_HEADS)
    score_scale = 1.0 / math.sqrt(HEAD_WIDTH)
    all_pos = lax.all_gather(positions, "ctx", axis=0, tiled=True)
    all_seg = doc_ids[all_pos]
    own_seg = doc_ids[positions]
    key_own = lax.dynamic_slice_in_dim(keys_in, key_value_group * HEAD_WIDTH, HEAD_WIDTH, 1)
    value_own = lax.dynamic_slice_in_dim(
        value_rows_input, key_value_group * HEAD_WIDTH, HEAD_WIDTH, 1
    )
    kv_pair = jnp.stack((key_own, value_own), axis=1)
    q_heads = queries.reshape(row_count, resident_heads, HEAD_WIDTH)

    def key_visible(row_start, row_num):
        return tile_visible(
            positions,
            own_seg,
            lax.dynamic_slice_in_dim(all_pos, row_start, row_num, 0),
            lax.dynamic_slice_in_dim(all_seg, row_start, row_num, 0),
        )

    def fold_keys(folded, shard_rows, row_start):
        visible = key_visible(row_start, shard_rows.shape[0])
        return forward_tile(
            folded, q_heads, shard_rows[:, 0], shard_rows[:, 1], visible, score_scale
        )

    start_state = (
        jnp.full((resident_heads, row_count), masked_fill, jnp.float32),
        jnp.zeros((resident_heads, row_count), jnp.float32),
        jnp.zeros((resident_heads, row_count, HEAD_WIDTH), jnp.float32),
    )

    def pass_step(turn_index, running):
        folded, travel = running
        travel = passed_along(travel, "ctx", 1)
        source = (ctx_index - turn_index - 1) % ctx_size
        return (fold_keys(folded, travel, source * row_count), travel)

    first_state = fold_keys(start_state, kv_pair, ctx_index * row_count)
    (row_max, row_total, accumulated), unused = lax.fori_loop(
        0, ctx_size - 1, pass_step, (first_state, kv_pair)
    )
    attended = (accumulated / row_total[:, :, None]).astype(jnp.bfloat16)
    log_totals = row_max + jnp.log(row_total)
    attended_rows = jnp.transpose(attended, (1, 0, 2)).reshape(
        row_count, resident_heads * HEAD_WIDTH
    )
    projected = lax.psum_scatter(
        jnp.dot(attended_rows, w_out, preferred_element_type=jnp.float32).astype(jnp.bfloat16),
        "ffn",
        scatter_dimension=0,
        tiled=True,
    ).astype(jnp.float32)
    hidden_bf = (resid_in.astype(jnp.float32) + projected).astype(jnp.bfloat16)
    hidden_f = lax.optimization_barrier(hidden_bf).astype(jnp.float32)
    inv_rms = lax.rsqrt(jnp.mean(hidden_f * hidden_f, axis=1, keepdims=True) + norm_eps)
    normed = (hidden_f * inv_rms * norm_gain).astype(jnp.bfloat16)
    normed_rows = lax.all_gather(normed, "ffn", axis=0, tiled=True)
    gate_pre = jnp.dot(normed_rows, w_gate, preferred_element_type=jnp.float32)
    up_proj = jnp.dot(normed_rows, w_up, preferred_element_type=jnp.float32)
    gate_sig = jax.nn.sigmoid(gate_pre)
    activated = (gate_pre * gate_sig * up_proj).astype(jnp.bfloat16)
    mixed = (
        hidden_f
        + lax.psum_scatter(
            jnp.dot(activated, w_down, preferred_element_type=jnp.float32).astype(jnp.bfloat16),
            "ffn",
            scatter_dimension=0,
            tiled=True,
        ).astype(jnp.float32)
    ).astype(jnp.bfloat16)
    cot_rows = lax.all_gather(cotangent, "ffn", axis=0, tiled=True)
    grad_act = jnp.dot(cot_rows, w_down.T, preferred_element_type=jnp.float32)
    grad_up = (grad_act * gate_pre * gate_sig).astype(jnp.bfloat16)
    grad_gate = (grad_act * up_proj * gate_sig * (1.0 + gate_pre * (1.0 - gate_sig))).astype(
        jnp.bfloat16
    )
    gate_part = grad_gate
    up_part = grad_up
    grad_normed = lax.psum_scatter(
        (
            jnp.dot(gate_part, w_gate.T, preferred_element_type=jnp.float32)
            + jnp.dot(up_part, w_up.T, preferred_element_type=jnp.float32)
        ).astype(jnp.bfloat16),
        "ffn",
        scatter_dimension=0,
        tiled=True,
    ).astype(jnp.float32)
    gained = grad_normed * norm_gain
    inv_cube = inv_rms * inv_rms * inv_rms
    grad_resid = (
        cotangent.astype(jnp.float32)
        + inv_rms * gained
        - hidden_f * inv_cube * jnp.mean(gained * hidden_f, axis=1, keepdims=True)
    ).astype(jnp.bfloat16)
    grad_gain = lax.psum(jnp.sum(grad_normed * hidden_f * inv_rms, axis=0), ("ctx", "ffn"))
    grad_rows = lax.all_gather(grad_resid, "ffn", axis=0, tiled=True)
    grad_attended = jnp.dot(grad_rows, w_out.T, preferred_element_type=jnp.float32).astype(
        jnp.bfloat16
    )
    grad_heads = grad_attended.reshape(row_count, resident_heads, HEAD_WIDTH)
    deltas = jnp.sum(
        grad_heads.astype(jnp.float32)
        * attended_rows.reshape(row_count, resident_heads, HEAD_WIDTH).astype(jnp.float32),
        axis=2,
    )
    delta_heads = deltas.T
    stats_all, deltas_all = (
        lax.all_gather(log_totals.T, "ctx", axis=0, tiled=True),
        lax.all_gather(deltas, "ctx", axis=0, tiled=True),
    )
    shard_rows = lax.all_gather(kv_pair, "ctx", axis=0, tiled=True)
    key_piece = shard_rows[:, 0]
    value_piece = shard_rows[:, 1]
    visible = key_visible(jnp.int32(0), shard_rows.shape[0])

    def update(running):
        scores = (
            jnp.einsum("rhd,kd->hrk", q_heads, key_piece, preferred_element_type=jnp.float32)
            * score_scale
        )
        scores = jnp.where(visible[None], scores, masked_fill)
        prob_weights = jnp.where(visible[None], jnp.exp(scores - log_totals[:, :, None]), 0.0)
        grad_probs = jnp.einsum(
            "rhd,kd->hrk", grad_heads, value_piece, preferred_element_type=jnp.float32
        )
        grad_scores = (prob_weights * (grad_probs - delta_heads[:, :, None])).astype(jnp.bfloat16)
        return (
            jnp.einsum("hrk,kd->rhd", grad_scores, key_piece, preferred_element_type=jnp.float32)
            * score_scale
        )

    grad_query = update(jnp.zeros((row_count, resident_heads, HEAD_WIDTH), jnp.float32))
    zero_block = jnp.zeros((row_count, HEAD_WIDTH), jnp.float32)
    shard_rows = (
        lax.all_gather(queries, "ctx", axis=0, tiled=True),
        lax.all_gather(grad_attended, "ctx", axis=0, tiled=True),
    )
    row_num = shard_rows[0].shape[0]
    q_piece = shard_rows[0].reshape(row_num, resident_heads, HEAD_WIDTH)
    g_piece = shard_rows[1].reshape(row_num, resident_heads, HEAD_WIDTH)
    fold_visible = tile_visible(all_pos, all_seg, positions, own_seg)
    stat_piece = stats_all.T
    delta_piece = deltas_all.T

    def update(running):
        scores = (
            jnp.einsum("qhd,kd->hqk", q_piece, key_own, preferred_element_type=jnp.float32)
            * score_scale
        )
        scores = jnp.where(fold_visible[None], scores, masked_fill)
        prob_weights = jnp.where(fold_visible[None], jnp.exp(scores - stat_piece[:, :, None]), 0.0)
        grad_probs = jnp.einsum(
            "qhd,kd->hqk", g_piece, value_own, preferred_element_type=jnp.float32
        )
        grad_scores = (prob_weights * (grad_probs - delta_piece[:, :, None])).astype(jnp.bfloat16)
        grad_key = (
            jnp.einsum("hqk,qhd->kd", grad_scores, q_piece, preferred_element_type=jnp.float32)
            * score_scale
        )
        grad_value = jnp.einsum(
            "hqk,qhd->kd",
            prob_weights.astype(jnp.bfloat16),
            g_piece,
            preferred_element_type=jnp.float32,
        )
        return (grad_key, grad_value)

    grad_key_own, grad_value_own = update((zero_block, zero_block))
    empty_rows = jnp.zeros((row_count, keys_in.shape[1]), jnp.float32)
    placed_key = lax.dynamic_update_slice_in_dim(
        empty_rows, grad_key_own, key_value_group * HEAD_WIDTH, 1
    )
    placed_value = lax.dynamic_update_slice_in_dim(
        empty_rows, grad_value_own, key_value_group * HEAD_WIDTH, 1
    )
    key_gradient_rows, value_gradient_rows = (
        lax.psum_scatter(
            placed_key.astype(jnp.bfloat16), "ffn", scatter_dimension=0, tiled=True
        ).astype(jnp.float32),
        lax.psum_scatter(
            placed_value.astype(jnp.bfloat16), "ffn", scatter_dimension=0, tiled=True
        ).astype(jnp.float32),
    )
    normed_cols, grad_cols, cot_cols = (
        lax.all_to_all(normed_rows, "ctx", split_axis=1, concat_axis=0, tiled=True),
        lax.all_to_all(grad_rows, "ctx", split_axis=1, concat_axis=0, tiled=True),
        lax.all_to_all(cot_rows, "ctx", split_axis=1, concat_axis=0, tiled=True),
    )
    gate_part = lax.all_gather(grad_gate, "ctx", axis=0, tiled=True)
    up_part = lax.all_gather(grad_up, "ctx", axis=0, tiled=True)
    attended_part = lax.all_gather(attended_rows, "ctx", axis=0, tiled=True)
    act_part = lax.all_gather(activated, "ctx", axis=0, tiled=True)
    row_num = gate_part.shape[0]
    grad_w_out = row_contract(attended_part, grad_cols)
    grad_w_gate = row_contract(normed_cols, gate_part)
    grad_w_up = row_contract(normed_cols, up_part)
    grad_w_down = row_contract(act_part, cot_cols)
    grad_queries = grad_query.reshape(row_count, resident_heads * HEAD_WIDTH).astype(jnp.bfloat16)
    return (
        mixed,
        grad_resid,
        grad_queries,
        key_gradient_rows,
        value_gradient_rows,
        grad_gain,
        grad_w_out,
        grad_w_gate,
        grad_w_up,
        grad_w_down,
    )


def solution(mesh):
    return jax.shard_map(
        body,
        mesh=mesh,
        in_specs=(
            P(("ctx", "ffn"), None),
            P("ctx", "ffn"),
            P("ctx", None),
            P("ctx", None),
            P("ffn", None),
            P(),
            P(None, "ffn"),
            P(None, "ffn"),
            P("ffn", None),
            P(("ctx", "ffn"), None),
            P("ctx"),
            P(),
        ),
        out_specs=(
            P(("ctx", "ffn"), None),
            P(("ctx", "ffn"), None),
            P("ctx", "ffn"),
            P(("ctx", "ffn"), None),
            P(("ctx", "ffn"), None),
            P(),
            P("ffn", "ctx"),
            P("ctx", "ffn"),
            P("ctx", "ffn"),
            P("ffn", "ctx"),
        ),
        check_vma=False,
    )
```

profile of v0, /device:TPU:0, one launch (start us, length us, event | category | flops | bytes accessed | tf_op | source)
XLA Modules:
  0.0 412.4 jit_solution(7695164197753614854)
XLA Ops:
  7.9 9.5 %all-gather = s32[4,1,128]{2,1,0:T(1,128)S(1)} all-gather(s32[1,1,128]{2,1,0:T(1,128)} %bitcast.208), channel_id=1, replica_groups=mesh['ctx'=4,'ffn'=8] {'ctx'}, dimensions={0}, use_global_device_ids=true | all-gather | bytes 2560 | tf_op jit(solution)/shard_map/all_gather | solution.py:67
  17.5 3.5 gather_fusion
  27.2 17.6 %while.21 = (s32[]{:T(128)}, f32[4,128]{1,0:T(4,128)S(1)}, f32[4,128]{1,0:T(4,128)S(1)}, f32[4,128,128]{2,1,0:T(8,128)S(1)}, bf16[128,2,128]{2,0,1:T(8,128)(2,1)...) while((s32[]{:T(128)}, f32[4,128]{1,0:T(4,128)S(1)}, ...), condition=%wide.region_5.6_spmd, body=%wide.region_2.5_spmd.sunk | while | flops 34325520 | bytes 2003336 | solution.py:104
  27.2 1.4 collective-permute-start
  28.9 3.5 collective-permute-done
  33.8 4.5 %collective-permute-done = bf16[128,2,128]{2,0,1:T(8,128)(2,1)S(1)} collective-permute-done((bf16[128,2,128]{2,0,1:T(8,128)(2,1)S(1)}, bf16[128,2,128]{2,0,1:T(8,128)(2,1)S(1)}, u32[]{:S(2)}, u32[]{:S(2)}) %collective-permute-start) | collective-permute-done | bytes 65568 | tf_op jit(solution)/shard_map/while/body/eval_jaxpr/ppermute | solution.py:19
  39.3 4.9 %collective-permute-done = bf16[128,2,128]{2,0,1:T(8,128)(2,1)S(1)} collective-permute-done((bf16[128,2,128]{2,0,1:T(8,128)(2,1)S(1)}, bf16[128,2,128]{2,0,1:T(8,128)(2,1)S(1)}, u32[]{:S(2)}, u32[]{:S(2)}) %collective-permute-start) | collective-permute-done | bytes 65568 | tf_op jit(solution)/shard_map/while/body/eval_jaxpr/ppermute | solution.py:19
  45.0 3.9 convolution_convert_fusion.1
  49.0 33.0 %reduce-scatter.6.cloned.1.call-done = bf16[16,4096]{1,0:T(8,128)(2,1)} async-done(((bf16[128,4096]{1,0:T(8,128)(2,1)}), bf16[16,4096]{1,0:T(8,128)(2,1)}) %reduce-scatter.6.cloned.1.call-update) | async-done | bytes 131088 | tf_op jit(solution)/shard_map/reduce_scatter | solution.py:112
  84.7 19.9 %all-gather.5.cloned.1.call-done = bf16[128,4096]{1,0:T(8,128)(2,1)} async-done(((bf16[16,4096]{1,0:T(8,128)(2,1)}), bf16[128,4096]{1,0:T(8,128)(2,1)}) %all-gather.5.cloned.1.call-update) | async-done | bytes 1048592 | tf_op jit(solution)/shard_map/all_gather | solution.py:122
  104.6 4.8 %fusion.83 = f32[128,896]{1,0:T(8,128)S(1)} fusion(bf16[128,4096]{1,0:T(8,128)(2,1)} %all-gather.5.cloned.1.call-done, bf16[4096,896]{1,0:T(8,128)(2,1)} %param.21), kind=kOutput, calls=%fused_computation.132 | convolution fusion | flops 939524096 | bytes 8847360 | tf_op jit(solution)/shard_map/dot_general | solution.py:124
  109.3 4.4 %fusion.82 = f32[128,896]{1,0:T(8,128)S(1)} fusion(bf16[128,4096]{1,0:T(8,128)(2,1)S(1)} %copy-done.2, bf16[4096,896]{1,0:T(8,128)(2,1)} %param.20), kind=kOutput, calls=%fused_computation.131 | convolution fusion | flops 939524096 | bytes 8847360 | tf_op jit(solution)/shard_map/dot_general | solution.py:123
  113.8 14.2 %all-gather.7.cloned.1.call-done = bf16[128,4096]{1,0:T(8,128)(2,1)} async-done(((bf16[16,4096]{1,0:T(8,128)(2,1)}), bf16[128,4096]{1,0:T(8,128)(2,1)}) %all-gather.7.cloned.1.call-update) | async-done | bytes 1048592 | tf_op jit(solution)/shard_map/all_gather | solution.py:136
  127.9 5.9 %multiply_convert_fusion = (bf16[128,896]{1,0:T(8,128)(2,1)S(1)}, bf16[128,896]{1,0:T(8,128)(2,1)S(1)}, bf16[128,896]{1,0:T(8,128)(2,1)S(1)}) fusion(f32[128,896]{1,0:T(8,128)S(1)} %fusion.82, f32[128,896]{1,0:T(8,128)S(1)} %fusion.83, bf16[128,4096]{1,0:T(8,128)(2,1)} %all-gather.7.cloned.1.call-done, bf16[896,4096]{1,0:T(8,128)(2,1)} %param.22), kind=kOutput, calls=%fused_computation.71 | convolution fusion | flops 941359104 | bytes 9994240 | tf_op jit(solution)/shard_map/dot_general | solution.py:137
  133.9 5.7 %fusion.84 = f32[128,4096]{1,0:T(8,128)S(1)} fusion(bf16[128,896]{1,0:T(8,128)(2,1)S(1)} %get-tuple-element.394, bf16[4096,896]{1,0:T(8,128)(2,1)} %param.20), kind=kOutput, calls=%fused_computation.133 | convolution fusion | flops 939524096 | bytes 9666560 | tf_op jit(solution)/shard_map/dot_general | solution.py:146
  139.7 6.5 %fusion.9 = bf16[128,4096]{1,0:T(8,128)(2,1)} fusion(f32[128,4096]{1,0:T(8,128)S(1)} %fusion.84, bf16[128,896]{1,0:T(8,128)(2,1)S(1)} %get-tuple-element.393, bf16[4096,896]{1,0:T(8,128)(2,1)} %param.21), kind=kOutput, calls=%fused_computation.19 | convolution fusion | flops 940572672 | bytes 10715136 | tf_op jit(solution)/shard_map/dot_general | solution.py:147
  146.3 5.4 %convolution_convert_fusion = bf16[128,4096]{1,0:T(8,128)(2,1)} fusion(bf16[128,896]{1,0:T(8,128)(2,1)S(1)} %get-tuple-element.395, bf16[896,4096]{1,0:T(8,128)(2,1)} %param.22), kind=kOutput, calls=%fused_computation.20 | convolution fusion | flops 940048384 | bytes 8617984 | tf_op jit(solution)/shard_map/dot_general | solution.py:130
  151.8 8.2 %all_gather.45 = f32[512,4]{0,1:T(4,128)S(1)} all-gather(f32[128,4]{0,1:T(4,128)S(1)} %bitcast.214), channel_id=1, replica_groups=mesh['ctx'=4,'ffn'=8] {'ctx'}, dimensions={0}, use_global_device_ids=true | all-gather | bytes 10240 | tf_op jit(solution)/shard_map/all_gather | solution.py:173
  160.2 18.2 %reduce-scatter.10.cloned.1.call-done = bf16[16,4096]{1,0:T(8,128)(2,1)} async-done(((bf16[128,4096]{1,0:T(8,128)(2,1)}), bf16[16,4096]{1,0:T(8,128)(2,1)}) %reduce-scatter.10.cloned.1.call-update) | async-done | bytes 131088 | tf_op jit(solution)/shard_map/reduce_scatter | solution.py:144
  178.4 1.7 fusion.56
  180.1 31.6 %reduce-scatter.8.cloned.1.call-done = bf16[16,4096]{1,0:T(8,128)(2,1)} async-done(((bf16[128,4096]{1,0:T(8,128)(2,1)}), bf16[16,4096]{1,0:T(8,128)(2,1)}) %reduce-scatter.8.cloned.1.call-update) | async-done | bytes 131088 | tf_op jit(solution)/shard_map/reduce_scatter | solution.py:129
  211.7 1.8 fusion.48
  213.5 11.6 %all_gather.48 = bf16[512,512]{0,1:T(8,128)(2,1)} all-gather(bf16[128,512]{0,1:T(8,128)(2,1)S(1)} %bitcast.206), channel_id=1, replica_groups=mesh['ctx'=4,'ffn'=8] {'ctx'}, dimensions={0}, use_global_device_ids=true | all-gather | bytes 655360 | tf_op jit(solution)/shard_map/all_gather | solution.py:256
  225.1 9.5 %all_gather.44 = bf16[512,512]{0,1:T(8,128)(2,1)S(1)} all-gather(bf16[128,512]{0,1:T(8,128)(2,1)S(1)} %copy.67), channel_id=1, replica_groups=mesh['ctx'=4,'ffn'=8] {'ctx'}, dimensions={0}, use_global_device_ids=true | all-gather | bytes 655360 | tf_op jit(solution)/shard_map/all_gather | solution.py:200
  234.6 2.4 copy.84
  237.0 4.2 %all-to-all-start.2 = ((bf16[128,4,1024]{0,2,1:T(8,128)(2,1)}), bf16[128,4,1024]{0,2,1:T(8,128)(2,1)}, u32[]{:S(2)}, u32[]{:S(2)}) async-start(bf16[128,4,1024]{0,2,1:T(8,128)(2,1)} %bitcast.39), calls=%async_computation.7 | async-start | bytes 2097152 | tf_op jit(solution)/shard_map/all_to_all | solution.py:252
  241.3 14.1 %all_gather.42 = bf16[512,2,128]{2,0,1:T(8,128)(2,1)S(1)} all-gather(bf16[128,2,128]{2,0,1:T(8,128)(2,1)S(1)} %pad_maximum_fusion), channel_id=1, replica_groups=mesh['ctx'=4,'ffn'=8] {'ctx'}, dimensions={0}, use_global_device_ids=true | all-gather | bytes 327680 | tf_op jit(solution)/shard_map/all_gather | solution.py:176
  255.5 1.4 fusion.23
  258.1 2.7 copy.85
  261.8 3.5 all-to-all-start.1
  265.4 21.3 %all_gather.50 = bf16[512,896]{1,0:T(8,128)(2,1)} all-gather(bf16[128,896]{1,0:T(8,128)(2,1)S(1)} %get-tuple-element.393), channel_id=1, replica_groups=mesh['ctx'=4,'ffn'=8] {'ctx'}, dimensions={0}, use_global_device_ids=true | all-gather | bytes 1146880 | tf_op jit(solution)/shard_map/all_gather | solution.py:255
  286.8 11.7 %all_gather.49 = bf16[512,896]{1,0:T(8,128)(2,1)S(1)} all-gather(bf16[128,896]{1,0:T(8,128)(2,1)} %copy-done.11), channel_id=1, replica_groups=mesh['ctx'=4,'ffn'=8] {'ctx'}, dimensions={0}, use_global_device_ids=true | all-gather | bytes 1146880 | tf_op jit(solution)/shard_map/all_gather | solution.py:254
  298.4 11.0 %all_gather.51 = bf16[512,896]{1,0:T(8,128)(2,1)S(1)} all-gather(bf16[128,896]{1,0:T(8,128)(2,1)} %copy-done.7), channel_id=1, replica_groups=mesh['ctx'=4,'ffn'=8] {'ctx'}, dimensions={0}, use_global_device_ids=true | all-gather | bytes 1146880 | tf_op jit(solution)/shard_map/all_gather | solution.py:257
  309.4 4.2 %fusion.88 = f32[896,1024]{1,0:T(8,128)} fusion(bf16[512,896]{1,0:T(8,128)(2,1)S(1)} %all_gather.51, bf16[512,1024]{1,0:T(8,128)(2,1)} %bitcast.198), kind=kOutput, calls=%fused_computation.137 | convolution fusion | flops 939524096 | bytes 5636096 | tf_op jit(solution)/shard_map/rd,rf->df/dot_general | solution.py:44
  313.7 4.0 convolution_convert_fusion.2
  318.5 7.7 %all_gather.47 = f32[512,4]{0,1:T(4,128)S(1)} all-gather(f32[128,4]{0,1:T(4,128)S(1)} %multiply_reduce_fusion), channel_id=1, replica_groups=mesh['ctx'=4,'ffn'=8] {'ctx'}, dimensions={0}, use_global_device_ids=true | all-gather | bytes 10240 | tf_op jit(solution)/shard_map/all_gather | solution.py:174
  326.2 9.4 %all_gather.46 = bf16[512,512]{1,0:T(8,128)(2,1)S(1)} all-gather(bf16[128,512]{1,0:T(8,128)(2,1)} %copy-done.9), channel_id=1, replica_groups=mesh['ctx'=4,'ffn'=8] {'ctx'}, dimensions={0}, use_global_device_ids=true | all-gather | bytes 655360 | tf_op jit(solution)/shard_map/all_gather | solution.py:201
  336.3 2.2 fusion.35
  338.6 4.4 %fusion.87 = f32[1024,896]{1,0:T(8,128)} fusion(bf16[512,1024]{1,0:T(8,128)(2,1)S(1)} %bitcast.192, bf16[512,896]{1,0:T(8,128)(2,1)} %all_gather.50), kind=kOutput, calls=%fused_computation.136 | convolution fusion | flops 939524096 | bytes 5636096 | tf_op jit(solution)/shard_map/rd,rf->df/dot_general | solution.py:44
  344.1 3.5 all-to-all-start
  348.4 2.2 fusion.33
  350.6 3.1 fusion.86
  353.7 42.2 %psum.7 = f32[4096]{0:T(1024)} all-reduce(f32[4096]{0:T(1024)} %get-tuple-element.365), channel_id=1, replica_groups=mesh['ctx'=4,'ffn'=8] {'ctx','ffn'}, use_global_device_ids=true, to_apply=%region_15.16 | all-reduce | flops 4096 | bytes 32768 | tf_op jit(solution)/shard_map/psum | solution.py:160
  395.9 1.9 fusion.31
  398.6 1.4 convert_element_type.130
  400.0 2.1 reduce-scatter.14.cloned.1.call-done
  402.1 1.4 convert_element_type.133
  403.5 2.0 fusion.85
  (121 shorter events, 19.8 us)
Async XLA Ops:
  7.2 10.3 %copy-start = (s32[512]{0:T(512)S(1)}, s32[512]{0:T(512)}, u32[]{:S(2)}) copy-start(s32[512]{0:T(512)} %param.25) | copy-start | bytes 6148
  7.2 20.0 %copy-start.15 = (s32[128]{0:T(128)S(1)}, s32[128]{0:T(128)}, u32[]{:S(2)}) copy-start(s32[128]{0:T(128)} %param.24) | copy-start | bytes 1540
  7.2 74.8 %reduce-scatter.6.cloned.1.call-start = ((), (), s32[]{:S(2)}) async-start(), calls=%async_computation.8 | async-start | bytes 1179648 | tf_op jit(solution)/shard_map/reduce_scatter | solution.py:112
  27.2 5.2 %collective-permute-start = (bf16[128,2,128]{2,0,1:T(8,128)(2,1)S(1)}, bf16[128,2,128]{2,0,1:T(8,128)(2,1)S(1)}, u32[]{:S(2)}, u32[]{:S(2)}) collective-permute-start(bf16[128,2,128]{2,0,1:T(8,128)(2,1)S(1)} %get-tuple-element.503), channel_id=1, source_target_pairs={{0,8},{8,16},{16,24},{24,0},{1,9},{9,17},{17,25},{25,1},{2,10},{10... | collective-permute-start | bytes 196616 | tf_op jit(solution)/shard_map/while/body/eval_jaxpr/ppermute | solution.py:19
  33.0 5.3 %collective-permute-start = (bf16[128,2,128]{2,0,1:T(8,128)(2,1)S(1)}, bf16[128,2,128]{2,0,1:T(8,128)(2,1)S(1)}, u32[]{:S(2)}, u32[]{:S(2)}) collective-permute-start(bf16[128,2,128]{2,0,1:T(8,128)(2,1)S(1)} %get-tuple-element.503), channel_id=1, source_target_pairs={{0,8},{8,16},{16,24},{24,0},{1,9},{9,17},{17,25},{25,1},{2,10},{10... | collective-permute-start | bytes 196616 | tf_op jit(solution)/shard_map/while/body/eval_jaxpr/ppermute | solution.py:19
  39.0 5.2 %collective-permute-start = (bf16[128,2,128]{2,0,1:T(8,128)(2,1)S(1)}, bf16[128,2,128]{2,0,1:T(8,128)(2,1)S(1)}, u32[]{:S(2)}, u32[]{:S(2)}) collective-permute-start(bf16[128,2,128]{2,0,1:T(8,128)(2,1)S(1)} %get-tuple-element.503), channel_id=1, source_target_pairs={{0,8},{8,16},{16,24},{24,0},{1,9},{9,17},{17,25},{25,1},{2,10},{10... | collective-permute-start | bytes 196616 | tf_op jit(solution)/shard_map/while/body/eval_jaxpr/ppermute | solution.py:19
  44.8 37.2 %copy-start.14 = (bf16[16,4096]{1,0:T(8,128)(2,1)S(1)}, bf16[16,4096]{1,0:T(8,128)(2,1)}, u32[]{:S(2)}) copy-start(bf16[16,4096]{1,0:T(8,128)(2,1)} %param.14) | copy-start | bytes 393220
  44.8 38.3 %copy-start.13 = (f32[4096]{0:T(1024)S(1)}, f32[4096]{0:T(1024)}, u32[]{:S(2)}) copy-start(f32[4096]{0:T(1024)} %param.19) | copy-start | bytes 49156
  48.9 55.6 %all-gather.5.cloned.1.call-start = ((), (), s32[]{:S(2)}) async-start(), calls=%async_computation.9 | async-start | bytes 1179648 | tf_op jit(solution)/shard_map/all_gather | solution.py:122
  83.9 44.1 %all-gather.7.cloned.1.call-start = ((), (), s32[]{:S(2)}) async-start(), calls=%async_computation.11 | async-start | bytes 1179648 | tf_op jit(solution)/shard_map/all_gather | solution.py:136
  84.6 93.8 %reduce-scatter.10.cloned.1.call-start = ((), (), s32[]{:S(2)}) async-start(), calls=%async_computation.12 | async-start | bytes 1179648 | tf_op jit(solution)/shard_map/reduce_scatter | solution.py:144
  104.6 4.8 %copy-start.2 = (bf16[128,4096]{1,0:T(8,128)(2,1)S(1)}, bf16[128,4096]{1,0:T(8,128)(2,1)}, u32[]{:S(2)}) copy-start(bf16[128,4096]{1,0:T(8,128)(2,1)} %all-gather.5.cloned.1.call-done) | copy-start | bytes 3145732
  133.9 5.8 %copy-start.11 = (bf16[128,896]{1,0:T(8,128)(2,1)}, bf16[128,896]{1,0:T(8,128)(2,1)S(1)}, u32[]{:S(2)}) copy-start(bf16[128,896]{1,0:T(8,128)(2,1)S(1)} %get-tuple-element.394) | copy-start | bytes 688132
  133.9 12.3 %copy-start.7 = (bf16[128,896]{1,0:T(8,128)(2,1)}, bf16[128,896]{1,0:T(8,128)(2,1)S(1)}, u32[]{:S(2)}) copy-start(bf16[128,896]{1,0:T(8,128)(2,1)S(1)} %get-tuple-element.395) | copy-start | bytes 688132
  146.2 65.5 %reduce-scatter.8.cloned.1.call-start = ((), (), s32[]{:S(2)}) async-start(), calls=%async_computation.10 | async-start | bytes 1179648 | tf_op jit(solution)/shard_map/reduce_scatter | solution.py:129
  146.2 65.4 %copy-start.12 = (bf16[16,4096]{1,0:T(8,128)(2,1)S(1)}, bf16[16,4096]{1,0:T(8,128)(2,1)}, u32[]{:S(2)}) copy-start(bf16[16,4096]{1,0:T(8,128)(2,1)} %param.23) | copy-start | bytes 393220
  151.7 162.0 %all-gather.9.cloned.1.call-start = ((), (), s32[]{:S(2)}) async-start(), calls=%async_computation.13 | async-start | bytes 1179648 | tf_op jit(solution)/shard_map/all_gather | solution.py:161
  234.6 23.5 %copy-start.6 = (bf16[512,512]{0,1:T(8,128)(2,1)}, bf16[512,512]{0,1:T(8,128)(2,1)S(1)}, u32[]{:S(2)}) copy-start(bf16[512,512]{0,1:T(8,128)(2,1)S(1)} %all_gather.44) | copy-start | bytes 1572868
  237.0 21.1 %all-to-all-start.2 = ((bf16[128,4,1024]{0,2,1:T(8,128)(2,1)}), bf16[128,4,1024]{0,2,1:T(8,128)(2,1)}, u32[]{:S(2)}, u32[]{:S(2)}) async-start(bf16[128,4,1024]{0,2,1:T(8,128)(2,1)} %bitcast.39), calls=%async_computation.7 | async-start | bytes 2097152 | tf_op jit(solution)/shard_map/all_to_all | solution.py:252
  255.4 1.5 copy-start.10
  258.1 78.2 %copy-start.3 = (f32[4,512,128]{1,2,0:T(8,128)}, f32[4,512,128]{1,2,0:T(8,128)S(1)}, u32[]{:S(2)}) copy-start(f32[4,512,128]{1,2,0:T(8,128)S(1)} %fusion.20) | copy-start | bytes 3145732
  261.8 76.8 %all-to-all-start.1 = ((bf16[128,4,1024]{2,0,1:T(8,128)(2,1)}), bf16[128,4,1024]{2,0,1:T(8,128)(2,1)S(1)}, u32[]{:S(2)}, u32[]{:S(2)}) async-start(bf16[128,4,1024]{2,0,1:T(8,128)(2,1)} %bitcast.196), calls=%async_computation.6 | async-start | bytes 2097152 | tf_op jit(solution)/shard_map/all_to_all | solution.py:250
  265.4 133.2 %reduce-scatter.12.cloned.1.call-start = ((), (), s32[]{:S(2)}) async-start(), calls=%async_computation.14 | async-start | bytes 294912 | tf_op jit(solution)/shard_map/reduce_scatter | solution.py:242
  317.7 0.6 copy-start.9
  317.8 0.7 copy-start.8
  338.6 4.4 %copy-start.4 = (bf16[128,4096]{1,0:T(8,128)(2,1)S(1)}, bf16[128,4096]{1,0:T(8,128)(2,1)}, u32[]{:S(2)}) copy-start(bf16[128,4096]{1,0:T(8,128)(2,1)} %all-gather.9.cloned.1.call-done) | copy-start | bytes 3145732
  344.1 59.4 %all-to-all-start = ((bf16[128,4,1024]{2,0,1:T(8,128)(2,1)}), bf16[128,4,1024]{2,0,1:T(8,128)(2,1)S(1)}, u32[]{:S(2)}, u32[]{:S(2)}) async-start(bf16[128,4,1024]{2,0,1:T(8,128)(2,1)} %bitcast.195), calls=%async_computation.5 | async-start | bytes 2097152 | tf_op jit(solution)/shard_map/all_to_all | solution.py:251
  347.6 54.5 %reduce-scatter.14.cloned.1.call-start = ((), (), s32[]{:S(2)}) async-start(), calls=%async_computation.15 | async-start | bytes 294912 | tf_op jit(solution)/shard_map/reduce_scatter | solution.py:245
  350.6 52.9 %copy-start.5 = (bf16[512,512]{0,1:T(8,128)(2,1)S(1)}, bf16[512,512]{0,1:T(8,128)(2,1)}, u32[]{:S(2)}) copy-start(bf16[512,512]{0,1:T(8,128)(2,1)} %all_gather.48) | copy-start | bytes 1572868
  350.6 54.9 %copy-start.1 = (s32[512]{0:T(512)S(1)}, s32[512]{0:T(512)}, u32[]{:S(2)}) copy-start(s32[512]{0:T(512)} %param.25) | copy-start | bytes 6148
Sparse Core Ops, SparseCore 0:
  49.0 32.8 reduce-scatter.5
  84.2 20.3 all-gather.4
  106.2 21.7 all-gather.6
  146.3 32.0 reduce-scatter.9
  181.1 30.5 reduce-scatter.7
  213.7 20.2 all-gather.8
  338.7 32.2 reduce-scatter.11
  373.4 28.6 reduce-scatter.13
where the time goes:
time: 414 us; the launch traced here: 412 us
  blocking collectives  156 us (38%)
  waiting for transfers between devices  133 us (32%)
  matrix products  66.7 us (16%)
  local copies, waits for them, and re-layouts  17.8 us (4%)
  between operations  14.6 us (4%)
  starting transfers between devices  13.7 us (3%)
  other arithmetic  10.6 us (3%)
    psum x1, blocking collectives, body(): lax.psum(jnp.sum(grad_normed * hidden_f * inv_rms, axis=0), ('ctx', 'ffn'))  42.2 us
    reduce_scatter x1, waiting for transfers between devices, body(): lax.psum_scatter(jnp.dot(attended_rows, w_out, preferred_element_type=jnp...  33 us
    reduce_scatter x1, waiting for transfers between devices, body(): lax.psum_scatter(jnp.dot(activated, w_down, preferred_element_type=jnp.fl...  31.6 us
    all_gather x1, blocking collectives, body(): up_part = lax.all_gather(grad_up, 'ctx', axis=0, tiled=True)  21.3 us
    all_gather x1, waiting for transfers between devices, body(): normed_rows = lax.all_gather(normed, 'ffn', axis=0, tiled=True)  19.9 us
    reduce_scatter x1, waiting for transfers between devices, body(): lax.psum_scatter((jnp.dot(gate_part, w_gate.T, preferred_element_type=jnp...  18.2 us
    all_gather x1, waiting for transfers between devices, body(): cot_rows = lax.all_gather(cotangent, 'ffn', axis=0, tiled=True)  14.2 us
    all_gather x1, blocking collectives, body(): shard_rows = lax.all_gather(kv_pair, 'ctx', axis=0, tiled=True)  14.1 us
  transfers between devices with their start and end apart: 14, of which 9 were waited for; matrix products, arithmetic and copies ran while one was open for 13% of the time, Pallas kernels for 0%

commit v1 on v0

v1 whole, which is shorter than its diff:
```python
import functools
import math

import jax
import jax.numpy as jnp
from jax import lax
from jax.experimental import pallas as pl
from jax.experimental.pallas import tpu as pltpu
from jax.sharding import PartitionSpec as P

QUERY_HEADS = 32
KEY_VALUE_HEADS = 8
HEAD_WIDTH = 128
STRIPE = 64

masked_fill = -1e30
norm_eps = 1e-05
score_scale = 1.0 / math.sqrt(HEAD_WIDTH)

F32 = jnp.float32
BF16 = jnp.bfloat16
NN = (((1,), (0,)), ((), ()))
NT = (((1,), (1,)), ((), ()))
TN = (((0,), (0,)), ((), ()))
VMEM = pl.BlockSpec(memory_space=pltpu.VMEM)
SMEM = pl.BlockSpec(memory_space=pltpu.SMEM)
ANY = pl.BlockSpec(memory_space=pl.ANY)


def dot(a, b, dims=NN):
    return lax.dot_general(a, b, dims, preferred_element_type=F32)


def params(megabytes=48):
    return pltpu.CompilerParams(vmem_limit_bytes=megabytes * 1024 * 1024)


def log2(n):
    assert n & (n - 1) == 0
    return n.bit_length() - 1


def relative_rows(f, rows, n_f):
    share, half = rows // n_f, n_f // 2
    r = lax.broadcasted_iota(jnp.int32, (rows, rows), 0)
    natural = lax.broadcasted_iota(jnp.int32, (rows, rows), 1)
    j = lax.shift_right_logical(r, log2(share))
    k = lax.shift_left(j & (half - 1), 1) | lax.shift_right_logical(j, log2(half))
    return natural == lax.shift_left(k ^ f, log2(share)) + (r & (share - 1))


def visibility(same_row, pieces, doc_ref, rows):
    pos = []
    for piece in pieces:
        coded = piece[2 * rows :, :].astype(F32)
        pos.append(coded[0:1] * STRIPE + coded[1:2])
    key_pos = jnp.concatenate(pos, axis=1)
    total = doc_ref.shape[1]
    where_is = lax.broadcasted_iota(jnp.int32, (total, key_pos.shape[1]), 0).astype(F32) == key_pos
    docs = jnp.broadcast_to(doc_ref[...].astype(F32), (8, total)).astype(BF16)
    key_seg = dot(docs, where_is.astype(F32).astype(BF16))[0:1]

    def to_column(row):
        return jnp.sum(jnp.where(same_row, row[:, :rows], 0.0), axis=1, keepdims=True)

    return (key_pos <= to_column(key_pos)) & (key_seg == to_column(key_seg))


def keys_and_values(pieces, rows):
    return (
        jnp.concatenate([p[:rows] for p in pieces], axis=0),
        jnp.concatenate([p[rows : 2 * rows] for p in pieces], axis=0),
    )


def attention_kernel(n_f, n_c, f_ref, q_ref, doc_ref, w_hbm, *refs):
    pieces, (keep_ref, give_ref, att_ref, lse_ref, w_ref, sem) = refs[:n_c], refs[n_c:]
    copy = pltpu.make_async_copy(w_hbm, w_ref, sem)
    copy.start()
    rows, width = q_ref.shape
    same_row = relative_rows(f_ref[0], rows, n_f)
    visible = visibility(same_row, pieces, doc_ref, rows)
    keys, values = keys_and_values(pieces, rows)
    q = dot(same_row.astype(F32).astype(BF16), q_ref[...]).astype(BF16)
    lane = lax.broadcasted_iota(jnp.int32, (rows, HEAD_WIDTH), 1)
    log_totals = jnp.zeros((rows, HEAD_WIDTH), F32)
    for h in range(width // HEAD_WIDTH):
        cols = slice(h * HEAD_WIDTH, (h + 1) * HEAD_WIDTH)
        scores = jnp.where(visible, dot(q[:, cols], keys, NT) * score_scale, masked_fill)
        row_max = jnp.max(scores, axis=1, keepdims=True)
        weights = jnp.exp(scores - row_max)
        row_total = jnp.sum(weights, axis=1, keepdims=True)
        att_ref[:, cols] = (dot(weights.astype(BF16), values) / row_total).astype(BF16)
        log_totals = jnp.where(lane == h, row_max + jnp.log(row_total), log_totals)
    lse_ref[...] = log_totals
    copy.wait()
    att = att_ref[...]
    tile = 512
    for start in range(0, w_ref.shape[1], tile):
        out = dot(att, w_ref[:, start : start + tile]).astype(BF16)
        keep_ref[:, start : start + tile] = out[: rows // 2]
        give_ref[:, start : start + tile] = out[rows // 2 :]


def attention_call(f, queries, doc_row, w_out, pieces, n_f):
    rows, width = queries.shape
    depth = w_out.shape[1]
    half = jax.ShapeDtypeStruct((rows // 2, depth), BF16)
    return pl.pallas_call(
        functools.partial(attention_kernel, n_f, len(pieces)),
        out_shape=(
            half,
            half,
            jax.ShapeDtypeStruct((rows, width), BF16),
            jax.ShapeDtypeStruct((rows, HEAD_WIDTH), F32),
        ),
        in_specs=[SMEM, VMEM, VMEM, ANY] + [VMEM] * len(pieces),
        out_specs=[VMEM] * 4,
        scratch_shapes=[pltpu.VMEM(w_out.shape, BF16), pltpu.SemaphoreType.DMA],
        compiler_params=params(),
        name="attention_and_projection",
    )(f, queries, doc_row, w_out, *pieces)


def attention_grad_kernel(
    n_f, n_c, f_ref, q_ref, doc_ref, att_ref, lse_ref, ga_ref, gb_ref, w_hbm, *refs
):
    pieces, (dq_ref, dkv_ref, w_ref, sem) = refs[:n_c], refs[n_c:]
    copy = pltpu.make_async_copy(w_hbm, w_ref, sem)
    copy.start()
    rows, width = q_ref.shape
    same_row = relative_rows(f_ref[0], rows, n_f)
    visible = visibility(same_row, pieces, doc_ref, rows)
    keys, values = keys_and_values(pieces, rows)
    order = same_row.astype(F32).astype(BF16)
    q = dot(order, q_ref[...]).astype(BF16)
    copy.wait()
    grad_rows = jnp.concatenate([ga_ref[...], gb_ref[...]], axis=0)
    grad_att = dot(grad_rows, w_ref[...], NT).astype(BF16)
    grad_keys = jnp.zeros(keys.shape, F32)
    grad_values = jnp.zeros(keys.shape, F32)
    grad_q = []
    for h in range(width // HEAD_WIDTH):
        cols = slice(h * HEAD_WIDTH, (h + 1) * HEAD_WIDTH)
        g = grad_att[:, cols]
        scores = jnp.where(visible, dot(q[:, cols], keys, NT) * score_scale, masked_fill)
        probs = jnp.exp(scores - lse_ref[:, h : h + 1])
        delta = jnp.sum(g.astype(F32) * att_ref[:, cols].astype(F32), axis=1, keepdims=True)
        grad_scores = (probs * (dot(g, values, NT) - delta)).astype(BF16)
        grad_q.append((dot(grad_scores, keys) * score_scale).astype(BF16))
        grad_keys = grad_keys + dot(grad_scores, q[:, cols], TN)
        grad_values = grad_values + dot(probs.astype(BF16), g, TN)
    dq_ref[...] = dot(order, jnp.concatenate(grad_q, axis=1), TN).astype(BF16)
    dkv_ref[:, :HEAD_WIDTH] = (grad_keys * score_scale).astype(BF16)
    dkv_ref[:, HEAD_WIDTH:] = grad_values.astype(BF16)


def attention_grad_call(f, queries, doc_row, att, lse, grad_a, grad_b, w_out, pieces, n_f):
    rows, width = queries.shape
    return pl.pallas_call(
        functools.partial(attention_grad_kernel, n_f, len(pieces)),
        out_shape=(
            jax.ShapeDtypeStruct((rows, width), BF16),
            jax.ShapeDtypeStruct((rows * len(pieces), 2 * HEAD_WIDTH), BF16),
        ),
        in_specs=[SMEM] + [VMEM] * 6 + [ANY] + [VMEM] * len(pieces),
        out_specs=[VMEM] * 2,
        scratch_shapes=[pltpu.VMEM(w_out.shape, BF16), pltpu.SemaphoreType.DMA],
        compiler_params=params(),
        name="attention_gradients",
    )(f, queries, doc_row, att, lse, grad_a, grad_b, w_out, *pieces)


def norm_kernel(resid_ref, gain_ref, *refs):
    terms, (hidden_ref, normed_ref) = refs[:-2], refs[-2:]
    total = resid_ref[...].astype(F32)
    total = total + functools.reduce(jnp.add, [t[...].astype(F32) for t in terms])
    hidden = total.astype(BF16)
    hidden_ref[...] = hidden
    hidden = hidden.astype(F32)
    inv_rms = lax.rsqrt(jnp.mean(hidden * hidden, axis=1, keepdims=True) + norm_eps)
    normed_ref[...] = (hidden * inv_rms * gain_ref[...]).astype(BF16)


def norm_call(resid, gain_row, terms):
    out = jax.ShapeDtypeStruct(resid.shape, BF16)
    return pl.pallas_call(
        norm_kernel,
        out_shape=(out, out),
        in_specs=[VMEM] * (2 + len(terms)),
        out_specs=[VMEM] * 2,
        compiler_params=params(),
        name="residual_and_norm",
    )(resid, gain_row, *terms)


def norm_grad_kernel(cot_ref, hidden_ref, gain_ref, *refs):
    terms, (grad_ref, gain_grad_ref) = refs[:-2], refs[-2:]
    grad_normed = functools.reduce(jnp.add, [t[...].astype(F32) for t in terms])
    hidden = hidden_ref[...].astype(F32)
    inv_rms = lax.rsqrt(jnp.mean(hidden * hidden, axis=1, keepdims=True) + norm_eps)
    gained = grad_normed * gain_ref[...]
    inv_cube = inv_rms * inv_rms * inv_rms
    grad_ref[...] = (
        cot_ref[...].astype(F32)
        + inv_rms * gained
        - hidden * inv_cube * jnp.mean(gained * hidden, axis=1, keepdims=True)
    ).astype(BF16)
    gain_grad_ref[...] = jnp.sum(grad_normed * hidden * inv_rms, axis=0, keepdims=True)


def norm_grad_call(cot, hidden, gain_row, terms):
    return pl.pallas_call(
        norm_grad_kernel,
        out_shape=(
            jax.ShapeDtypeStruct(cot.shape, BF16),
            jax.ShapeDtypeStruct(gain_row.shape, F32),
        ),
        in_specs=[VMEM] * (3 + len(terms)),
        out_specs=[VMEM] * 2,
        compiler_params=params(),
        name="norm_gradients",
    )(cot, hidden, gain_row, *terms)


def gate_up_kernel(xa_ref, xb_ref, wg_ref, wu_ref, ga_ref, out_ref, gate_acc, up_acc):
    depth, width = wg_ref.shape
    half = xa_ref.shape[0]
    tile = 512
    gate_acc[...] = jnp.zeros_like(gate_acc)
    up_acc[...] = jnp.zeros_like(up_acc)

    @pl.loop(0, depth // tile)
    def _(step):
        at = pl.ds(pl.multiple_of(step * tile, tile), tile)
        x = jnp.concatenate([xa_ref[:, at], xb_ref[:, at]], axis=0)
        gate_acc[...] += dot(x, wg_ref[at, :])
        up_acc[...] += dot(x, wu_ref[at, :])

    gate, up, grad_act = gate_acc[...], up_acc[...], ga_ref[...]
    sig = jax.nn.sigmoid(gate)
    out_ref[:, :width] = (gate * sig * up).astype(BF16)
    out_ref[:, width : 2 * width] = (grad_act * up * sig * (1.0 + gate * (1.0 - sig))).astype(BF16)
    out_ref[:, 2 * width :] = (grad_act * gate * sig).astype(BF16)


def gate_up_call(xa, xb, w_gate, w_up, grad_act):
    depth, width = w_gate.shape
    rows = grad_act.shape[0]
    return pl.pallas_call(
        gate_up_kernel,
        out_shape=jax.ShapeDtypeStruct((rows, 3 * width), BF16),
        in_specs=[VMEM] * 5,
        out_specs=VMEM,
        scratch_shapes=[pltpu.VMEM((rows, width), F32)] * 2,
        compiler_params=params(24),
        name="gate_up_and_gradients",
    )(xa, xb, w_gate, w_up, grad_act)


def normed_grad_kernel(pay_ref, wg_ref, wu_ref, keep_ref, give_ref):
    depth, width = wg_ref.shape
    half = keep_ref.shape[0]
    tile = 512

    @pl.loop(0, depth // tile)
    def _(step):
        at = pl.ds(pl.multiple_of(step * tile, tile), tile)
        out = dot(pay_ref[:, width : 2 * width], wg_ref[at, :], NT)
        out = (out + dot(pay_ref[:, 2 * width :], wu_ref[at, :], NT)).astype(BF16)
        keep_ref[:, at] = out[:half]
        give_ref[:, at] = out[half:]


def normed_grad_call(pay, w_gate, w_up):
    depth, width = w_gate.shape
    rows = pay.shape[0]
    out = jax.ShapeDtypeStruct((rows // 2, depth), BF16)
    return pl.pallas_call(
        normed_grad_kernel,
        out_shape=(out, out),
        in_specs=[VMEM] * 3,
        out_specs=[VMEM] * 2,
        compiler_params=params(24),
        name="normed_gradients",
    )(pay, w_gate, w_up)


def down_kernel(pay_ref, w_ref, keep_ref, give_ref):
    out = dot(pay_ref[:, : w_ref.shape[0]], w_ref[...]).astype(BF16)
    half = keep_ref.shape[0]
    keep_ref[...] = out[:half]
    give_ref[...] = out[half:]


def down_call(pay, w_down, tile=512):
    width, depth = w_down.shape
    rows = pay.shape[0]
    o_spec = pl.BlockSpec((rows // 2, tile), lambda i: (0, i))
    out = jax.ShapeDtypeStruct((rows // 2, depth), BF16)
    return pl.pallas_call(
        down_kernel,
        grid=(depth // tile,),
        out_shape=(out, out),
        in_specs=[
            pl.BlockSpec(pay.shape, lambda i: (0, 0)),
            pl.BlockSpec((width, tile), lambda i: (0, i)),
        ],
        out_specs=[o_spec, o_spec],
        compiler_params=params(),
        name="down_projection",
    )(pay, w_down)


def body(
    resid_in,
    queries,
    keys_in,
    value_rows_input,
    w_out,
    norm_gain,
    w_gate,
    w_up,
    w_down,
    cotangent,
    positions,
    doc_ids,
):
    rows = queries.shape[0]
    heads = queries.shape[1] // HEAD_WIDTH
    n_c, n_f = lax.axis_size("ctx"), lax.axis_size("ffn")
    c, f = lax.axis_index("ctx"), lax.axis_index("ffn")
    share, half = rows // n_f, n_f // 2
    depth = resid_in.shape[1]
    hidden_units = w_gate.shape[1]
    group = f * heads // (QUERY_HEADS // KEY_VALUE_HEADS)
    f_ref = f.astype(jnp.int32).reshape(1)
    gain_row = norm_gain.reshape(1, depth)
    doc_row = doc_ids.reshape(1, -1)

    def exchange(x, axis, k):
        return lax.ppermute(x, axis, [(i, i ^ k) for i in range(lax.axis_size(axis))])

    def gather_rows(x):
        mine = jnp.concatenate([x] + [exchange(x, "ffn", 2 * m) for m in range(1, half)], axis=0)
        return mine, exchange(mine, "ffn", 1)

    def scatter_rows(keep, give):
        total = (keep.astype(F32) + exchange(give, "ffn", 1).astype(F32)).astype(BF16)
        blocks = [total[m * share : (m + 1) * share] for m in range(half)]
        return [blocks[0]] + [exchange(blocks[m], "ffn", 2 * m) for m in range(1, half)]

    def gather_ctx(x):
        return jnp.concatenate([x] + [exchange(x, "ctx", k) for k in range(1, n_c)], axis=0)

    def sum_everywhere(x):
        x = x + exchange(x, "ffn", 1)
        x = functools.reduce(jnp.add, [x] + [exchange(x, "ffn", 2 * m) for m in range(1, half)])
        return functools.reduce(jnp.add, [x] + [exchange(x, "ctx", k) for k in range(1, n_c)])

    col_count = depth // n_c

    def gather_columns(a, b):
        def part(k):
            start = (c ^ k) * col_count
            return jnp.concatenate(
                [lax.dynamic_slice_in_dim(t, start, col_count, 1) for t in (a, b)], axis=0
            )

        return jnp.concatenate([part(0)] + [exchange(part(k), "ctx", k) for k in range(1, n_c)], 0)

    def head_slice(x):
        return lax.dynamic_slice_in_dim(x, group * HEAD_WIDTH, HEAD_WIDTH, 1)

    coded = jnp.concatenate([positions // STRIPE, positions % STRIPE]).astype(BF16)
    coded = coded.reshape(2, -1)
    coded = jnp.concatenate([coded, jnp.zeros((14, coded.shape[1]), BF16)], axis=0)
    payload = jnp.concatenate([head_slice(keys_in), head_slice(value_rows_input), coded], axis=0)
    pieces = [payload] + [exchange(payload, "ctx", k) for k in range(1, n_c)]
    cot_a, cot_b = gather_rows(cotangent)

    keep, give, att, lse = attention_call(f_ref, queries, doc_row, w_out, pieces, n_f)
    hidden, normed = norm_call(resid_in, gain_row, scatter_rows(keep, give))
    normed_a, normed_b = gather_rows(normed)

    grad_act = dot(jnp.concatenate([cot_a, cot_b], axis=0), w_down, NT)
    cot_cols = gather_columns(cot_a, cot_b)
    att_all = gather_ctx(att)

    pay = gate_up_call(normed_a, normed_b, w_gate, w_up, grad_act)
    keep, give = normed_grad_call(pay, w_gate, w_up)
    terms = scatter_rows(keep, give)
    pay_all = gather_ctx(pay)
    normed_cols = gather_columns(normed_a, normed_b)
    down_keep, down_give = down_call(pay, w_down)
    grad_resid, gain_part = norm_grad_call(cotangent, hidden, gain_row, terms)
    grad_a, grad_b = gather_rows(grad_resid)
    grad_gain = sum_everywhere(gain_part).reshape(depth)

    grad_w_down = dot(pay_all[:, :hidden_units], cot_cols, TN)
    grad_w_gate = dot(normed_cols, pay_all[:, hidden_units : 2 * hidden_units], TN)
    grad_w_up = dot(normed_cols, pay_all[:, 2 * hidden_units :], TN)

    grad_queries, dkv = attention_grad_call(
        f_ref, queries, doc_row, att, lse, grad_a, grad_b, w_out, pieces, n_f
    )
    grad_cols = gather_columns(grad_a, grad_b)
    grad_w_out = dot(att_all, grad_cols, TN)

    mixed_terms = scatter_rows(down_keep, down_give)
    mixed = functools.reduce(jnp.add, [t.astype(F32) for t in mixed_terms])
    mixed = (hidden.astype(F32) + mixed).astype(BF16)

    dkv_own = dkv[:rows].astype(F32)
    for k in range(1, n_c):
        dkv_own = dkv_own + exchange(dkv[k * rows : (k + 1) * rows], "ctx", k).astype(F32)
    dkv_own = dkv_own.astype(BF16).reshape(n_f, share, 2 * HEAD_WIDTH)
    dkv_heads = lax.all_to_all(dkv_own, "ffn", 0, 0).astype(F32)
    dkv_heads = dkv_heads.reshape(
        KEY_VALUE_HEADS, n_f // KEY_VALUE_HEADS, share, 2, HEAD_WIDTH
    ).sum(axis=1)
    dkv_heads = jnp.transpose(dkv_heads, (2, 1, 0, 3)).reshape(2, share, -1)
    return (
        mixed,
        grad_resid,
        grad_queries,
        dkv_heads[0],
        dkv_heads[1],
        grad_gain,
        grad_w_out,
        grad_w_gate,
        grad_w_up,
        grad_w_down,
    )


def solution(mesh):
    return jax.shard_map(
        body,
        mesh=mesh,
        in_specs=(
            P(("ctx", "ffn"), None),
            P("ctx", "ffn"),
            P("ctx", None),
            P("ctx", None),
            P("ffn", None),
            P(),
            P(None, "ffn"),
            P(None, "ffn"),
            P("ffn", None),
            P(("ctx", "ffn"), None),
            P("ctx"),
            P(),
        ),
        out_specs=(
            P(("ctx", "ffn"), None),
            P(("ctx", "ffn"), None),
            P("ctx", "ffn"),
            P(("ctx", "ffn"), None),
            P(("ctx", "ffn"), None),
            P(),
            P("ffn", "ctx"),
            P("ctx", "ffn"),
            P("ctx", "ffn"),
            P("ffn", "ctx"),
        ),
        check_vma=False,
    )
```

time: 414 us -> 204 us (0.49)
  blocking collectives: 156 us -> 0 us
  waiting for transfers between devices: 133 us -> 62.1 us
  starting transfers between devices: 13.7 us -> 79.5 us
  matrix products: 66.7 us -> 17.9 us
  Pallas kernels: 0 us -> 23.9 us
  between operations: 14.6 us -> 1.34 us
  local copies, waits for them, and re-layouts: 17.8 us -> 10.5 us
    all_gather x10 -> x0, blocking collectives: 114 us -> none  [the longest x1 21.3 us: body(): up_part = lax.all_gather(grad_up, 'ctx', axis=0, tiled=True)]
    reduce_scatter x5 -> x0, waiting for transfers between devices: 85 us -> none  [the longest x1 33 us: body(): lax.psum_scatter(jnp.dot(attended_rows, w_out, preferred_element_type=jnp...]
    ppermute x3 -> x52, starting transfers between devices: 2.06 us -> 75.6 us  [exchange(): lax.ppermute(x, axis, [(i, i ^ k) for i in range(lax.axis_size(axis))])]
    dot_general x25 -> x5, matrix products: 66.7 us -> 17.9 us  [dot(): return lax.dot_general(a, b, dims, preferred_element_type=F32)]
    ppermute x3 -> x52, waiting for transfers between devices: 12.9 us -> 58.2 us  [exchange(): lax.ppermute(x, axis, [(i, i ^ k) for i in range(lax.axis_size(axis))])]
    psum x1 -> x0, blocking collectives: 42.2 us -> none  [body(): lax.psum(jnp.sum(grad_normed * hidden_f * inv_rms, axis=0), ('ctx', 'ffn'))]
    all_gather x3 -> x0, waiting for transfers between devices: 34.1 us -> none  [the longest x1 19.9 us: body(): normed_rows = lax.all_gather(normed, 'ffn', axis=0, tiled=True)]
    pallas_call x0 -> x7, Pallas kernels: none -> 23.9 us  [the longest x1 6.57 us: down_call(): pl.pallas_call(down_kernel, grid=(depth // tile,), out_shape=(out, out),...]
  transfers between devices with their start and end apart: 14 -> 53, of which waited for: 9 -> 19; matrix products, arithmetic and copies ran while one was open for 13% -> 14% of each run, Pallas kernels for 0% -> 12%
where the time goes in v1:
time: 204 us; the launch traced here: 203 us
  starting transfers between devices  79.5 us (39%)
  waiting for transfers between devices  62.1 us (30%)
  Pallas kernels  23.9 us (12%)
  matrix products  17.9 us (9%)
  local copies, waits for them, and re-layouts  10.5 us (5%)
  other arithmetic  7.81 us (4%)
    ppermute x52, starting transfers between devices, exchange(): lax.ppermute(x, axis, [(i, i ^ k) for i in range(lax.axis_size(axis))])  75.6 us
    ppermute x52, waiting for transfers between devices, exchange(): lax.ppermute(x, axis, [(i, i ^ k) for i in range(lax.axis_size(axis))])  58.2 us
    dot_general x5, matrix products, dot(): return lax.dot_general(a, b, dims, preferred_element_type=F32)  17.9 us
    unnamed x43, local copies, waits for them, and re-layouts  8.09 us
    pallas_call x1, Pallas kernels, down_call(): pl.pallas_call(down_kernel, grid=(depth // tile,), out_shape=(out, out),...  6.57 us
    pallas_call x1, Pallas kernels, normed_grad_call(): pl.pallas_call(normed_grad_kernel, out_shape=(out, out), in_specs=[VMEM]...  5.79 us
    pallas_call x1, Pallas kernels, attention_grad_call(): pl.pallas_call(functools.partial(attention_grad_kernel, n_f, len(pieces))...  4.16 us
  transfers between devices with their start and end apart: 53, of which 19 were waited for; matrix products, arithmetic and copies ran while one was open for 14% of the time, Pallas kernels for 12%

profile of v1, /device:TPU:0, one launch (start us, length us, event | category | flops | bytes accessed | tf_op | source)
XLA Modules:
  0.0 203.1 jit_solution(10834382723842858551)
XLA Ops:
  0.6 3.1 %collective-permute-start.11 = (bf16[16,4096]{1,0:T(8,128)(2,1)}, bf16[16,4096]{1,0:T(8,128)(2,1)S(1)}, u32[]{:S(2)}, u32[]{:S(2)}) collective-permute-start(bf16[16,4096]{1,0:T(8,128)(2,1)} %cot_ref.1), channel_id=1, source_target_pairs={{0,2},{1,3},{2,0},{3,1},{4,6},{5,7},{6,4},{7,5},{8,10},{9,11},{10,... | collective-permute-start | bytes 393224 | tf_op jit(solution)/shard_map/ppermute | solution.py:342
  3.7 2.6 %collective-permute-start.12 = (bf16[16,4096]{1,0:T(8,128)(2,1)}, bf16[16,4096]{1,0:T(8,128)(2,1)S(1)}, u32[]{:S(2)}, u32[]{:S(2)}) collective-permute-start(bf16[16,4096]{1,0:T(8,128)(2,1)} %cot_ref.1), channel_id=1, source_target_pairs={{0,4},{1,5},{2,6},{3,7},{4,0},{5,1},{6,2},{7,3},{8,12},{9,13},{10,... | collective-permute-start | bytes 393224 | tf_op jit(solution)/shard_map/ppermute | solution.py:342
  8.0 1.6 collective-permute-start
  12.6 2.0 collective-permute-done.1.refs_2_
  14.6 1.7 collective-permute-done.2.refs_3_
  16.3 2.2 %copy-done.1 = bf16[512,4096]{1,0:T(8,128)(2,1)S(1)} copy-done((bf16[512,4096]{1,0:T(8,128)(2,1)S(1)}, bf16[512,4096]{1,0:T(8,128)(2,1)}, u32[]{:S(2)}) %copy-start.1) | copy-done | bytes 4194328
  20.0 2.4 %attention_and_projection.1 = (bf16[64,4096]{1,0:T(8,128)(2,1)S(1)}, bf16[64,4096]{1,0:T(8,128)(2,1)S(1)}, bf16[128,512]{1,0:T(8,128)(2,1)S(1)}, f32[128,128]{1,0:T(8,128)S(1)}) custom-call(s32[1]{0:T(128)} %bitcast.1.f_ref, bf16[128,512]{1,0:T(8,128)(2,1)S(1)} %copy-done.4, s32[1,512]{1,0:T(1,128)S(1)} %bitcast.30, bf16[512,4096]{1,0:T(8,128)(2,1)S(1)} %copy-done.1, ...), custom_call_target="tpu_custom_call" | custom-call | tf_op jit(solution)/shard_map/attention_and_projection/pallas_call | solution.py:109
  25.5 3.6 %collective-permute-start.6 = (bf16[16,4096]{1,0:T(8,128)(2,1)S(1)}, bf16[16,4096]{1,0:T(8,128)(2,1)S(1)}, u32[]{:S(2)}, u32[]{:S(2)}) collective-permute-start(bf16[16,4096]{1,0:T(8,128)(2,1)S(1)} %get-tuple-element.69), channel_id=1, source_target_pairs={{0,6},{1,7},{2,4},{3,5},{4,2},{5,3},{6,0},{7,1},{8,14},{9,15},{10,... | collective-permute-start | bytes 393224 | tf_op jit(solution)/shard_map/ppermute | solution.py:342
  31.8 1.8 collective-permute-start.51
  33.5 4.5 %collective-permute-done.5.refs_2_ = bf16[16,4096]{1,0:T(8,128)(2,1)S(1)} collective-permute-done((bf16[16,4096]{1,0:T(8,128)(2,1)S(1)}, bf16[16,4096]{1,0:T(8,128)(2,1)S(1)}, u32[]{:S(2)}, u32[]{:S(2)}) %collective-permute-start.5) | collective-permute-done | bytes 131104 | tf_op jit(solution)/shard_map/ppermute | solution.py:342
  38.2 2.4 %collective-permute-start.7 = (bf16[16,4096]{1,0:T(8,128)(2,1)S(1)}, bf16[16,4096]{1,0:T(8,128)(2,1)S(1)}, u32[]{:S(2)}, u32[]{:S(2)}) collective-permute-start(bf16[16,4096]{1,0:T(8,128)(2,1)S(1)} %get-tuple-element.27), channel_id=1, source_target_pairs={{0,2},{1,3},{2,0},{3,1},{4,6},{5,7},{6,4},{7,5},{8,10},{9,11},{10,... | collective-permute-start | bytes 393224 | tf_op jit(solution)/shard_map/ppermute | solution.py:342
  40.7 3.7 %collective-permute-done.7 = bf16[16,4096]{1,0:T(8,128)(2,1)S(1)} collective-permute-done((bf16[16,4096]{1,0:T(8,128)(2,1)S(1)}, bf16[16,4096]{1,0:T(8,128)(2,1)S(1)}, u32[]{:S(2)}, u32[]{:S(2)}) %collective-permute-start.7) | collective-permute-done | bytes 131104 | tf_op jit(solution)/shard_map/ppermute | solution.py:342
  44.4 1.7 collective-permute-start.9
  46.1 6.2 %collective-permute-done.8 = bf16[16,4096]{1,0:T(8,128)(2,1)S(1)} collective-permute-done((bf16[16,4096]{1,0:T(8,128)(2,1)S(1)}, bf16[16,4096]{1,0:T(8,128)(2,1)S(1)}, u32[]{:S(2)}, u32[]{:S(2)}) %collective-permute-start.8) | collective-permute-done | bytes 131104 | tf_op jit(solution)/shard_map/ppermute | solution.py:342
  52.5 5.7 %fusion.22.ga_ref = f32[128,896]{1,0:T(8,128)S(1)} fusion(bf16[128,4096]{1,0:T(8,128)(2,1)S(1)} %constant_dynamic-update-slice_fusion.8, bf16[896,4096]{1,0:T(8,128)(2,1)} %w_ref.1), kind=kOutput, calls=%fused_computation.101 | convolution fusion | flops 939524096 | bytes 8847360 | tf_op jit(solution)/shard_map/dot_general | solution.py:31
  59.3 3.9 %gate_up_and_gradients.1.pay_ref = bf16[128,2688]{1,0:T(8,128)(2,1)S(1)} custom-call(bf16[64,4096]{1,0:T(8,128)(2,1)S(1)} %constant_dynamic-update-slice_fusion.xa_ref, bf16[64,4096]{1,0:T(8,128)(2,1)S(1)} %collective-permute-done.10.xb_ref, bf16[4096,896]{1,0:T(8,128)(2,1)S(1)} %bitcast.27, bf16[4096,896]{1,0:T(8,128)(2,1)S(1)} %copy-done, ...), custom_call_target="tpu_custom_call" | custom-call | tf_op jit(solution)/shard_map/gate_up_and_gradients/pallas_call | solution.py:250
  63.2 5.8 %normed_gradients.1 = (bf16[64,4096]{1,0:T(8,128)(2,1)S(1)}, bf16[64,4096]{1,0:T(8,128)(2,1)S(1)}) custom-call(bf16[128,2688]{1,0:T(8,128)(2,1)S(1)} %gate_up_and_gradients.1.pay_ref, bf16[4096,896]{1,0:T(8,128)(2,1)S(1)} %bitcast.27, bf16[4096,896]{1,0:T(8,128)(2,1)S(1)} %copy-done), custom_call_target="tpu_custom_call" | custom-call | tf_op jit(solution)/shard_map/normed_gradients/pallas_call | solution.py:279
  71.0 6.6 %down_projection.1 = (bf16[64,4096]{1,0:T(8,128)(2,1)S(1)}, bf16[64,4096]{1,0:T(8,128)(2,1)S(1)}) custom-call(bf16[128,2688]{1,0:T(8,128)(2,1)S(1)} %gate_up_and_gradients.1.pay_ref, bf16[896,4096]{1,0:T(8,128)(2,1)} %w_ref.1), custom_call_target="tpu_custom_call" | custom-call | tf_op jit(solution)/shard_map/down_projection/pallas_call | solution.py:301
  78.5 2.2 %collective-permute-start.45 = (bf16[128,1024]{1,0:T(8,128)(2,1)S(1)}, bf16[128,1024]{1,0:T(8,128)(2,1)S(1)}, u32[]{:S(2)}, u32[]{:S(2)}) collective-permute-start(bf16[128,1024]{1,0:T(8,128)(2,1)S(1)} %pad_maximum_fusion.6), channel_id=1, source_target_pairs={{0,24},{8,16},{16,8},{24,0},{1,25},{9,17},{17,9},{25,1},{2,26},{10... | collective-permute-start | bytes 786440 | tf_op jit(solution)/shard_map/ppermute | solution.py:342
  81.0 2.5 %collective-permute-start.20 = (bf16[16,4096]{1,0:T(8,128)(2,1)S(1)}, bf16[16,4096]{1,0:T(8,128)(2,1)S(1)}, u32[]{:S(2)}, u32[]{:S(2)}) collective-permute-start(bf16[16,4096]{1,0:T(8,128)(2,1)S(1)} %get-tuple-element.64), channel_id=1, source_target_pairs={{0,2},{1,3},{2,0},{3,1},{4,6},{5,7},{6,4},{7,5},{8,10},{9,11},{10,... | collective-permute-start | bytes 393224 | tf_op jit(solution)/shard_map/ppermute | solution.py:342
  83.5 2.4 %collective-permute-start.22 = (bf16[16,4096]{1,0:T(8,128)(2,1)S(1)}, bf16[16,4096]{1,0:T(8,128)(2,1)S(1)}, u32[]{:S(2)}, u32[]{:S(2)}) collective-permute-start(bf16[16,4096]{1,0:T(8,128)(2,1)S(1)} %get-tuple-element.62), channel_id=1, source_target_pairs={{0,6},{1,7},{2,4},{3,5},{4,2},{5,3},{6,0},{7,1},{8,14},{9,15},{10,... | collective-permute-start | bytes 393224 | tf_op jit(solution)/shard_map/ppermute | solution.py:342
  86.1 5.3 %collective-permute-done.44 = bf16[128,1024]{1,0:T(8,128)(2,1)S(1)} collective-permute-done((bf16[128,1024]{1,0:T(8,128)(2,1)S(1)}, bf16[128,1024]{1,0:T(8,128)(2,1)S(1)}, u32[]{:S(2)}, u32[]{:S(2)}) %collective-permute-start.44) | collective-permute-done | bytes 262176 | tf_op jit(solution)/shard_map/ppermute | solution.py:342
  91.4 2.5 %collective-permute-start.16 = (bf16[16,4096]{1,0:T(8,128)(2,1)S(1)}, bf16[16,4096]{1,0:T(8,128)(2,1)S(1)}, u32[]{:S(2)}, u32[]{:S(2)}) collective-permute-start(bf16[16,4096]{1,0:T(8,128)(2,1)S(1)} %get-tuple-element.66), channel_id=1, source_target_pairs={{0,2},{1,3},{2,0},{3,1},{4,6},{5,7},{6,4},{7,5},{8,10},{9,11},{10,... | collective-permute-start | bytes 393224 | tf_op jit(solution)/shard_map/ppermute | solution.py:342
  93.9 2.4 %collective-permute-start.18 = (bf16[16,4096]{1,0:T(8,128)(2,1)S(1)}, bf16[16,4096]{1,0:T(8,128)(2,1)S(1)}, u32[]{:S(2)}, u32[]{:S(2)}) collective-permute-start(bf16[16,4096]{1,0:T(8,128)(2,1)S(1)} %get-tuple-element.67), channel_id=1, source_target_pairs={{0,6},{1,7},{2,4},{3,5},{4,2},{5,3},{6,0},{7,1},{8,14},{9,15},{10,... | collective-permute-start | bytes 393224 | tf_op jit(solution)/shard_map/ppermute | solution.py:342
  100.1 7.5 %collective-permute-done.17 = bf16[16,4096]{1,0:T(8,128)(2,1)S(1)} collective-permute-done((bf16[16,4096]{1,0:T(8,128)(2,1)S(1)}, bf16[16,4096]{1,0:T(8,128)(2,1)S(1)}, u32[]{:S(2)}, u32[]{:S(2)}) %collective-permute-start.17) | collective-permute-done | bytes 131104 | tf_op jit(solution)/shard_map/ppermute | solution.py:342
  111.4 6.9 %collective-permute-done.46 = bf16[128,2688]{1,0:T(8,128)(2,1)S(1)} collective-permute-done((bf16[128,2688]{1,0:T(8,128)(2,1)S(1)}, bf16[128,2688]{1,0:T(8,128)(2,1)S(1)}, u32[]{:S(2)}, u32[]{:S(2)}) %collective-permute-start.46) | collective-permute-done | bytes 688160 | tf_op jit(solution)/shard_map/ppermute | solution.py:342
  118.3 5.4 %collective-permute-start.31 = (f32[1,4096]{1,0:T(1,128)S(1)}, f32[1,4096]{1,0:T(1,128)S(1)}, u32[]{:S(2)}, u32[]{:S(2)}) collective-permute-start(f32[1,4096]{1,0:T(1,128)S(1)} %add.107), channel_id=1, source_target_pairs={{0,2},{1,3},{2,0},{3,1},{4,6},{5,7},{6,4},{7,5},{8,10},{9,11},{10,... | collective-permute-start | bytes 49160 | tf_op jit(solution)/shard_map/ppermute | solution.py:342
  123.8 8.1 %collective-permute-done.47 = bf16[128,2688]{1,0:T(8,128)(2,1)S(1)} collective-permute-done((bf16[128,2688]{1,0:T(8,128)(2,1)S(1)}, bf16[128,2688]{1,0:T(8,128)(2,1)S(1)}, u32[]{:S(2)}, u32[]{:S(2)}) %collective-permute-start.47) | collective-permute-done | bytes 688160 | tf_op jit(solution)/shard_map/ppermute | solution.py:342
  131.9 2.4 %collective-permute-start.32 = (f32[1,4096]{1,0:T(1,128)S(1)}, f32[1,4096]{1,0:T(1,128)S(1)}, u32[]{:S(2)}, u32[]{:S(2)}) collective-permute-start(f32[1,4096]{1,0:T(1,128)S(1)} %add.107), channel_id=1, source_target_pairs={{0,4},{1,5},{2,6},{3,7},{4,0},{5,1},{6,2},{7,3},{8,12},{9,13},{10,... | collective-permute-start | bytes 49160 | tf_op jit(solution)/shard_map/ppermute | solution.py:342
  134.3 6.6 %collective-permute-start.33 = (f32[1,4096]{1,0:T(1,128)S(1)}, f32[1,4096]{1,0:T(1,128)S(1)}, u32[]{:S(2)}, u32[]{:S(2)}) collective-permute-start(f32[1,4096]{1,0:T(1,128)S(1)} %add.107), channel_id=1, source_target_pairs={{0,6},{1,7},{2,4},{3,5},{4,2},{5,3},{6,0},{7,1},{8,14},{9,15},{10,... | collective-permute-start | bytes 49160 | tf_op jit(solution)/shard_map/ppermute | solution.py:342
  140.9 3.7 %pad_maximum_fusion = bf16[512,2688]{1,0:T(8,128)(2,1)S(1)} fusion(bf16[128,2688]{1,0:T(8,128)(2,1)S(1)} %collective-permute-done.48, bf16[128,2688]{1,0:T(8,128)(2,1)S(1)} %collective-permute-done.47, bf16[128,2688]{1,0:T(8,128)(2,1)S(1)} %collective-permute-done.46, bf16[128,2688]{1,0:T(8,128)(2,1)S(1)} %gate_up_and_gradients.1.pay_ref), kind=kLoop, calls=%fused_computation | loop fusion | flops 11010048 | bytes 5505024 | tf_op jit(solution)/shard_map/concatenate | solution.py:354
  144.6 3.1 %fusion.2 = f32[1024,896]{1,0:T(8,128)} fusion(bf16[512,1024]{1,0:T(8,128)(2,1)S(1)} %constant_dynamic-update-slice_fusion.20, bf16[512,2688]{1,0:T(8,128)(2,1)S(1)} %pad_maximum_fusion), kind=kOutput, calls=%fused_computation.6 | convolution fusion | flops 939524096 | bytes 5636096 | tf_op jit(solution)/shard_map/dot_general | solution.py:31
  147.7 3.1 %fusion.4 = f32[1024,896]{1,0:T(8,128)} fusion(bf16[512,1024]{1,0:T(8,128)(2,1)S(1)} %constant_dynamic-update-slice_fusion.20, bf16[512,2688]{1,0:T(8,128)(2,1)S(1)} %pad_maximum_fusion), kind=kOutput, calls=%fused_computation.8 | convolution fusion | flops 939524096 | bytes 5636096 | tf_op jit(solution)/shard_map/dot_general | solution.py:31
  150.8 3.0 %fusion = f32[896,1024]{1,0:T(8,128)} fusion(bf16[512,1024]{1,0:T(8,128)(2,1)S(1)} %constant_dynamic-update-slice_fusion.23, bf16[512,2688]{1,0:T(8,128)(2,1)S(1)} %pad_maximum_fusion), kind=kOutput, calls=%fused_computation.4 | convolution fusion | flops 939524096 | bytes 5636096 | tf_op jit(solution)/shard_map/dot_general | solution.py:31
  154.4 3.8 %collective-permute-start.25 = (bf16[16,4096]{1,0:T(8,128)(2,1)S(1)}, bf16[16,4096]{1,0:T(8,128)(2,1)S(1)}, u32[]{:S(2)}, u32[]{:S(2)}) collective-permute-start(bf16[16,4096]{1,0:T(8,128)(2,1)S(1)} %copy-done.10), channel_id=1, source_target_pairs={{0,6},{1,7},{2,4},{3,5},{4,2},{5,3},{6,0},{7,1},{8,14},{9,15},{10,... | collective-permute-start | bytes 393224 | tf_op jit(solution)/shard_map/ppermute | solution.py:342
  158.3 1.9 collective-permute-done.23
  160.2 1.8 collective-permute-start.34
  162.7 3.5 %collective-permute-start.36 = (f32[1,4096]{1,0:T(1,128)S(1)}, f32[1,4096]{1,0:T(1,128)S(1)}, u32[]{:S(2)}, u32[]{:S(2)}) collective-permute-start(f32[1,4096]{1,0:T(1,128)S(1)} %add_add_fusion.1), channel_id=1, source_target_pairs={{0,24},{8,16},{16,8},{24,0},{1,25},{9,17},{17,9},{25,1},{2,26},{10... | collective-permute-start | bytes 49160 | tf_op jit(solution)/shard_map/ppermute | solution.py:342
  166.3 1.6 collective-permute-done.36
  168.6 4.2 %attention_gradients.1 = (bf16[128,512]{1,0:T(8,128)(2,1)}, bf16[512,256]{1,0:T(8,128)(2,1)S(1)}) custom-call(s32[1]{0:T(128)} %bitcast.1.f_ref, bf16[128,512]{1,0:T(8,128)(2,1)S(1)} %copy-done.5, s32[1,512]{1,0:T(1,128)S(1)} %bitcast.31, bf16[128,512]{1,0:T(8,128)(2,1)S(1)} %get-tuple-element.33.att_ref, f32[128,128]{1,0:T(8,128)S(1)} %get-tuple-element.34.lse_ref, ...), custom_call_target="tpu_custom_call" | custom-call | tf_op jit(solution)/shard_map/attention_gradients/pallas_call | solution.py:160
  174.3 2.0 collective-permute-start.28
  177.8 2.8 %collective-permute-start.42 = (bf16[128,1024]{1,0:T(8,128)(2,1)S(1)}, bf16[128,1024]{1,0:T(8,128)(2,1)S(1)}, u32[]{:S(2)}, u32[]{:S(2)}) collective-permute-start(bf16[128,1024]{1,0:T(8,128)(2,1)S(1)} %pad_maximum_fusion.3), channel_id=1, source_target_pairs={{0,24},{8,16},{16,8},{24,0},{1,25},{9,17},{17,9},{25,1},{2,26},{10... | collective-permute-start | bytes 786440 | tf_op jit(solution)/shard_map/ppermute | solution.py:342
  182.9 3.9 %all-to-all-start = ((bf16[8,16,256]{2,1,0:T(8,128)(2,1)}), bf16[8,16,256]{2,1,0:T(8,128)(2,1)S(1)}, u32[]{:S(2)}, u32[]{:S(2)}) async-start(bf16[8,16,256]{2,1,0:T(8,128)(2,1)} %bitcast.4), calls=%async_computation | async-start | bytes 131072 | tf_op jit(solution)/shard_map/all_to_all | solution.py:418
  186.8 1.9 collective-permute-start.41
  188.8 4.0 %all-to-all-done = bf16[8,16,256]{2,1,0:T(8,128)(2,1)S(1)} async-done(((bf16[8,16,256]{2,1,0:T(8,128)(2,1)}), bf16[8,16,256]{2,1,0:T(8,128)(2,1)S(1)}, u32[]{:S(2)}, u32[]{:S(2)}) %all-to-all-start) | async-done | bytes 65568 | tf_op jit(solution)/shard_map/all_to_all | solution.py:418
  194.2 2.3 %collective-permute-start.39 = (bf16[128,512]{1,0:T(8,128)(2,1)S(1)}, bf16[128,512]{1,0:T(8,128)(2,1)S(1)}, u32[]{:S(2)}, u32[]{:S(2)}) collective-permute-start(bf16[128,512]{1,0:T(8,128)(2,1)S(1)} %get-tuple-element.33.att_ref), channel_id=1, source_target_pairs={{0,24},{8,16},{16,8},{24,0},{1,25},{9,17},{17,9},{25,1},{2,26},{10... | collective-permute-start | bytes 393224 | tf_op jit(solution)/shard_map/ppermute | solution.py:342
  196.7 3.5 %collective-permute-done.39 = bf16[128,512]{1,0:T(8,128)(2,1)S(1)} collective-permute-done((bf16[128,512]{1,0:T(8,128)(2,1)S(1)}, bf16[128,512]{1,0:T(8,128)(2,1)S(1)}, u32[]{:S(2)}, u32[]{:S(2)}) %collective-permute-start.39) | collective-permute-done | bytes 131104 | tf_op jit(solution)/shard_map/ppermute | solution.py:342
  200.2 3.0 %fusion.6 = f32[512,1024]{1,0:T(8,128)} fusion(bf16[512,1024]{1,0:T(8,128)(2,1)S(1)} %constant_dynamic-update-slice_fusion.17, bf16[128,512]{1,0:T(8,128)(2,1)S(1)} %collective-permute-done.39, bf16[128,512]{1,0:T(8,128)(2,1)} %collective-permute-done.38, bf16[128,512]{1,0:T(8,128)(2,1)S(1)} %collective-permute-done.37, ...), kind=kOutput, calls=%fused_computation.10 | convolution fusion | flops 538968064 | bytes 3670016 | tf_op jit(solution)/shard_map/dot_general | solution.py:31
  (158 shorter events, 33.0 us)
Async XLA Ops:
  0.6 21.9 %collective-permute-start.11 = (bf16[16,4096]{1,0:T(8,128)(2,1)}, bf16[16,4096]{1,0:T(8,128)(2,1)S(1)}, u32[]{:S(2)}, u32[]{:S(2)}) collective-permute-start(bf16[16,4096]{1,0:T(8,128)(2,1)} %cot_ref.1), channel_id=1, source_target_pairs={{0,2},{1,3},{2,0},{3,1},{4,6},{5,7},{6,4},{7,5},{8,10},{9,11},{10,... | collective-permute-start | bytes 393224 | tf_op jit(solution)/shard_map/ppermute | solution.py:342
  3.7 18.8 %collective-permute-start.12 = (bf16[16,4096]{1,0:T(8,128)(2,1)}, bf16[16,4096]{1,0:T(8,128)(2,1)S(1)}, u32[]{:S(2)}, u32[]{:S(2)}) collective-permute-start(bf16[16,4096]{1,0:T(8,128)(2,1)} %cot_ref.1), channel_id=1, source_target_pairs={{0,4},{1,5},{2,6},{3,7},{4,0},{5,1},{6,2},{7,3},{8,12},{9,13},{10,... | collective-permute-start | bytes 393224 | tf_op jit(solution)/shard_map/ppermute | solution.py:342
  8.0 4.5 %collective-permute-start = (bf16[272,128]{1,0:T(8,128)(2,1)S(1)}, bf16[272,128]{1,0:T(8,128)(2,1)S(1)}, u32[]{:S(2)}, u32[]{:S(2)}) collective-permute-start(bf16[272,128]{1,0:T(8,128)(2,1)S(1)} %maximum_maximum_fusion.refs_0_), channel_id=1, source_target_pairs={{0,8},{8,0},{16,24},{24,16},{1,9},{9,1},{17,25},{25,17},{2,10},{10... | collective-permute-start | bytes 208904 | tf_op jit(solution)/shard_map/ppermute | solution.py:342
  9.5 5.1 %collective-permute-start.1 = (bf16[272,128]{1,0:T(8,128)(2,1)S(1)}, bf16[272,128]{1,0:T(8,128)(2,1)S(1)}, u32[]{:S(2)}, u32[]{:S(2)}) collective-permute-start(bf16[272,128]{1,0:T(8,128)(2,1)S(1)} %maximum_maximum_fusion.refs_0_), channel_id=1, source_target_pairs={{0,16},{8,24},{16,0},{24,8},{1,17},{9,25},{17,1},{25,9},{2,18},{10... | collective-permute-start | bytes 208904 | tf_op jit(solution)/shard_map/ppermute | solution.py:342
  11.0 5.2 %collective-permute-start.2 = (bf16[272,128]{1,0:T(8,128)(2,1)S(1)}, bf16[272,128]{1,0:T(8,128)(2,1)S(1)}, u32[]{:S(2)}, u32[]{:S(2)}) collective-permute-start(bf16[272,128]{1,0:T(8,128)(2,1)S(1)} %maximum_maximum_fusion.refs_0_), channel_id=1, source_target_pairs={{0,24},{8,16},{16,8},{24,0},{1,25},{9,17},{17,9},{25,1},{2,26},{10... | collective-permute-start | bytes 208904 | tf_op jit(solution)/shard_map/ppermute | solution.py:342
  12.5 10.1 %collective-permute-start.13 = (bf16[16,4096]{1,0:T(8,128)(2,1)}, bf16[16,4096]{1,0:T(8,128)(2,1)S(1)}, u32[]{:S(2)}, u32[]{:S(2)}) collective-permute-start(bf16[16,4096]{1,0:T(8,128)(2,1)} %cot_ref.1), channel_id=1, source_target_pairs={{0,6},{1,7},{2,4},{3,5},{4,2},{5,3},{6,0},{7,1},{8,14},{9,15},{10,... | collective-permute-start | bytes 393224 | tf_op jit(solution)/shard_map/ppermute | solution.py:342
  22.7 6.4 %collective-permute-start.14 = (bf16[64,4096]{1,0:T(8,128)(2,1)S(1)}, bf16[64,4096]{1,0:T(8,128)(2,1)S(1)}, u32[]{:S(2)}, u32[]{:S(2)}) collective-permute-start(bf16[64,4096]{1,0:T(8,128)(2,1)S(1)} %get-tuple-element.78), channel_id=1, source_target_pairs={{0,1},{1,0},{2,3},{3,2},{4,5},{5,4},{6,7},{7,6},{8,9},{9,8},{10,11... | collective-permute-start | bytes 1572872 | tf_op jit(solution)/shard_map/ppermute | solution.py:342
  24.6 7.2 %collective-permute-start.4 = (bf16[16,4096]{1,0:T(8,128)(2,1)S(1)}, bf16[16,4096]{1,0:T(8,128)(2,1)S(1)}, u32[]{:S(2)}, u32[]{:S(2)}) collective-permute-start(bf16[16,4096]{1,0:T(8,128)(2,1)S(1)} %get-tuple-element.71), channel_id=1, source_target_pairs={{0,2},{1,3},{2,0},{3,1},{4,6},{5,7},{6,4},{7,5},{8,10},{9,11},{10,... | collective-permute-start | bytes 393224 | tf_op jit(solution)/shard_map/ppermute | solution.py:342
  25.1 12.9 %collective-permute-start.5 = (bf16[16,4096]{1,0:T(8,128)(2,1)S(1)}, bf16[16,4096]{1,0:T(8,128)(2,1)S(1)}, u32[]{:S(2)}, u32[]{:S(2)}) collective-permute-start(bf16[16,4096]{1,0:T(8,128)(2,1)S(1)} %get-tuple-element.70), channel_id=1, source_target_pairs={{0,4},{1,5},{2,6},{3,7},{4,0},{5,1},{6,2},{7,3},{8,12},{9,13},{10,... | collective-permute-start | bytes 393224 | tf_op jit(solution)/shard_map/ppermute | solution.py:342
  25.5 12.5 %collective-permute-start.6 = (bf16[16,4096]{1,0:T(8,128)(2,1)S(1)}, bf16[16,4096]{1,0:T(8,128)(2,1)S(1)}, u32[]{:S(2)}, u32[]{:S(2)}) collective-permute-start(bf16[16,4096]{1,0:T(8,128)(2,1)S(1)} %get-tuple-element.69), channel_id=1, source_target_pairs={{0,6},{1,7},{2,4},{3,5},{4,2},{5,3},{6,0},{7,1},{8,14},{9,15},{10,... | collective-permute-start | bytes 393224 | tf_op jit(solution)/shard_map/ppermute | solution.py:342
  29.8 28.4 %collective-permute-start.49 = (bf16[128,1024]{1,0:T(8,128)(2,1)}, bf16[128,1024]{1,0:T(8,128)(2,1)S(1)}, u32[]{:S(2)}, u32[]{:S(2)}) collective-permute-start(bf16[128,1024]{1,0:T(8,128)(2,1)} %pad_maximum_fusion.7), channel_id=1, source_target_pairs={{0,8},{8,0},{16,24},{24,16},{1,9},{9,1},{17,25},{25,17},{2,10},{10... | collective-permute-start | bytes 786440 | tf_op jit(solution)/shard_map/ppermute | solution.py:342
  30.4 27.9 %collective-permute-start.50 = (bf16[128,1024]{1,0:T(8,128)(2,1)S(1)}, bf16[128,1024]{1,0:T(8,128)(2,1)}, u32[]{:S(2)}, u32[]{:S(2)}) collective-permute-start(bf16[128,1024]{1,0:T(8,128)(2,1)S(1)} %pad_maximum_fusion.8), channel_id=1, source_target_pairs={{0,16},{8,24},{16,0},{24,8},{1,17},{9,25},{17,1},{25,9},{2,18},{10... | collective-permute-start | bytes 786440 | tf_op jit(solution)/shard_map/ppermute | solution.py:342
  31.8 38.3 %collective-permute-start.51 = (bf16[128,1024]{1,0:T(8,128)(2,1)S(1)}, bf16[128,1024]{1,0:T(8,128)(2,1)}, u32[]{:S(2)}, u32[]{:S(2)}) collective-permute-start(bf16[128,1024]{1,0:T(8,128)(2,1)S(1)} %pad_maximum_fusion.9), channel_id=1, source_target_pairs={{0,24},{8,16},{16,8},{24,0},{1,25},{9,17},{17,9},{25,1},{2,26},{10... | collective-permute-start | bytes 786440 | tf_op jit(solution)/shard_map/ppermute | solution.py:342
  38.2 6.2 %collective-permute-start.7 = (bf16[16,4096]{1,0:T(8,128)(2,1)S(1)}, bf16[16,4096]{1,0:T(8,128)(2,1)S(1)}, u32[]{:S(2)}, u32[]{:S(2)}) collective-permute-start(bf16[16,4096]{1,0:T(8,128)(2,1)S(1)} %get-tuple-element.27), channel_id=1, source_target_pairs={{0,2},{1,3},{2,0},{3,1},{4,6},{5,7},{6,4},{7,5},{8,10},{9,11},{10,... | collective-permute-start | bytes 393224 | tf_op jit(solution)/shard_map/ppermute | solution.py:342
  40.6 11.7 %collective-permute-start.8 = (bf16[16,4096]{1,0:T(8,128)(2,1)S(1)}, bf16[16,4096]{1,0:T(8,128)(2,1)S(1)}, u32[]{:S(2)}, u32[]{:S(2)}) collective-permute-start(bf16[16,4096]{1,0:T(8,128)(2,1)S(1)} %get-tuple-element.27), channel_id=1, source_target_pairs={{0,4},{1,5},{2,6},{3,7},{4,0},{5,1},{6,2},{7,3},{8,12},{9,13},{10,... | collective-permute-start | bytes 393224 | tf_op jit(solution)/shard_map/ppermute | solution.py:342
  44.4 7.9 %collective-permute-start.9 = (bf16[16,4096]{1,0:T(8,128)(2,1)S(1)}, bf16[16,4096]{1,0:T(8,128)(2,1)S(1)}, u32[]{:S(2)}, u32[]{:S(2)}) collective-permute-start(bf16[16,4096]{1,0:T(8,128)(2,1)S(1)} %get-tuple-element.27), channel_id=1, source_target_pairs={{0,6},{1,7},{2,4},{3,5},{4,2},{5,3},{6,0},{7,1},{8,14},{9,15},{10,... | collective-permute-start | bytes 393224 | tf_op jit(solution)/shard_map/ppermute | solution.py:342
  52.4 6.8 %collective-permute-start.10 = (bf16[64,4096]{1,0:T(8,128)(2,1)S(1)}, bf16[64,4096]{1,0:T(8,128)(2,1)S(1)}, u32[]{:S(2)}, u32[]{:S(2)}) collective-permute-start(bf16[64,4096]{1,0:T(8,128)(2,1)S(1)} %constant_dynamic-update-slice_fusion.xa_ref), channel_id=1, source_target_pairs={{0,1},{1,0},{2,3},{3,2},{4,5},{5,4},{6,7},{7,6},{8,9},{9,8},{10,11... | collective-permute-start | bytes 1572872 | tf_op jit(solution)/shard_map/ppermute | solution.py:342
  69.0 11.8 %collective-permute-start.19 = (bf16[64,4096]{1,0:T(8,128)(2,1)S(1)}, bf16[64,4096]{1,0:T(8,128)(2,1)S(1)}, u32[]{:S(2)}, u32[]{:S(2)}) collective-permute-start(bf16[64,4096]{1,0:T(8,128)(2,1)S(1)} %get-tuple-element.31), channel_id=1, source_target_pairs={{0,1},{1,0},{2,3},{3,2},{4,5},{5,4},{6,7},{7,6},{8,9},{9,8},{10,11... | collective-permute-start | bytes 1572872 | tf_op jit(solution)/shard_map/ppermute | solution.py:342
  69.5 11.3 %collective-permute-start.43 = (bf16[128,1024]{1,0:T(8,128)(2,1)S(1)}, bf16[128,1024]{1,0:T(8,128)(2,1)S(1)}, u32[]{:S(2)}, u32[]{:S(2)}) collective-permute-start(bf16[128,1024]{1,0:T(8,128)(2,1)S(1)} %pad_maximum_fusion.4), channel_id=1, source_target_pairs={{0,8},{8,0},{16,24},{24,16},{1,9},{9,1},{17,25},{25,17},{2,10},{10... | collective-permute-start | bytes 786440 | tf_op jit(solution)/shard_map/ppermute | solution.py:342
  77.7 13.8 %collective-permute-start.44 = (bf16[128,1024]{1,0:T(8,128)(2,1)S(1)}, bf16[128,1024]{1,0:T(8,128)(2,1)S(1)}, u32[]{:S(2)}, u32[]{:S(2)}) collective-permute-start(bf16[128,1024]{1,0:T(8,128)(2,1)S(1)} %pad_maximum_fusion.5), channel_id=1, source_target_pairs={{0,16},{8,24},{16,0},{24,8},{1,17},{9,25},{17,1},{25,9},{2,18},{10... | collective-permute-start | bytes 786440 | tf_op jit(solution)/shard_map/ppermute | solution.py:342
  78.5 15.4 %collective-permute-start.45 = (bf16[128,1024]{1,0:T(8,128)(2,1)S(1)}, bf16[128,1024]{1,0:T(8,128)(2,1)S(1)}, u32[]{:S(2)}, u32[]{:S(2)}) collective-permute-start(bf16[128,1024]{1,0:T(8,128)(2,1)S(1)} %pad_maximum_fusion.6), channel_id=1, source_target_pairs={{0,24},{8,16},{16,8},{24,0},{1,25},{9,17},{17,9},{25,1},{2,26},{10... | collective-permute-start | bytes 786440 | tf_op jit(solution)/shard_map/ppermute | solution.py:342
  81.0 12.9 %collective-permute-start.20 = (bf16[16,4096]{1,0:T(8,128)(2,1)S(1)}, bf16[16,4096]{1,0:T(8,128)(2,1)S(1)}, u32[]{:S(2)}, u32[]{:S(2)}) collective-permute-start(bf16[16,4096]{1,0:T(8,128)(2,1)S(1)} %get-tuple-element.64), channel_id=1, source_target_pairs={{0,2},{1,3},{2,0},{3,1},{4,6},{5,7},{6,4},{7,5},{8,10},{9,11},{10,... | collective-permute-start | bytes 393224 | tf_op jit(solution)/shard_map/ppermute | solution.py:342
  83.5 13.6 %collective-permute-start.21 = (bf16[16,4096]{1,0:T(8,128)(2,1)S(1)}, bf16[16,4096]{1,0:T(8,128)(2,1)S(1)}, u32[]{:S(2)}, u32[]{:S(2)}) collective-permute-start(bf16[16,4096]{1,0:T(8,128)(2,1)S(1)} %get-tuple-element.63), channel_id=1, source_target_pairs={{0,4},{1,5},{2,6},{3,7},{4,0},{5,1},{6,2},{7,3},{8,12},{9,13},{10,... | collective-permute-start | bytes 393224 | tf_op jit(solution)/shard_map/ppermute | solution.py:342
  83.5 14.4 %collective-permute-start.22 = (bf16[16,4096]{1,0:T(8,128)(2,1)S(1)}, bf16[16,4096]{1,0:T(8,128)(2,1)S(1)}, u32[]{:S(2)}, u32[]{:S(2)}) collective-permute-start(bf16[16,4096]{1,0:T(8,128)(2,1)S(1)} %get-tuple-element.62), channel_id=1, source_target_pairs={{0,6},{1,7},{2,4},{3,5},{4,2},{5,3},{6,0},{7,1},{8,14},{9,15},{10,... | collective-permute-start | bytes 393224 | tf_op jit(solution)/shard_map/ppermute | solution.py:342
  91.4 8.7 %collective-permute-start.16 = (bf16[16,4096]{1,0:T(8,128)(2,1)S(1)}, bf16[16,4096]{1,0:T(8,128)(2,1)S(1)}, u32[]{:S(2)}, u32[]{:S(2)}) collective-permute-start(bf16[16,4096]{1,0:T(8,128)(2,1)S(1)} %get-tuple-element.66), channel_id=1, source_target_pairs={{0,2},{1,3},{2,0},{3,1},{4,6},{5,7},{6,4},{7,5},{8,10},{9,11},{10,... | collective-permute-start | bytes 393224 | tf_op jit(solution)/shard_map/ppermute | solution.py:342
  93.9 13.7 %collective-permute-start.17 = (bf16[16,4096]{1,0:T(8,128)(2,1)S(1)}, bf16[16,4096]{1,0:T(8,128)(2,1)S(1)}, u32[]{:S(2)}, u32[]{:S(2)}) collective-permute-start(bf16[16,4096]{1,0:T(8,128)(2,1)S(1)} %get-tuple-element.68), channel_id=1, source_target_pairs={{0,4},{1,5},{2,6},{3,7},{4,0},{5,1},{6,2},{7,3},{8,12},{9,13},{10,... | collective-permute-start | bytes 393224 | tf_op jit(solution)/shard_map/ppermute | solution.py:342
  93.9 14.4 %collective-permute-start.18 = (bf16[16,4096]{1,0:T(8,128)(2,1)S(1)}, bf16[16,4096]{1,0:T(8,128)(2,1)S(1)}, u32[]{:S(2)}, u32[]{:S(2)}) collective-permute-start(bf16[16,4096]{1,0:T(8,128)(2,1)S(1)} %get-tuple-element.67), channel_id=1, source_target_pairs={{0,6},{1,7},{2,4},{3,5},{4,2},{5,3},{6,0},{7,1},{8,14},{9,15},{10,... | collective-permute-start | bytes 393224 | tf_op jit(solution)/shard_map/ppermute | solution.py:342
  97.2 99.5 %collective-permute-start.37 = (bf16[128,512]{1,0:T(8,128)(2,1)S(1)}, bf16[128,512]{1,0:T(8,128)(2,1)S(1)}, u32[]{:S(2)}, u32[]{:S(2)}) collective-permute-start(bf16[128,512]{1,0:T(8,128)(2,1)S(1)} %get-tuple-element.33.att_ref), channel_id=1, source_target_pairs={{0,8},{8,0},{16,24},{24,16},{1,9},{9,1},{17,25},{25,17},{2,10},{10... | collective-permute-start | bytes 393224 | tf_op jit(solution)/shard_map/ppermute | solution.py:342
  97.9 20.4 %collective-permute-start.46 = (bf16[128,2688]{1,0:T(8,128)(2,1)S(1)}, bf16[128,2688]{1,0:T(8,128)(2,1)S(1)}, u32[]{:S(2)}, u32[]{:S(2)}) collective-permute-start(bf16[128,2688]{1,0:T(8,128)(2,1)S(1)} %gate_up_and_gradients.1.pay_ref), channel_id=1, source_target_pairs={{0,8},{8,0},{16,24},{24,16},{1,9},{9,1},{17,25},{25,17},{2,10},{10... | collective-permute-start | bytes 2064392 | tf_op jit(solution)/shard_map/ppermute | solution.py:342
  100.1 31.8 %collective-permute-start.47 = (bf16[128,2688]{1,0:T(8,128)(2,1)S(1)}, bf16[128,2688]{1,0:T(8,128)(2,1)S(1)}, u32[]{:S(2)}, u32[]{:S(2)}) collective-permute-start(bf16[128,2688]{1,0:T(8,128)(2,1)S(1)} %gate_up_and_gradients.1.pay_ref), channel_id=1, source_target_pairs={{0,16},{8,24},{16,0},{24,8},{1,17},{9,25},{17,1},{25,9},{2,18},{10... | collective-permute-start | bytes 2064392 | tf_op jit(solution)/shard_map/ppermute | solution.py:342
  107.6 26.6 %collective-permute-start.48 = (bf16[128,2688]{1,0:T(8,128)(2,1)S(1)}, bf16[128,2688]{1,0:T(8,128)(2,1)S(1)}, u32[]{:S(2)}, u32[]{:S(2)}) collective-permute-start(bf16[128,2688]{1,0:T(8,128)(2,1)S(1)} %gate_up_and_gradients.1.pay_ref), channel_id=1, source_target_pairs={{0,24},{8,16},{16,8},{24,0},{1,25},{9,17},{17,9},{25,1},{2,26},{10... | collective-permute-start | bytes 2064392 | tf_op jit(solution)/shard_map/ppermute | solution.py:342
  110.0 86.7 %collective-permute-start.38 = (bf16[128,512]{1,0:T(8,128)(2,1)S(1)}, bf16[128,512]{1,0:T(8,128)(2,1)}, u32[]{:S(2)}, u32[]{:S(2)}) collective-permute-start(bf16[128,512]{1,0:T(8,128)(2,1)S(1)} %get-tuple-element.33.att_ref), channel_id=1, source_target_pairs={{0,16},{8,24},{16,0},{24,8},{1,17},{9,25},{17,1},{25,9},{2,18},{10... | collective-permute-start | bytes 393224 | tf_op jit(solution)/shard_map/ppermute | solution.py:342
  118.3 35.5 %collective-permute-start.31 = (f32[1,4096]{1,0:T(1,128)S(1)}, f32[1,4096]{1,0:T(1,128)S(1)}, u32[]{:S(2)}, u32[]{:S(2)}) collective-permute-start(f32[1,4096]{1,0:T(1,128)S(1)} %add.107), channel_id=1, source_target_pairs={{0,2},{1,3},{2,0},{3,1},{4,6},{5,7},{6,4},{7,5},{8,10},{9,11},{10,... | collective-permute-start | bytes 49160 | tf_op jit(solution)/shard_map/ppermute | solution.py:342
  131.9 22.0 %collective-permute-start.32 = (f32[1,4096]{1,0:T(1,128)S(1)}, f32[1,4096]{1,0:T(1,128)S(1)}, u32[]{:S(2)}, u32[]{:S(2)}) collective-permute-start(f32[1,4096]{1,0:T(1,128)S(1)} %add.107), channel_id=1, source_target_pairs={{0,4},{1,5},{2,6},{3,7},{4,0},{5,1},{6,2},{7,3},{8,12},{9,13},{10,... | collective-permute-start | bytes 49160 | tf_op jit(solution)/shard_map/ppermute | solution.py:342
  134.3 20.2 %collective-permute-start.33 = (f32[1,4096]{1,0:T(1,128)S(1)}, f32[1,4096]{1,0:T(1,128)S(1)}, u32[]{:S(2)}, u32[]{:S(2)}) collective-permute-start(f32[1,4096]{1,0:T(1,128)S(1)} %add.107), channel_id=1, source_target_pairs={{0,6},{1,7},{2,4},{3,5},{4,2},{5,3},{6,0},{7,1},{8,14},{9,15},{10,... | collective-permute-start | bytes 49160 | tf_op jit(solution)/shard_map/ppermute | solution.py:342
  153.8 6.4 %collective-permute-start.23 = (bf16[16,4096]{1,0:T(8,128)(2,1)S(1)}, bf16[16,4096]{1,0:T(8,128)(2,1)S(1)}, u32[]{:S(2)}, u32[]{:S(2)}) collective-permute-start(bf16[16,4096]{1,0:T(8,128)(2,1)S(1)} %copy-done.10), channel_id=1, source_target_pairs={{0,2},{1,3},{2,0},{3,1},{4,6},{5,7},{6,4},{7,5},{8,10},{9,11},{10,... | collective-permute-start | bytes 393224 | tf_op jit(solution)/shard_map/ppermute | solution.py:342
  153.9 8.2 %collective-permute-start.24 = (bf16[16,4096]{1,0:T(8,128)(2,1)S(1)}, bf16[16,4096]{1,0:T(8,128)(2,1)S(1)}, u32[]{:S(2)}, u32[]{:S(2)}) collective-permute-start(bf16[16,4096]{1,0:T(8,128)(2,1)S(1)} %copy-done.10), channel_id=1, source_target_pairs={{0,4},{1,5},{2,6},{3,7},{4,0},{5,1},{6,2},{7,3},{8,12},{9,13},{10,... | collective-permute-start | bytes 393224 | tf_op jit(solution)/shard_map/ppermute | solution.py:342
  154.4 8.3 %collective-permute-start.25 = (bf16[16,4096]{1,0:T(8,128)(2,1)S(1)}, bf16[16,4096]{1,0:T(8,128)(2,1)S(1)}, u32[]{:S(2)}, u32[]{:S(2)}) collective-permute-start(bf16[16,4096]{1,0:T(8,128)(2,1)S(1)} %copy-done.10), channel_id=1, source_target_pairs={{0,6},{1,7},{2,4},{3,5},{4,2},{5,3},{6,0},{7,1},{8,14},{9,15},{10,... | collective-permute-start | bytes 393224 | tf_op jit(solution)/shard_map/ppermute | solution.py:342
  160.2 5.9 %collective-permute-start.34 = (f32[1,4096]{1,0:T(1,128)S(1)}, f32[1,4096]{1,0:T(1,128)S(1)}, u32[]{:S(2)}, u32[]{:S(2)}) collective-permute-start(f32[1,4096]{1,0:T(1,128)S(1)} %add_add_fusion.1), channel_id=1, source_target_pairs={{0,8},{8,0},{16,24},{24,16},{1,9},{9,1},{17,25},{25,17},{2,10},{10... | collective-permute-start | bytes 49160 | tf_op jit(solution)/shard_map/ppermute | solution.py:342
  162.7 5.2 %collective-permute-start.36 = (f32[1,4096]{1,0:T(1,128)S(1)}, f32[1,4096]{1,0:T(1,128)S(1)}, u32[]{:S(2)}, u32[]{:S(2)}) collective-permute-start(f32[1,4096]{1,0:T(1,128)S(1)} %add_add_fusion.1), channel_id=1, source_target_pairs={{0,24},{8,16},{16,8},{24,0},{1,25},{9,17},{17,9},{25,1},{2,26},{10... | collective-permute-start | bytes 49160 | tf_op jit(solution)/shard_map/ppermute | solution.py:342
  172.8 5.0 %collective-permute-start.27 = (bf16[128,256]{1,0:T(8,128)(2,1)S(1)}, bf16[128,256]{1,0:T(8,128)(2,1)S(1)}, u32[]{:S(2)}, u32[]{:S(2)}) collective-permute-start(bf16[128,256]{1,0:T(8,128)(2,1)S(1)} %get-tuple-element.73), channel_id=1, source_target_pairs={{0,8},{8,0},{16,24},{24,16},{1,9},{9,1},{17,25},{25,17},{2,10},{10... | collective-permute-start | bytes 196616 | tf_op jit(solution)/shard_map/ppermute | solution.py:342
  174.3 6.8 %collective-permute-start.28 = (bf16[128,256]{1,0:T(8,128)(2,1)S(1)}, bf16[128,256]{1,0:T(8,128)(2,1)S(1)}, u32[]{:S(2)}, u32[]{:S(2)}) collective-permute-start(bf16[128,256]{1,0:T(8,128)(2,1)S(1)} %get-tuple-element.75), channel_id=1, source_target_pairs={{0,16},{8,24},{16,0},{24,8},{1,17},{9,25},{17,1},{25,9},{2,18},{10... | collective-permute-start | bytes 196616 | tf_op jit(solution)/shard_map/ppermute | solution.py:342
  176.3 5.9 %collective-permute-start.29 = (bf16[128,256]{1,0:T(8,128)(2,1)S(1)}, bf16[128,256]{1,0:T(8,128)(2,1)S(1)}, u32[]{:S(2)}, u32[]{:S(2)}) collective-permute-start(bf16[128,256]{1,0:T(8,128)(2,1)S(1)} %get-tuple-element.74), channel_id=1, source_target_pairs={{0,24},{8,16},{16,8},{24,0},{1,25},{9,17},{17,9},{25,1},{2,26},{10... | collective-permute-start | bytes 196616 | tf_op jit(solution)/shard_map/ppermute | solution.py:342
  177.8 18.8 %collective-permute-start.42 = (bf16[128,1024]{1,0:T(8,128)(2,1)S(1)}, bf16[128,1024]{1,0:T(8,128)(2,1)S(1)}, u32[]{:S(2)}, u32[]{:S(2)}) collective-permute-start(bf16[128,1024]{1,0:T(8,128)(2,1)S(1)} %pad_maximum_fusion.3), channel_id=1, source_target_pairs={{0,24},{8,16},{16,8},{24,0},{1,25},{9,17},{17,9},{25,1},{2,26},{10... | collective-permute-start | bytes 786440 | tf_op jit(solution)/shard_map/ppermute | solution.py:342
  181.1 13.1 %collective-permute-start.40 = (bf16[128,1024]{1,0:T(8,128)(2,1)S(1)}, bf16[128,1024]{1,0:T(8,128)(2,1)S(1)}, u32[]{:S(2)}, u32[]{:S(2)}) collective-permute-start(bf16[128,1024]{1,0:T(8,128)(2,1)S(1)} %pad_maximum_fusion.1), channel_id=1, source_target_pairs={{0,8},{8,0},{16,24},{24,16},{1,9},{9,1},{17,25},{25,17},{2,10},{10... | collective-permute-start | bytes 786440 | tf_op jit(solution)/shard_map/ppermute | solution.py:342
  182.9 9.8 %all-to-all-start = ((bf16[8,16,256]{2,1,0:T(8,128)(2,1)}), bf16[8,16,256]{2,1,0:T(8,128)(2,1)S(1)}, u32[]{:S(2)}, u32[]{:S(2)}) async-start(bf16[8,16,256]{2,1,0:T(8,128)(2,1)} %bitcast.4), calls=%async_computation | async-start | bytes 131072 | tf_op jit(solution)/shard_map/all_to_all | solution.py:418
  186.8 9.7 %collective-permute-start.41 = (bf16[128,1024]{1,0:T(8,128)(2,1)S(1)}, bf16[128,1024]{1,0:T(8,128)(2,1)S(1)}, u32[]{:S(2)}, u32[]{:S(2)}) collective-permute-start(bf16[128,1024]{1,0:T(8,128)(2,1)S(1)} %pad_maximum_fusion.2), channel_id=1, source_target_pairs={{0,16},{8,24},{16,0},{24,8},{1,17},{9,25},{17,1},{25,9},{2,18},{10... | collective-permute-start | bytes 786440 | tf_op jit(solution)/shard_map/ppermute | solution.py:342
  194.2 6.0 %collective-permute-start.39 = (bf16[128,512]{1,0:T(8,128)(2,1)S(1)}, bf16[128,512]{1,0:T(8,128)(2,1)S(1)}, u32[]{:S(2)}, u32[]{:S(2)}) collective-permute-start(bf16[128,512]{1,0:T(8,128)(2,1)S(1)} %get-tuple-element.33.att_ref), channel_id=1, source_target_pairs={{0,24},{8,16},{16,8},{24,0},{1,25},{9,17},{17,9},{25,1},{2,26},{10... | collective-permute-start | bytes 393224 | tf_op jit(solution)/shard_map/ppermute | solution.py:342
  (18 other events, 189.3 us)

commit v2 on v1

v2 whole, which is shorter than its diff:
```python
import functools
import math

import jax
import jax.numpy as jnp
from jax import lax
from jax.experimental import pallas as pl
from jax.experimental.pallas import tpu as pltpu
from jax.sharding import PartitionSpec as P

QUERY_HEADS = 32
KEY_VALUE_HEADS = 8
HEAD_WIDTH = 128
STRIPE = 64

masked_fill = -1e30
norm_eps = 1e-05
score_scale = 1.0 / math.sqrt(HEAD_WIDTH)

F32 = jnp.float32
BF16 = jnp.bfloat16
NN = (((1,), (0,)), ((), ()))
NT = (((1,), (1,)), ((), ()))
TN = (((0,), (0,)), ((), ()))
VMEM = pl.BlockSpec(memory_space=pltpu.VMEM)
SMEM = pl.BlockSpec(memory_space=pltpu.SMEM)
ANY = pl.BlockSpec(memory_space=pl.ANY)


def dot(a, b, dims=NN):
    return lax.dot_general(a, b, dims, preferred_element_type=F32)


def params(megabytes=48):
    return pltpu.CompilerParams(vmem_limit_bytes=megabytes * 1024 * 1024)


def cost(microseconds):
    return pl.CostEstimate(
        flops=int(microseconds * 5e8), bytes_accessed=int(microseconds * 2e6), transcendentals=0
    )


def fetch(sources, targets, sems):
    copies = [pltpu.make_async_copy(s, t, sems.at[i]) for i, (s, t) in enumerate(zip(sources, targets))]
    for copy in copies:
        copy.start()
    return copies


def scratch_like(*arrays):
    return [pltpu.VMEM(a.shape, a.dtype) for a in arrays] + [
        pltpu.SemaphoreType.DMA((len(arrays),))
    ]


def log2(n):
    assert n & (n - 1) == 0
    return n.bit_length() - 1


def relative_rows(f, rows, n_f):
    share, half = rows // n_f, n_f // 2
    r = lax.broadcasted_iota(jnp.int32, (rows, rows), 0)
    natural = lax.broadcasted_iota(jnp.int32, (rows, rows), 1)
    j = lax.shift_right_logical(r, log2(share))
    k = lax.shift_left(j & (half - 1), 1) | lax.shift_right_logical(j, log2(half))
    return natural == lax.shift_left(k ^ f, log2(share)) + (r & (share - 1))


def visibility(same_row, pieces, rows):
    coded = [piece[2 * rows :, :].astype(F32) for piece in pieces]
    key_pos = jnp.concatenate([t[0:1] * STRIPE + t[1:2] for t in coded], axis=1)
    key_seg = jnp.concatenate([t[2:3] for t in coded], axis=1)

    def to_column(row):
        return jnp.sum(jnp.where(same_row, row[:, :rows], 0.0), axis=1, keepdims=True)

    return (key_pos <= to_column(key_pos)) & (key_seg == to_column(key_seg))


def keys_and_values(pieces, rows):
    return (
        jnp.concatenate([p[:rows] for p in pieces], axis=0),
        jnp.concatenate([p[rows : 2 * rows] for p in pieces], axis=0),
    )


def prepare_kernel(
    n_f, f_ref, group_ref, q_hbm, k_hbm, v_hbm, pos_hbm, doc_hbm, q_out, payload, *scratch
):
    q_ref, pos_ref, doc_ref, sems = scratch
    rows = q_ref.shape[0]
    cols = pl.ds(pl.multiple_of(group_ref[0] * HEAD_WIDTH, HEAD_WIDTH), HEAD_WIDTH)
    copies = fetch(
        [pos_hbm, doc_hbm, q_hbm, k_hbm.at[:, cols], v_hbm.at[:, cols]],
        [pos_ref, doc_ref, q_ref, payload.at[pl.ds(0, rows)], payload.at[pl.ds(rows, rows)]],
        sems,
    )
    same_row = relative_rows(f_ref[0], rows, n_f)
    line = lax.broadcasted_iota(jnp.int32, (16, rows), 0)
    copies[0].wait()
    copies[1].wait()
    pos = pos_ref[...]
    total = doc_ref.shape[1]
    where_is = lax.broadcasted_iota(jnp.int32, (total, rows), 0) == pos
    docs = jnp.broadcast_to(doc_ref[...].astype(F32), (8, total)).astype(BF16)
    seg = dot(docs, where_is.astype(F32).astype(BF16))[0:1]
    high = lax.shift_right_logical(pos, log2(STRIPE))
    low = pos & (STRIPE - 1)
    coded = jnp.where(line == 0, high.astype(F32), jnp.where(line == 1, low.astype(F32), 0.0))
    payload[2 * rows :, :] = jnp.where(line == 2, seg, coded).astype(BF16)
    copies[2].wait()
    q_out[...] = dot(same_row.astype(F32).astype(BF16), q_ref[...]).astype(BF16)
    copies[3].wait()
    copies[4].wait()


def prepare_call(f, group, queries, keys_in, values_in, pos_row, doc_row, n_f):
    rows = queries.shape[0]
    assert rows == HEAD_WIDTH
    return pl.pallas_call(
        functools.partial(prepare_kernel, n_f),
        out_shape=(
            jax.ShapeDtypeStruct(queries.shape, BF16),
            jax.ShapeDtypeStruct((2 * rows + 16, HEAD_WIDTH), BF16),
        ),
        in_specs=[SMEM, SMEM] + [ANY] * 5,
        out_specs=[VMEM] * 2,
        scratch_shapes=scratch_like(queries, pos_row, doc_row)[:-1]
        + [pltpu.SemaphoreType.DMA((5,))],
        compiler_params=params(58),
        cost_estimate=cost(2),
        name="prepare_attention",
    )(f, group, queries, keys_in, values_in, pos_row, doc_row)


def attention_kernel(n_f, n_c, f_ref, *refs):
    sources, refs = refs[: n_c + 2], refs[n_c + 2 :]
    (keep_ref, give_ref, att_ref, lse_ref), scratch, sems = refs[:4], refs[4:-1], refs[-1]
    copies = fetch(sources, scratch, sems)
    q_ref, pieces, w_ref = scratch[0], scratch[1:-1], scratch[-1]
    for copy in copies[:-1]:
        copy.wait()
    rows, width = q_ref.shape
    same_row = relative_rows(f_ref[0], rows, n_f)
    visible = visibility(same_row, pieces, rows)
    keys, values = keys_and_values(pieces, rows)
    q = q_ref[...]
    lane = lax.broadcasted_iota(jnp.int32, (rows, HEAD_WIDTH), 1)
    log_totals = jnp.zeros((rows, HEAD_WIDTH), F32)
    for h in range(width // HEAD_WIDTH):
        cols = slice(h * HEAD_WIDTH, (h + 1) * HEAD_WIDTH)
        scores = jnp.where(visible, dot(q[:, cols], keys, NT) * score_scale, masked_fill)
        row_max = jnp.max(scores, axis=1, keepdims=True)
        weights = jnp.exp(scores - row_max)
        row_total = jnp.sum(weights, axis=1, keepdims=True)
        att_ref[:, cols] = (dot(weights.astype(BF16), values) / row_total).astype(BF16)
        log_totals = jnp.where(lane == h, row_max + jnp.log(row_total), log_totals)
    lse_ref[...] = log_totals
    copies[-1].wait()
    att = att_ref[...]
    tile = 512
    for start in range(0, w_ref.shape[1], tile):
        out = dot(att, w_ref[:, start : start + tile]).astype(BF16)
        keep_ref[:, start : start + tile] = out[: rows // 2]
        give_ref[:, start : start + tile] = out[rows // 2 :]


def attention_call(f, queries, w_out, pieces, n_f):
    rows, width = queries.shape
    depth = w_out.shape[1]
    half = jax.ShapeDtypeStruct((rows // 2, depth), BF16)
    att = jax.ShapeDtypeStruct((rows, width), BF16)
    lse = jax.ShapeDtypeStruct((rows, HEAD_WIDTH), F32)
    return pl.pallas_call(
        functools.partial(attention_kernel, n_f, len(pieces)),
        out_shape=(half, half, att, lse),
        in_specs=[SMEM] + [ANY] * (2 + len(pieces)),
        out_specs=[VMEM] * 4,
        scratch_shapes=scratch_like(queries, *pieces, w_out),
        compiler_params=params(56),
        cost_estimate=cost(4),
        name="attention_and_projection",
    )(f, queries, *pieces, w_out)


def fold(row):
    width = 2 * HEAD_WIDTH
    return [row[:, i : i + width] for i in range(0, row.shape[1], width)]


def attention_grad_kernel(n_f, n_c, f_ref, *refs):
    pieces, refs = refs[:n_c], refs[n_c:]
    q_ref, att_ref, lse_ref, gain_ref, ga_ref, gb_ref, w_ref = refs[:7]
    dq_ref, dkv_refs = refs[7], refs[8:]
    rows, width = q_ref.shape
    same_row = relative_rows(f_ref[0], rows, n_f)
    visible = visibility(same_row, pieces, rows)
    keys, values = keys_and_values(pieces, rows)
    order = same_row.astype(F32).astype(BF16)
    q = q_ref[...]
    grad_rows = jnp.concatenate([ga_ref[...], gb_ref[...]], axis=0)
    grad_att = dot(grad_rows, w_ref[...], NT).astype(BF16)
    grad_keys = jnp.zeros(keys.shape, F32)
    grad_values = jnp.zeros(keys.shape, F32)
    grad_q = []
    for h in range(width // HEAD_WIDTH):
        cols = slice(h * HEAD_WIDTH, (h + 1) * HEAD_WIDTH)
        g = grad_att[:, cols]
        scores = jnp.where(visible, dot(q[:, cols], keys, NT) * score_scale, masked_fill)
        probs = jnp.exp(scores - lse_ref[:, h : h + 1])
        delta = jnp.sum(g.astype(F32) * att_ref[:, cols].astype(F32), axis=1, keepdims=True)
        grad_scores = (probs * (dot(g, values, NT) - delta)).astype(BF16)
        grad_q.append((dot(grad_scores, keys) * score_scale).astype(BF16))
        grad_keys = grad_keys + dot(grad_scores, q[:, cols], TN)
        grad_values = grad_values + dot(probs.astype(BF16), g, TN)
    dq_ref[...] = dot(order, jnp.concatenate(grad_q, axis=1), TN).astype(BF16)
    high = gain_ref[...].astype(BF16)
    low = (gain_ref[...] - high.astype(F32)).astype(BF16)
    lines = fold(high) + fold(low)
    for k, dkv_ref in enumerate(dkv_refs):
        part = slice(k * rows, (k + 1) * rows)
        dkv_ref[:rows, :HEAD_WIDTH] = (grad_keys[part] * score_scale).astype(BF16)
        dkv_ref[:rows, HEAD_WIDTH:] = grad_values[part].astype(BF16)
        for i, line in enumerate(lines):
            dkv_ref[rows + i : rows + i + 1, :] = line


def attention_grad_call(f, queries, att, lse, gain, grad_a, grad_b, w_out, pieces, n_f):
    rows, width = queries.shape
    n_c = len(pieces)
    dkv = jax.ShapeDtypeStruct((rows + gain.shape[1] // HEAD_WIDTH, 2 * HEAD_WIDTH), BF16)
    return pl.pallas_call(
        functools.partial(attention_grad_kernel, n_f, n_c),
        out_shape=(jax.ShapeDtypeStruct((rows, width), BF16),) + (dkv,) * n_c,
        in_specs=[SMEM] + [VMEM] * (7 + n_c),
        out_specs=(VMEM,) * (1 + n_c),
        compiler_params=params(24),
        cost_estimate=cost(4),
        name="attention_gradients",
    )(f, *pieces, queries, att, lse, gain, grad_a, grad_b, w_out)


def norm_kernel(resid_ref, gain_ref, *refs):
    terms, (hidden_ref, normed_ref) = refs[:-2], refs[-2:]
    total = resid_ref[...].astype(F32)
    total = total + functools.reduce(jnp.add, [t[...].astype(F32) for t in terms])
    hidden = total.astype(BF16)
    hidden_ref[...] = hidden
    hidden = hidden.astype(F32)
    inv_rms = lax.rsqrt(jnp.mean(hidden * hidden, axis=1, keepdims=True) + norm_eps)
    normed_ref[...] = (hidden * inv_rms * gain_ref[...]).astype(BF16)


def norm_call(resid, gain_row, terms):
    out = jax.ShapeDtypeStruct(resid.shape, BF16)
    return pl.pallas_call(
        norm_kernel,
        out_shape=(out, out),
        in_specs=[VMEM] * (2 + len(terms)),
        out_specs=[VMEM] * 2,
        compiler_params=params(8),
        cost_estimate=cost(8),
        name="residual_and_norm",
    )(resid, gain_row, *terms)


def norm_grad_kernel(cot_ref, hidden_ref, gain_ref, *refs):
    terms, (grad_ref, gain_grad_ref) = refs[:-2], refs[-2:]
    grad_normed = functools.reduce(jnp.add, [t[...].astype(F32) for t in terms])
    hidden = hidden_ref[...].astype(F32)
    inv_rms = lax.rsqrt(jnp.mean(hidden * hidden, axis=1, keepdims=True) + norm_eps)
    gained = grad_normed * gain_ref[...]
    inv_cube = inv_rms * inv_rms * inv_rms
    grad_ref[...] = (
        cot_ref[...].astype(F32)
        + inv_rms * gained
        - hidden * inv_cube * jnp.mean(gained * hidden, axis=1, keepdims=True)
    ).astype(BF16)
    gain_grad_ref[...] = jnp.sum(grad_normed * hidden * inv_rms, axis=0, keepdims=True)


def norm_grad_call(cot, hidden, gain_row, terms):
    return pl.pallas_call(
        norm_grad_kernel,
        out_shape=(
            jax.ShapeDtypeStruct(cot.shape, BF16),
            jax.ShapeDtypeStruct(gain_row.shape, F32),
        ),
        in_specs=[VMEM] * (3 + len(terms)),
        out_specs=[VMEM] * 2,
        compiler_params=params(8),
        cost_estimate=cost(8),
        name="norm_gradients",
    )(cot, hidden, gain_row, *terms)


def gate_up_kernel(xa_ref, xb_ref, wg_ref, wu_ref, ga_ref, out_ref, gate_acc, up_acc):
    depth, width = wg_ref.shape
    half = xa_ref.shape[0]
    tile = 512
    gate_acc[...] = jnp.zeros_like(gate_acc)
    up_acc[...] = jnp.zeros_like(up_acc)

    @pl.loop(0, depth // tile)
    def _(step):
        at = pl.ds(pl.multiple_of(step * tile, tile), tile)
        x = jnp.concatenate([xa_ref[:, at], xb_ref[:, at]], axis=0)
        gate_acc[...] += dot(x, wg_ref[at, :])
        up_acc[...] += dot(x, wu_ref[at, :])

    gate, up, grad_act = gate_acc[...], up_acc[...], ga_ref[...]
    sig = jax.nn.sigmoid(gate)
    out_ref[:, :width] = (gate * sig * up).astype(BF16)
    out_ref[:, width : 2 * width] = (grad_act * up * sig * (1.0 + gate * (1.0 - sig))).astype(BF16)
    out_ref[:, 2 * width :] = (grad_act * gate * sig).astype(BF16)


def gate_up_call(xa, xb, w_gate, w_up, grad_act):
    depth, width = w_gate.shape
    rows = grad_act.shape[0]
    return pl.pallas_call(
        gate_up_kernel,
        out_shape=jax.ShapeDtypeStruct((rows, 3 * width), BF16),
        in_specs=[VMEM] * 5,
        out_specs=VMEM,
        scratch_shapes=[pltpu.VMEM((rows, width), F32)] * 2,
        compiler_params=params(24),
        cost_estimate=cost(2),
        name="gate_up_and_gradients",
    )(xa, xb, w_gate, w_up, grad_act)


def normed_grad_kernel(pay_ref, wg_ref, wu_ref, keep_ref, give_ref):
    depth, width = wg_ref.shape
    half = keep_ref.shape[0]
    tile = 512

    @pl.loop(0, depth // tile)
    def _(step):
        at = pl.ds(pl.multiple_of(step * tile, tile), tile)
        out = dot(pay_ref[:, width : 2 * width], wg_ref[at, :], NT)
        out = (out + dot(pay_ref[:, 2 * width :], wu_ref[at, :], NT)).astype(BF16)
        keep_ref[:, at] = out[:half]
        give_ref[:, at] = out[half:]


def normed_grad_call(pay, w_gate, w_up):
    depth, width = w_gate.shape
    rows = pay.shape[0]
    out = jax.ShapeDtypeStruct((rows // 2, depth), BF16)
    return pl.pallas_call(
        normed_grad_kernel,
        out_shape=(out, out),
        in_specs=[VMEM] * 3,
        out_specs=[VMEM] * 2,
        compiler_params=params(24),
        cost_estimate=cost(2),
        name="normed_gradients",
    )(pay, w_gate, w_up)


def column_blocks_kernel(c_ref, a_ref, *out_refs):
    cols = a_ref.shape[1] // len(out_refs)
    for k, out_ref in enumerate(out_refs):
        start = pl.multiple_of((c_ref[0] ^ k) * cols, 128)
        out_ref[...] = a_ref[:, pl.ds(start, cols)]


def column_blocks(c, a, n_c):
    rows, depth = a.shape
    return pl.pallas_call(
        column_blocks_kernel,
        out_shape=(jax.ShapeDtypeStruct((rows, depth // n_c), BF16),) * n_c,
        in_specs=[SMEM, VMEM],
        out_specs=(VMEM,) * n_c,
        compiler_params=params(8),
        cost_estimate=cost(1),
        name="column_blocks",
    )(c, a)


def take(refs, pieces, width):
    return jnp.concatenate([refs[i][r : r + n, at : at + width] for i, r, n, at in pieces], axis=0)


def weight_grad_kernel(left, right, n_left, widths, *refs):
    out_ref = refs[-1]
    rhs = take(refs[n_left:-1], right, widths[1])
    tile = 256
    for at in range(0, widths[0], tile):
        size = min(tile, widths[0] - at)
        lhs = take(refs[:n_left], [(i, r, n, first + at) for i, r, n, first in left], size)
        out_ref[at : at + size, :] = dot(lhs, rhs, TN)


def weight_grad_call(left, left_refs, right, right_refs, widths, name):
    return pl.pallas_call(
        functools.partial(weight_grad_kernel, left, right, len(left_refs), widths),
        out_shape=jax.ShapeDtypeStruct(widths, F32),
        in_specs=[VMEM] * (len(left_refs) + len(right_refs)),
        out_specs=VMEM,
        compiler_params=params(16),
        cost_estimate=cost(4),
        name=name,
    )(*left_refs, *right_refs)


def sum_kernel(n_f, rows, *refs):
    parts, out_ref = refs[:-1], refs[-1]
    share = rows // n_f
    lines = (parts[0].shape[0] - rows) // 2

    def tree(values):
        while len(values) > 1:
            values = [values[i] + values[i + 1] for i in range(0, len(values), 2)]
        return values[0]

    total = tree([p[:rows, :].astype(F32) for p in parts]).astype(BF16)
    gain = tree(
        [p[rows : rows + lines, :].astype(F32) + p[rows + lines :, :].astype(F32) for p in parts]
    )
    high = gain.astype(BF16)
    low = (gain - high.astype(F32)).astype(BF16)
    for f in range(n_f):
        out_ref[f, :lines, :] = high
        out_ref[f, lines : 2 * lines, :] = low
        out_ref[f, 2 * lines :, :] = total[f * share : (f + 1) * share]


def sum_call(parts, rows, n_f):
    lines = parts[0].shape[0] - rows
    return pl.pallas_call(
        functools.partial(sum_kernel, n_f, rows),
        out_shape=jax.ShapeDtypeStruct((n_f, lines + rows // n_f, 2 * HEAD_WIDTH), BF16),
        in_specs=[VMEM] * len(parts),
        out_specs=VMEM,
        compiler_params=params(8),
        cost_estimate=cost(1),
        name="sum_over_ctx",
    )(*parts)


def heads_kernel(n_f, in_ref, dk_ref, dv_ref, gain_ref):
    per_head = n_f // KEY_VALUE_HEADS
    width = 2 * HEAD_WIDTH
    lines = gain_ref.shape[1] // width
    for g in range(KEY_VALUE_HEADS):
        total = in_ref[g * per_head, 2 * lines :, :].astype(F32)
        for other in range(1, per_head):
            total = total + in_ref[g * per_head + other, 2 * lines :, :].astype(F32)
        dk_ref[:, g * HEAD_WIDTH : (g + 1) * HEAD_WIDTH] = total[:, :HEAD_WIDTH]
        dv_ref[:, g * HEAD_WIDTH : (g + 1) * HEAD_WIDTH] = total[:, HEAD_WIDTH:]
    gain = functools.reduce(
        jnp.add,
        [
            in_ref[f, :lines, :].astype(F32) + in_ref[f, lines : 2 * lines, :].astype(F32)
            for f in range(n_f)
        ],
    )
    for i in range(lines):
        gain_ref[:, i * width : (i + 1) * width] = gain[i : i + 1]


def heads_call(parts, depth, n_f):
    share = parts.shape[1] - depth // HEAD_WIDTH
    out = jax.ShapeDtypeStruct((share, KEY_VALUE_HEADS * HEAD_WIDTH), F32)
    return pl.pallas_call(
        functools.partial(heads_kernel, n_f),
        out_shape=(out, out, jax.ShapeDtypeStruct((1, depth), F32)),
        in_specs=[VMEM],
        out_specs=[VMEM] * 3,
        compiler_params=params(8),
        cost_estimate=cost(1),
        name="place_heads",
    )(parts)


def body(
    resid_in,
    queries,
    keys_in,
    value_rows_input,
    w_out,
    norm_gain,
    w_gate,
    w_up,
    w_down,
    cotangent,
    positions,
    doc_ids,
):
    rows = queries.shape[0]
    heads = queries.shape[1] // HEAD_WIDTH
    n_c, n_f = lax.axis_size("ctx"), lax.axis_size("ffn")
    c, f = lax.axis_index("ctx"), lax.axis_index("ffn")
    share, half = rows // n_f, n_f // 2
    depth = resid_in.shape[1]
    hidden_units = w_gate.shape[1]
    group = f * heads // (QUERY_HEADS // KEY_VALUE_HEADS)
    gain_row = norm_gain.reshape(1, depth)

    def exchange(x, axis, k):
        return lax.ppermute(x, axis, [(i, i ^ k) for i in range(lax.axis_size(axis))])

    def gather_rows(x):
        return jnp.concatenate([x] + [exchange(x, "ffn", 2 * m) for m in range(1, half)], axis=0)

    def beside(x):
        return exchange(x, "ffn", 1)

    def pair_sum(keep, give):
        return (keep.astype(F32) + beside(give).astype(F32)).astype(BF16)

    def scatter_rows(total):
        blocks = [total[m * share : (m + 1) * share] for m in range(half)]
        return [blocks[0]] + [exchange(blocks[m], "ffn", 2 * m) for m in range(1, half)]

    def after(x, *earlier):
        return lax.optimization_barrier((x, earlier))[0]

    bits = range(log2(n_c))

    def to_columns(blocks):
        return [blocks[0]] + [exchange(blocks[k], "ctx", k) for k in range(1, n_c)]

    cols = depth // n_c
    width = heads * HEAD_WIDTH
    pair = rows // 2
    f_ref = f.astype(jnp.int32).reshape(1)
    c_ref = c.astype(jnp.int32).reshape(1)
    q_rel, payload = prepare_call(
        f_ref,
        group.astype(jnp.int32).reshape(1),
        queries,
        keys_in,
        value_rows_input,
        positions.reshape(1, -1),
        doc_ids.reshape(1, -1),
        n_f,
    )
    pieces = [payload] + [exchange(payload, "ctx", k) for k in range(1, n_c)]
    cot_a = gather_rows(cotangent)
    cot_b = beside(cot_a)

    keep, give, att, lse = attention_call(f_ref, q_rel, w_out, pieces, n_f)
    terms = scatter_rows(pair_sum(keep, give))

    assert 2 * width == cols
    cot_blocks = list(column_blocks(c_ref, cot_a, n_c))
    att_blocks = [jnp.concatenate([att[:pair], att[pair:]], axis=1)]

    def crossing(bit):
        moving = [k for k in range(n_c) if k >> bit & 1]
        return moving, jnp.concatenate([cot_blocks[k] for k in moving] + att_blocks, axis=0)

    def crossed(moving, message):
        parts = [message[i : i + pair] for i in range(0, message.shape[0], pair)]
        for k, part in zip(moving, parts):
            cot_blocks[k] = part
        att_blocks.extend(parts[len(moving) :])

    moving, message = crossing(0)
    terms[0] = after(terms[0], message)
    hidden, normed = norm_call(resid_in, gain_row, terms)
    crossed(moving, exchange(message, "ctx", 1))

    grad_act = dot(jnp.concatenate([cot_a, cot_b], axis=0), w_down, NT)
    normed_a = gather_rows(normed)
    for bit in bits[1:]:
        moving, message = crossing(bit)
        if bit == bits[-1]:
            normed_a = after(normed_a, grad_act, message)
        crossed(moving, exchange(message, "ctx", 1 << bit))
    normed_b = beside(normed_a)
    normed_cols = to_columns(column_blocks(c_ref, normed_a, n_c))

    pay = gate_up_call(normed_a, normed_b, w_gate, w_up, grad_act)
    keep, give = normed_grad_call(pay, w_gate, w_up)
    normed_cols = jnp.concatenate(normed_cols, axis=0)
    give = after(give, normed_cols)
    total = pair_sum(keep, give)
    terms = scatter_rows(total)
    normed_side = beside(after(normed_cols, total))
    cot_cols = after(jnp.concatenate(cot_blocks, axis=0), total)
    cot_side = beside(cot_cols)

    late = after(pay, total)
    first, second = late[:pair], late[pair:]
    for bit in bits:
        first = jnp.concatenate([first, exchange(first, "ctx", 1 << bit)], axis=0)
        second = jnp.concatenate([second, exchange(second, "ctx", n_c >> 1 >> bit)], axis=0)
        if bit == bits[-2]:
            down = dot(after(pay, total)[:, :hidden_units], w_down).astype(BF16)
            terms[0] = after(terms[0], first, second, down)
            grad_resid, gain_part = norm_grad_call(cotangent, hidden, gain_row, terms)
            first, second = after((first, second), grad_resid)

    grad_a = gather_rows(grad_resid)
    down_total = pair_sum(down[:pair], down[pair:])
    grad_a = after(grad_a, down_total)
    grad_b = beside(grad_a)
    mixed_terms = scatter_rows(after(down_total, grad_a))

    grad_queries, *parts = attention_grad_call(
        f_ref, q_rel, att, lse, gain_part, grad_a, grad_b, w_out, pieces, n_f
    )
    parts = [parts[0]] + [exchange(parts[k], "ctx", k) for k in range(1, n_c)]
    grad_cols = to_columns(column_blocks(c_ref, after(grad_a, parts[1]), n_c))
    grad_cols = jnp.concatenate(grad_cols, axis=0)
    grad_side = beside(grad_cols)

    first, second = after((first, second), parts[0])
    reversed_bits = [sum((k >> b & 1) << (len(bits) - 1 - b) for b in bits) for k in range(n_c)]

    def hidden_part(i):
        at = i * hidden_units
        return [(0, 0, n_c * pair, at)] + [(1, k * pair, pair, at) for k in reversed_bits]

    columns = [(0, 0, n_c * pair, 0), (1, 0, n_c * pair, 0)]
    att_rows = [(k, 0, pair, 0) for k in range(n_c)] + [(k, 0, pair, width) for k in range(n_c)]
    normed_pair, shape = (normed_cols, normed_side), (cols, hidden_units)
    both = (first, second)
    grad_w_gate = weight_grad_call(columns, normed_pair, hidden_part(1), both, shape, "grad_w_gate")
    grad_w_up = weight_grad_call(columns, normed_pair, hidden_part(2), both, shape, "grad_w_up")
    grad_w_down = weight_grad_call(
        hidden_part(0), both, columns, (cot_cols, cot_side), (hidden_units, cols), "grad_w_down"
    )
    grad_w_out = weight_grad_call(
        att_rows, att_blocks, columns, (grad_cols, grad_side), (width, cols), "grad_w_out"
    )

    mixed = functools.reduce(jnp.add, [t.astype(F32) for t in mixed_terms])
    mixed = (hidden.astype(F32) + mixed).astype(BF16)

    grad_keys, grad_values, grad_gain = heads_call(
        lax.all_to_all(sum_call(parts, rows, n_f), "ffn", 0, 0), depth, n_f
    )
    return (
        mixed,
        grad_resid,
        grad_queries,
        grad_keys,
        grad_values,
        grad_gain.reshape(depth),
        grad_w_out,
        grad_w_gate,
        grad_w_up,
        grad_w_down,
    )


def solution(mesh):
    return jax.shard_map(
        body,
        mesh=mesh,
        in_specs=(
            P(("ctx", "ffn"), None),
            P("ctx", "ffn"),
            P("ctx", None),
            P("ctx", None),
            P("ffn", None),
            P(),
            P(None, "ffn"),
            P(None, "ffn"),
            P("ffn", None),
            P(("ctx", "ffn"), None),
            P("ctx"),
            P(),
        ),
        out_specs=(
            P(("ctx", "ffn"), None),
            P(("ctx", "ffn"), None),
            P("ctx", "ffn"),
            P(("ctx", "ffn"), None),
            P(("ctx", "ffn"), None),
            P(),
            P("ffn", "ctx"),
            P("ctx", "ffn"),
            P("ctx", "ffn"),
            P("ffn", "ctx"),
        ),
        check_vma=False,
    )
```

time: 204 us -> 176 us (0.86)
  starting transfers between devices: 79.5 us -> 61 us
  matrix products: 17.9 us -> 3.7 us
  Pallas kernels: 23.9 us -> 36.5 us
  other arithmetic: 7.81 us -> 3.3 us
  local copies, waits for them, and re-layouts: 10.5 us -> 7.1 us
    ppermute x52 -> x45, starting transfers between devices: 75.6 us -> 53.4 us  [exchange(): lax.ppermute(x, axis, [(i, i ^ k) for i in range(lax.axis_size(axis))])]
    dot_general x5 -> x2, matrix products: 17.9 us -> 3.7 us  [dot(): return lax.dot_general(a, b, dims, preferred_element_type=F32)]
    pallas_call x2 -> x11, Pallas kernels: 10.7 us -> 21 us  [the longest x4 13.7 us: weight_grad_call(): pl.pallas_call(functools.partial(weight_grad_kernel, left, right, len(lef...]
    ppermute x52 -> x45, waiting for transfers between devices: 58.2 us -> 62.9 us  [exchange(): lax.ppermute(x, axis, [(i, i ^ k) for i in range(lax.axis_size(axis))])]
    all_to_all x1, waiting for transfers between devices: 3.95 us -> 0.05 us  [body(): lax.all_to_all(sum_call(parts, rows, n_f), 'ffn', 0, 0)]
    all_to_all x1, starting transfers between devices: 3.9 us -> 7.58 us  [body(): lax.all_to_all(sum_call(parts, rows, n_f), 'ffn', 0, 0)]
    unnamed x43 -> x64, local copies, waits for them, and re-layouts: 8.09 us -> 4.53 us
    concatenate x11 -> x10, other arithmetic: 4.66 us -> 2.17 us  [the longest x2 0.97 us: gather_rows(): jnp.concatenate([x] + [exchange(x, 'ffn', 2 * m) for m in range(1, half)]...]
  transfers between devices with their start and end apart: 53 -> 46, of which waited for: 19 -> 22; matrix products, arithmetic and copies ran while one was open for 14% -> 6% of each run, Pallas kernels for 12% -> 11%
where the time goes in v2:
time: 176 us
  waiting for transfers between devices  62.9 us (36%)
  starting transfers between devices  61 us (35%)
  Pallas kernels  36.5 us (21%)
  local copies, waits for them, and re-layouts  7.1 us (4%)
  matrix products  3.7 us (2%)
  other arithmetic  3.3 us (2%)
    ppermute x45, waiting for transfers between devices, exchange(): lax.ppermute(x, axis, [(i, i ^ k) for i in range(lax.axis_size(axis))])  62.9 us
    ppermute x45, starting transfers between devices, exchange(): lax.ppermute(x, axis, [(i, i ^ k) for i in range(lax.axis_size(axis))])  53.4 us
    pallas_call x4, Pallas kernels, weight_grad_call(): pl.pallas_call(functools.partial(weight_grad_kernel, left, right, len(lef...  13.7 us
    all_to_all x1, starting transfers between devices, body(): lax.all_to_all(sum_call(parts, rows, n_f), 'ffn', 0, 0)  7.58 us
    pallas_call x1, Pallas kernels, normed_grad_call(): pl.pallas_call(normed_grad_kernel, out_shape=(out, out), in_specs=[VMEM]...  5.79 us
    unnamed x64, local copies, waits for them, and re-layouts  4.53 us
    pallas_call x1, Pallas kernels, attention_call(): pl.pallas_call(functools.partial(attention_kernel, n_f, len(pieces)), out...  4.3 us
    pallas_call x1, Pallas kernels, gate_up_call(): pl.pallas_call(gate_up_kernel, out_shape=jax.ShapeDtypeStruct((rows, 3 *...  4.21 us
  transfers between devices with their start and end apart: 46, of which 22 were waited for; matrix products, arithmetic and copies ran while one was open for 6% of the time, Pallas kernels for 11%

profile of v2, /device:TPU:0, one launch (start us, length us, event | category | flops | bytes accessed | tf_op | source)
XLA Modules:
  0.0 175.8 jit_solution(5769016535456689510)
XLA Ops:
  0.7 1.9 %prepare_attention.1 = (bf16[128,512]{1,0:T(8,128)(2,1)}, bf16[272,128]{1,0:T(8,128)(2,1)}) custom-call(s32[1]{0:T(128)} %bitcast.1.f_ref, s32[1]{0:T(128)} %bitcast.2.group_ref, bf16[128,512]{1,0:T(8,128)(2,1)} %q_hbm.1, bf16[128,1024]{1,0:T(8,128)(2,1)} %k_hbm.1, bf16[128,1024]{1,0:T(8,128)(2,1)} %v_hbm.1, s32[1,128]{1,0:T(1,128)} %bitcast.19, ...), custom_call_target="tpu_custom_call" | custom-call | flops 1000000000 | bytes 4000000 | tf_op jit(solution)/shard_map/prepare_attention/pallas_call | solution.py:122
  2.5 3.0 %collective-permute-start = (bf16[272,128]{1,0:T(8,128)(2,1)}, bf16[272,128]{1,0:T(8,128)(2,1)S(1)}, u32[]{:S(2)}, u32[]{:S(2)}) collective-permute-start(bf16[272,128]{1,0:T(8,128)(2,1)} %get-tuple-element.57.refs_1_.refs_0_), channel_id=1, source_target_pairs={{0,8},{8,0},{16,24},{24,16},{1,9},{9,1},{17,25},{25,17},{2,10},{10... | collective-permute-start | bytes 208904 | tf_op jit(solution)/shard_map/ppermute | solution.py:505
  5.5 1.5 collective-permute-start.1
  7.1 2.0 %collective-permute-start.4 = (bf16[16,4096]{1,0:T(8,128)(2,1)S(1)}, bf16[16,4096]{1,0:T(8,128)(2,1)S(1)}, u32[]{:S(2)}, u32[]{:S(2)}) collective-permute-start(bf16[16,4096]{1,0:T(8,128)(2,1)S(1)} %copy-done.3), channel_id=1, source_target_pairs={{0,2},{1,3},{2,0},{3,1},{4,6},{5,7},{6,4},{7,5},{8,10},{9,11},{10,... | collective-permute-start | bytes 393224 | tf_op jit(solution)/shard_map/ppermute | solution.py:505
  9.1 2.6 %collective-permute-start.5 = (bf16[16,4096]{1,0:T(8,128)(2,1)S(1)}, bf16[16,4096]{1,0:T(8,128)(2,1)S(1)}, u32[]{:S(2)}, u32[]{:S(2)}) collective-permute-start(bf16[16,4096]{1,0:T(8,128)(2,1)S(1)} %copy-done.3), channel_id=1, source_target_pairs={{0,4},{1,5},{2,6},{3,7},{4,0},{5,1},{6,2},{7,3},{8,12},{9,13},{10,... | collective-permute-start | bytes 393224 | tf_op jit(solution)/shard_map/ppermute | solution.py:505
  13.1 4.3 %attention_and_projection.1 = (bf16[64,4096]{1,0:T(8,128)(2,1)}, bf16[64,4096]{1,0:T(8,128)(2,1)}, bf16[128,512]{1,0:T(8,128)(2,1)}, f32[128,128]{1,0:T(8,128)}) custom-call(s32[1]{0:T(128)} %bitcast.1.f_ref, bf16[128,512]{1,0:T(8,128)(2,1)} %get-tuple-element.56.refs_0_.refs_4_, bf16[272,128]{1,0:T(8,128)(2,1)} %get-tuple-element.57.refs_1_.refs_0_, ...), custom_call_target="tpu_custom_call" | custom-call | flops 2000000000 | bytes 8000000 | tf_op jit(solution)/shard_map/attention_and_projection/pallas_call | solution.py:176
  18.4 2.8 %collective-permute-done.5 = bf16[16,4096]{1,0:T(8,128)(2,1)S(1)} collective-permute-done((bf16[16,4096]{1,0:T(8,128)(2,1)S(1)}, bf16[16,4096]{1,0:T(8,128)(2,1)S(1)}, u32[]{:S(2)}, u32[]{:S(2)}) %collective-permute-start.5) | collective-permute-done | bytes 131104 | tf_op jit(solution)/shard_map/ppermute | solution.py:505
  21.4 1.6 collective-permute-start.14
  23.4 5.8 %collective-permute-done.14 = bf16[192,1024]{1,0:T(8,128)(2,1)S(1)} collective-permute-done((bf16[192,1024]{1,0:T(8,128)(2,1)S(1)}, bf16[192,1024]{1,0:T(8,128)(2,1)S(1)}, u32[]{:S(2)}, u32[]{:S(2)}) %collective-permute-start.14) | collective-permute-done | bytes 393248 | tf_op jit(solution)/shard_map/ppermute | solution.py:505
  29.5 3.6 %collective-permute-start.7 = (bf16[16,4096]{1,0:T(8,128)(2,1)S(1)}, bf16[16,4096]{1,0:T(8,128)(2,1)S(1)}, u32[]{:S(2)}, u32[]{:S(2)}) collective-permute-start(bf16[16,4096]{1,0:T(8,128)(2,1)S(1)} %get-tuple-element.115), channel_id=1, source_target_pairs={{0,2},{1,3},{2,0},{3,1},{4,6},{5,7},{6,4},{7,5},{8,10},{9,11},{10,... | collective-permute-start | bytes 393224 | tf_op jit(solution)/shard_map/ppermute | solution.py:505
  34.0 1.6 collective-permute-start.9
  36.3 7.1 %collective-permute-done.8.refs_2_ = bf16[16,4096]{1,0:T(8,128)(2,1)S(1)} collective-permute-done((bf16[16,4096]{1,0:T(8,128)(2,1)S(1)}, bf16[16,4096]{1,0:T(8,128)(2,1)S(1)}, u32[]{:S(2)}, u32[]{:S(2)}) %collective-permute-start.8) | collective-permute-done | bytes 131104 | tf_op jit(solution)/shard_map/ppermute | solution.py:505
  43.7 2.2 %collective-permute-start.10 = (bf16[16,4096]{1,0:T(8,128)(2,1)S(1)}, bf16[16,4096]{1,0:T(8,128)(2,1)S(1)}, u32[]{:S(2)}, u32[]{:S(2)}) collective-permute-start(bf16[16,4096]{1,0:T(8,128)(2,1)S(1)} %get-tuple-element.65), channel_id=1, source_target_pairs={{0,2},{1,3},{2,0},{3,1},{4,6},{5,7},{6,4},{7,5},{8,10},{9,11},{10,... | collective-permute-start | bytes 393224 | tf_op jit(solution)/shard_map/ppermute | solution.py:505
  46.6 1.7 collective-permute-start.12
  48.3 2.4 %fusion.8.ga_ref = f32[128,896]{1,0:T(8,128)S(1)} fusion(bf16[128,4096]{1,0:T(8,128)(2,1)S(1)} %constant_dynamic-update-slice_fusion.4, bf16[896,4096]{1,0:T(8,128)(2,1)S(1)} %bitcast.17), kind=kOutput, calls=%fused_computation.40 | convolution fusion | flops 939524096 | bytes 8847360 | tf_op jit(solution)/shard_map/dot_general | solution.py:31
  50.8 6.9 %collective-permute-done.11 = bf16[16,4096]{1,0:T(8,128)(2,1)S(1)} collective-permute-done((bf16[16,4096]{1,0:T(8,128)(2,1)S(1)}, bf16[16,4096]{1,0:T(8,128)(2,1)S(1)}, u32[]{:S(2)}, u32[]{:S(2)}) %collective-permute-start.11) | collective-permute-done | bytes 131104 | tf_op jit(solution)/shard_map/ppermute | solution.py:505
  57.9 1.5 collective-permute-start.16
  59.4 1.5 collective-permute-start.17
  61.5 2.6 %collective-permute-done.16 = bf16[64,1024]{1,0:T(8,128)(2,1)S(1)} collective-permute-done((bf16[64,1024]{1,0:T(8,128)(2,1)S(1)}, bf16[64,1024]{1,0:T(8,128)(2,1)S(1)}, u32[]{:S(2)}, u32[]{:S(2)}) %collective-permute-start.16) | collective-permute-done | bytes 131104 | tf_op jit(solution)/shard_map/ppermute | solution.py:505
  64.1 3.7 %collective-permute-done.17 = bf16[64,1024]{1,0:T(8,128)(2,1)S(1)} collective-permute-done((bf16[64,1024]{1,0:T(8,128)(2,1)S(1)}, bf16[64,1024]{1,0:T(8,128)(2,1)S(1)}, u32[]{:S(2)}, u32[]{:S(2)}) %collective-permute-start.17) | collective-permute-done | bytes 131104 | tf_op jit(solution)/shard_map/ppermute | solution.py:505
  67.9 4.2 %gate_up_and_gradients.1.pay_ref = bf16[128,2688]{1,0:T(8,128)(2,1)S(1)} custom-call(bf16[64,4096]{1,0:T(8,128)(2,1)S(1)} %pad_maximum_fusion.4.xa_ref.a_ref, bf16[64,4096]{1,0:T(8,128)(2,1)S(1)} %collective-permute-done.15.xb_ref, bf16[4096,896]{1,0:T(8,128)(2,1)S(1)} %bitcast.11, bf16[4096,896]{1,0:T(8,128)(2,1)S(1)} %bitcast.13, f32[128,896]{1,0:T(8,128)S(1)} %fusion.8.ga_ref), custom_call_target="tpu_custom_call" | custom-call | flops 1000000000 | bytes 4000000 | tf_op jit(solution)/shard_map/gate_up_and_gradients/pallas_call | solution.py:323
  72.1 5.8 %normed_gradients.1 = (bf16[64,4096]{1,0:T(8,128)(2,1)S(1)}, bf16[64,4096]{1,0:T(8,128)(2,1)S(1)}) custom-call(bf16[128,2688]{1,0:T(8,128)(2,1)S(1)} %gate_up_and_gradients.1.pay_ref, bf16[4096,896]{1,0:T(8,128)(2,1)S(1)} %bitcast.11, bf16[4096,896]{1,0:T(8,128)(2,1)S(1)} %bitcast.13), custom_call_target="tpu_custom_call" | custom-call | flops 1000000000 | bytes 4000000 | tf_op jit(solution)/shard_map/normed_gradients/pallas_call | solution.py:353
  78.0 1.9 %collective-permute-done.19 = bf16[64,4096]{1,0:T(8,128)(2,1)S(1)} collective-permute-done((bf16[64,4096]{1,0:T(8,128)(2,1)S(1)}, bf16[64,4096]{1,0:T(8,128)(2,1)S(1)}, u32[]{:S(2)}, u32[]{:S(2)}) %collective-permute-start.19) | collective-permute-done | bytes 524320 | tf_op jit(solution)/shard_map/ppermute | solution.py:505
  80.2 1.6 collective-permute-start.22
  82.3 2.1 %collective-permute-start.23 = (bf16[16,4096]{1,0:T(8,128)(2,1)S(1)}, bf16[16,4096]{1,0:T(8,128)(2,1)S(1)}, u32[]{:S(2)}, u32[]{:S(2)}) collective-permute-start(bf16[16,4096]{1,0:T(8,128)(2,1)S(1)} %get-tuple-element.111), channel_id=1, source_target_pairs={{0,2},{1,3},{2,0},{3,1},{4,6},{5,7},{6,4},{7,5},{8,10},{9,11},{10,... | collective-permute-start | bytes 393224 | tf_op jit(solution)/shard_map/ppermute | solution.py:505
  85.0 1.8 %collective-permute-start.25 = (bf16[16,4096]{1,0:T(8,128)(2,1)S(1)}, bf16[16,4096]{1,0:T(8,128)(2,1)S(1)}, u32[]{:S(2)}, u32[]{:S(2)}) collective-permute-start(bf16[16,4096]{1,0:T(8,128)(2,1)S(1)} %get-tuple-element.109), channel_id=1, source_target_pairs={{0,6},{1,7},{2,4},{3,5},{4,2},{5,3},{6,0},{7,1},{8,14},{9,15},{10,... | collective-permute-start | bytes 393224 | tf_op jit(solution)/shard_map/ppermute | solution.py:505
  88.0 2.3 %collective-permute-done.22 = bf16[64,2688]{1,0:T(8,128)(2,1)S(1)} collective-permute-done((bf16[64,2688]{1,0:T(8,128)(2,1)S(1)}, bf16[64,2688]{1,0:T(8,128)(2,1)S(1)}, u32[]{:S(2)}, u32[]{:S(2)}) %collective-permute-start.22) | collective-permute-done | bytes 344096 | tf_op jit(solution)/shard_map/ppermute | solution.py:505
  91.7 5.2 %collective-permute-done.24.refs_2_ = bf16[16,4096]{1,0:T(8,128)(2,1)S(1)} collective-permute-done((bf16[16,4096]{1,0:T(8,128)(2,1)S(1)}, bf16[16,4096]{1,0:T(8,128)(2,1)S(1)}, u32[]{:S(2)}, u32[]{:S(2)}) %collective-permute-start.24) | collective-permute-done | bytes 131104 | tf_op jit(solution)/shard_map/ppermute | solution.py:505
  97.8 2.1 %collective-permute-start.26 = (bf16[16,4096]{1,0:T(8,128)(2,1)}, bf16[16,4096]{1,0:T(8,128)(2,1)S(1)}, u32[]{:S(2)}, u32[]{:S(2)}) collective-permute-start(bf16[16,4096]{1,0:T(8,128)(2,1)} %get-tuple-element.47), channel_id=1, source_target_pairs={{0,2},{1,3},{2,0},{3,1},{4,6},{5,7},{6,4},{7,5},{8,10},{9,11},{10,... | collective-permute-start | bytes 393224 | tf_op jit(solution)/shard_map/ppermute | solution.py:505
  100.5 1.8 %collective-permute-start.28 = (bf16[16,4096]{1,0:T(8,128)(2,1)}, bf16[16,4096]{1,0:T(8,128)(2,1)S(1)}, u32[]{:S(2)}, u32[]{:S(2)}) collective-permute-start(bf16[16,4096]{1,0:T(8,128)(2,1)} %get-tuple-element.47), channel_id=1, source_target_pairs={{0,6},{1,7},{2,4},{3,5},{4,2},{5,3},{6,0},{7,1},{8,14},{9,15},{10,... | collective-permute-start | bytes 393224 | tf_op jit(solution)/shard_map/ppermute | solution.py:505
  104.2 7.7 %collective-permute-done.27 = bf16[16,4096]{1,0:T(8,128)(2,1)S(1)} collective-permute-done((bf16[16,4096]{1,0:T(8,128)(2,1)}, bf16[16,4096]{1,0:T(8,128)(2,1)S(1)}, u32[]{:S(2)}, u32[]{:S(2)}) %collective-permute-start.27) | collective-permute-done | bytes 131104 | tf_op jit(solution)/shard_map/ppermute | solution.py:505
  113.2 2.0 %collective-permute-start.29 = (bf16[16,4096]{1,0:T(8,128)(2,1)S(1)}, bf16[16,4096]{1,0:T(8,128)(2,1)S(1)}, u32[]{:S(2)}, u32[]{:S(2)}) collective-permute-start(bf16[16,4096]{1,0:T(8,128)(2,1)S(1)} %get-tuple-element.106), channel_id=1, source_target_pairs={{0,2},{1,3},{2,0},{3,1},{4,6},{5,7},{6,4},{7,5},{8,10},{9,11},{10,... | collective-permute-start | bytes 393224 | tf_op jit(solution)/shard_map/ppermute | solution.py:505
  116.0 1.6 collective-permute-start.31
  119.7 1.5 collective-permute-start.43
  121.2 5.8 %collective-permute-done.30 = bf16[16,4096]{1,0:T(8,128)(2,1)S(1)} collective-permute-done((bf16[16,4096]{1,0:T(8,128)(2,1)S(1)}, bf16[16,4096]{1,0:T(8,128)(2,1)S(1)}, u32[]{:S(2)}, u32[]{:S(2)}) %collective-permute-start.30) | collective-permute-done | bytes 131104 | tf_op jit(solution)/shard_map/ppermute | solution.py:505
  130.2 3.7 %attention_gradients.1 = (bf16[128,512]{1,0:T(8,128)(2,1)}, bf16[160,256]{1,0:T(8,128)(2,1)S(1)}, bf16[160,256]{1,0:T(8,128)(2,1)S(1)}, bf16[160,256]{1,0:T(8,128)(2,1)S(1)}, bf16[160,256]{1,0:T(8,128)(2,1)S(1)}) custom-call(s32[1]{0:T(128)} %bitcast.1.f_ref, bf16[272,128]{1,0:T(8,128)(2,1)S(1)} %copy-done.9, bf16[272,128]{1,0:T(8,128)(2,1)S(1)} %copy-done.11, ...), custom_call_target="tpu_custom_call" | custom-call | flops 2000000000 | bytes 8000000 | tf_op jit(solution)/shard_map/attention_gradients/pallas_call | solution.py:234
  134.8 2.7 %collective-permute-done.43 = bf16[128,2688]{1,0:T(8,128)(2,1)S(1)} collective-permute-done((bf16[128,2688]{1,0:T(8,128)(2,1)S(1)}, bf16[128,2688]{1,0:T(8,128)(2,1)S(1)}, u32[]{:S(2)}, u32[]{:S(2)}) %collective-permute-start.43) | collective-permute-done | bytes 688160 | tf_op jit(solution)/shard_map/ppermute | solution.py:505
  138.9 1.6 collective-permute-start.37
  141.1 1.5 collective-permute-start.38
  144.0 1.3 collective-permute-start.39
  146.0 2.0 %collective-permute-done.38 = bf16[64,1024]{1,0:T(8,128)(2,1)S(1)} collective-permute-done((bf16[64,1024]{1,0:T(8,128)(2,1)S(1)}, bf16[64,1024]{1,0:T(8,128)(2,1)S(1)}, u32[]{:S(2)}, u32[]{:S(2)}) %collective-permute-start.38) | collective-permute-done | bytes 131104 | tf_op jit(solution)/shard_map/ppermute | solution.py:505
  148.0 1.4 collective-permute-start.35
  151.0 3.1 %grad_w_up.1 = f32[1024,896]{1,0:T(8,128)} custom-call(bf16[256,1024]{1,0:T(8,128)(2,1)S(1)} %constant_dynamic-update-slice_fusion.9.refs_0_, bf16[256,1024]{1,0:T(8,128)(2,1)S(1)} %collective-permute-done.41.refs_1_, bf16[256,2688]{1,0:T(8,128)(2,1)S(1)} %pad_maximum_fusion.refs_2_.refs_0_, bf16[256,2688]{1,0:T(8,128)(2,1)S(1)} %pad_maximum_fusion.1.refs_3_.refs_1_), custom_call_target="tpu_custom_call" | custom-call | flops 2000000000 | bytes 8000000 | tf_op jit(solution)/shard_map/grad_w_up/pallas_call | solution.py:399
  154.9 7.6 %all-to-all-start = ((bf16[8,48,256]{2,1,0:T(8,128)(2,1)}), bf16[8,48,256]{2,1,0:T(8,128)(2,1)}, u32[]{:S(2)}, u32[]{:S(2)}) async-start(bf16[8,48,256]{2,1,0:T(8,128)(2,1)} %copy-done.2), calls=%async_computation | async-start | bytes 393216 | tf_op jit(solution)/shard_map/all_to_all | solution.py:638
  163.5 3.1 %grad_w_gate.1 = f32[1024,896]{1,0:T(8,128)} custom-call(bf16[256,1024]{1,0:T(8,128)(2,1)S(1)} %constant_dynamic-update-slice_fusion.9.refs_0_, bf16[256,1024]{1,0:T(8,128)(2,1)S(1)} %copy-done.1, bf16[256,2688]{1,0:T(8,128)(2,1)S(1)} %pad_maximum_fusion.refs_2_.refs_0_, bf16[256,2688]{1,0:T(8,128)(2,1)S(1)} %pad_maximum_fusion.1.refs_3_.refs_1_), custom_call_target="tpu_custom_call" | custom-call | flops 2000000000 | bytes 8000000 | tf_op jit(solution)/shard_map/grad_w_gate/pallas_call | solution.py:399
  166.7 4.2 %grad_w_down.1 = f32[896,1024]{1,0:T(8,128)} custom-call(bf16[256,2688]{1,0:T(8,128)(2,1)S(1)} %pad_maximum_fusion.refs_2_.refs_0_, bf16[256,2688]{1,0:T(8,128)(2,1)S(1)} %pad_maximum_fusion.1.refs_3_.refs_1_, bf16[256,1024]{1,0:T(8,128)(2,1)} %pad_maximum_fusion.7.refs_2_, bf16[256,1024]{1,0:T(8,128)(2,1)} %collective-permute-done.44.refs_3_), custom_call_target="tpu_custom_call" | custom-call | flops 2000000000 | bytes 8000000 | tf_op jit(solution)/shard_map/grad_w_down/pallas_call | solution.py:399
  170.9 1.6 place_heads.1
  172.5 3.3 %grad_w_out.1 = f32[512,1024]{1,0:T(8,128)} custom-call(bf16[64,1024]{1,0:T(8,128)(2,1)S(1)} %pad_maximum_fusion.8.refs_0_, bf16[64,1024]{1,0:T(8,128)(2,1)S(1)} %get-tuple-element.118.refs_1_, bf16[64,1024]{1,0:T(8,128)(2,1)S(1)} %copy-done.6, bf16[64,1024]{1,0:T(8,128)(2,1)S(1)} %copy-done.5, ...), custom_call_target="tpu_custom_call" | custom-call | flops 2000000000 | bytes 8000000 | tf_op jit(solution)/shard_map/grad_w_out/pallas_call | solution.py:399
  (155 shorter events, 29.6 us)
Async XLA Ops:
  2.5 9.2 %collective-permute-start = (bf16[272,128]{1,0:T(8,128)(2,1)}, bf16[272,128]{1,0:T(8,128)(2,1)S(1)}, u32[]{:S(2)}, u32[]{:S(2)}) collective-permute-start(bf16[272,128]{1,0:T(8,128)(2,1)} %get-tuple-element.57.refs_1_.refs_0_), channel_id=1, source_target_pairs={{0,8},{8,0},{16,24},{24,16},{1,9},{9,1},{17,25},{25,17},{2,10},{10... | collective-permute-start | bytes 208904 | tf_op jit(solution)/shard_map/ppermute | solution.py:505
  5.5 6.6 %collective-permute-start.1 = (bf16[272,128]{1,0:T(8,128)(2,1)}, bf16[272,128]{1,0:T(8,128)(2,1)S(1)}, u32[]{:S(2)}, u32[]{:S(2)}) collective-permute-start(bf16[272,128]{1,0:T(8,128)(2,1)} %get-tuple-element.57.refs_1_.refs_0_), channel_id=1, source_target_pairs={{0,16},{8,24},{16,0},{24,8},{1,17},{9,25},{17,1},{25,9},{2,18},{10... | collective-permute-start | bytes 208904 | tf_op jit(solution)/shard_map/ppermute | solution.py:505
  7.1 5.4 %collective-permute-start.2 = (bf16[272,128]{1,0:T(8,128)(2,1)}, bf16[272,128]{1,0:T(8,128)(2,1)S(1)}, u32[]{:S(2)}, u32[]{:S(2)}) collective-permute-start(bf16[272,128]{1,0:T(8,128)(2,1)} %get-tuple-element.57.refs_1_.refs_0_), channel_id=1, source_target_pairs={{0,24},{8,16},{16,8},{24,0},{1,25},{9,17},{17,9},{25,1},{2,26},{10... | collective-permute-start | bytes 208904 | tf_op jit(solution)/shard_map/ppermute | solution.py:505
  7.1 11.3 %collective-permute-start.4 = (bf16[16,4096]{1,0:T(8,128)(2,1)S(1)}, bf16[16,4096]{1,0:T(8,128)(2,1)S(1)}, u32[]{:S(2)}, u32[]{:S(2)}) collective-permute-start(bf16[16,4096]{1,0:T(8,128)(2,1)S(1)} %copy-done.3), channel_id=1, source_target_pairs={{0,2},{1,3},{2,0},{3,1},{4,6},{5,7},{6,4},{7,5},{8,10},{9,11},{10,... | collective-permute-start | bytes 393224 | tf_op jit(solution)/shard_map/ppermute | solution.py:505
  9.1 12.1 %collective-permute-start.5 = (bf16[16,4096]{1,0:T(8,128)(2,1)S(1)}, bf16[16,4096]{1,0:T(8,128)(2,1)S(1)}, u32[]{:S(2)}, u32[]{:S(2)}) collective-permute-start(bf16[16,4096]{1,0:T(8,128)(2,1)S(1)} %copy-done.3), channel_id=1, source_target_pairs={{0,4},{1,5},{2,6},{3,7},{4,0},{5,1},{6,2},{7,3},{8,12},{9,13},{10,... | collective-permute-start | bytes 393224 | tf_op jit(solution)/shard_map/ppermute | solution.py:505
  11.8 9.5 %collective-permute-start.6 = (bf16[16,4096]{1,0:T(8,128)(2,1)S(1)}, bf16[16,4096]{1,0:T(8,128)(2,1)S(1)}, u32[]{:S(2)}, u32[]{:S(2)}) collective-permute-start(bf16[16,4096]{1,0:T(8,128)(2,1)S(1)} %copy-done.3), channel_id=1, source_target_pairs={{0,6},{1,7},{2,4},{3,5},{4,2},{5,3},{6,0},{7,1},{8,14},{9,15},{10,... | collective-permute-start | bytes 393224 | tf_op jit(solution)/shard_map/ppermute | solution.py:505
  13.1 35.2 %slice-start.4 = ((s8[7340032]{0:T(1024)(128)(4,1)}), s8[3145728]{0:T(1024)(128)(4,1)S(1)}, s32[]{:S(2)}) async-start(s8[7340032]{0:T(1024)(128)(4,1)} %bitcast.16), calls=%async_computation.5 | async-start | bytes 6291456
  21.4 7.8 %collective-permute-start.14 = (bf16[192,1024]{1,0:T(8,128)(2,1)S(1)}, bf16[192,1024]{1,0:T(8,128)(2,1)S(1)}, u32[]{:S(2)}, u32[]{:S(2)}) collective-permute-start(bf16[192,1024]{1,0:T(8,128)(2,1)S(1)} %maximum_maximum_fusion), channel_id=1, source_target_pairs={{0,8},{8,0},{16,24},{24,16},{1,9},{9,1},{17,25},{25,17},{2,10},{10... | collective-permute-start | bytes 1179656 | tf_op jit(solution)/shard_map/ppermute | solution.py:505
  22.9 6.4 %collective-permute-start.3 = (bf16[64,4096]{1,0:T(8,128)(2,1)S(1)}, bf16[64,4096]{1,0:T(8,128)(2,1)S(1)}, u32[]{:S(2)}, u32[]{:S(2)}) collective-permute-start(bf16[64,4096]{1,0:T(8,128)(2,1)S(1)} %copy-done.20), channel_id=1, source_target_pairs={{0,1},{1,0},{2,3},{3,2},{4,5},{5,4},{6,7},{7,6},{8,9},{9,8},{10,11... | collective-permute-start | bytes 1572872 | tf_op jit(solution)/shard_map/ppermute | solution.py:505
  22.9 12.6 %collective-permute-start.13 = (bf16[64,4096]{1,0:T(8,128)(2,1)S(1)}, bf16[64,4096]{1,0:T(8,128)(2,1)S(1)}, u32[]{:S(2)}, u32[]{:S(2)}) collective-permute-start(bf16[64,4096]{1,0:T(8,128)(2,1)S(1)} %get-tuple-element.121.a_ref), channel_id=1, source_target_pairs={{0,1},{1,0},{2,3},{3,2},{4,5},{5,4},{6,7},{7,6},{8,9},{9,8},{10,11... | collective-permute-start | bytes 1572872 | tf_op jit(solution)/shard_map/ppermute | solution.py:505
  29.5 6.8 %collective-permute-start.7 = (bf16[16,4096]{1,0:T(8,128)(2,1)S(1)}, bf16[16,4096]{1,0:T(8,128)(2,1)S(1)}, u32[]{:S(2)}, u32[]{:S(2)}) collective-permute-start(bf16[16,4096]{1,0:T(8,128)(2,1)S(1)} %get-tuple-element.115), channel_id=1, source_target_pairs={{0,2},{1,3},{2,0},{3,1},{4,6},{5,7},{6,4},{7,5},{8,10},{9,11},{10,... | collective-permute-start | bytes 393224 | tf_op jit(solution)/shard_map/ppermute | solution.py:505
  33.1 10.3 %collective-permute-start.8 = (bf16[16,4096]{1,0:T(8,128)(2,1)S(1)}, bf16[16,4096]{1,0:T(8,128)(2,1)S(1)}, u32[]{:S(2)}, u32[]{:S(2)}) collective-permute-start(bf16[16,4096]{1,0:T(8,128)(2,1)S(1)} %get-tuple-element.114), channel_id=1, source_target_pairs={{0,4},{1,5},{2,6},{3,7},{4,0},{5,1},{6,2},{7,3},{8,12},{9,13},{10,... | collective-permute-start | bytes 393224 | tf_op jit(solution)/shard_map/ppermute | solution.py:505
  34.0 9.4 %collective-permute-start.9 = (bf16[16,4096]{1,0:T(8,128)(2,1)S(1)}, bf16[16,4096]{1,0:T(8,128)(2,1)S(1)}, u32[]{:S(2)}, u32[]{:S(2)}) collective-permute-start(bf16[16,4096]{1,0:T(8,128)(2,1)S(1)} %get-tuple-element.113), channel_id=1, source_target_pairs={{0,6},{1,7},{2,4},{3,5},{4,2},{5,3},{6,0},{7,1},{8,14},{9,15},{10,... | collective-permute-start | bytes 393224 | tf_op jit(solution)/shard_map/ppermute | solution.py:505
  43.4 24.5 %slice-start.2 = ((s8[7340032]{0:T(1024)(128)(4,1)}), s8[4194304]{0:T(1024)(128)(4,1)S(1)}, s32[]{:S(2)}) async-start(s8[7340032]{0:T(1024)(128)(4,1)} %bitcast.12), calls=%async_computation.3 | async-start | bytes 8388608
  43.7 7.1 %collective-permute-start.10 = (bf16[16,4096]{1,0:T(8,128)(2,1)S(1)}, bf16[16,4096]{1,0:T(8,128)(2,1)S(1)}, u32[]{:S(2)}, u32[]{:S(2)}) collective-permute-start(bf16[16,4096]{1,0:T(8,128)(2,1)S(1)} %get-tuple-element.65), channel_id=1, source_target_pairs={{0,2},{1,3},{2,0},{3,1},{4,6},{5,7},{6,4},{7,5},{8,10},{9,11},{10,... | collective-permute-start | bytes 393224 | tf_op jit(solution)/shard_map/ppermute | solution.py:505
  45.9 11.8 %collective-permute-start.11 = (bf16[16,4096]{1,0:T(8,128)(2,1)S(1)}, bf16[16,4096]{1,0:T(8,128)(2,1)S(1)}, u32[]{:S(2)}, u32[]{:S(2)}) collective-permute-start(bf16[16,4096]{1,0:T(8,128)(2,1)S(1)} %get-tuple-element.65), channel_id=1, source_target_pairs={{0,4},{1,5},{2,6},{3,7},{4,0},{5,1},{6,2},{7,3},{8,12},{9,13},{10,... | collective-permute-start | bytes 393224 | tf_op jit(solution)/shard_map/ppermute | solution.py:505
  46.6 11.1 %collective-permute-start.12 = (bf16[16,4096]{1,0:T(8,128)(2,1)S(1)}, bf16[16,4096]{1,0:T(8,128)(2,1)S(1)}, u32[]{:S(2)}, u32[]{:S(2)}) collective-permute-start(bf16[16,4096]{1,0:T(8,128)(2,1)S(1)} %get-tuple-element.65), channel_id=1, source_target_pairs={{0,6},{1,7},{2,4},{3,5},{4,2},{5,3},{6,0},{7,1},{8,14},{9,15},{10,... | collective-permute-start | bytes 393224 | tf_op jit(solution)/shard_map/ppermute | solution.py:505
  57.7 10.1 %collective-permute-start.15 = (bf16[64,4096]{1,0:T(8,128)(2,1)S(1)}, bf16[64,4096]{1,0:T(8,128)(2,1)S(1)}, u32[]{:S(2)}, u32[]{:S(2)}) collective-permute-start(bf16[64,4096]{1,0:T(8,128)(2,1)S(1)} %pad_maximum_fusion.4.xa_ref.a_ref), channel_id=1, source_target_pairs={{0,1},{1,0},{2,3},{3,2},{4,5},{5,4},{6,7},{7,6},{8,9},{9,8},{10,11... | collective-permute-start | bytes 1572872 | tf_op jit(solution)/shard_map/ppermute | solution.py:505
  57.9 6.2 %collective-permute-start.16 = (bf16[64,1024]{1,0:T(8,128)(2,1)S(1)}, bf16[64,1024]{1,0:T(8,128)(2,1)S(1)}, u32[]{:S(2)}, u32[]{:S(2)}) collective-permute-start(bf16[64,1024]{1,0:T(8,128)(2,1)S(1)} %get-tuple-element.71), channel_id=1, source_target_pairs={{0,8},{8,0},{16,24},{24,16},{1,9},{9,1},{17,25},{25,17},{2,10},{10... | collective-permute-start | bytes 393224 | tf_op jit(solution)/shard_map/ppermute | solution.py:505
  59.4 8.4 %collective-permute-start.17 = (bf16[64,1024]{1,0:T(8,128)(2,1)S(1)}, bf16[64,1024]{1,0:T(8,128)(2,1)S(1)}, u32[]{:S(2)}, u32[]{:S(2)}) collective-permute-start(bf16[64,1024]{1,0:T(8,128)(2,1)S(1)} %get-tuple-element.72), channel_id=1, source_target_pairs={{0,16},{8,24},{16,0},{24,8},{1,17},{9,25},{17,1},{25,9},{2,18},{10... | collective-permute-start | bytes 393224 | tf_op jit(solution)/shard_map/ppermute | solution.py:505
  61.0 6.9 %collective-permute-start.18 = (bf16[64,1024]{1,0:T(8,128)(2,1)S(1)}, bf16[64,1024]{1,0:T(8,128)(2,1)S(1)}, u32[]{:S(2)}, u32[]{:S(2)}) collective-permute-start(bf16[64,1024]{1,0:T(8,128)(2,1)S(1)} %get-tuple-element.73), channel_id=1, source_target_pairs={{0,24},{8,16},{16,8},{24,0},{1,25},{9,17},{17,9},{25,1},{2,26},{10... | collective-permute-start | bytes 393224 | tf_op jit(solution)/shard_map/ppermute | solution.py:505
  77.9 2.0 %collective-permute-start.19 = (bf16[64,4096]{1,0:T(8,128)(2,1)S(1)}, bf16[64,4096]{1,0:T(8,128)(2,1)S(1)}, u32[]{:S(2)}, u32[]{:S(2)}) collective-permute-start(bf16[64,4096]{1,0:T(8,128)(2,1)S(1)} %get-tuple-element.74), channel_id=1, source_target_pairs={{0,1},{1,0},{2,3},{3,2},{4,5},{5,4},{6,7},{7,6},{8,9},{9,8},{10,11... | collective-permute-start | bytes 1572872 | tf_op jit(solution)/shard_map/ppermute | solution.py:505
  80.2 10.2 %collective-permute-start.22 = (bf16[64,2688]{1,0:T(8,128)(2,1)S(1)}, bf16[64,2688]{1,0:T(8,128)(2,1)S(1)}, u32[]{:S(2)}, u32[]{:S(2)}) collective-permute-start(bf16[64,2688]{1,0:T(8,128)(2,1)S(1)} %get-tuple-element.102), channel_id=1, source_target_pairs={{0,16},{8,24},{16,0},{24,8},{1,17},{9,25},{17,1},{25,9},{2,18},{10... | collective-permute-start | bytes 1032200 | tf_op jit(solution)/shard_map/ppermute | solution.py:505
  81.8 9.8 %collective-permute-start.21 = (bf16[64,2688]{1,0:T(8,128)(2,1)S(1)}, bf16[64,2688]{1,0:T(8,128)(2,1)S(1)}, u32[]{:S(2)}, u32[]{:S(2)}) collective-permute-start(bf16[64,2688]{1,0:T(8,128)(2,1)S(1)} %get-tuple-element.103), channel_id=1, source_target_pairs={{0,8},{8,0},{16,24},{24,16},{1,9},{9,1},{17,25},{25,17},{2,10},{10... | collective-permute-start | bytes 1032200 | tf_op jit(solution)/shard_map/ppermute | solution.py:505
  82.3 9.4 %collective-permute-start.23 = (bf16[16,4096]{1,0:T(8,128)(2,1)S(1)}, bf16[16,4096]{1,0:T(8,128)(2,1)S(1)}, u32[]{:S(2)}, u32[]{:S(2)}) collective-permute-start(bf16[16,4096]{1,0:T(8,128)(2,1)S(1)} %get-tuple-element.111), channel_id=1, source_target_pairs={{0,2},{1,3},{2,0},{3,1},{4,6},{5,7},{6,4},{7,5},{8,10},{9,11},{10,... | collective-permute-start | bytes 393224 | tf_op jit(solution)/shard_map/ppermute | solution.py:505
  84.4 12.5 %collective-permute-start.24 = (bf16[16,4096]{1,0:T(8,128)(2,1)S(1)}, bf16[16,4096]{1,0:T(8,128)(2,1)S(1)}, u32[]{:S(2)}, u32[]{:S(2)}) collective-permute-start(bf16[16,4096]{1,0:T(8,128)(2,1)S(1)} %get-tuple-element.110), channel_id=1, source_target_pairs={{0,4},{1,5},{2,6},{3,7},{4,0},{5,1},{6,2},{7,3},{8,12},{9,13},{10,... | collective-permute-start | bytes 393224 | tf_op jit(solution)/shard_map/ppermute | solution.py:505
  85.0 11.9 %collective-permute-start.25 = (bf16[16,4096]{1,0:T(8,128)(2,1)S(1)}, bf16[16,4096]{1,0:T(8,128)(2,1)S(1)}, u32[]{:S(2)}, u32[]{:S(2)}) collective-permute-start(bf16[16,4096]{1,0:T(8,128)(2,1)S(1)} %get-tuple-element.109), channel_id=1, source_target_pairs={{0,6},{1,7},{2,4},{3,5},{4,2},{5,3},{6,0},{7,1},{8,14},{9,15},{10,... | collective-permute-start | bytes 393224 | tf_op jit(solution)/shard_map/ppermute | solution.py:505
  97.8 6.4 %collective-permute-start.26 = (bf16[16,4096]{1,0:T(8,128)(2,1)}, bf16[16,4096]{1,0:T(8,128)(2,1)S(1)}, u32[]{:S(2)}, u32[]{:S(2)}) collective-permute-start(bf16[16,4096]{1,0:T(8,128)(2,1)} %get-tuple-element.47), channel_id=1, source_target_pairs={{0,2},{1,3},{2,0},{3,1},{4,6},{5,7},{6,4},{7,5},{8,10},{9,11},{10,... | collective-permute-start | bytes 393224 | tf_op jit(solution)/shard_map/ppermute | solution.py:505
  99.9 12.1 %collective-permute-start.27 = (bf16[16,4096]{1,0:T(8,128)(2,1)}, bf16[16,4096]{1,0:T(8,128)(2,1)S(1)}, u32[]{:S(2)}, u32[]{:S(2)}) collective-permute-start(bf16[16,4096]{1,0:T(8,128)(2,1)} %get-tuple-element.47), channel_id=1, source_target_pairs={{0,4},{1,5},{2,6},{3,7},{4,0},{5,1},{6,2},{7,3},{8,12},{9,13},{10,... | collective-permute-start | bytes 393224 | tf_op jit(solution)/shard_map/ppermute | solution.py:505
  100.5 11.5 %collective-permute-start.28 = (bf16[16,4096]{1,0:T(8,128)(2,1)}, bf16[16,4096]{1,0:T(8,128)(2,1)S(1)}, u32[]{:S(2)}, u32[]{:S(2)}) collective-permute-start(bf16[16,4096]{1,0:T(8,128)(2,1)} %get-tuple-element.47), channel_id=1, source_target_pairs={{0,6},{1,7},{2,4},{3,5},{4,2},{5,3},{6,0},{7,1},{8,14},{9,15},{10,... | collective-permute-start | bytes 393224 | tf_op jit(solution)/shard_map/ppermute | solution.py:505
  102.3 10.7 %collective-permute-start.20 = (bf16[64,4096]{1,0:T(8,128)(2,1)S(1)}, bf16[64,4096]{1,0:T(8,128)(2,1)S(1)}, u32[]{:S(2)}, u32[]{:S(2)}) collective-permute-start(bf16[64,4096]{1,0:T(8,128)(2,1)S(1)} %slice.109), channel_id=1, source_target_pairs={{0,1},{1,0},{2,3},{3,2},{4,5},{5,4},{6,7},{7,6},{8,9},{9,8},{10,11... | collective-permute-start | bytes 1572872 | tf_op jit(solution)/shard_map/ppermute | solution.py:505
  102.4 15.3 %collective-permute-start.36 = (bf16[256,1024]{1,0:T(8,128)(2,1)S(1)}, bf16[256,1024]{1,0:T(8,128)(2,1)S(1)}, u32[]{:S(2)}, u32[]{:S(2)}) collective-permute-start(bf16[256,1024]{1,0:T(8,128)(2,1)S(1)} %pad_maximum_fusion.5), channel_id=1, source_target_pairs={{0,16},{8,24},{16,0},{24,8},{1,17},{9,25},{17,1},{25,9},{2,18},{10... | collective-permute-start | bytes 1572872 | tf_op jit(solution)/shard_map/ppermute | solution.py:505
  113.2 6.5 %collective-permute-start.29 = (bf16[16,4096]{1,0:T(8,128)(2,1)S(1)}, bf16[16,4096]{1,0:T(8,128)(2,1)S(1)}, u32[]{:S(2)}, u32[]{:S(2)}) collective-permute-start(bf16[16,4096]{1,0:T(8,128)(2,1)S(1)} %get-tuple-element.106), channel_id=1, source_target_pairs={{0,2},{1,3},{2,0},{3,1},{4,6},{5,7},{6,4},{7,5},{8,10},{9,11},{10,... | collective-permute-start | bytes 393224 | tf_op jit(solution)/shard_map/ppermute | solution.py:505
  115.2 11.8 %collective-permute-start.30 = (bf16[16,4096]{1,0:T(8,128)(2,1)S(1)}, bf16[16,4096]{1,0:T(8,128)(2,1)S(1)}, u32[]{:S(2)}, u32[]{:S(2)}) collective-permute-start(bf16[16,4096]{1,0:T(8,128)(2,1)S(1)} %get-tuple-element.108), channel_id=1, source_target_pairs={{0,4},{1,5},{2,6},{3,7},{4,0},{5,1},{6,2},{7,3},{8,12},{9,13},{10,... | collective-permute-start | bytes 393224 | tf_op jit(solution)/shard_map/ppermute | solution.py:505
  116.0 12.2 %collective-permute-start.31 = (bf16[16,4096]{1,0:T(8,128)(2,1)S(1)}, bf16[16,4096]{1,0:T(8,128)(2,1)S(1)}, u32[]{:S(2)}, u32[]{:S(2)}) collective-permute-start(bf16[16,4096]{1,0:T(8,128)(2,1)S(1)} %get-tuple-element.107), channel_id=1, source_target_pairs={{0,6},{1,7},{2,4},{3,5},{4,2},{5,3},{6,0},{7,1},{8,14},{9,15},{10,... | collective-permute-start | bytes 393224 | tf_op jit(solution)/shard_map/ppermute | solution.py:505
  119.2 47.4 %collective-permute-start.44 = (bf16[256,1024]{1,0:T(8,128)(2,1)}, bf16[256,1024]{1,0:T(8,128)(2,1)}, u32[]{:S(2)}, u32[]{:S(2)}) collective-permute-start(bf16[256,1024]{1,0:T(8,128)(2,1)} %pad_maximum_fusion.7.refs_2_), channel_id=1, source_target_pairs={{0,1},{1,0},{2,3},{3,2},{4,5},{5,4},{6,7},{7,6},{8,9},{9,8},{10,11... | collective-permute-start | bytes 1572872 | tf_op jit(solution)/shard_map/ppermute | solution.py:505
  119.2 31.8 %collective-permute-start.41 = (bf16[256,1024]{1,0:T(8,128)(2,1)S(1)}, bf16[256,1024]{1,0:T(8,128)(2,1)S(1)}, u32[]{:S(2)}, u32[]{:S(2)}) collective-permute-start(bf16[256,1024]{1,0:T(8,128)(2,1)S(1)} %constant_dynamic-update-slice_fusion.9.refs_0_), channel_id=1, source_target_pairs={{0,1},{1,0},{2,3},{3,2},{4,5},{5,4},{6,7},{7,6},{8,9},{9,8},{10,11... | collective-permute-start | bytes 1572872 | tf_op jit(solution)/shard_map/ppermute | solution.py:505
  119.7 17.7 %collective-permute-start.43 = (bf16[128,2688]{1,0:T(8,128)(2,1)S(1)}, bf16[128,2688]{1,0:T(8,128)(2,1)S(1)}, u32[]{:S(2)}, u32[]{:S(2)}) collective-permute-start(bf16[128,2688]{1,0:T(8,128)(2,1)S(1)} %pad_maximum_fusion.3), channel_id=1, source_target_pairs={{0,8},{8,0},{16,24},{24,16},{1,9},{9,1},{17,25},{25,17},{2,10},{10... | collective-permute-start | bytes 2064392 | tf_op jit(solution)/shard_map/ppermute | solution.py:505
  127.0 13.4 %collective-permute-start.42 = (bf16[128,2688]{1,0:T(8,128)(2,1)S(1)}, bf16[128,2688]{1,0:T(8,128)(2,1)S(1)}, u32[]{:S(2)}, u32[]{:S(2)}) collective-permute-start(bf16[128,2688]{1,0:T(8,128)(2,1)S(1)} %pad_maximum_fusion.2), channel_id=1, source_target_pairs={{0,16},{8,24},{16,0},{24,8},{1,17},{9,25},{17,1},{25,9},{2,18},{10... | collective-permute-start | bytes 2064392 | tf_op jit(solution)/shard_map/ppermute | solution.py:505
  128.2 1.9 %collective-permute-start.32 = (bf16[64,4096]{1,0:T(8,128)(2,1)S(1)}, bf16[64,4096]{1,0:T(8,128)(2,1)S(1)}, u32[]{:S(2)}, u32[]{:S(2)}) collective-permute-start(bf16[64,4096]{1,0:T(8,128)(2,1)S(1)} %pad_maximum_fusion.6.refs_8_.a_ref), channel_id=1, source_target_pairs={{0,1},{1,0},{2,3},{3,2},{4,5},{5,4},{6,7},{7,6},{8,9},{9,8},{10,11... | collective-permute-start | bytes 1572872 | tf_op jit(solution)/shard_map/ppermute | solution.py:505
  133.9 4.9 %collective-permute-start.33 = (bf16[160,256]{1,0:T(8,128)(2,1)S(1)}, bf16[160,256]{1,0:T(8,128)(2,1)S(1)}, u32[]{:S(2)}, u32[]{:S(2)}) collective-permute-start(bf16[160,256]{1,0:T(8,128)(2,1)S(1)} %get-tuple-element.84), channel_id=1, source_target_pairs={{0,8},{8,0},{16,24},{24,16},{1,9},{9,1},{17,25},{25,17},{2,10},{10... | collective-permute-start | bytes 245768 | tf_op jit(solution)/shard_map/ppermute | solution.py:505
  138.9 5.2 %collective-permute-start.37 = (bf16[64,1024]{1,0:T(8,128)(2,1)S(1)}, bf16[64,1024]{1,0:T(8,128)(2,1)S(1)}, u32[]{:S(2)}, u32[]{:S(2)}) collective-permute-start(bf16[64,1024]{1,0:T(8,128)(2,1)S(1)} %get-tuple-element.92), channel_id=1, source_target_pairs={{0,8},{8,0},{16,24},{24,16},{1,9},{9,1},{17,25},{25,17},{2,10},{10... | collective-permute-start | bytes 393224 | tf_op jit(solution)/shard_map/ppermute | solution.py:505
  140.5 13.6 %collective-permute-start.34 = (bf16[160,256]{1,0:T(8,128)(2,1)S(1)}, bf16[160,256]{1,0:T(8,128)(2,1)S(1)}, u32[]{:S(2)}, u32[]{:S(2)}) collective-permute-start(bf16[160,256]{1,0:T(8,128)(2,1)S(1)} %get-tuple-element.85), channel_id=1, source_target_pairs={{0,16},{8,24},{16,0},{24,8},{1,17},{9,25},{17,1},{25,9},{2,18},{10... | collective-permute-start | bytes 245768 | tf_op jit(solution)/shard_map/ppermute | solution.py:505
  141.1 6.9 %collective-permute-start.38 = (bf16[64,1024]{1,0:T(8,128)(2,1)S(1)}, bf16[64,1024]{1,0:T(8,128)(2,1)S(1)}, u32[]{:S(2)}, u32[]{:S(2)}) collective-permute-start(bf16[64,1024]{1,0:T(8,128)(2,1)S(1)} %get-tuple-element.93), channel_id=1, source_target_pairs={{0,16},{8,24},{16,0},{24,8},{1,17},{9,25},{17,1},{25,9},{2,18},{10... | collective-permute-start | bytes 393224 | tf_op jit(solution)/shard_map/ppermute | solution.py:505
  144.0 6.3 %collective-permute-start.39 = (bf16[64,1024]{1,0:T(8,128)(2,1)S(1)}, bf16[64,1024]{1,0:T(8,128)(2,1)S(1)}, u32[]{:S(2)}, u32[]{:S(2)}) collective-permute-start(bf16[64,1024]{1,0:T(8,128)(2,1)S(1)} %get-tuple-element.94), channel_id=1, source_target_pairs={{0,24},{8,16},{16,8},{24,0},{1,25},{9,17},{17,9},{25,1},{2,26},{10... | collective-permute-start | bytes 393224 | tf_op jit(solution)/shard_map/ppermute | solution.py:505
  148.0 6.1 %collective-permute-start.35 = (bf16[160,256]{1,0:T(8,128)(2,1)S(1)}, bf16[160,256]{1,0:T(8,128)(2,1)S(1)}, u32[]{:S(2)}, u32[]{:S(2)}) collective-permute-start(bf16[160,256]{1,0:T(8,128)(2,1)S(1)} %get-tuple-element.86), channel_id=1, source_target_pairs={{0,24},{8,16},{16,8},{24,0},{1,25},{9,17},{17,9},{25,1},{2,26},{10... | collective-permute-start | bytes 245768 | tf_op jit(solution)/shard_map/ppermute | solution.py:505
  151.0 21.5 %collective-permute-start.40 = (bf16[256,1024]{1,0:T(8,128)(2,1)}, bf16[256,1024]{1,0:T(8,128)(2,1)}, u32[]{:S(2)}, u32[]{:S(2)}) collective-permute-start(bf16[256,1024]{1,0:T(8,128)(2,1)} %constant_dynamic-update-slice_fusion.13.refs_4_), channel_id=1, source_target_pairs={{0,1},{1,0},{2,3},{3,2},{4,5},{5,4},{6,7},{7,6},{8,9},{9,8},{10,11... | collective-permute-start | bytes 1572872 | tf_op jit(solution)/shard_map/ppermute | solution.py:505
  154.9 16.0 %all-to-all-start = ((bf16[8,48,256]{2,1,0:T(8,128)(2,1)}), bf16[8,48,256]{2,1,0:T(8,128)(2,1)}, u32[]{:S(2)}, u32[]{:S(2)}) async-start(bf16[8,48,256]{2,1,0:T(8,128)(2,1)} %copy-done.2), calls=%async_computation | async-start | bytes 393216 | tf_op jit(solution)/shard_map/all_to_all | solution.py:638
  (25 other events, 312.2 us)

commit v3 on v2

--- a/solution.py
+++ b/solution.py
@@ -407,74 +407,78 @@
     )(*left_refs, *right_refs)
 
 
-def sum_kernel(n_f, rows, *refs):
-    parts, out_ref = refs[:-1], refs[-1]
-    share = rows // n_f
-    lines = (parts[0].shape[0] - rows) // 2
-
-    def tree(values):
-        while len(values) > 1:
-            values = [values[i] + values[i + 1] for i in range(0, len(values), 2)]
-        return values[0]
-
-    total = tree([p[:rows, :].astype(F32) for p in parts]).astype(BF16)
-    gain = tree(
+def tree_sum(values):
+    while len(values) > 1:
+        values = [values[i] + values[i + 1] for i in range(0, len(values), 2)]
+    return values[0]
+
+
+def sum_kernel(n_f, rows, f_ref, *refs):
+    parts, (own_ref, beside_ref, total_ref) = refs[:-3], refs[-3:]
+    share, lines = rows // n_f, (parts[0].shape[0] - rows) // 2
+    total_ref[...] = tree_sum([p[:rows, :].astype(F32) for p in parts])
+    gain = tree_sum(
         [p[rows : rows + lines, :].astype(F32) + p[rows + lines :, :].astype(F32) for p in parts]
     )
     high = gain.astype(BF16)
     low = (gain - high.astype(F32)).astype(BF16)
-    for f in range(n_f):
-        out_ref[f, :lines, :] = high
-        out_ref[f, lines : 2 * lines, :] = low
-        out_ref[f, 2 * lines :, :] = total[f * share : (f + 1) * share]
-
-
-def sum_call(parts, rows, n_f):
+    for k in range(n_f):
+        out_ref = (own_ref, beside_ref)[k % 2]
+        start = pl.multiple_of((f_ref[0] ^ k) * share, share)
+        out_ref[k // 2, :lines, :] = high
+        out_ref[k // 2, lines : 2 * lines, :] = low
+        out_ref[k // 2, 2 * lines :, :] = total_ref[pl.ds(start, share), :].astype(BF16)
+
+
+def sum_call(f, parts, rows, n_f):
     lines = parts[0].shape[0] - rows
+    out = jax.ShapeDtypeStruct((n_f // 2, lines + rows // n_f, 2 * HEAD_WIDTH), BF16)
     return pl.pallas_call(
         functools.partial(sum_kernel, n_f, rows),
-        out_shape=jax.ShapeDtypeStruct((n_f, lines + rows // n_f, 2 * HEAD_WIDTH), BF16),
-        in_specs=[VMEM] * len(parts),
-        out_specs=VMEM,
+        out_shape=(out, out),
+        in_specs=[SMEM] + [VMEM] * len(parts),
+        out_specs=(VMEM, VMEM),
+        scratch_shapes=[pltpu.VMEM((rows, 2 * HEAD_WIDTH), F32)],
         compiler_params=params(8),
         cost_estimate=cost(1),
         name="sum_over_ctx",
-    )(*parts)
-
-
-def heads_kernel(n_f, in_ref, dk_ref, dv_ref, gain_ref):
+    )(f, *parts)
+
+
+def heads_kernel(n_f, f_ref, *refs):
+    in_refs, (dk_ref, dv_ref, gain_ref) = refs[:-3], refs[-3:]
     per_head = n_f // KEY_VALUE_HEADS
     width = 2 * HEAD_WIDTH
     lines = gain_ref.shape[1] // width
-    for g in range(KEY_VALUE_HEADS):
-        total = in_ref[g * per_head, 2 * lines :, :].astype(F32)
-        for other in range(1, per_head):
-            total = total + in_ref[g * per_head + other, 2 * lines :, :].astype(F32)
-        dk_ref[:, g * HEAD_WIDTH : (g + 1) * HEAD_WIDTH] = total[:, :HEAD_WIDTH]
-        dv_ref[:, g * HEAD_WIDTH : (g + 1) * HEAD_WIDTH] = total[:, HEAD_WIDTH:]
-    gain = functools.reduce(
-        jnp.add,
+    chunks = [(ref, i) for ref in in_refs for i in range(2)]
+    for k in range(0, n_f, per_head):
+        total = tree_sum([r[i, 2 * lines :, :].astype(F32) for r, i in chunks[k : k + per_head]])
+        head = lax.shift_right_logical(f_ref[0] ^ k, log2(per_head))
+        at = pl.ds(pl.multiple_of(head * HEAD_WIDTH, HEAD_WIDTH), HEAD_WIDTH)
+        dk_ref[:, at] = total[:, :HEAD_WIDTH]
+        dv_ref[:, at] = total[:, HEAD_WIDTH:]
+    gain = tree_sum(
         [
-            in_ref[f, :lines, :].astype(F32) + in_ref[f, lines : 2 * lines, :].astype(F32)
-            for f in range(n_f)
-        ],
+            r[i, :lines, :].astype(F32) + r[i, lines : 2 * lines, :].astype(F32)
+            for r, i in chunks
+        ]
     )
     for i in range(lines):
         gain_ref[:, i * width : (i + 1) * width] = gain[i : i + 1]
 
 
-def heads_call(parts, depth, n_f):
-    share = parts.shape[1] - depth // HEAD_WIDTH
+def heads_call(f, pairs, depth, n_f):
+    share = pairs[0].shape[1] - depth // HEAD_WIDTH
     out = jax.ShapeDtypeStruct((share, KEY_VALUE_HEADS * HEAD_WIDTH), F32)
     return pl.pallas_call(
         functools.partial(heads_kernel, n_f),
         out_shape=(out, out, jax.ShapeDtypeStruct((1, depth), F32)),
-        in_specs=[VMEM],
+        in_specs=[SMEM] + [VMEM] * len(pairs),
         out_specs=[VMEM] * 3,
         compiler_params=params(8),
         cost_estimate=cost(1),
         name="place_heads",
-    )(parts)
+    )(f, *pairs)
 
 
 def body(
@@ -542,13 +546,14 @@
     )
     pieces = [payload] + [exchange(payload, "ctx", k) for k in range(1, n_c)]
     cot_a = gather_rows(cotangent)
-    cot_b = beside(cot_a)
 
     keep, give, att, lse = attention_call(f_ref, q_rel, w_out, pieces, n_f)
     terms = scatter_rows(pair_sum(keep, give))
 
     assert 2 * width == cols
-    cot_blocks = list(column_blocks(c_ref, cot_a, n_c))
+    cot_late = after(cot_a, terms[1])
+    cot_b = beside(cot_late)
+    cot_blocks = list(column_blocks(c_ref, cot_late, n_c))
     att_blocks = [jnp.concatenate([att[:pair], att[pair:]], axis=1)]
 
     def crossing(bit):
@@ -561,41 +566,66 @@
             cot_blocks[k] = part
         att_blocks.extend(parts[len(moving) :])
 
-    moving, message = crossing(0)
-    terms[0] = after(terms[0], message)
     hidden, normed = norm_call(resid_in, gain_row, terms)
-    crossed(moving, exchange(message, "ctx", 1))
-
-    grad_act = dot(jnp.concatenate([cot_a, cot_b], axis=0), w_down, NT)
     normed_a = gather_rows(normed)
-    for bit in bits[1:]:
+    for bit in bits:
         moving, message = crossing(bit)
         if bit == bits[-1]:
+            grad_act = dot(jnp.concatenate([cot_late, cot_b], axis=0), w_down, NT)
             normed_a = after(normed_a, grad_act, message)
         crossed(moving, exchange(message, "ctx", 1 << bit))
     normed_b = beside(normed_a)
-    normed_cols = to_columns(column_blocks(c_ref, normed_a, n_c))
 
     pay = gate_up_call(normed_a, normed_b, w_gate, w_up, grad_act)
     keep, give = normed_grad_call(pay, w_gate, w_up)
-    normed_cols = jnp.concatenate(normed_cols, axis=0)
-    give = after(give, normed_cols)
     total = pair_sum(keep, give)
     terms = scatter_rows(total)
-    normed_side = beside(after(normed_cols, total))
     cot_cols = after(jnp.concatenate(cot_blocks, axis=0), total)
     cot_side = beside(cot_cols)
 
-    late = after(pay, total)
-    first, second = late[:pair], late[pair:]
-    for bit in bits:
-        first = jnp.concatenate([first, exchange(first, "ctx", 1 << bit)], axis=0)
-        second = jnp.concatenate([second, exchange(second, "ctx", n_c >> 1 >> bit)], axis=0)
-        if bit == bits[-2]:
-            down = dot(after(pay, total)[:, :hidden_units], w_down).astype(BF16)
-            terms[0] = after(terms[0], first, second, down)
+    late, normed_late = after((pay, normed_a), total)
+    normed_blocks = column_blocks(c_ref, normed_late, n_c)
+
+    class Half:
+        def __init__(self, side):
+            self.side = side
+            self.order = list(bits) if side == 0 else list(bits)[::-1]
+            lanes = slice(side * cols // 2, (side + 1) * cols // 2)
+            self.columns = [block[:, lanes] for block in normed_blocks]
+            self.arrays = [late]
+            self.rows = {0: (0, side * pair, 0)}
+
+        def row(self, k):
+            array, start, at = self.rows[k]
+            return self.arrays[array][start : start + pair, at : at + 3 * hidden_units]
+
+        def message(self, step):
+            bit = self.order[step]
+            self.held = list(self.rows)
+            self.moving = [k for k in range(n_c) if k >> bit & 1]
+            parts = [self.row(k) for k in self.held] + [self.columns[k] for k in self.moving]
+            return jnp.concatenate(parts, axis=1)
+
+        def send(self, step, message):
+            bit = self.order[step]
+            self.arrays.append(exchange(message, "ctx", 1 << bit))
+            at = 0
+            for k in self.held:
+                self.rows[k | 1 << bit] = (len(self.arrays) - 1, 0, at)
+                at += 3 * hidden_units
+            for k in self.moving:
+                self.columns[k] = self.arrays[-1][:, at : at + cols // 2]
+                at += cols // 2
+
+    halves = [Half(0), Half(1)]
+    for step in bits:
+        messages = [h.message(step) for h in halves]
+        if step == bits[-1]:
+            down = dot(late[:, :hidden_units], w_down).astype(BF16)
+            terms[0] = after(terms[0], messages[0], messages[1], down)
             grad_resid, gain_part = norm_grad_call(cotangent, hidden, gain_row, terms)
-            first, second = after((first, second), grad_resid)
+        for h, message in zip(halves, messages):
+            h.send(step, message)
 
     grad_a = gather_rows(grad_resid)
     down_total = pair_sum(down[:pair], down[pair:])
@@ -607,25 +637,42 @@
         f_ref, q_rel, att, lse, gain_part, grad_a, grad_b, w_out, pieces, n_f
     )
     parts = [parts[0]] + [exchange(parts[k], "ctx", k) for k in range(1, n_c)]
-    grad_cols = to_columns(column_blocks(c_ref, after(grad_a, parts[1]), n_c))
+    grad_cols = to_columns(column_blocks(c_ref, after(grad_a, *parts), n_c))
     grad_cols = jnp.concatenate(grad_cols, axis=0)
     grad_side = beside(grad_cols)
 
-    first, second = after((first, second), parts[0])
-    reversed_bits = [sum((k >> b & 1) << (len(bits) - 1 - b) for b in bits) for k in range(n_c)]
+    own_chunks, beside_chunks = sum_call(f_ref, parts, rows, n_f)
+    chunks = jnp.stack([own_chunks, beside(beside_chunks)], axis=1)
+    chunks = [chunks[0]] + [exchange(chunks[m], "ffn", 2 * m) for m in range(1, half)]
+    grad_keys, grad_values, grad_gain = heads_call(f_ref, chunks, depth, n_f)
+
+    normed_cols = jnp.concatenate(
+        [jnp.concatenate([h.columns[k] for h in halves], axis=1) for k in range(n_c)], axis=0
+    )
+    normed_cols = after(normed_cols, parts[0])
+    normed_side = beside(normed_cols)
+    offset = len(halves[0].arrays)
+    hidden_refs = halves[0].arrays + halves[1].arrays
 
     def hidden_part(i):
-        at = i * hidden_units
-        return [(0, 0, n_c * pair, at)] + [(1, k * pair, pair, at) for k in reversed_bits]
+        pieces = []
+        for side, h in enumerate(halves):
+            for k in range(n_c):
+                array, start, at = h.rows[k]
+                pieces.append((array + side * offset, start, pair, at + i * hidden_units))
+        return pieces
 
     columns = [(0, 0, n_c * pair, 0), (1, 0, n_c * pair, 0)]
     att_rows = [(k, 0, pair, 0) for k in range(n_c)] + [(k, 0, pair, width) for k in range(n_c)]
     normed_pair, shape = (normed_cols, normed_side), (cols, hidden_units)
-    both = (first, second)
-    grad_w_gate = weight_grad_call(columns, normed_pair, hidden_part(1), both, shape, "grad_w_gate")
-    grad_w_up = weight_grad_call(columns, normed_pair, hidden_part(2), both, shape, "grad_w_up")
+    grad_w_gate = weight_grad_call(
+        columns, normed_pair, hidden_part(1), hidden_refs, shape, "grad_w_gate"
+    )
+    grad_w_up = weight_grad_call(
+        columns, normed_pair, hidden_part(2), hidden_refs, shape, "grad_w_up"
+    )
     grad_w_down = weight_grad_call(
-        hidden_part(0), both, columns, (cot_cols, cot_side), (hidden_units, cols), "grad_w_down"
+        hidden_part(0), hidden_refs, columns, (cot_cols, cot_side), shape[::-1], "grad_w_down"
     )
     grad_w_out = weight_grad_call(
         att_rows, att_blocks, columns, (grad_cols, grad_side), (width, cols), "grad_w_out"
@@ -634,9 +681,6 @@
     mixed = functools.reduce(jnp.add, [t.astype(F32) for t in mixed_terms])
     mixed = (hidden.astype(F32) + mixed).astype(BF16)
 
-    grad_keys, grad_values, grad_gain = heads_call(
-        lax.all_to_all(sum_call(parts, rows, n_f), "ffn", 0, 0), depth, n_f
-    )
     return (
         mixed,
         grad_resid,

time: 176 us -> 155 us (0.88)
  starting transfers between devices: 61 us -> 51.1 us
  local copies, waits for them, and re-layouts: 7.1 us -> 2 us
  Pallas kernels: 36.5 us -> 32.9 us
  waiting for transfers between devices: 62.9 us -> 60 us
    all_to_all x1 -> x0, starting transfers between devices: 7.58 us -> none  [body(): lax.all_to_all(sum_call(parts, rows, n_f), 'ffn', 0, 0)]
    unnamed x64 -> x43, local copies, waits for them, and re-layouts: 4.53 us -> 0.73 us
    ppermute x45 -> x46, waiting for transfers between devices: 62.9 us -> 60 us  [exchange(): lax.ppermute(x, axis, [(i, i ^ k) for i in range(lax.axis_size(axis))])]
    pallas_call x4, Pallas kernels: 13.7 us -> 11.3 us  [weight_grad_call(): pl.pallas_call(functools.partial(weight_grad_kernel, left, right, len(lef...]
    ppermute x45 -> x46, starting transfers between devices: 53.4 us -> 51.1 us  [exchange(): lax.ppermute(x, axis, [(i, i ^ k) for i in range(lax.axis_size(axis))])]
  transfers between devices with their start and end apart: 46 -> 46, of which waited for: 22 -> 21; matrix products, arithmetic and copies ran while one was open for 6% -> 4% of each run, Pallas kernels for 11% -> 16%
where the time goes in v3:
time: 155 us
  waiting for transfers between devices  60 us (39%)
  starting transfers between devices  51.1 us (33%)
  Pallas kernels  32.9 us (21%)
  matrix products  3.78 us (2%)
  other arithmetic  3.56 us (2%)
  local copies, waits for them, and re-layouts  2 us (1%)
    ppermute x46, waiting for transfers between devices, exchange(): lax.ppermute(x, axis, [(i, i ^ k) for i in range(lax.axis_size(axis))])  60 us
    ppermute x46, starting transfers between devices, exchange(): lax.ppermute(x, axis, [(i, i ^ k) for i in range(lax.axis_size(axis))])  51.1 us
    pallas_call x4, Pallas kernels, weight_grad_call(): pl.pallas_call(functools.partial(weight_grad_kernel, left, right, len(lef...  11.3 us
    pallas_call x1, Pallas kernels, normed_grad_call(): pl.pallas_call(normed_grad_kernel, out_shape=(out, out), in_specs=[VMEM]...  5.98 us
    pallas_call x1, Pallas kernels, attention_call(): pl.pallas_call(functools.partial(attention_kernel, n_f, len(pieces)), out...  4.2 us
    pallas_call x1, Pallas kernels, gate_up_call(): pl.pallas_call(gate_up_kernel, out_shape=jax.ShapeDtypeStruct((rows, 3 *...  3.98 us
    dot_general x2, matrix products, dot(): return lax.dot_general(a, b, dims, preferred_element_type=F32)  3.78 us
    pallas_call x1, Pallas kernels, attention_grad_call(): pl.pallas_call(functools.partial(attention_grad_kernel, n_f, n_c), out_sh...  3.7 us
  transfers between devices with their start and end apart: 46, of which 21 were waited for; matrix products, arithmetic and copies ran while one was open for 4% of the time, Pallas kernels for 16%

profile of v3, /device:TPU:0, one launch (start us, length us, event | category | flops | bytes accessed | tf_op | source)
XLA Modules:
  0.0 154.7 jit_solution(16336120686496645040)
XLA Ops:
  0.7 1.8 %prepare_attention.1 = (bf16[128,512]{1,0:T(8,128)(2,1)}, bf16[272,128]{1,0:T(8,128)(2,1)}) custom-call(s32[1]{0:T(128)} %bitcast.1.f_ref, s32[1]{0:T(128)} %bitcast.2.group_ref, bf16[128,512]{1,0:T(8,128)(2,1)} %q_hbm.1, bf16[128,1024]{1,0:T(8,128)(2,1)} %k_hbm.1, bf16[128,1024]{1,0:T(8,128)(2,1)} %v_hbm.1, s32[1,128]{1,0:T(1,128)} %bitcast.30, ...), custom_call_target="tpu_custom_call" | custom-call | flops 1000000000 | bytes 4000000 | tf_op jit(solution)/shard_map/prepare_attention/pallas_call | solution.py:122
  2.5 3.0 %collective-permute-start = (bf16[272,128]{1,0:T(8,128)(2,1)}, bf16[272,128]{1,0:T(8,128)(2,1)S(1)}, u32[]{:S(2)}, u32[]{:S(2)}) collective-permute-start(bf16[272,128]{1,0:T(8,128)(2,1)} %get-tuple-element.55.refs_1_.refs_0_), channel_id=1, source_target_pairs={{0,8},{8,0},{16,24},{24,16},{1,9},{9,1},{17,25},{25,17},{2,10},{10... | collective-permute-start | bytes 208904 | tf_op jit(solution)/shard_map/ppermute | solution.py:509
  5.5 1.5 collective-permute-start.1
  8.3 1.8 %collective-permute-done.1.refs_3_.refs_2_ = bf16[272,128]{1,0:T(8,128)(2,1)S(1)} collective-permute-done((bf16[272,128]{1,0:T(8,128)(2,1)}, bf16[272,128]{1,0:T(8,128)(2,1)S(1)}, u32[]{:S(2)}, u32[]{:S(2)}) %collective-permute-start.1) | collective-permute-done | bytes 69664 | tf_op jit(solution)/shard_map/ppermute | solution.py:509
  10.0 2.4 %collective-permute-done.2.refs_4_.refs_3_ = bf16[272,128]{1,0:T(8,128)(2,1)S(1)} collective-permute-done((bf16[272,128]{1,0:T(8,128)(2,1)}, bf16[272,128]{1,0:T(8,128)(2,1)S(1)}, u32[]{:S(2)}, u32[]{:S(2)}) %collective-permute-start.2) | collective-permute-done | bytes 69664 | tf_op jit(solution)/shard_map/ppermute | solution.py:509
  13.1 4.2 %attention_and_projection.1 = (bf16[64,4096]{1,0:T(8,128)(2,1)}, bf16[64,4096]{1,0:T(8,128)(2,1)}, bf16[128,512]{1,0:T(8,128)(2,1)}, f32[128,128]{1,0:T(8,128)}) custom-call(s32[1]{0:T(128)} %bitcast.1.f_ref, bf16[128,512]{1,0:T(8,128)(2,1)} %get-tuple-element.54.refs_0_.refs_4_, bf16[272,128]{1,0:T(8,128)(2,1)} %get-tuple-element.55.refs_1_.refs_0_, ...), custom_call_target="tpu_custom_call" | custom-call | flops 2000000000 | bytes 8000000 | tf_op jit(solution)/shard_map/attention_and_projection/pallas_call | solution.py:176
  17.4 1.6 %collective-permute-start.10 = (bf16[16,4096]{1,0:T(8,128)(2,1)S(1)}, bf16[16,4096]{1,0:T(8,128)(2,1)S(1)}, u32[]{:S(2)}, u32[]{:S(2)}) collective-permute-start(bf16[16,4096]{1,0:T(8,128)(2,1)S(1)} %copy-done.1), channel_id=1, source_target_pairs={{0,2},{1,3},{2,0},{3,1},{4,6},{5,7},{6,4},{7,5},{8,10},{9,11},{10,... | collective-permute-start | bytes 393224 | tf_op jit(solution)/shard_map/ppermute | solution.py:509
  19.0 2.6 %collective-permute-start.11 = (bf16[16,4096]{1,0:T(8,128)(2,1)S(1)}, bf16[16,4096]{1,0:T(8,128)(2,1)S(1)}, u32[]{:S(2)}, u32[]{:S(2)}) collective-permute-start(bf16[16,4096]{1,0:T(8,128)(2,1)S(1)} %copy-done.1), channel_id=1, source_target_pairs={{0,4},{1,5},{2,6},{3,7},{4,0},{5,1},{6,2},{7,3},{8,12},{9,13},{10,... | collective-permute-start | bytes 393224 | tf_op jit(solution)/shard_map/ppermute | solution.py:509
  24.7 3.5 %collective-permute-start.5 = (bf16[16,4096]{1,0:T(8,128)(2,1)S(1)}, bf16[16,4096]{1,0:T(8,128)(2,1)S(1)}, u32[]{:S(2)}, u32[]{:S(2)}) collective-permute-start(bf16[16,4096]{1,0:T(8,128)(2,1)S(1)} %get-tuple-element.114), channel_id=1, source_target_pairs={{0,4},{1,5},{2,6},{3,7},{4,0},{5,1},{6,2},{7,3},{8,12},{9,13},{10,... | collective-permute-start | bytes 393224 | tf_op jit(solution)/shard_map/ppermute | solution.py:509
  28.5 3.5 %collective-permute-done.11 = bf16[16,4096]{1,0:T(8,128)(2,1)S(1)} collective-permute-done((bf16[16,4096]{1,0:T(8,128)(2,1)S(1)}, bf16[16,4096]{1,0:T(8,128)(2,1)S(1)}, u32[]{:S(2)}, u32[]{:S(2)}) %collective-permute-start.11) | collective-permute-done | bytes 131104 | tf_op jit(solution)/shard_map/ppermute | solution.py:509
  32.3 10.9 %collective-permute-done.5.refs_2_ = bf16[16,4096]{1,0:T(8,128)(2,1)S(1)} collective-permute-done((bf16[16,4096]{1,0:T(8,128)(2,1)S(1)}, bf16[16,4096]{1,0:T(8,128)(2,1)S(1)}, u32[]{:S(2)}, u32[]{:S(2)}) %collective-permute-start.5) | collective-permute-done | bytes 131104 | tf_op jit(solution)/shard_map/ppermute | solution.py:509
  43.5 2.6 %collective-permute-start.7 = (bf16[16,4096]{1,0:T(8,128)(2,1)S(1)}, bf16[16,4096]{1,0:T(8,128)(2,1)S(1)}, u32[]{:S(2)}, u32[]{:S(2)}) collective-permute-start(bf16[16,4096]{1,0:T(8,128)(2,1)S(1)} %get-tuple-element.59), channel_id=1, source_target_pairs={{0,2},{1,3},{2,0},{3,1},{4,6},{5,7},{6,4},{7,5},{8,10},{9,11},{10,... | collective-permute-start | bytes 393224 | tf_op jit(solution)/shard_map/ppermute | solution.py:509
  47.2 1.4 collective-permute-start.9
  50.4 8.1 %collective-permute-done.8 = bf16[16,4096]{1,0:T(8,128)(2,1)S(1)} collective-permute-done((bf16[16,4096]{1,0:T(8,128)(2,1)S(1)}, bf16[16,4096]{1,0:T(8,128)(2,1)S(1)}, u32[]{:S(2)}, u32[]{:S(2)}) %collective-permute-start.8) | collective-permute-done | bytes 131104 | tf_op jit(solution)/shard_map/ppermute | solution.py:509
  58.6 1.7 %collective-permute-done.14 = bf16[192,1024]{1,0:T(8,128)(2,1)S(1)} collective-permute-done((bf16[192,1024]{1,0:T(8,128)(2,1)S(1)}, bf16[192,1024]{1,0:T(8,128)(2,1)S(1)}, u32[]{:S(2)}, u32[]{:S(2)}) %collective-permute-start.14) | collective-permute-done | bytes 393248 | tf_op jit(solution)/shard_map/ppermute | solution.py:509
  60.4 2.5 %fusion.ga_ref = f32[128,896]{1,0:T(8,128)S(1)} fusion(bf16[896,4096]{1,0:T(8,128)(2,1)S(1)} %bitcast.27, bf16[64,4096]{1,0:T(8,128)(2,1)S(1)} %collective-permute-done.13, bf16[64,4096]{1,0:T(8,128)(2,1)S(1)} %pad_maximum_fusion.3.a_ref), kind=kOutput, calls=%fused_computation.1 | convolution fusion | flops 941621248 | bytes 8847360 | tf_op jit(solution)/shard_map/dot_general | solution.py:31
  63.5 1.3 collective-permute-done.15.xb_ref
  64.9 4.0 %gate_up_and_gradients.1.pay_ref.refs_2_.refs_5_.refs_0_.refs_3_ = bf16[128,2688]{1,0:T(8,128)(2,1)S(1)} custom-call(bf16[64,4096]{1,0:T(8,128)(2,1)S(1)} %pad_maximum_fusion.2.xa_ref.a_ref, bf16[64,4096]{1,0:T(8,128)(2,1)S(1)} %collective-permute-done.15.xb_ref, bf16[4096,896]{1,0:T(8,128)(2,1)S(1)} %bitcast.20, bf16[4096,896]{1,0:T(8,128)(2,1)S(1)} %bitcast.22, ...), custom_call_target="tpu_custom_call" | custom-call | flops 1000000000 | bytes 4000000 | tf_op jit(solution)/shard_map/gate_up_and_gradients/pallas_call | solution.py:323
  68.9 6.0 %normed_gradients.1 = (bf16[64,4096]{1,0:T(8,128)(2,1)S(1)}, bf16[64,4096]{1,0:T(8,128)(2,1)S(1)}) custom-call(bf16[128,2688]{1,0:T(8,128)(2,1)S(1)} %gate_up_and_gradients.1.pay_ref.refs_2_.refs_5_.refs_0_.refs_3_, bf16[4096,896]{1,0:T(8,128)(2,1)S(1)} %bitcast.20, bf16[4096,896]{1,0:T(8,128)(2,1)S(1)} %bitcast.22), custom_call_target="tpu_custom_call" | custom-call | flops 1000000000 | bytes 4000000 | tf_op jit(solution)/shard_map/normed_gradients/pallas_call | solution.py:353
  75.0 2.2 %collective-permute-done.37 = bf16[256,1024]{1,0:T(8,128)(2,1)S(1)} collective-permute-done((bf16[256,1024]{1,0:T(8,128)(2,1)S(1)}, bf16[256,1024]{1,0:T(8,128)(2,1)S(1)}, u32[]{:S(2)}, u32[]{:S(2)}) %collective-permute-start.37) | collective-permute-done | bytes 524320 | tf_op jit(solution)/shard_map/ppermute | solution.py:509
  80.0 2.0 %collective-permute-start.21 = (bf16[16,4096]{1,0:T(8,128)(2,1)S(1)}, bf16[16,4096]{1,0:T(8,128)(2,1)S(1)}, u32[]{:S(2)}, u32[]{:S(2)}) collective-permute-start(bf16[16,4096]{1,0:T(8,128)(2,1)S(1)} %get-tuple-element.110), channel_id=1, source_target_pairs={{0,4},{1,5},{2,6},{3,7},{4,0},{5,1},{6,2},{7,3},{8,12},{9,13},{10,... | collective-permute-start | bytes 393224 | tf_op jit(solution)/shard_map/ppermute | solution.py:509
  82.0 1.4 collective-permute-start.22
  83.4 1.3 convolution_convert_fusion
  84.7 5.5 %collective-permute-done.19.refs_6_.refs_4_ = bf16[64,3712]{1,0:T(8,128)(2,1)S(1)} collective-permute-done((bf16[64,3712]{1,0:T(8,128)(2,1)S(1)}, bf16[64,3712]{1,0:T(8,128)(2,1)S(1)}, u32[]{:S(2)}, u32[]{:S(2)}) %collective-permute-start.19) | collective-permute-done | bytes 475168 | tf_op jit(solution)/shard_map/ppermute | solution.py:509
  91.3 1.6 %collective-permute-start.43 = (bf16[64,6400]{1,0:T(8,128)(2,1)S(1)}, bf16[64,6400]{1,0:T(8,128)(2,1)S(1)}, u32[]{:S(2)}, u32[]{:S(2)}) collective-permute-start(bf16[64,6400]{1,0:T(8,128)(2,1)S(1)} %pad_maximum_fusion), channel_id=1, source_target_pairs={{0,16},{8,24},{16,0},{24,8},{1,17},{9,25},{17,1},{25,9},{2,18},{10... | collective-permute-start | bytes 2457608 | tf_op jit(solution)/shard_map/ppermute | solution.py:509
  93.8 1.3 collective-permute-start.23
  95.1 1.8 %collective-permute-start.24 = (bf16[16,4096]{1,0:T(8,128)(2,1)}, bf16[16,4096]{1,0:T(8,128)(2,1)S(1)}, u32[]{:S(2)}, u32[]{:S(2)}) collective-permute-start(bf16[16,4096]{1,0:T(8,128)(2,1)} %get-tuple-element.45), channel_id=1, source_target_pairs={{0,4},{1,5},{2,6},{3,7},{4,0},{5,1},{6,2},{7,3},{8,12},{9,13},{10,... | collective-permute-start | bytes 393224 | tf_op jit(solution)/shard_map/ppermute | solution.py:509
  96.9 1.4 collective-permute-start.25
  98.4 1.5 collective-permute-done.23
  99.9 7.1 %collective-permute-done.24 = bf16[16,4096]{1,0:T(8,128)(2,1)S(1)} collective-permute-done((bf16[16,4096]{1,0:T(8,128)(2,1)}, bf16[16,4096]{1,0:T(8,128)(2,1)S(1)}, u32[]{:S(2)}, u32[]{:S(2)}) %collective-permute-start.24) | collective-permute-done | bytes 131104 | tf_op jit(solution)/shard_map/ppermute | solution.py:509
  108.1 2.0 %collective-permute-start.26 = (bf16[16,4096]{1,0:T(8,128)(2,1)S(1)}, bf16[16,4096]{1,0:T(8,128)(2,1)S(1)}, u32[]{:S(2)}, u32[]{:S(2)}) collective-permute-start(bf16[16,4096]{1,0:T(8,128)(2,1)S(1)} %get-tuple-element.106), channel_id=1, source_target_pairs={{0,2},{1,3},{2,0},{3,1},{4,6},{5,7},{6,4},{7,5},{8,10},{9,11},{10,... | collective-permute-start | bytes 393224 | tf_op jit(solution)/shard_map/ppermute | solution.py:509
  111.4 1.4 collective-permute-start.28
  112.8 3.7 %attention_gradients.1 = (bf16[128,512]{1,0:T(8,128)(2,1)}, bf16[160,256]{1,0:T(8,128)(2,1)S(1)}, bf16[160,256]{1,0:T(8,128)(2,1)S(1)}, bf16[160,256]{1,0:T(8,128)(2,1)S(1)}, bf16[160,256]{1,0:T(8,128)(2,1)S(1)}) custom-call(s32[1]{0:T(128)} %bitcast.1.f_ref, bf16[272,128]{1,0:T(8,128)(2,1)S(1)} %copy-done.4, bf16[272,128]{1,0:T(8,128)(2,1)S(1)} %copy-done.6, ...), custom_call_target="tpu_custom_call" | custom-call | flops 2000000000 | bytes 8000000 | tf_op jit(solution)/shard_map/attention_gradients/pallas_call | solution.py:234
  116.6 1.5 collective-permute-start.30
  118.1 4.9 %collective-permute-done.27 = bf16[16,4096]{1,0:T(8,128)(2,1)S(1)} collective-permute-done((bf16[16,4096]{1,0:T(8,128)(2,1)S(1)}, bf16[16,4096]{1,0:T(8,128)(2,1)S(1)}, u32[]{:S(2)}, u32[]{:S(2)}) %collective-permute-start.27) | collective-permute-done | bytes 131104 | tf_op jit(solution)/shard_map/ppermute | solution.py:509
  123.0 1.5 collective-permute-start.31
  124.5 1.5 collective-permute-start.32
  127.5 2.4 %collective-permute-done.32.refs_3_ = bf16[160,256]{1,0:T(8,128)(2,1)S(1)} collective-permute-done((bf16[160,256]{1,0:T(8,128)(2,1)S(1)}, bf16[160,256]{1,0:T(8,128)(2,1)S(1)}, u32[]{:S(2)}, u32[]{:S(2)}) %collective-permute-start.32) | collective-permute-done | bytes 81952 | tf_op jit(solution)/shard_map/ppermute | solution.py:509
  129.9 1.6 %collective-permute-start.38 = (bf16[64,1024]{1,0:T(8,128)(2,1)S(1)}, bf16[64,1024]{1,0:T(8,128)(2,1)S(1)}, u32[]{:S(2)}, u32[]{:S(2)}) collective-permute-start(bf16[64,1024]{1,0:T(8,128)(2,1)S(1)} %get-tuple-element.91), channel_id=1, source_target_pairs={{0,8},{8,0},{16,24},{24,16},{1,9},{9,1},{17,25},{25,17},{2,10},{10... | collective-permute-start | bytes 393224 | tf_op jit(solution)/shard_map/ppermute | solution.py:509
  132.1 1.5 collective-permute-start.40
  135.2 2.1 %collective-permute-start.34 = (bf16[2,48,256]{2,1,0:T(8,128)(2,1)S(1)}, bf16[2,48,256]{2,1,0:T(8,128)(2,1)S(1)}, u32[]{:S(2)}, u32[]{:S(2)}) collective-permute-start(bf16[2,48,256]{2,1,0:T(8,128)(2,1)S(1)} %get-tuple-element.126), channel_id=1, source_target_pairs={{0,2},{1,3},{2,0},{3,1},{4,6},{5,7},{6,4},{7,5},{8,10},{9,11},{10,... | collective-permute-start | bytes 147464 | tf_op jit(solution)/shard_map/ppermute | solution.py:509
  137.4 2.3 %collective-permute-start.35 = (bf16[2,48,256]{2,1,0:T(8,128)(2,1)S(1)}, bf16[2,48,256]{2,1,0:T(8,128)(2,1)S(1)}, u32[]{:S(2)}, u32[]{:S(2)}) collective-permute-start(bf16[2,48,256]{2,1,0:T(8,128)(2,1)S(1)} %get-tuple-element.127), channel_id=1, source_target_pairs={{0,4},{1,5},{2,6},{3,7},{4,0},{5,1},{6,2},{7,3},{8,12},{9,13},{10,... | collective-permute-start | bytes 147464 | tf_op jit(solution)/shard_map/ppermute | solution.py:509
  139.7 1.3 collective-permute-start.36
  141.1 3.0 %grad_w_down.1 = f32[896,1024]{1,0:T(8,128)} custom-call(bf16[128,2688]{1,0:T(8,128)(2,1)S(1)} %gate_up_and_gradients.1.pay_ref.refs_2_.refs_5_.refs_0_.refs_3_, bf16[64,3712]{1,0:T(8,128)(2,1)S(1)} %collective-permute-done.18.refs_3_.refs_1_, bf16[64,6400]{1,0:T(8,128)(2,1)S(1)} %collective-permute-done.43.refs_4_.refs_2_, ...), custom_call_target="tpu_custom_call" | custom-call | flops 2000000000 | bytes 8000000 | tf_op jit(solution)/shard_map/grad_w_down/pallas_call | solution.py:399
  144.1 1.6 %collective-permute-done.36.refs_3_ = bf16[2,48,256]{2,1,0:T(8,128)(2,1)S(1)} collective-permute-done((bf16[2,48,256]{2,1,0:T(8,128)(2,1)S(1)}, bf16[2,48,256]{2,1,0:T(8,128)(2,1)S(1)}, u32[]{:S(2)}, u32[]{:S(2)}) %collective-permute-start.36) | collective-permute-done | bytes 49184 | tf_op jit(solution)/shard_map/ppermute | solution.py:509
  146.3 3.1 %grad_w_up.1 = f32[1024,896]{1,0:T(8,128)} custom-call(bf16[256,1024]{1,0:T(8,128)(2,1)S(1)} %maximum_maximum_fusion.refs_0_, bf16[256,1024]{1,0:T(8,128)(2,1)S(1)} %collective-permute-done.44.refs_1_, bf16[128,2688]{1,0:T(8,128)(2,1)S(1)} %gate_up_and_gradients.1.pay_ref.refs_2_.refs_5_.refs_0_.refs_3_, ...), custom_call_target="tpu_custom_call" | custom-call | flops 2000000000 | bytes 8000000 | tf_op jit(solution)/shard_map/grad_w_up/pallas_call | solution.py:399
  149.5 3.1 %grad_w_gate.1 = f32[1024,896]{1,0:T(8,128)} custom-call(bf16[256,1024]{1,0:T(8,128)(2,1)S(1)} %maximum_maximum_fusion.refs_0_, bf16[256,1024]{1,0:T(8,128)(2,1)S(1)} %collective-permute-done.44.refs_1_, bf16[128,2688]{1,0:T(8,128)(2,1)S(1)} %gate_up_and_gradients.1.pay_ref.refs_2_.refs_5_.refs_0_.refs_3_, ...), custom_call_target="tpu_custom_call" | custom-call | flops 2000000000 | bytes 8000000 | tf_op jit(solution)/shard_map/grad_w_gate/pallas_call | solution.py:399
  152.6 2.1 %grad_w_out.1 = f32[512,1024]{1,0:T(8,128)} custom-call(bf16[64,1024]{1,0:T(8,128)(2,1)S(1)} %pad_maximum_fusion.9.refs_0_, bf16[64,1024]{1,0:T(8,128)(2,1)S(1)} %get-tuple-element.122.refs_1_, bf16[64,1024]{1,0:T(8,128)(2,1)S(1)} %get-tuple-element.105.refs_2_, bf16[64,1024]{1,0:T(8,128)(2,1)S(1)} %get-tuple-element.104.refs_3_, ...), custom_call_target="tpu_custom_call" | custom-call | flops 2000000000 | bytes 8000000 | tf_op jit(solution)/shard_map/grad_w_out/pallas_call | solution.py:399
  (144 shorter events, 21.2 us)
Async XLA Ops:
  2.5 5.8 %collective-permute-start = (bf16[272,128]{1,0:T(8,128)(2,1)}, bf16[272,128]{1,0:T(8,128)(2,1)S(1)}, u32[]{:S(2)}, u32[]{:S(2)}) collective-permute-start(bf16[272,128]{1,0:T(8,128)(2,1)} %get-tuple-element.55.refs_1_.refs_0_), channel_id=1, source_target_pairs={{0,8},{8,0},{16,24},{24,16},{1,9},{9,1},{17,25},{25,17},{2,10},{10... | collective-permute-start | bytes 208904 | tf_op jit(solution)/shard_map/ppermute | solution.py:509
  5.5 4.5 %collective-permute-start.1 = (bf16[272,128]{1,0:T(8,128)(2,1)}, bf16[272,128]{1,0:T(8,128)(2,1)S(1)}, u32[]{:S(2)}, u32[]{:S(2)}) collective-permute-start(bf16[272,128]{1,0:T(8,128)(2,1)} %get-tuple-element.55.refs_1_.refs_0_), channel_id=1, source_target_pairs={{0,16},{8,24},{16,0},{24,8},{1,17},{9,25},{17,1},{25,9},{2,18},{10... | collective-permute-start | bytes 208904 | tf_op jit(solution)/shard_map/ppermute | solution.py:509
  7.0 5.4 %collective-permute-start.2 = (bf16[272,128]{1,0:T(8,128)(2,1)}, bf16[272,128]{1,0:T(8,128)(2,1)S(1)}, u32[]{:S(2)}, u32[]{:S(2)}) collective-permute-start(bf16[272,128]{1,0:T(8,128)(2,1)} %get-tuple-element.55.refs_1_.refs_0_), channel_id=1, source_target_pairs={{0,24},{8,16},{16,8},{24,0},{1,25},{9,17},{17,9},{25,1},{2,26},{10... | collective-permute-start | bytes 208904 | tf_op jit(solution)/shard_map/ppermute | solution.py:509
  17.3 25.9 %copy-start.3 = (bf16[16,4096]{1,0:T(8,128)(2,1)S(1)}, bf16[16,4096]{1,0:T(8,128)(2,1)}, u32[]{:S(2)}) copy-start(bf16[16,4096]{1,0:T(8,128)(2,1)} %resid_ref.1) | copy-start | bytes 393220
  17.3 5.4 %collective-permute-start.3 = (bf16[64,4096]{1,0:T(8,128)(2,1)}, bf16[64,4096]{1,0:T(8,128)(2,1)S(1)}, u32[]{:S(2)}, u32[]{:S(2)}) collective-permute-start(bf16[64,4096]{1,0:T(8,128)(2,1)} %get-tuple-element.57), channel_id=1, source_target_pairs={{0,1},{1,0},{2,3},{3,2},{4,5},{5,4},{6,7},{7,6},{8,9},{9,8},{10,11... | collective-permute-start | bytes 1572872 | tf_op jit(solution)/shard_map/ppermute | solution.py:509
  17.4 10.8 %collective-permute-start.10 = (bf16[16,4096]{1,0:T(8,128)(2,1)S(1)}, bf16[16,4096]{1,0:T(8,128)(2,1)S(1)}, u32[]{:S(2)}, u32[]{:S(2)}) collective-permute-start(bf16[16,4096]{1,0:T(8,128)(2,1)S(1)} %copy-done.1), channel_id=1, source_target_pairs={{0,2},{1,3},{2,0},{3,1},{4,6},{5,7},{6,4},{7,5},{8,10},{9,11},{10,... | collective-permute-start | bytes 393224 | tf_op jit(solution)/shard_map/ppermute | solution.py:509
  19.0 12.9 %collective-permute-start.11 = (bf16[16,4096]{1,0:T(8,128)(2,1)S(1)}, bf16[16,4096]{1,0:T(8,128)(2,1)S(1)}, u32[]{:S(2)}, u32[]{:S(2)}) collective-permute-start(bf16[16,4096]{1,0:T(8,128)(2,1)S(1)} %copy-done.1), channel_id=1, source_target_pairs={{0,4},{1,5},{2,6},{3,7},{4,0},{5,1},{6,2},{7,3},{8,12},{9,13},{10,... | collective-permute-start | bytes 393224 | tf_op jit(solution)/shard_map/ppermute | solution.py:509
  21.6 10.4 %collective-permute-start.12 = (bf16[16,4096]{1,0:T(8,128)(2,1)S(1)}, bf16[16,4096]{1,0:T(8,128)(2,1)S(1)}, u32[]{:S(2)}, u32[]{:S(2)}) collective-permute-start(bf16[16,4096]{1,0:T(8,128)(2,1)S(1)} %copy-done.1), channel_id=1, source_target_pairs={{0,6},{1,7},{2,4},{3,5},{4,2},{5,3},{6,0},{7,1},{8,14},{9,15},{10,... | collective-permute-start | bytes 393224 | tf_op jit(solution)/shard_map/ppermute | solution.py:509
  23.9 8.4 %collective-permute-start.4 = (bf16[16,4096]{1,0:T(8,128)(2,1)S(1)}, bf16[16,4096]{1,0:T(8,128)(2,1)S(1)}, u32[]{:S(2)}, u32[]{:S(2)}) collective-permute-start(bf16[16,4096]{1,0:T(8,128)(2,1)S(1)} %get-tuple-element.115), channel_id=1, source_target_pairs={{0,2},{1,3},{2,0},{3,1},{4,6},{5,7},{6,4},{7,5},{8,10},{9,11},{10,... | collective-permute-start | bytes 393224 | tf_op jit(solution)/shard_map/ppermute | solution.py:509
  24.7 18.5 %collective-permute-start.5 = (bf16[16,4096]{1,0:T(8,128)(2,1)S(1)}, bf16[16,4096]{1,0:T(8,128)(2,1)S(1)}, u32[]{:S(2)}, u32[]{:S(2)}) collective-permute-start(bf16[16,4096]{1,0:T(8,128)(2,1)S(1)} %get-tuple-element.114), channel_id=1, source_target_pairs={{0,4},{1,5},{2,6},{3,7},{4,0},{5,1},{6,2},{7,3},{8,12},{9,13},{10,... | collective-permute-start | bytes 393224 | tf_op jit(solution)/shard_map/ppermute | solution.py:509
  28.2 15.0 %collective-permute-start.6 = (bf16[16,4096]{1,0:T(8,128)(2,1)S(1)}, bf16[16,4096]{1,0:T(8,128)(2,1)S(1)}, u32[]{:S(2)}, u32[]{:S(2)}) collective-permute-start(bf16[16,4096]{1,0:T(8,128)(2,1)S(1)} %get-tuple-element.113), channel_id=1, source_target_pairs={{0,6},{1,7},{2,4},{3,5},{4,2},{5,3},{6,0},{7,1},{8,14},{9,15},{10,... | collective-permute-start | bytes 393224 | tf_op jit(solution)/shard_map/ppermute | solution.py:509
  32.0 32.9 %slice-start.2 = ((s8[7340032]{0:T(1024)(128)(4,1)}), s8[4194304]{0:T(1024)(128)(4,1)S(1)}, s32[]{:S(2)}) async-start(s8[7340032]{0:T(1024)(128)(4,1)} %bitcast.21), calls=%async_computation.2 | async-start | bytes 8388608
  43.5 6.9 %collective-permute-start.7 = (bf16[16,4096]{1,0:T(8,128)(2,1)S(1)}, bf16[16,4096]{1,0:T(8,128)(2,1)S(1)}, u32[]{:S(2)}, u32[]{:S(2)}) collective-permute-start(bf16[16,4096]{1,0:T(8,128)(2,1)S(1)} %get-tuple-element.59), channel_id=1, source_target_pairs={{0,2},{1,3},{2,0},{3,1},{4,6},{5,7},{6,4},{7,5},{8,10},{9,11},{10,... | collective-permute-start | bytes 393224 | tf_op jit(solution)/shard_map/ppermute | solution.py:509
  46.1 12.4 %collective-permute-start.8 = (bf16[16,4096]{1,0:T(8,128)(2,1)S(1)}, bf16[16,4096]{1,0:T(8,128)(2,1)S(1)}, u32[]{:S(2)}, u32[]{:S(2)}) collective-permute-start(bf16[16,4096]{1,0:T(8,128)(2,1)S(1)} %get-tuple-element.59), channel_id=1, source_target_pairs={{0,4},{1,5},{2,6},{3,7},{4,0},{5,1},{6,2},{7,3},{8,12},{9,13},{10,... | collective-permute-start | bytes 393224 | tf_op jit(solution)/shard_map/ppermute | solution.py:509
  47.2 11.3 %collective-permute-start.9 = (bf16[16,4096]{1,0:T(8,128)(2,1)S(1)}, bf16[16,4096]{1,0:T(8,128)(2,1)S(1)}, u32[]{:S(2)}, u32[]{:S(2)}) collective-permute-start(bf16[16,4096]{1,0:T(8,128)(2,1)S(1)} %get-tuple-element.59), channel_id=1, source_target_pairs={{0,6},{1,7},{2,4},{3,5},{4,2},{5,3},{6,0},{7,1},{8,14},{9,15},{10,... | collective-permute-start | bytes 393224 | tf_op jit(solution)/shard_map/ppermute | solution.py:509
  48.6 11.8 %collective-permute-start.13 = (bf16[64,4096]{1,0:T(8,128)(2,1)S(1)}, bf16[64,4096]{1,0:T(8,128)(2,1)S(1)}, u32[]{:S(2)}, u32[]{:S(2)}) collective-permute-start(bf16[64,4096]{1,0:T(8,128)(2,1)S(1)} %pad_maximum_fusion.3.a_ref), channel_id=1, source_target_pairs={{0,1},{1,0},{2,3},{3,2},{4,5},{5,4},{6,7},{7,6},{8,9},{9,8},{10,11... | collective-permute-start | bytes 1572872 | tf_op jit(solution)/shard_map/ppermute | solution.py:509
  48.7 11.6 %collective-permute-start.14 = (bf16[192,1024]{1,0:T(8,128)(2,1)S(1)}, bf16[192,1024]{1,0:T(8,128)(2,1)S(1)}, u32[]{:S(2)}, u32[]{:S(2)}) collective-permute-start(bf16[192,1024]{1,0:T(8,128)(2,1)S(1)} %maximum_maximum_fusion.1), channel_id=1, source_target_pairs={{0,8},{8,0},{16,24},{24,16},{1,9},{9,1},{17,25},{25,17},{2,10},{10... | collective-permute-start | bytes 1179656 | tf_op jit(solution)/shard_map/ppermute | solution.py:509
  62.9 2.0 %collective-permute-start.15 = (bf16[64,4096]{1,0:T(8,128)(2,1)S(1)}, bf16[64,4096]{1,0:T(8,128)(2,1)S(1)}, u32[]{:S(2)}, u32[]{:S(2)}) collective-permute-start(bf16[64,4096]{1,0:T(8,128)(2,1)S(1)} %pad_maximum_fusion.2.xa_ref.a_ref), channel_id=1, source_target_pairs={{0,1},{1,0},{2,3},{3,2},{4,5},{5,4},{6,7},{7,6},{8,9},{9,8},{10,11... | collective-permute-start | bytes 1572872 | tf_op jit(solution)/shard_map/ppermute | solution.py:509
  62.9 14.3 %collective-permute-start.37 = (bf16[256,1024]{1,0:T(8,128)(2,1)S(1)}, bf16[256,1024]{1,0:T(8,128)(2,1)S(1)}, u32[]{:S(2)}, u32[]{:S(2)}) collective-permute-start(bf16[256,1024]{1,0:T(8,128)(2,1)S(1)} %pad_maximum_fusion.4), channel_id=1, source_target_pairs={{0,16},{8,24},{16,0},{24,8},{1,17},{9,25},{17,1},{25,9},{2,18},{10... | collective-permute-start | bytes 1572872 | tf_op jit(solution)/shard_map/ppermute | solution.py:509
  74.8 2.5 %collective-permute-start.16 = (bf16[64,4096]{1,0:T(8,128)(2,1)S(1)}, bf16[64,4096]{1,0:T(8,128)(2,1)S(1)}, u32[]{:S(2)}, u32[]{:S(2)}) collective-permute-start(bf16[64,4096]{1,0:T(8,128)(2,1)S(1)} %get-tuple-element.67), channel_id=1, source_target_pairs={{0,1},{1,0},{2,3},{3,2},{4,5},{5,4},{6,7},{7,6},{8,9},{9,8},{10,11... | collective-permute-start | bytes 1572872 | tf_op jit(solution)/shard_map/ppermute | solution.py:509
  77.7 12.5 %collective-permute-start.19 = (bf16[64,3712]{1,0:T(8,128)(2,1)S(1)}, bf16[64,3712]{1,0:T(8,128)(2,1)S(1)}, u32[]{:S(2)}, u32[]{:S(2)}) collective-permute-start(bf16[64,3712]{1,0:T(8,128)(2,1)S(1)} %pad_maximum_fusion.8), channel_id=1, source_target_pairs={{0,16},{8,24},{16,0},{24,8},{1,17},{9,25},{17,1},{25,9},{2,18},{10... | collective-permute-start | bytes 1425416 | tf_op jit(solution)/shard_map/ppermute | solution.py:509
  78.4 12.2 %collective-permute-start.18 = (bf16[64,3712]{1,0:T(8,128)(2,1)S(1)}, bf16[64,3712]{1,0:T(8,128)(2,1)S(1)}, u32[]{:S(2)}, u32[]{:S(2)}) collective-permute-start(bf16[64,3712]{1,0:T(8,128)(2,1)S(1)} %pad_maximum_fusion.7), channel_id=1, source_target_pairs={{0,8},{8,0},{16,24},{24,16},{1,9},{9,1},{17,25},{25,17},{2,10},{10... | collective-permute-start | bytes 1425416 | tf_op jit(solution)/shard_map/ppermute | solution.py:509
  79.0 12.3 %collective-permute-start.20 = (bf16[16,4096]{1,0:T(8,128)(2,1)S(1)}, bf16[16,4096]{1,0:T(8,128)(2,1)S(1)}, u32[]{:S(2)}, u32[]{:S(2)}) collective-permute-start(bf16[16,4096]{1,0:T(8,128)(2,1)S(1)} %get-tuple-element.111), channel_id=1, source_target_pairs={{0,2},{1,3},{2,0},{3,1},{4,6},{5,7},{6,4},{7,5},{8,10},{9,11},{10,... | collective-permute-start | bytes 393224 | tf_op jit(solution)/shard_map/ppermute | solution.py:509
  80.0 12.9 %collective-permute-start.21 = (bf16[16,4096]{1,0:T(8,128)(2,1)S(1)}, bf16[16,4096]{1,0:T(8,128)(2,1)S(1)}, u32[]{:S(2)}, u32[]{:S(2)}) collective-permute-start(bf16[16,4096]{1,0:T(8,128)(2,1)S(1)} %get-tuple-element.110), channel_id=1, source_target_pairs={{0,4},{1,5},{2,6},{3,7},{4,0},{5,1},{6,2},{7,3},{8,12},{9,13},{10,... | collective-permute-start | bytes 393224 | tf_op jit(solution)/shard_map/ppermute | solution.py:509
  82.0 10.9 %collective-permute-start.22 = (bf16[16,4096]{1,0:T(8,128)(2,1)S(1)}, bf16[16,4096]{1,0:T(8,128)(2,1)S(1)}, u32[]{:S(2)}, u32[]{:S(2)}) collective-permute-start(bf16[16,4096]{1,0:T(8,128)(2,1)S(1)} %get-tuple-element.109), channel_id=1, source_target_pairs={{0,6},{1,7},{2,4},{3,5},{4,2},{5,3},{6,0},{7,1},{8,14},{9,15},{10,... | collective-permute-start | bytes 393224 | tf_op jit(solution)/shard_map/ppermute | solution.py:509
  90.2 6.6 %collective-permute-start.17 = (bf16[64,4096]{1,0:T(8,128)(2,1)S(1)}, bf16[64,4096]{1,0:T(8,128)(2,1)S(1)}, u32[]{:S(2)}, u32[]{:S(2)}) collective-permute-start(bf16[64,4096]{1,0:T(8,128)(2,1)S(1)} %slice.194), channel_id=1, source_target_pairs={{0,1},{1,0},{2,3},{3,2},{4,5},{5,4},{6,7},{7,6},{8,9},{9,8},{10,11... | collective-permute-start | bytes 1572872 | tf_op jit(solution)/shard_map/ppermute | solution.py:509
  90.6 41.5 %collective-permute-start.42 = (bf16[64,6400]{1,0:T(8,128)(2,1)S(1)}, bf16[64,6400]{1,0:T(8,128)(2,1)S(1)}, u32[]{:S(2)}, u32[]{:S(2)}) collective-permute-start(bf16[64,6400]{1,0:T(8,128)(2,1)S(1)} %pad_maximum_fusion.1), channel_id=1, source_target_pairs={{0,8},{8,0},{16,24},{24,16},{1,9},{9,1},{17,25},{25,17},{2,10},{10... | collective-permute-start | bytes 2457608 | tf_op jit(solution)/shard_map/ppermute | solution.py:509
  91.3 42.4 %collective-permute-start.43 = (bf16[64,6400]{1,0:T(8,128)(2,1)S(1)}, bf16[64,6400]{1,0:T(8,128)(2,1)S(1)}, u32[]{:S(2)}, u32[]{:S(2)}) collective-permute-start(bf16[64,6400]{1,0:T(8,128)(2,1)S(1)} %pad_maximum_fusion), channel_id=1, source_target_pairs={{0,16},{8,24},{16,0},{24,8},{1,17},{9,25},{17,1},{25,9},{2,18},{10... | collective-permute-start | bytes 2457608 | tf_op jit(solution)/shard_map/ppermute | solution.py:509
  93.8 6.1 %collective-permute-start.23 = (bf16[16,4096]{1,0:T(8,128)(2,1)}, bf16[16,4096]{1,0:T(8,128)(2,1)S(1)}, u32[]{:S(2)}, u32[]{:S(2)}) collective-permute-start(bf16[16,4096]{1,0:T(8,128)(2,1)} %get-tuple-element.45), channel_id=1, source_target_pairs={{0,2},{1,3},{2,0},{3,1},{4,6},{5,7},{6,4},{7,5},{8,10},{9,11},{10,... | collective-permute-start | bytes 393224 | tf_op jit(solution)/shard_map/ppermute | solution.py:509
  95.1 11.9 %collective-permute-start.24 = (bf16[16,4096]{1,0:T(8,128)(2,1)}, bf16[16,4096]{1,0:T(8,128)(2,1)S(1)}, u32[]{:S(2)}, u32[]{:S(2)}) collective-permute-start(bf16[16,4096]{1,0:T(8,128)(2,1)} %get-tuple-element.45), channel_id=1, source_target_pairs={{0,4},{1,5},{2,6},{3,7},{4,0},{5,1},{6,2},{7,3},{8,12},{9,13},{10,... | collective-permute-start | bytes 393224 | tf_op jit(solution)/shard_map/ppermute | solution.py:509
  96.9 10.2 %collective-permute-start.25 = (bf16[16,4096]{1,0:T(8,128)(2,1)}, bf16[16,4096]{1,0:T(8,128)(2,1)S(1)}, u32[]{:S(2)}, u32[]{:S(2)}) collective-permute-start(bf16[16,4096]{1,0:T(8,128)(2,1)} %get-tuple-element.45), channel_id=1, source_target_pairs={{0,6},{1,7},{2,4},{3,5},{4,2},{5,3},{6,0},{7,1},{8,14},{9,15},{10,... | collective-permute-start | bytes 393224 | tf_op jit(solution)/shard_map/ppermute | solution.py:509
  108.0 3.4 %collective-permute-start.29 = (bf16[64,4096]{1,0:T(8,128)(2,1)S(1)}, bf16[64,4096]{1,0:T(8,128)(2,1)S(1)}, u32[]{:S(2)}, u32[]{:S(2)}) collective-permute-start(bf16[64,4096]{1,0:T(8,128)(2,1)S(1)} %pad_maximum_fusion.5.refs_8_.a_ref), channel_id=1, source_target_pairs={{0,1},{1,0},{2,3},{3,2},{4,5},{5,4},{6,7},{7,6},{8,9},{9,8},{10,11... | collective-permute-start | bytes 1572872 | tf_op jit(solution)/shard_map/ppermute | solution.py:509
  108.1 8.5 %collective-permute-start.26 = (bf16[16,4096]{1,0:T(8,128)(2,1)S(1)}, bf16[16,4096]{1,0:T(8,128)(2,1)S(1)}, u32[]{:S(2)}, u32[]{:S(2)}) collective-permute-start(bf16[16,4096]{1,0:T(8,128)(2,1)S(1)} %get-tuple-element.106), channel_id=1, source_target_pairs={{0,2},{1,3},{2,0},{3,1},{4,6},{5,7},{6,4},{7,5},{8,10},{9,11},{10,... | collective-permute-start | bytes 393224 | tf_op jit(solution)/shard_map/ppermute | solution.py:509
  110.1 12.9 %collective-permute-start.27 = (bf16[16,4096]{1,0:T(8,128)(2,1)S(1)}, bf16[16,4096]{1,0:T(8,128)(2,1)S(1)}, u32[]{:S(2)}, u32[]{:S(2)}) collective-permute-start(bf16[16,4096]{1,0:T(8,128)(2,1)S(1)} %get-tuple-element.108), channel_id=1, source_target_pairs={{0,4},{1,5},{2,6},{3,7},{4,0},{5,1},{6,2},{7,3},{8,12},{9,13},{10,... | collective-permute-start | bytes 393224 | tf_op jit(solution)/shard_map/ppermute | solution.py:509
  111.4 13.1 %collective-permute-start.28 = (bf16[16,4096]{1,0:T(8,128)(2,1)S(1)}, bf16[16,4096]{1,0:T(8,128)(2,1)S(1)}, u32[]{:S(2)}, u32[]{:S(2)}) collective-permute-start(bf16[16,4096]{1,0:T(8,128)(2,1)S(1)} %get-tuple-element.107), channel_id=1, source_target_pairs={{0,6},{1,7},{2,4},{3,5},{4,2},{5,3},{6,0},{7,1},{8,14},{9,15},{10,... | collective-permute-start | bytes 393224 | tf_op jit(solution)/shard_map/ppermute | solution.py:509
  116.6 10.2 %collective-permute-start.30 = (bf16[160,256]{1,0:T(8,128)(2,1)S(1)}, bf16[160,256]{1,0:T(8,128)(2,1)S(1)}, u32[]{:S(2)}, u32[]{:S(2)}) collective-permute-start(bf16[160,256]{1,0:T(8,128)(2,1)S(1)} %get-tuple-element.81), channel_id=1, source_target_pairs={{0,8},{8,0},{16,24},{24,16},{1,9},{9,1},{17,25},{25,17},{2,10},{10... | collective-permute-start | bytes 245768 | tf_op jit(solution)/shard_map/ppermute | solution.py:509
  123.0 4.4 %collective-permute-start.31 = (bf16[160,256]{1,0:T(8,128)(2,1)S(1)}, bf16[160,256]{1,0:T(8,128)(2,1)S(1)}, u32[]{:S(2)}, u32[]{:S(2)}) collective-permute-start(bf16[160,256]{1,0:T(8,128)(2,1)S(1)} %get-tuple-element.82), channel_id=1, source_target_pairs={{0,16},{8,24},{16,0},{24,8},{1,17},{9,25},{17,1},{25,9},{2,18},{10... | collective-permute-start | bytes 245768 | tf_op jit(solution)/shard_map/ppermute | solution.py:509
  124.5 5.3 %collective-permute-start.32 = (bf16[160,256]{1,0:T(8,128)(2,1)S(1)}, bf16[160,256]{1,0:T(8,128)(2,1)S(1)}, u32[]{:S(2)}, u32[]{:S(2)}) collective-permute-start(bf16[160,256]{1,0:T(8,128)(2,1)S(1)} %get-tuple-element.83), channel_id=1, source_target_pairs={{0,24},{8,16},{16,8},{24,0},{1,25},{9,17},{17,9},{25,1},{2,26},{10... | collective-permute-start | bytes 245768 | tf_op jit(solution)/shard_map/ppermute | solution.py:509
  126.8 14.3 %collective-permute-start.45 = (bf16[256,1024]{1,0:T(8,128)(2,1)S(1)}, bf16[256,1024]{1,0:T(8,128)(2,1)S(1)}, u32[]{:S(2)}, u32[]{:S(2)}) collective-permute-start(bf16[256,1024]{1,0:T(8,128)(2,1)S(1)} %pad_maximum_fusion.6.refs_6_), channel_id=1, source_target_pairs={{0,1},{1,0},{2,3},{3,2},{4,5},{5,4},{6,7},{7,6},{8,9},{9,8},{10,11... | collective-permute-start | bytes 1572872 | tf_op jit(solution)/shard_map/ppermute | solution.py:509
  129.9 5.3 %collective-permute-start.38 = (bf16[64,1024]{1,0:T(8,128)(2,1)S(1)}, bf16[64,1024]{1,0:T(8,128)(2,1)S(1)}, u32[]{:S(2)}, u32[]{:S(2)}) collective-permute-start(bf16[64,1024]{1,0:T(8,128)(2,1)S(1)} %get-tuple-element.91), channel_id=1, source_target_pairs={{0,8},{8,0},{16,24},{24,16},{1,9},{9,1},{17,25},{25,17},{2,10},{10... | collective-permute-start | bytes 393224 | tf_op jit(solution)/shard_map/ppermute | solution.py:509
  131.5 5.9 %collective-permute-start.39 = (bf16[64,1024]{1,0:T(8,128)(2,1)S(1)}, bf16[64,1024]{1,0:T(8,128)(2,1)S(1)}, u32[]{:S(2)}, u32[]{:S(2)}) collective-permute-start(bf16[64,1024]{1,0:T(8,128)(2,1)S(1)} %get-tuple-element.92), channel_id=1, source_target_pairs={{0,16},{8,24},{16,0},{24,8},{1,17},{9,25},{17,1},{25,9},{2,18},{10... | collective-permute-start | bytes 393224 | tf_op jit(solution)/shard_map/ppermute | solution.py:509
  132.1 7.6 %collective-permute-start.40 = (bf16[64,1024]{1,0:T(8,128)(2,1)S(1)}, bf16[64,1024]{1,0:T(8,128)(2,1)S(1)}, u32[]{:S(2)}, u32[]{:S(2)}) collective-permute-start(bf16[64,1024]{1,0:T(8,128)(2,1)S(1)} %get-tuple-element.93), channel_id=1, source_target_pairs={{0,24},{8,16},{16,8},{24,0},{1,25},{9,17},{17,9},{25,1},{2,26},{10... | collective-permute-start | bytes 393224 | tf_op jit(solution)/shard_map/ppermute | solution.py:509
  133.7 1.4 collective-permute-start.33
  135.0 11.3 %collective-permute-start.44 = (bf16[256,1024]{1,0:T(8,128)(2,1)S(1)}, bf16[256,1024]{1,0:T(8,128)(2,1)S(1)}, u32[]{:S(2)}, u32[]{:S(2)}) collective-permute-start(bf16[256,1024]{1,0:T(8,128)(2,1)S(1)} %maximum_maximum_fusion.refs_0_), channel_id=1, source_target_pairs={{0,1},{1,0},{2,3},{3,2},{4,5},{5,4},{6,7},{7,6},{8,9},{9,8},{10,11... | collective-permute-start | bytes 1572872 | tf_op jit(solution)/shard_map/ppermute | solution.py:509
  135.2 8.9 %collective-permute-start.34 = (bf16[2,48,256]{2,1,0:T(8,128)(2,1)S(1)}, bf16[2,48,256]{2,1,0:T(8,128)(2,1)S(1)}, u32[]{:S(2)}, u32[]{:S(2)}) collective-permute-start(bf16[2,48,256]{2,1,0:T(8,128)(2,1)S(1)} %get-tuple-element.126), channel_id=1, source_target_pairs={{0,2},{1,3},{2,0},{3,1},{4,6},{5,7},{6,4},{7,5},{8,10},{9,11},{10,... | collective-permute-start | bytes 147464 | tf_op jit(solution)/shard_map/ppermute | solution.py:509
  137.4 6.7 %collective-permute-start.35 = (bf16[2,48,256]{2,1,0:T(8,128)(2,1)S(1)}, bf16[2,48,256]{2,1,0:T(8,128)(2,1)S(1)}, u32[]{:S(2)}, u32[]{:S(2)}) collective-permute-start(bf16[2,48,256]{2,1,0:T(8,128)(2,1)S(1)} %get-tuple-element.127), channel_id=1, source_target_pairs={{0,4},{1,5},{2,6},{3,7},{4,0},{5,1},{6,2},{7,3},{8,12},{9,13},{10,... | collective-permute-start | bytes 147464 | tf_op jit(solution)/shard_map/ppermute | solution.py:509
  139.7 6.0 %collective-permute-start.36 = (bf16[2,48,256]{2,1,0:T(8,128)(2,1)S(1)}, bf16[2,48,256]{2,1,0:T(8,128)(2,1)S(1)}, u32[]{:S(2)}, u32[]{:S(2)}) collective-permute-start(bf16[2,48,256]{2,1,0:T(8,128)(2,1)S(1)} %get-tuple-element.124), channel_id=1, source_target_pairs={{0,6},{1,7},{2,4},{3,5},{4,2},{5,3},{6,0},{7,1},{8,14},{9,15},{10,... | collective-permute-start | bytes 147464 | tf_op jit(solution)/shard_map/ppermute | solution.py:509
  141.0 11.6 %collective-permute-start.41 = (bf16[256,1024]{1,0:T(8,128)(2,1)S(1)}, bf16[256,1024]{1,0:T(8,128)(2,1)S(1)}, u32[]{:S(2)}, u32[]{:S(2)}) collective-permute-start(bf16[256,1024]{1,0:T(8,128)(2,1)S(1)} %constant_dynamic-update-slice_fusion.refs_4_), channel_id=1, source_target_pairs={{0,1},{1,0},{2,3},{3,2},{4,5},{5,4},{6,7},{7,6},{8,9},{9,8},{10,11... | collective-permute-start | bytes 1572872 | tf_op jit(solution)/shard_map/ppermute | solution.py:509
  (18 other events, 267.3 us)

commit v4 on v3

--- a/solution.py
+++ b/solution.py
@@ -267,17 +267,19 @@
 
 
 def norm_grad_kernel(cot_ref, hidden_ref, gain_ref, *refs):
-    terms, (grad_ref, gain_grad_ref) = refs[:-2], refs[-2:]
+    terms, (grad_ref, copy_ref, gain_grad_ref) = refs[:-3], refs[-3:]
     grad_normed = functools.reduce(jnp.add, [t[...].astype(F32) for t in terms])
     hidden = hidden_ref[...].astype(F32)
     inv_rms = lax.rsqrt(jnp.mean(hidden * hidden, axis=1, keepdims=True) + norm_eps)
     gained = grad_normed * gain_ref[...]
     inv_cube = inv_rms * inv_rms * inv_rms
-    grad_ref[...] = (
+    grad = (
         cot_ref[...].astype(F32)
         + inv_rms * gained
         - hidden * inv_cube * jnp.mean(gained * hidden, axis=1, keepdims=True)
     ).astype(BF16)
+    grad_ref[...] = grad
+    copy_ref[...] = grad
     gain_grad_ref[...] = jnp.sum(grad_normed * hidden * inv_rms, axis=0, keepdims=True)
 
 
@@ -285,11 +287,12 @@
     return pl.pallas_call(
         norm_grad_kernel,
         out_shape=(
+            jax.ShapeDtypeStruct(cot.shape, BF16),
             jax.ShapeDtypeStruct(cot.shape, BF16),
             jax.ShapeDtypeStruct(gain_row.shape, F32),
         ),
         in_specs=[VMEM] * (3 + len(terms)),
-        out_specs=[VMEM] * 2,
+        out_specs=[VMEM] * 3,
         compiler_params=params(8),
         cost_estimate=cost(8),
         name="norm_gradients",
@@ -385,24 +388,41 @@
     return jnp.concatenate([refs[i][r : r + n, at : at + width] for i, r, n, at in pieces], axis=0)
 
 
-def weight_grad_kernel(left, right, n_left, widths, *refs):
-    out_ref = refs[-1]
-    rhs = take(refs[n_left:-1], right, widths[1])
+def weight_grad_kernel(left, right, n_left, tiled, *refs):
+    operands, (out_hbm, out_ref, sems) = refs[:-3], refs[-3:]
+    height, width = out_ref.shape
+    left_refs, right_refs = operands[:n_left], operands[n_left:]
     tile = 256
-    for at in range(0, widths[0], tile):
-        size = min(tile, widths[0] - at)
-        lhs = take(refs[:n_left], [(i, r, n, first + at) for i, r, n, first in left], size)
-        out_ref[at : at + size, :] = dot(lhs, rhs, TN)
-
-
-def weight_grad_call(left, left_refs, right, right_refs, widths, name):
-    return pl.pallas_call(
-        functools.partial(weight_grad_kernel, left, right, len(left_refs), widths),
+    copies = []
+    fixed = take(right_refs, right, width) if tiled == 0 else take(left_refs, left, height)
+    for n, at in enumerate(range(0, out_ref.shape[tiled], tile)):
+        size = min(tile, out_ref.shape[tiled] - at)
+        if tiled == 0:
+            moving = take(left_refs, [(i, r, m, first + at) for i, r, m, first in left], size)
+            where = (pl.ds(at, size), slice(None))
+            out_ref[where] = dot(moving, fixed, TN)
+        else:
+            moving = take(right_refs, [(i, r, m, first + at) for i, r, m, first in right], size)
+            where = (slice(None), pl.ds(at, size))
+            out_ref[where] = dot(fixed, moving, TN)
+        copies.append(pltpu.make_async_copy(out_ref.at[where], out_hbm.at[where], sems.at[n]))
+        copies[-1].start()
+    for copy in copies:
+        copy.wait()
+
+
+def weight_grad_call(left, left_refs, right, right_refs, widths, tiled, name):
+    return pl.pallas_call(
+        functools.partial(weight_grad_kernel, left, right, len(left_refs), tiled),
         out_shape=jax.ShapeDtypeStruct(widths, F32),
         in_specs=[VMEM] * (len(left_refs) + len(right_refs)),
-        out_specs=VMEM,
-        compiler_params=params(16),
-        cost_estimate=cost(4),
+        out_specs=ANY,
+        scratch_shapes=[
+            pltpu.VMEM(widths, F32),
+            pltpu.SemaphoreType.DMA((-(-widths[tiled] // 256),)),
+        ],
+        compiler_params=params(20),
+        cost_estimate=cost(3),
         name=name,
     )(*left_refs, *right_refs)
 
@@ -548,11 +568,14 @@
     cot_a = gather_rows(cotangent)
 
     keep, give, att, lse = attention_call(f_ref, q_rel, w_out, pieces, n_f)
-    terms = scatter_rows(pair_sum(keep, give))
+    total = after(pair_sum(keep, give), cot_a)
+    terms = scatter_rows(total)
+    cot_b = beside(after(cot_a, total))
+    terms[0] = after(terms[0], cot_b)
+    hidden, normed = norm_call(resid_in, gain_row, terms)
 
     assert 2 * width == cols
-    cot_late = after(cot_a, terms[1])
-    cot_b = beside(cot_late)
+    cot_late = after(cot_a, normed)
     cot_blocks = list(column_blocks(c_ref, cot_late, n_c))
     att_blocks = [jnp.concatenate([att[:pair], att[pair:]], axis=1)]
 
@@ -566,12 +589,11 @@
             cot_blocks[k] = part
         att_blocks.extend(parts[len(moving) :])
 
-    hidden, normed = norm_call(resid_in, gain_row, terms)
     normed_a = gather_rows(normed)
     for bit in bits:
         moving, message = crossing(bit)
         if bit == bits[-1]:
-            grad_act = dot(jnp.concatenate([cot_late, cot_b], axis=0), w_down, NT)
+            grad_act = dot(jnp.concatenate([cot_a, cot_b], axis=0), w_down, NT)
             normed_a = after(normed_a, grad_act, message)
         crossed(moving, exchange(message, "ctx", 1 << bit))
     normed_b = beside(normed_a)
@@ -580,6 +602,7 @@
     keep, give = normed_grad_call(pay, w_gate, w_up)
     total = pair_sum(keep, give)
     terms = scatter_rows(total)
+
     cot_cols = after(jnp.concatenate(cot_blocks, axis=0), total)
     cot_side = beside(cot_cols)
 
@@ -623,11 +646,11 @@
         if step == bits[-1]:
             down = dot(late[:, :hidden_units], w_down).astype(BF16)
             terms[0] = after(terms[0], messages[0], messages[1], down)
-            grad_resid, gain_part = norm_grad_call(cotangent, hidden, gain_row, terms)
+            grad_resid, grad_send, gain_part = norm_grad_call(cotangent, hidden, gain_row, terms)
         for h, message in zip(halves, messages):
             h.send(step, message)
 
-    grad_a = gather_rows(grad_resid)
+    grad_a = gather_rows(grad_send)
     down_total = pair_sum(down[:pair], down[pair:])
     grad_a = after(grad_a, down_total)
     grad_b = beside(grad_a)
@@ -666,16 +689,16 @@
     att_rows = [(k, 0, pair, 0) for k in range(n_c)] + [(k, 0, pair, width) for k in range(n_c)]
     normed_pair, shape = (normed_cols, normed_side), (cols, hidden_units)
     grad_w_gate = weight_grad_call(
-        columns, normed_pair, hidden_part(1), hidden_refs, shape, "grad_w_gate"
+        columns, normed_pair, hidden_part(1), hidden_refs, shape, 0, "grad_w_gate"
     )
     grad_w_up = weight_grad_call(
-        columns, normed_pair, hidden_part(2), hidden_refs, shape, "grad_w_up"
+        columns, normed_pair, hidden_part(2), hidden_refs, shape, 0, "grad_w_up"
     )
     grad_w_down = weight_grad_call(
-        hidden_part(0), hidden_refs, columns, (cot_cols, cot_side), shape[::-1], "grad_w_down"
+        hidden_part(0), hidden_refs, columns, (cot_cols, cot_side), shape[::-1], 1, "grad_w_down"
     )
     grad_w_out = weight_grad_call(
-        att_rows, att_blocks, columns, (grad_cols, grad_side), (width, cols), "grad_w_out"
+        att_rows, att_blocks, columns, (grad_cols, grad_side), (width, cols), 1, "grad_w_out"
     )
 
     mixed = functools.reduce(jnp.add, [t.astype(F32) for t in mixed_terms])

time: 155 us -> 145 us (0.935)
  waiting for transfers between devices: 60 us -> 53 us
  Pallas kernels: 32.9 us -> 30.7 us
    ppermute x46, waiting for transfers between devices: 60 us -> 53 us  [exchange(): lax.ppermute(x, axis, [(i, i ^ k) for i in range(lax.axis_size(axis))])]
    pallas_call x4, Pallas kernels: 11.3 us -> 9.01 us  [weight_grad_call(): pl.pallas_call(functools.partial(weight_grad_kernel, left, right, len(lef...]
  transfers between devices with their start and end apart: 46 -> 46, of which waited for: 21 -> 23; matrix products, arithmetic and copies ran while one was open for 4% -> 4% of each run, Pallas kernels for 16% -> 19%
where the time goes in v4:
time: 145 us; the launch traced here: 144 us
  waiting for transfers between devices  53 us (37%)
  starting transfers between devices  51.4 us (35%)
  Pallas kernels  30.7 us (21%)
  matrix products  3.78 us (3%)
  other arithmetic  2.63 us (2%)
  between operations  1.54 us (1%)
    ppermute x46, waiting for transfers between devices, exchange(): lax.ppermute(x, axis, [(i, i ^ k) for i in range(lax.axis_size(axis))])  53 us
    ppermute x46, starting transfers between devices, exchange(): lax.ppermute(x, axis, [(i, i ^ k) for i in range(lax.axis_size(axis))])  51.4 us
    pallas_call x4, Pallas kernels, weight_grad_call(): pl.pallas_call(functools.partial(weight_grad_kernel, left, right, len(lef...  9.01 us
    pallas_call x1, Pallas kernels, normed_grad_call(): pl.pallas_call(normed_grad_kernel, out_shape=(out, out), in_specs=[VMEM]...  5.97 us
    pallas_call x1, Pallas kernels, attention_call(): pl.pallas_call(functools.partial(attention_kernel, n_f, len(pieces)), out...  4.17 us
    pallas_call x1, Pallas kernels, gate_up_call(): pl.pallas_call(gate_up_kernel, out_shape=jax.ShapeDtypeStruct((rows, 3 *...  4.03 us
    dot_general x2, matrix products, dot(): return lax.dot_general(a, b, dims, preferred_element_type=F32)  3.78 us
    pallas_call x1, Pallas kernels, attention_grad_call(): pl.pallas_call(functools.partial(attention_grad_kernel, n_f, n_c), out_sh...  3.72 us
  transfers between devices with their start and end apart: 46, of which 23 were waited for; matrix products, arithmetic and copies ran while one was open for 4% of the time, Pallas kernels for 19%

profile of v4, /device:TPU:0, one launch (start us, length us, event | category | flops | bytes accessed | tf_op | source)
XLA Modules:
  0.0 144.4 jit_solution(6760451152434730865)
XLA Ops:
  0.7 1.9 %prepare_attention.1 = (bf16[128,512]{1,0:T(8,128)(2,1)}, bf16[272,128]{1,0:T(8,128)(2,1)}) custom-call(s32[1]{0:T(128)} %bitcast.1.f_ref, s32[1]{0:T(128)} %bitcast.2.group_ref, bf16[128,512]{1,0:T(8,128)(2,1)} %q_hbm.1, bf16[128,1024]{1,0:T(8,128)(2,1)} %k_hbm.1, bf16[128,1024]{1,0:T(8,128)(2,1)} %v_hbm.1, s32[1,128]{1,0:T(1,128)} %bitcast.31, ...), custom_call_target="tpu_custom_call" | custom-call | flops 1000000000 | bytes 4000000 | tf_op jit(solution)/shard_map/prepare_attention/pallas_call | solution.py:122
  2.5 3.0 %collective-permute-start = (bf16[272,128]{1,0:T(8,128)(2,1)}, bf16[272,128]{1,0:T(8,128)(2,1)S(1)}, u32[]{:S(2)}, u32[]{:S(2)}) collective-permute-start(bf16[272,128]{1,0:T(8,128)(2,1)} %get-tuple-element.59.refs_1_.refs_0_), channel_id=1, source_target_pairs={{0,8},{8,0},{16,24},{24,16},{1,9},{9,1},{17,25},{25,17},{2,10},{10... | collective-permute-start | bytes 208904 | tf_op jit(solution)/shard_map/ppermute | solution.py:529
  5.5 1.5 %collective-permute-start.1 = (bf16[272,128]{1,0:T(8,128)(2,1)}, bf16[272,128]{1,0:T(8,128)(2,1)S(1)}, u32[]{:S(2)}, u32[]{:S(2)}) collective-permute-start(bf16[272,128]{1,0:T(8,128)(2,1)} %get-tuple-element.59.refs_1_.refs_0_), channel_id=1, source_target_pairs={{0,16},{8,24},{16,0},{24,8},{1,17},{9,25},{17,1},{25,9},{2,18},{10... | collective-permute-start | bytes 208904 | tf_op jit(solution)/shard_map/ppermute | solution.py:529
  7.1 2.0 %collective-permute-start.4 = (bf16[16,4096]{1,0:T(8,128)(2,1)S(1)}, bf16[16,4096]{1,0:T(8,128)(2,1)S(1)}, u32[]{:S(2)}, u32[]{:S(2)}) collective-permute-start(bf16[16,4096]{1,0:T(8,128)(2,1)S(1)} %copy-done), channel_id=1, source_target_pairs={{0,2},{1,3},{2,0},{3,1},{4,6},{5,7},{6,4},{7,5},{8,10},{9,11},{10,... | collective-permute-start | bytes 393224 | tf_op jit(solution)/shard_map/ppermute | solution.py:529
  9.1 2.6 %collective-permute-start.5 = (bf16[16,4096]{1,0:T(8,128)(2,1)S(1)}, bf16[16,4096]{1,0:T(8,128)(2,1)S(1)}, u32[]{:S(2)}, u32[]{:S(2)}) collective-permute-start(bf16[16,4096]{1,0:T(8,128)(2,1)S(1)} %copy-done), channel_id=1, source_target_pairs={{0,4},{1,5},{2,6},{3,7},{4,0},{5,1},{6,2},{7,3},{8,12},{9,13},{10,... | collective-permute-start | bytes 393224 | tf_op jit(solution)/shard_map/ppermute | solution.py:529
  13.1 4.2 %attention_and_projection.1 = (bf16[64,4096]{1,0:T(8,128)(2,1)}, bf16[64,4096]{1,0:T(8,128)(2,1)}, bf16[128,512]{1,0:T(8,128)(2,1)}, f32[128,128]{1,0:T(8,128)}) custom-call(s32[1]{0:T(128)} %bitcast.1.f_ref, bf16[128,512]{1,0:T(8,128)(2,1)} %get-tuple-element.58.refs_0_.refs_4_, bf16[272,128]{1,0:T(8,128)(2,1)} %get-tuple-element.59.refs_1_.refs_0_, ...), custom_call_target="tpu_custom_call" | custom-call | flops 2000000000 | bytes 8000000 | tf_op jit(solution)/shard_map/attention_and_projection/pallas_call | solution.py:176
  17.4 3.8 %collective-permute-done.5 = bf16[16,4096]{1,0:T(8,128)(2,1)S(1)} collective-permute-done((bf16[16,4096]{1,0:T(8,128)(2,1)S(1)}, bf16[16,4096]{1,0:T(8,128)(2,1)S(1)}, u32[]{:S(2)}, u32[]{:S(2)}) %collective-permute-start.5) | collective-permute-done | bytes 131104 | tf_op jit(solution)/shard_map/ppermute | solution.py:529
  22.6 2.5 %collective-permute-start.10 = (bf16[16,4096]{1,0:T(8,128)(2,1)S(1)}, bf16[16,4096]{1,0:T(8,128)(2,1)S(1)}, u32[]{:S(2)}, u32[]{:S(2)}) collective-permute-start(bf16[16,4096]{1,0:T(8,128)(2,1)S(1)} %get-tuple-element.121), channel_id=1, source_target_pairs={{0,6},{1,7},{2,4},{3,5},{4,2},{5,3},{6,0},{7,1},{8,14},{9,15},{10,... | collective-permute-start | bytes 393224 | tf_op jit(solution)/shard_map/ppermute | solution.py:529
  27.1 3.7 %collective-permute-done.10.refs_3_ = bf16[16,4096]{1,0:T(8,128)(2,1)S(1)} collective-permute-done((bf16[16,4096]{1,0:T(8,128)(2,1)S(1)}, bf16[16,4096]{1,0:T(8,128)(2,1)S(1)}, u32[]{:S(2)}, u32[]{:S(2)}) %collective-permute-start.10) | collective-permute-done | bytes 131104 | tf_op jit(solution)/shard_map/ppermute | solution.py:529
  30.8 3.0 %collective-permute-done.8.refs_1_ = bf16[16,4096]{1,0:T(8,128)(2,1)S(1)} collective-permute-done((bf16[16,4096]{1,0:T(8,128)(2,1)S(1)}, bf16[16,4096]{1,0:T(8,128)(2,1)S(1)}, u32[]{:S(2)}, u32[]{:S(2)}) %collective-permute-start.8) | collective-permute-done | bytes 131104 | tf_op jit(solution)/shard_map/ppermute | solution.py:529
  33.8 4.5 %collective-permute-done.9.refs_2_ = bf16[16,4096]{1,0:T(8,128)(2,1)S(1)} collective-permute-done((bf16[16,4096]{1,0:T(8,128)(2,1)S(1)}, bf16[16,4096]{1,0:T(8,128)(2,1)S(1)}, u32[]{:S(2)}, u32[]{:S(2)}) %collective-permute-start.9) | collective-permute-done | bytes 131104 | tf_op jit(solution)/shard_map/ppermute | solution.py:529
  38.6 3.0 %collective-permute-start.12 = (bf16[16,4096]{1,0:T(8,128)(2,1)S(1)}, bf16[16,4096]{1,0:T(8,128)(2,1)S(1)}, u32[]{:S(2)}, u32[]{:S(2)}) collective-permute-start(bf16[16,4096]{1,0:T(8,128)(2,1)S(1)} %get-tuple-element.66), channel_id=1, source_target_pairs={{0,4},{1,5},{2,6},{3,7},{4,0},{5,1},{6,2},{7,3},{8,12},{9,13},{10,... | collective-permute-start | bytes 393224 | tf_op jit(solution)/shard_map/ppermute | solution.py:529
  43.1 1.6 %collective-permute-start.14 = (bf16[192,1024]{1,0:T(8,128)(2,1)S(1)}, bf16[192,1024]{1,0:T(8,128)(2,1)S(1)}, u32[]{:S(2)}, u32[]{:S(2)}) collective-permute-start(bf16[192,1024]{1,0:T(8,128)(2,1)S(1)} %maximum_maximum_fusion.1), channel_id=1, source_target_pairs={{0,8},{8,0},{16,24},{24,16},{1,9},{9,1},{17,25},{25,17},{2,10},{10... | collective-permute-start | bytes 1179656 | tf_op jit(solution)/shard_map/ppermute | solution.py:529
  44.8 2.5 %fusion.22.ga_ref = f32[128,896]{1,0:T(8,128)S(1)} fusion(bf16[128,4096]{1,0:T(8,128)(2,1)S(1)} %constant_dynamic-update-slice_fusion.4, bf16[896,4096]{1,0:T(8,128)(2,1)S(1)} %bitcast.28), kind=kOutput, calls=%fused_computation.58 | convolution fusion | flops 939524096 | bytes 8847360 | tf_op jit(solution)/shard_map/dot_general | solution.py:31
  47.2 4.4 %collective-permute-done.12 = bf16[16,4096]{1,0:T(8,128)(2,1)S(1)} collective-permute-done((bf16[16,4096]{1,0:T(8,128)(2,1)S(1)}, bf16[16,4096]{1,0:T(8,128)(2,1)S(1)}, u32[]{:S(2)}, u32[]{:S(2)}) %collective-permute-start.12) | collective-permute-done | bytes 131104 | tf_op jit(solution)/shard_map/ppermute | solution.py:529
  51.7 1.4 collective-permute-done.14
  53.2 1.6 %collective-permute-start.37 = (bf16[256,1024]{1,0:T(8,128)(2,1)S(1)}, bf16[256,1024]{1,0:T(8,128)(2,1)S(1)}, u32[]{:S(2)}, u32[]{:S(2)}) collective-permute-start(bf16[256,1024]{1,0:T(8,128)(2,1)S(1)} %pad_maximum_fusion.3), channel_id=1, source_target_pairs={{0,16},{8,24},{16,0},{24,8},{1,17},{9,25},{17,1},{25,9},{2,18},{10... | collective-permute-start | bytes 1572872 | tf_op jit(solution)/shard_map/ppermute | solution.py:529
  55.2 4.0 %gate_up_and_gradients.1.pay_ref.refs_2_.refs_5_.refs_0_.refs_3_ = bf16[128,2688]{1,0:T(8,128)(2,1)S(1)} custom-call(bf16[64,4096]{1,0:T(8,128)(2,1)S(1)} %pad_maximum_fusion.2.xa_ref.a_ref, bf16[64,4096]{1,0:T(8,128)(2,1)S(1)} %collective-permute-done.15.xb_ref, bf16[4096,896]{1,0:T(8,128)(2,1)S(1)} %bitcast.21, bf16[4096,896]{1,0:T(8,128)(2,1)S(1)} %bitcast.23, ...), custom_call_target="tpu_custom_call" | custom-call | flops 1000000000 | bytes 4000000 | tf_op jit(solution)/shard_map/gate_up_and_gradients/pallas_call | solution.py:326
  59.2 6.0 %normed_gradients.1 = (bf16[64,4096]{1,0:T(8,128)(2,1)S(1)}, bf16[64,4096]{1,0:T(8,128)(2,1)S(1)}) custom-call(bf16[128,2688]{1,0:T(8,128)(2,1)S(1)} %gate_up_and_gradients.1.pay_ref.refs_2_.refs_5_.refs_0_.refs_3_, bf16[4096,896]{1,0:T(8,128)(2,1)S(1)} %bitcast.21, bf16[4096,896]{1,0:T(8,128)(2,1)S(1)} %bitcast.23), custom_call_target="tpu_custom_call" | custom-call | flops 1000000000 | bytes 4000000 | tf_op jit(solution)/shard_map/normed_gradients/pallas_call | solution.py:356
  65.4 2.2 %collective-permute-done.37 = bf16[256,1024]{1,0:T(8,128)(2,1)S(1)} collective-permute-done((bf16[256,1024]{1,0:T(8,128)(2,1)S(1)}, bf16[256,1024]{1,0:T(8,128)(2,1)S(1)}, u32[]{:S(2)}, u32[]{:S(2)}) %collective-permute-start.37) | collective-permute-done | bytes 524320 | tf_op jit(solution)/shard_map/ppermute | solution.py:529
  68.1 1.6 %collective-permute-start.19 = (bf16[64,3712]{1,0:T(8,128)(2,1)S(1)}, bf16[64,3712]{1,0:T(8,128)(2,1)S(1)}, u32[]{:S(2)}, u32[]{:S(2)}) collective-permute-start(bf16[64,3712]{1,0:T(8,128)(2,1)S(1)} %pad_maximum_fusion.7), channel_id=1, source_target_pairs={{0,16},{8,24},{16,0},{24,8},{1,17},{9,25},{17,1},{25,9},{2,18},{10... | collective-permute-start | bytes 1425416 | tf_op jit(solution)/shard_map/ppermute | solution.py:529
  69.7 1.6 %collective-permute-start.18 = (bf16[64,3712]{1,0:T(8,128)(2,1)S(1)}, bf16[64,3712]{1,0:T(8,128)(2,1)S(1)}, u32[]{:S(2)}, u32[]{:S(2)}) collective-permute-start(bf16[64,3712]{1,0:T(8,128)(2,1)S(1)} %pad_maximum_fusion.6), channel_id=1, source_target_pairs={{0,8},{8,0},{16,24},{24,16},{1,9},{9,1},{17,25},{25,17},{2,10},{10... | collective-permute-start | bytes 1425416 | tf_op jit(solution)/shard_map/ppermute | solution.py:529
  72.0 2.3 %collective-permute-start.21 = (bf16[16,4096]{1,0:T(8,128)(2,1)S(1)}, bf16[16,4096]{1,0:T(8,128)(2,1)S(1)}, u32[]{:S(2)}, u32[]{:S(2)}) collective-permute-start(bf16[16,4096]{1,0:T(8,128)(2,1)S(1)} %get-tuple-element.118), channel_id=1, source_target_pairs={{0,4},{1,5},{2,6},{3,7},{4,0},{5,1},{6,2},{7,3},{8,12},{9,13},{10,... | collective-permute-start | bytes 393224 | tf_op jit(solution)/shard_map/ppermute | solution.py:529
  74.3 1.3 collective-permute-start.22
  77.0 3.5 %collective-permute-done.19.refs_6_.refs_4_ = bf16[64,3712]{1,0:T(8,128)(2,1)S(1)} collective-permute-done((bf16[64,3712]{1,0:T(8,128)(2,1)S(1)}, bf16[64,3712]{1,0:T(8,128)(2,1)S(1)}, u32[]{:S(2)}, u32[]{:S(2)}) %collective-permute-start.19) | collective-permute-done | bytes 475168 | tf_op jit(solution)/shard_map/ppermute | solution.py:529
  81.9 1.5 %collective-permute-start.42 = (bf16[64,6400]{1,0:T(8,128)(2,1)S(1)}, bf16[64,6400]{1,0:T(8,128)(2,1)S(1)}, u32[]{:S(2)}, u32[]{:S(2)}) collective-permute-start(bf16[64,6400]{1,0:T(8,128)(2,1)S(1)} %pad_maximum_fusion.1), channel_id=1, source_target_pairs={{0,8},{8,0},{16,24},{24,16},{1,9},{9,1},{17,25},{25,17},{2,10},{10... | collective-permute-start | bytes 2457608 | tf_op jit(solution)/shard_map/ppermute | solution.py:529
  85.1 2.0 %collective-permute-start.23 = (bf16[16,4096]{1,0:T(8,128)(2,1)S(1)}, bf16[16,4096]{1,0:T(8,128)(2,1)S(1)}, u32[]{:S(2)}, u32[]{:S(2)}) collective-permute-start(bf16[16,4096]{1,0:T(8,128)(2,1)S(1)} %get-tuple-element.81), channel_id=1, source_target_pairs={{0,2},{1,3},{2,0},{3,1},{4,6},{5,7},{6,4},{7,5},{8,10},{9,11},{10,... | collective-permute-start | bytes 393224 | tf_op jit(solution)/shard_map/ppermute | solution.py:529
  88.2 1.4 collective-permute-start.25
  89.7 2.0 %collective-permute-done.23 = bf16[16,4096]{1,0:T(8,128)(2,1)S(1)} collective-permute-done((bf16[16,4096]{1,0:T(8,128)(2,1)S(1)}, bf16[16,4096]{1,0:T(8,128)(2,1)S(1)}, u32[]{:S(2)}, u32[]{:S(2)}) %collective-permute-start.23) | collective-permute-done | bytes 131104 | tf_op jit(solution)/shard_map/ppermute | solution.py:529
  91.7 7.1 %collective-permute-done.24 = bf16[16,4096]{1,0:T(8,128)(2,1)S(1)} collective-permute-done((bf16[16,4096]{1,0:T(8,128)(2,1)S(1)}, bf16[16,4096]{1,0:T(8,128)(2,1)S(1)}, u32[]{:S(2)}, u32[]{:S(2)}) %collective-permute-start.24) | collective-permute-done | bytes 131104 | tf_op jit(solution)/shard_map/ppermute | solution.py:529
  99.0 2.0 %collective-permute-start.26 = (bf16[16,4096]{1,0:T(8,128)(2,1)S(1)}, bf16[16,4096]{1,0:T(8,128)(2,1)S(1)}, u32[]{:S(2)}, u32[]{:S(2)}) collective-permute-start(bf16[16,4096]{1,0:T(8,128)(2,1)S(1)} %get-tuple-element.114), channel_id=1, source_target_pairs={{0,2},{1,3},{2,0},{3,1},{4,6},{5,7},{6,4},{7,5},{8,10},{9,11},{10,... | collective-permute-start | bytes 393224 | tf_op jit(solution)/shard_map/ppermute | solution.py:529
  102.0 1.4 collective-permute-start.28
  103.5 3.7 %attention_gradients.1 = (bf16[128,512]{1,0:T(8,128)(2,1)}, bf16[160,256]{1,0:T(8,128)(2,1)S(1)}, bf16[160,256]{1,0:T(8,128)(2,1)S(1)}, bf16[160,256]{1,0:T(8,128)(2,1)S(1)}, bf16[160,256]{1,0:T(8,128)(2,1)S(1)}) custom-call(s32[1]{0:T(128)} %bitcast.1.f_ref, bf16[272,128]{1,0:T(8,128)(2,1)S(1)} %copy-done.4, bf16[272,128]{1,0:T(8,128)(2,1)S(1)} %copy-done.6, ...), custom_call_target="tpu_custom_call" | custom-call | flops 2000000000 | bytes 8000000 | tf_op jit(solution)/shard_map/attention_gradients/pallas_call | solution.py:234
  107.9 6.0 %collective-permute-done.27 = bf16[16,4096]{1,0:T(8,128)(2,1)S(1)} collective-permute-done((bf16[16,4096]{1,0:T(8,128)(2,1)S(1)}, bf16[16,4096]{1,0:T(8,128)(2,1)S(1)}, u32[]{:S(2)}, u32[]{:S(2)}) %collective-permute-start.27) | collective-permute-done | bytes 131104 | tf_op jit(solution)/shard_map/ppermute | solution.py:529
  114.3 1.5 %collective-permute-start.32 = (bf16[160,256]{1,0:T(8,128)(2,1)S(1)}, bf16[160,256]{1,0:T(8,128)(2,1)S(1)}, u32[]{:S(2)}, u32[]{:S(2)}) collective-permute-start(bf16[160,256]{1,0:T(8,128)(2,1)S(1)} %get-tuple-element.91), channel_id=1, source_target_pairs={{0,24},{8,16},{16,8},{24,0},{1,25},{9,17},{17,9},{25,1},{2,26},{10... | collective-permute-start | bytes 245768 | tf_op jit(solution)/shard_map/ppermute | solution.py:529
  116.6 1.7 %collective-permute-done.31.refs_2_ = bf16[160,256]{1,0:T(8,128)(2,1)S(1)} collective-permute-done((bf16[160,256]{1,0:T(8,128)(2,1)S(1)}, bf16[160,256]{1,0:T(8,128)(2,1)S(1)}, u32[]{:S(2)}, u32[]{:S(2)}) %collective-permute-start.31) | collective-permute-done | bytes 81952 | tf_op jit(solution)/shard_map/ppermute | solution.py:529
  118.3 1.4 collective-permute-done.32.refs_3_
  120.3 1.6 %collective-permute-start.39 = (bf16[64,1024]{1,0:T(8,128)(2,1)S(1)}, bf16[64,1024]{1,0:T(8,128)(2,1)S(1)}, u32[]{:S(2)}, u32[]{:S(2)}) collective-permute-start(bf16[64,1024]{1,0:T(8,128)(2,1)S(1)} %get-tuple-element.100), channel_id=1, source_target_pairs={{0,16},{8,24},{16,0},{24,8},{1,17},{9,25},{17,1},{25,9},{2,18},{10... | collective-permute-start | bytes 393224 | tf_op jit(solution)/shard_map/ppermute | solution.py:529
  122.0 1.5 %collective-permute-start.40 = (bf16[64,1024]{1,0:T(8,128)(2,1)S(1)}, bf16[64,1024]{1,0:T(8,128)(2,1)S(1)}, u32[]{:S(2)}, u32[]{:S(2)}) collective-permute-start(bf16[64,1024]{1,0:T(8,128)(2,1)S(1)} %get-tuple-element.101), channel_id=1, source_target_pairs={{0,24},{8,16},{16,8},{24,0},{1,25},{9,17},{17,9},{25,1},{2,26},{10... | collective-permute-start | bytes 393224 | tf_op jit(solution)/shard_map/ppermute | solution.py:529
  123.6 1.6 %collective-permute-done.38 = bf16[64,1024]{1,0:T(8,128)(2,1)S(1)} collective-permute-done((bf16[64,1024]{1,0:T(8,128)(2,1)S(1)}, bf16[64,1024]{1,0:T(8,128)(2,1)S(1)}, u32[]{:S(2)}, u32[]{:S(2)}) %collective-permute-start.38) | collective-permute-done | bytes 131104 | tf_op jit(solution)/shard_map/ppermute | solution.py:529
  125.3 2.6 %collective-permute-done.40 = bf16[64,1024]{1,0:T(8,128)(2,1)S(1)} collective-permute-done((bf16[64,1024]{1,0:T(8,128)(2,1)S(1)}, bf16[64,1024]{1,0:T(8,128)(2,1)S(1)}, u32[]{:S(2)}, u32[]{:S(2)}) %collective-permute-start.40) | collective-permute-done | bytes 131104 | tf_op jit(solution)/shard_map/ppermute | solution.py:529
  129.2 1.8 %collective-permute-start.35 = (bf16[2,48,256]{2,1,0:T(8,128)(2,1)S(1)}, bf16[2,48,256]{2,1,0:T(8,128)(2,1)S(1)}, u32[]{:S(2)}, u32[]{:S(2)}) collective-permute-start(bf16[2,48,256]{2,1,0:T(8,128)(2,1)S(1)} %get-tuple-element.135), channel_id=1, source_target_pairs={{0,4},{1,5},{2,6},{3,7},{4,0},{5,1},{6,2},{7,3},{8,12},{9,13},{10,... | collective-permute-start | bytes 147464 | tf_op jit(solution)/shard_map/ppermute | solution.py:529
  131.1 1.4 collective-permute-start.36
  132.5 2.5 %grad_w_down.1 = f32[896,1024]{1,0:T(8,128)} custom-call(bf16[128,2688]{1,0:T(8,128)(2,1)S(1)} %gate_up_and_gradients.1.pay_ref.refs_2_.refs_5_.refs_0_.refs_3_, bf16[64,3712]{1,0:T(8,128)(2,1)S(1)} %collective-permute-done.18.refs_3_.refs_1_, bf16[64,6400]{1,0:T(8,128)(2,1)S(1)} %collective-permute-done.43.refs_4_.refs_2_, ...), custom_call_target="tpu_custom_call" | custom-call | flops 1500000000 | bytes 6000000 | tf_op jit(solution)/shard_map/grad_w_down/pallas_call | solution.py:415
  135.4 1.6 %collective-permute-done.36.refs_3_ = bf16[2,48,256]{2,1,0:T(8,128)(2,1)S(1)} collective-permute-done((bf16[2,48,256]{2,1,0:T(8,128)(2,1)S(1)}, bf16[2,48,256]{2,1,0:T(8,128)(2,1)S(1)}, u32[]{:S(2)}, u32[]{:S(2)}) %collective-permute-start.36) | collective-permute-done | bytes 49184 | tf_op jit(solution)/shard_map/ppermute | solution.py:529
  137.7 2.3 %grad_w_up.1 = f32[1024,896]{1,0:T(8,128)} custom-call(bf16[256,1024]{1,0:T(8,128)(2,1)S(1)} %maximum_maximum_fusion.refs_0_, bf16[256,1024]{1,0:T(8,128)(2,1)S(1)} %collective-permute-done.44.refs_1_, bf16[128,2688]{1,0:T(8,128)(2,1)S(1)} %gate_up_and_gradients.1.pay_ref.refs_2_.refs_5_.refs_0_.refs_3_, ...), custom_call_target="tpu_custom_call" | custom-call | flops 1500000000 | bytes 6000000 | tf_op jit(solution)/shard_map/grad_w_up/pallas_call | solution.py:415
  140.0 2.3 %grad_w_gate.1 = f32[1024,896]{1,0:T(8,128)} custom-call(bf16[256,1024]{1,0:T(8,128)(2,1)S(1)} %maximum_maximum_fusion.refs_0_, bf16[256,1024]{1,0:T(8,128)(2,1)S(1)} %collective-permute-done.44.refs_1_, bf16[128,2688]{1,0:T(8,128)(2,1)S(1)} %gate_up_and_gradients.1.pay_ref.refs_2_.refs_5_.refs_0_.refs_3_, ...), custom_call_target="tpu_custom_call" | custom-call | flops 1500000000 | bytes 6000000 | tf_op jit(solution)/shard_map/grad_w_gate/pallas_call | solution.py:415
  142.4 1.8 %grad_w_out.1 = f32[512,1024]{1,0:T(8,128)} custom-call(bf16[64,1024]{1,0:T(8,128)(2,1)S(1)} %pad_maximum_fusion.8.refs_0_, bf16[64,1024]{1,0:T(8,128)(2,1)S(1)} %get-tuple-element.130.refs_1_, bf16[64,1024]{1,0:T(8,128)(2,1)S(1)} %get-tuple-element.113.refs_2_, bf16[64,1024]{1,0:T(8,128)(2,1)S(1)} %get-tuple-element.112.refs_3_, ...), custom_call_target="tpu_custom_call" | custom-call | flops 1500000000 | bytes 6000000 | tf_op jit(solution)/shard_map/grad_w_out/pallas_call | solution.py:415
  (148 shorter events, 20.3 us)
Async XLA Ops:
  2.5 9.2 %collective-permute-start = (bf16[272,128]{1,0:T(8,128)(2,1)}, bf16[272,128]{1,0:T(8,128)(2,1)S(1)}, u32[]{:S(2)}, u32[]{:S(2)}) collective-permute-start(bf16[272,128]{1,0:T(8,128)(2,1)} %get-tuple-element.59.refs_1_.refs_0_), channel_id=1, source_target_pairs={{0,8},{8,0},{16,24},{24,16},{1,9},{9,1},{17,25},{25,17},{2,10},{10... | collective-permute-start | bytes 208904 | tf_op jit(solution)/shard_map/ppermute | solution.py:529
  5.5 6.6 %collective-permute-start.1 = (bf16[272,128]{1,0:T(8,128)(2,1)}, bf16[272,128]{1,0:T(8,128)(2,1)S(1)}, u32[]{:S(2)}, u32[]{:S(2)}) collective-permute-start(bf16[272,128]{1,0:T(8,128)(2,1)} %get-tuple-element.59.refs_1_.refs_0_), channel_id=1, source_target_pairs={{0,16},{8,24},{16,0},{24,8},{1,17},{9,25},{17,1},{25,9},{2,18},{10... | collective-permute-start | bytes 208904 | tf_op jit(solution)/shard_map/ppermute | solution.py:529
  7.1 5.4 %collective-permute-start.2 = (bf16[272,128]{1,0:T(8,128)(2,1)}, bf16[272,128]{1,0:T(8,128)(2,1)S(1)}, u32[]{:S(2)}, u32[]{:S(2)}) collective-permute-start(bf16[272,128]{1,0:T(8,128)(2,1)} %get-tuple-element.59.refs_1_.refs_0_), channel_id=1, source_target_pairs={{0,24},{8,16},{16,8},{24,0},{1,25},{9,17},{17,9},{25,1},{2,26},{10... | collective-permute-start | bytes 208904 | tf_op jit(solution)/shard_map/ppermute | solution.py:529
  7.1 10.3 %collective-permute-start.4 = (bf16[16,4096]{1,0:T(8,128)(2,1)S(1)}, bf16[16,4096]{1,0:T(8,128)(2,1)S(1)}, u32[]{:S(2)}, u32[]{:S(2)}) collective-permute-start(bf16[16,4096]{1,0:T(8,128)(2,1)S(1)} %copy-done), channel_id=1, source_target_pairs={{0,2},{1,3},{2,0},{3,1},{4,6},{5,7},{6,4},{7,5},{8,10},{9,11},{10,... | collective-permute-start | bytes 393224 | tf_op jit(solution)/shard_map/ppermute | solution.py:529
  9.1 12.1 %collective-permute-start.5 = (bf16[16,4096]{1,0:T(8,128)(2,1)S(1)}, bf16[16,4096]{1,0:T(8,128)(2,1)S(1)}, u32[]{:S(2)}, u32[]{:S(2)}) collective-permute-start(bf16[16,4096]{1,0:T(8,128)(2,1)S(1)} %copy-done), channel_id=1, source_target_pairs={{0,4},{1,5},{2,6},{3,7},{4,0},{5,1},{6,2},{7,3},{8,12},{9,13},{10,... | collective-permute-start | bytes 393224 | tf_op jit(solution)/shard_map/ppermute | solution.py:529
  11.8 9.5 %collective-permute-start.6 = (bf16[16,4096]{1,0:T(8,128)(2,1)S(1)}, bf16[16,4096]{1,0:T(8,128)(2,1)S(1)}, u32[]{:S(2)}, u32[]{:S(2)}) collective-permute-start(bf16[16,4096]{1,0:T(8,128)(2,1)S(1)} %copy-done), channel_id=1, source_target_pairs={{0,6},{1,7},{2,4},{3,5},{4,2},{5,3},{6,0},{7,1},{8,14},{9,15},{10,... | collective-permute-start | bytes 393224 | tf_op jit(solution)/shard_map/ppermute | solution.py:529
  17.3 21.0 %copy-start.3 = (bf16[16,4096]{1,0:T(8,128)(2,1)S(1)}, bf16[16,4096]{1,0:T(8,128)(2,1)}, u32[]{:S(2)}) copy-start(bf16[16,4096]{1,0:T(8,128)(2,1)} %resid_ref.1) | copy-start | bytes 393220
  17.3 21.0 %copy-start.11 = (f32[4096]{0:T(1024)S(1)}, f32[4096]{0:T(1024)}, u32[]{:S(2)}) copy-start(f32[4096]{0:T(1024)} %param.17) | copy-start | bytes 49156
  17.3 3.9 %collective-permute-start.3 = (bf16[64,4096]{1,0:T(8,128)(2,1)}, bf16[64,4096]{1,0:T(8,128)(2,1)S(1)}, u32[]{:S(2)}, u32[]{:S(2)}) collective-permute-start(bf16[64,4096]{1,0:T(8,128)(2,1)} %get-tuple-element.61), channel_id=1, source_target_pairs={{0,1},{1,0},{2,3},{3,2},{4,5},{5,4},{6,7},{7,6},{8,9},{9,8},{10,11... | collective-permute-start | bytes 1572872 | tf_op jit(solution)/shard_map/ppermute | solution.py:529
  22.4 4.6 %collective-permute-start.7 = (bf16[64,4096]{1,0:T(8,128)(2,1)S(1)}, bf16[64,4096]{1,0:T(8,128)(2,1)S(1)}, u32[]{:S(2)}, u32[]{:S(2)}) collective-permute-start(bf16[64,4096]{1,0:T(8,128)(2,1)S(1)} %get-tuple-element.67.a_ref), channel_id=1, source_target_pairs={{0,1},{1,0},{2,3},{3,2},{4,5},{5,4},{6,7},{7,6},{8,9},{9,8},{10,11... | collective-permute-start | bytes 1572872 | tf_op jit(solution)/shard_map/ppermute | solution.py:529
  22.6 8.2 %collective-permute-start.10 = (bf16[16,4096]{1,0:T(8,128)(2,1)S(1)}, bf16[16,4096]{1,0:T(8,128)(2,1)S(1)}, u32[]{:S(2)}, u32[]{:S(2)}) collective-permute-start(bf16[16,4096]{1,0:T(8,128)(2,1)S(1)} %get-tuple-element.121), channel_id=1, source_target_pairs={{0,6},{1,7},{2,4},{3,5},{4,2},{5,3},{6,0},{7,1},{8,14},{9,15},{10,... | collective-permute-start | bytes 393224 | tf_op jit(solution)/shard_map/ppermute | solution.py:529
  25.1 8.7 %collective-permute-start.8 = (bf16[16,4096]{1,0:T(8,128)(2,1)S(1)}, bf16[16,4096]{1,0:T(8,128)(2,1)S(1)}, u32[]{:S(2)}, u32[]{:S(2)}) collective-permute-start(bf16[16,4096]{1,0:T(8,128)(2,1)S(1)} %get-tuple-element.123), channel_id=1, source_target_pairs={{0,2},{1,3},{2,0},{3,1},{4,6},{5,7},{6,4},{7,5},{8,10},{9,11},{10,... | collective-permute-start | bytes 393224 | tf_op jit(solution)/shard_map/ppermute | solution.py:529
  26.1 12.2 %collective-permute-start.9 = (bf16[16,4096]{1,0:T(8,128)(2,1)S(1)}, bf16[16,4096]{1,0:T(8,128)(2,1)S(1)}, u32[]{:S(2)}, u32[]{:S(2)}) collective-permute-start(bf16[16,4096]{1,0:T(8,128)(2,1)S(1)} %get-tuple-element.122), channel_id=1, source_target_pairs={{0,4},{1,5},{2,6},{3,7},{4,0},{5,1},{6,2},{7,3},{8,12},{9,13},{10,... | collective-permute-start | bytes 393224 | tf_op jit(solution)/shard_map/ppermute | solution.py:529
  38.6 8.7 %collective-permute-start.11 = (bf16[16,4096]{1,0:T(8,128)(2,1)S(1)}, bf16[16,4096]{1,0:T(8,128)(2,1)S(1)}, u32[]{:S(2)}, u32[]{:S(2)}) collective-permute-start(bf16[16,4096]{1,0:T(8,128)(2,1)S(1)} %get-tuple-element.66), channel_id=1, source_target_pairs={{0,2},{1,3},{2,0},{3,1},{4,6},{5,7},{6,4},{7,5},{8,10},{9,11},{10,... | collective-permute-start | bytes 393224 | tf_op jit(solution)/shard_map/ppermute | solution.py:529
  38.6 13.0 %collective-permute-start.12 = (bf16[16,4096]{1,0:T(8,128)(2,1)S(1)}, bf16[16,4096]{1,0:T(8,128)(2,1)S(1)}, u32[]{:S(2)}, u32[]{:S(2)}) collective-permute-start(bf16[16,4096]{1,0:T(8,128)(2,1)S(1)} %get-tuple-element.66), channel_id=1, source_target_pairs={{0,4},{1,5},{2,6},{3,7},{4,0},{5,1},{6,2},{7,3},{8,12},{9,13},{10,... | collective-permute-start | bytes 393224 | tf_op jit(solution)/shard_map/ppermute | solution.py:529
  41.7 10.0 %collective-permute-start.13 = (bf16[16,4096]{1,0:T(8,128)(2,1)S(1)}, bf16[16,4096]{1,0:T(8,128)(2,1)S(1)}, u32[]{:S(2)}, u32[]{:S(2)}) collective-permute-start(bf16[16,4096]{1,0:T(8,128)(2,1)S(1)} %get-tuple-element.66), channel_id=1, source_target_pairs={{0,6},{1,7},{2,4},{3,5},{4,2},{5,3},{6,0},{7,1},{8,14},{9,15},{10,... | collective-permute-start | bytes 393224 | tf_op jit(solution)/shard_map/ppermute | solution.py:529
  43.1 10.0 %collective-permute-start.14 = (bf16[192,1024]{1,0:T(8,128)(2,1)S(1)}, bf16[192,1024]{1,0:T(8,128)(2,1)S(1)}, u32[]{:S(2)}, u32[]{:S(2)}) collective-permute-start(bf16[192,1024]{1,0:T(8,128)(2,1)S(1)} %maximum_maximum_fusion.1), channel_id=1, source_target_pairs={{0,8},{8,0},{16,24},{24,16},{1,9},{9,1},{17,25},{25,17},{2,10},{10... | collective-permute-start | bytes 1179656 | tf_op jit(solution)/shard_map/ppermute | solution.py:529
  53.2 2.0 %collective-permute-start.15 = (bf16[64,4096]{1,0:T(8,128)(2,1)S(1)}, bf16[64,4096]{1,0:T(8,128)(2,1)S(1)}, u32[]{:S(2)}, u32[]{:S(2)}) collective-permute-start(bf16[64,4096]{1,0:T(8,128)(2,1)S(1)} %pad_maximum_fusion.2.xa_ref.a_ref), channel_id=1, source_target_pairs={{0,1},{1,0},{2,3},{3,2},{4,5},{5,4},{6,7},{7,6},{8,9},{9,8},{10,11... | collective-permute-start | bytes 1572872 | tf_op jit(solution)/shard_map/ppermute | solution.py:529
  53.2 14.3 %collective-permute-start.37 = (bf16[256,1024]{1,0:T(8,128)(2,1)S(1)}, bf16[256,1024]{1,0:T(8,128)(2,1)S(1)}, u32[]{:S(2)}, u32[]{:S(2)}) collective-permute-start(bf16[256,1024]{1,0:T(8,128)(2,1)S(1)} %pad_maximum_fusion.3), channel_id=1, source_target_pairs={{0,16},{8,24},{16,0},{24,8},{1,17},{9,25},{17,1},{25,9},{2,18},{10... | collective-permute-start | bytes 1572872 | tf_op jit(solution)/shard_map/ppermute | solution.py:529
  65.2 2.5 %collective-permute-start.16 = (bf16[64,4096]{1,0:T(8,128)(2,1)S(1)}, bf16[64,4096]{1,0:T(8,128)(2,1)S(1)}, u32[]{:S(2)}, u32[]{:S(2)}) collective-permute-start(bf16[64,4096]{1,0:T(8,128)(2,1)S(1)} %get-tuple-element.74), channel_id=1, source_target_pairs={{0,1},{1,0},{2,3},{3,2},{4,5},{5,4},{6,7},{7,6},{8,9},{9,8},{10,11... | collective-permute-start | bytes 1572872 | tf_op jit(solution)/shard_map/ppermute | solution.py:529
  68.1 12.5 %collective-permute-start.19 = (bf16[64,3712]{1,0:T(8,128)(2,1)S(1)}, bf16[64,3712]{1,0:T(8,128)(2,1)S(1)}, u32[]{:S(2)}, u32[]{:S(2)}) collective-permute-start(bf16[64,3712]{1,0:T(8,128)(2,1)S(1)} %pad_maximum_fusion.7), channel_id=1, source_target_pairs={{0,16},{8,24},{16,0},{24,8},{1,17},{9,25},{17,1},{25,9},{2,18},{10... | collective-permute-start | bytes 1425416 | tf_op jit(solution)/shard_map/ppermute | solution.py:529
  69.7 12.2 %collective-permute-start.18 = (bf16[64,3712]{1,0:T(8,128)(2,1)S(1)}, bf16[64,3712]{1,0:T(8,128)(2,1)S(1)}, u32[]{:S(2)}, u32[]{:S(2)}) collective-permute-start(bf16[64,3712]{1,0:T(8,128)(2,1)S(1)} %pad_maximum_fusion.6), channel_id=1, source_target_pairs={{0,8},{8,0},{16,24},{24,16},{1,9},{9,1},{17,25},{25,17},{2,10},{10... | collective-permute-start | bytes 1425416 | tf_op jit(solution)/shard_map/ppermute | solution.py:529
  71.3 12.3 %collective-permute-start.20 = (bf16[16,4096]{1,0:T(8,128)(2,1)S(1)}, bf16[16,4096]{1,0:T(8,128)(2,1)S(1)}, u32[]{:S(2)}, u32[]{:S(2)}) collective-permute-start(bf16[16,4096]{1,0:T(8,128)(2,1)S(1)} %get-tuple-element.119), channel_id=1, source_target_pairs={{0,2},{1,3},{2,0},{3,1},{4,6},{5,7},{6,4},{7,5},{8,10},{9,11},{10,... | collective-permute-start | bytes 393224 | tf_op jit(solution)/shard_map/ppermute | solution.py:529
  72.0 12.1 %collective-permute-start.21 = (bf16[16,4096]{1,0:T(8,128)(2,1)S(1)}, bf16[16,4096]{1,0:T(8,128)(2,1)S(1)}, u32[]{:S(2)}, u32[]{:S(2)}) collective-permute-start(bf16[16,4096]{1,0:T(8,128)(2,1)S(1)} %get-tuple-element.118), channel_id=1, source_target_pairs={{0,4},{1,5},{2,6},{3,7},{4,0},{5,1},{6,2},{7,3},{8,12},{9,13},{10,... | collective-permute-start | bytes 393224 | tf_op jit(solution)/shard_map/ppermute | solution.py:529
  74.3 9.9 %collective-permute-start.22 = (bf16[16,4096]{1,0:T(8,128)(2,1)S(1)}, bf16[16,4096]{1,0:T(8,128)(2,1)S(1)}, u32[]{:S(2)}, u32[]{:S(2)}) collective-permute-start(bf16[16,4096]{1,0:T(8,128)(2,1)S(1)} %get-tuple-element.117), channel_id=1, source_target_pairs={{0,6},{1,7},{2,4},{3,5},{4,2},{5,3},{6,0},{7,1},{8,14},{9,15},{10,... | collective-permute-start | bytes 393224 | tf_op jit(solution)/shard_map/ppermute | solution.py:529
  80.6 7.7 %collective-permute-start.17 = (bf16[64,4096]{1,0:T(8,128)(2,1)S(1)}, bf16[64,4096]{1,0:T(8,128)(2,1)S(1)}, u32[]{:S(2)}, u32[]{:S(2)}) collective-permute-start(bf16[64,4096]{1,0:T(8,128)(2,1)S(1)} %slice.190), channel_id=1, source_target_pairs={{0,1},{1,0},{2,3},{3,2},{4,5},{5,4},{6,7},{7,6},{8,9},{9,8},{10,11... | collective-permute-start | bytes 1572872 | tf_op jit(solution)/shard_map/ppermute | solution.py:529
  81.9 40.1 %collective-permute-start.42 = (bf16[64,6400]{1,0:T(8,128)(2,1)S(1)}, bf16[64,6400]{1,0:T(8,128)(2,1)S(1)}, u32[]{:S(2)}, u32[]{:S(2)}) collective-permute-start(bf16[64,6400]{1,0:T(8,128)(2,1)S(1)} %pad_maximum_fusion.1), channel_id=1, source_target_pairs={{0,8},{8,0},{16,24},{24,16},{1,9},{9,1},{17,25},{25,17},{2,10},{10... | collective-permute-start | bytes 2457608 | tf_op jit(solution)/shard_map/ppermute | solution.py:529
  83.5 39.9 %collective-permute-start.43 = (bf16[64,6400]{1,0:T(8,128)(2,1)S(1)}, bf16[64,6400]{1,0:T(8,128)(2,1)S(1)}, u32[]{:S(2)}, u32[]{:S(2)}) collective-permute-start(bf16[64,6400]{1,0:T(8,128)(2,1)S(1)} %pad_maximum_fusion), channel_id=1, source_target_pairs={{0,16},{8,24},{16,0},{24,8},{1,17},{9,25},{17,1},{25,9},{2,18},{10... | collective-permute-start | bytes 2457608 | tf_op jit(solution)/shard_map/ppermute | solution.py:529
  85.1 6.6 %collective-permute-start.23 = (bf16[16,4096]{1,0:T(8,128)(2,1)S(1)}, bf16[16,4096]{1,0:T(8,128)(2,1)S(1)}, u32[]{:S(2)}, u32[]{:S(2)}) collective-permute-start(bf16[16,4096]{1,0:T(8,128)(2,1)S(1)} %get-tuple-element.81), channel_id=1, source_target_pairs={{0,2},{1,3},{2,0},{3,1},{4,6},{5,7},{6,4},{7,5},{8,10},{9,11},{10,... | collective-permute-start | bytes 393224 | tf_op jit(solution)/shard_map/ppermute | solution.py:529
  87.2 11.6 %collective-permute-start.24 = (bf16[16,4096]{1,0:T(8,128)(2,1)S(1)}, bf16[16,4096]{1,0:T(8,128)(2,1)S(1)}, u32[]{:S(2)}, u32[]{:S(2)}) collective-permute-start(bf16[16,4096]{1,0:T(8,128)(2,1)S(1)} %get-tuple-element.81), channel_id=1, source_target_pairs={{0,4},{1,5},{2,6},{3,7},{4,0},{5,1},{6,2},{7,3},{8,12},{9,13},{10,... | collective-permute-start | bytes 393224 | tf_op jit(solution)/shard_map/ppermute | solution.py:529
  88.2 10.6 %collective-permute-start.25 = (bf16[16,4096]{1,0:T(8,128)(2,1)S(1)}, bf16[16,4096]{1,0:T(8,128)(2,1)S(1)}, u32[]{:S(2)}, u32[]{:S(2)}) collective-permute-start(bf16[16,4096]{1,0:T(8,128)(2,1)S(1)} %get-tuple-element.81), channel_id=1, source_target_pairs={{0,6},{1,7},{2,4},{3,5},{4,2},{5,3},{6,0},{7,1},{8,14},{9,15},{10,... | collective-permute-start | bytes 393224 | tf_op jit(solution)/shard_map/ppermute | solution.py:529
  98.8 3.2 %collective-permute-start.29 = (bf16[64,4096]{1,0:T(8,128)(2,1)S(1)}, bf16[64,4096]{1,0:T(8,128)(2,1)S(1)}, u32[]{:S(2)}, u32[]{:S(2)}) collective-permute-start(bf16[64,4096]{1,0:T(8,128)(2,1)S(1)} %pad_maximum_fusion.4.refs_8_.a_ref), channel_id=1, source_target_pairs={{0,1},{1,0},{2,3},{3,2},{4,5},{5,4},{6,7},{7,6},{8,9},{9,8},{10,11... | collective-permute-start | bytes 1572872 | tf_op jit(solution)/shard_map/ppermute | solution.py:529
  99.0 8.4 %collective-permute-start.26 = (bf16[16,4096]{1,0:T(8,128)(2,1)S(1)}, bf16[16,4096]{1,0:T(8,128)(2,1)S(1)}, u32[]{:S(2)}, u32[]{:S(2)}) collective-permute-start(bf16[16,4096]{1,0:T(8,128)(2,1)S(1)} %get-tuple-element.114), channel_id=1, source_target_pairs={{0,2},{1,3},{2,0},{3,1},{4,6},{5,7},{6,4},{7,5},{8,10},{9,11},{10,... | collective-permute-start | bytes 393224 | tf_op jit(solution)/shard_map/ppermute | solution.py:529
  101.0 12.9 %collective-permute-start.27 = (bf16[16,4096]{1,0:T(8,128)(2,1)S(1)}, bf16[16,4096]{1,0:T(8,128)(2,1)S(1)}, u32[]{:S(2)}, u32[]{:S(2)}) collective-permute-start(bf16[16,4096]{1,0:T(8,128)(2,1)S(1)} %get-tuple-element.116), channel_id=1, source_target_pairs={{0,4},{1,5},{2,6},{3,7},{4,0},{5,1},{6,2},{7,3},{8,12},{9,13},{10,... | collective-permute-start | bytes 393224 | tf_op jit(solution)/shard_map/ppermute | solution.py:529
  102.0 12.3 %collective-permute-start.28 = (bf16[16,4096]{1,0:T(8,128)(2,1)S(1)}, bf16[16,4096]{1,0:T(8,128)(2,1)S(1)}, u32[]{:S(2)}, u32[]{:S(2)}) collective-permute-start(bf16[16,4096]{1,0:T(8,128)(2,1)S(1)} %get-tuple-element.115), channel_id=1, source_target_pairs={{0,6},{1,7},{2,4},{3,5},{4,2},{5,3},{6,0},{7,1},{8,14},{9,15},{10,... | collective-permute-start | bytes 393224 | tf_op jit(solution)/shard_map/ppermute | solution.py:529
  107.4 9.3 %collective-permute-start.30 = (bf16[160,256]{1,0:T(8,128)(2,1)S(1)}, bf16[160,256]{1,0:T(8,128)(2,1)S(1)}, u32[]{:S(2)}, u32[]{:S(2)}) collective-permute-start(bf16[160,256]{1,0:T(8,128)(2,1)S(1)} %get-tuple-element.89), channel_id=1, source_target_pairs={{0,8},{8,0},{16,24},{24,16},{1,9},{9,1},{17,25},{25,17},{2,10},{10... | collective-permute-start | bytes 245768 | tf_op jit(solution)/shard_map/ppermute | solution.py:529
  113.9 4.4 %collective-permute-start.31 = (bf16[160,256]{1,0:T(8,128)(2,1)S(1)}, bf16[160,256]{1,0:T(8,128)(2,1)S(1)}, u32[]{:S(2)}, u32[]{:S(2)}) collective-permute-start(bf16[160,256]{1,0:T(8,128)(2,1)S(1)} %get-tuple-element.90), channel_id=1, source_target_pairs={{0,16},{8,24},{16,0},{24,8},{1,17},{9,25},{17,1},{25,9},{2,18},{10... | collective-permute-start | bytes 245768 | tf_op jit(solution)/shard_map/ppermute | solution.py:529
  114.3 5.3 %collective-permute-start.32 = (bf16[160,256]{1,0:T(8,128)(2,1)S(1)}, bf16[160,256]{1,0:T(8,128)(2,1)S(1)}, u32[]{:S(2)}, u32[]{:S(2)}) collective-permute-start(bf16[160,256]{1,0:T(8,128)(2,1)S(1)} %get-tuple-element.91), channel_id=1, source_target_pairs={{0,24},{8,16},{16,8},{24,0},{1,25},{9,17},{17,9},{25,1},{2,26},{10... | collective-permute-start | bytes 245768 | tf_op jit(solution)/shard_map/ppermute | solution.py:529
  116.6 14.4 %collective-permute-start.45 = (bf16[256,1024]{1,0:T(8,128)(2,1)S(1)}, bf16[256,1024]{1,0:T(8,128)(2,1)S(1)}, u32[]{:S(2)}, u32[]{:S(2)}) collective-permute-start(bf16[256,1024]{1,0:T(8,128)(2,1)S(1)} %pad_maximum_fusion.5.refs_6_), channel_id=1, source_target_pairs={{0,1},{1,0},{2,3},{3,2},{4,5},{5,4},{6,7},{7,6},{8,9},{9,8},{10,11... | collective-permute-start | bytes 1572872 | tf_op jit(solution)/shard_map/ppermute | solution.py:529
  119.7 5.5 %collective-permute-start.38 = (bf16[64,1024]{1,0:T(8,128)(2,1)S(1)}, bf16[64,1024]{1,0:T(8,128)(2,1)S(1)}, u32[]{:S(2)}, u32[]{:S(2)}) collective-permute-start(bf16[64,1024]{1,0:T(8,128)(2,1)S(1)} %get-tuple-element.99), channel_id=1, source_target_pairs={{0,8},{8,0},{16,24},{24,16},{1,9},{9,1},{17,25},{25,17},{2,10},{10... | collective-permute-start | bytes 393224 | tf_op jit(solution)/shard_map/ppermute | solution.py:529
  120.3 5.0 %collective-permute-start.39 = (bf16[64,1024]{1,0:T(8,128)(2,1)S(1)}, bf16[64,1024]{1,0:T(8,128)(2,1)S(1)}, u32[]{:S(2)}, u32[]{:S(2)}) collective-permute-start(bf16[64,1024]{1,0:T(8,128)(2,1)S(1)} %get-tuple-element.100), channel_id=1, source_target_pairs={{0,16},{8,24},{16,0},{24,8},{1,17},{9,25},{17,1},{25,9},{2,18},{10... | collective-permute-start | bytes 393224 | tf_op jit(solution)/shard_map/ppermute | solution.py:529
  122.0 5.9 %collective-permute-start.40 = (bf16[64,1024]{1,0:T(8,128)(2,1)S(1)}, bf16[64,1024]{1,0:T(8,128)(2,1)S(1)}, u32[]{:S(2)}, u32[]{:S(2)}) collective-permute-start(bf16[64,1024]{1,0:T(8,128)(2,1)S(1)} %get-tuple-element.101), channel_id=1, source_target_pairs={{0,24},{8,16},{16,8},{24,0},{1,25},{9,17},{17,9},{25,1},{2,26},{10... | collective-permute-start | bytes 393224 | tf_op jit(solution)/shard_map/ppermute | solution.py:529
  123.5 4.5 %collective-permute-start.33 = (bf16[4,48,256]{2,1,0:T(8,128)(2,1)S(1)}, bf16[4,48,256]{2,1,0:T(8,128)(2,1)S(1)}, u32[]{:S(2)}, u32[]{:S(2)}) collective-permute-start(bf16[4,48,256]{2,1,0:T(8,128)(2,1)S(1)} %get-tuple-element.93), channel_id=1, source_target_pairs={{0,1},{1,0},{2,3},{3,2},{4,5},{5,4},{6,7},{7,6},{8,9},{9,8},{10,11... | collective-permute-start | bytes 294920 | tf_op jit(solution)/shard_map/ppermute | solution.py:529
  125.2 12.5 %collective-permute-start.44 = (bf16[256,1024]{1,0:T(8,128)(2,1)S(1)}, bf16[256,1024]{1,0:T(8,128)(2,1)S(1)}, u32[]{:S(2)}, u32[]{:S(2)}) collective-permute-start(bf16[256,1024]{1,0:T(8,128)(2,1)S(1)} %maximum_maximum_fusion.refs_0_), channel_id=1, source_target_pairs={{0,1},{1,0},{2,3},{3,2},{4,5},{5,4},{6,7},{7,6},{8,9},{9,8},{10,11... | collective-permute-start | bytes 1572872 | tf_op jit(solution)/shard_map/ppermute | solution.py:529
  127.9 14.4 %collective-permute-start.41 = (bf16[256,1024]{1,0:T(8,128)(2,1)S(1)}, bf16[256,1024]{1,0:T(8,128)(2,1)S(1)}, u32[]{:S(2)}, u32[]{:S(2)}) collective-permute-start(bf16[256,1024]{1,0:T(8,128)(2,1)S(1)} %constant_dynamic-update-slice_fusion.9.refs_4_), channel_id=1, source_target_pairs={{0,1},{1,0},{2,3},{3,2},{4,5},{5,4},{6,7},{7,6},{8,9},{9,8},{10,11... | collective-permute-start | bytes 1572872 | tf_op jit(solution)/shard_map/ppermute | solution.py:529
  128.1 7.0 %collective-permute-start.34 = (bf16[2,48,256]{2,1,0:T(8,128)(2,1)S(1)}, bf16[2,48,256]{2,1,0:T(8,128)(2,1)S(1)}, u32[]{:S(2)}, u32[]{:S(2)}) collective-permute-start(bf16[2,48,256]{2,1,0:T(8,128)(2,1)S(1)} %get-tuple-element.134), channel_id=1, source_target_pairs={{0,2},{1,3},{2,0},{3,1},{4,6},{5,7},{6,4},{7,5},{8,10},{9,11},{10,... | collective-permute-start | bytes 147464 | tf_op jit(solution)/shard_map/ppermute | solution.py:529
  129.2 6.2 %collective-permute-start.35 = (bf16[2,48,256]{2,1,0:T(8,128)(2,1)S(1)}, bf16[2,48,256]{2,1,0:T(8,128)(2,1)S(1)}, u32[]{:S(2)}, u32[]{:S(2)}) collective-permute-start(bf16[2,48,256]{2,1,0:T(8,128)(2,1)S(1)} %get-tuple-element.135), channel_id=1, source_target_pairs={{0,4},{1,5},{2,6},{3,7},{4,0},{5,1},{6,2},{7,3},{8,12},{9,13},{10,... | collective-permute-start | bytes 147464 | tf_op jit(solution)/shard_map/ppermute | solution.py:529
  131.1 5.9 %collective-permute-start.36 = (bf16[2,48,256]{2,1,0:T(8,128)(2,1)S(1)}, bf16[2,48,256]{2,1,0:T(8,128)(2,1)S(1)}, u32[]{:S(2)}, u32[]{:S(2)}) collective-permute-start(bf16[2,48,256]{2,1,0:T(8,128)(2,1)S(1)} %get-tuple-element.132), channel_id=1, source_target_pairs={{0,6},{1,7},{2,4},{3,5},{4,2},{5,3},{6,0},{7,1},{8,14},{9,15},{10,... | collective-permute-start | bytes 147464 | tf_op jit(solution)/shard_map/ppermute | solution.py:529
  (18 other events, 211.7 us)

commit v5 on v4

--- a/solution.py
+++ b/solution.py
@@ -299,25 +299,19 @@
     )(cot, hidden, gain_row, *terms)
 
 
-def gate_up_kernel(xa_ref, xb_ref, wg_ref, wu_ref, ga_ref, out_ref, gate_acc, up_acc):
-    depth, width = wg_ref.shape
-    half = xa_ref.shape[0]
-    tile = 512
-    gate_acc[...] = jnp.zeros_like(gate_acc)
-    up_acc[...] = jnp.zeros_like(up_acc)
-
-    @pl.loop(0, depth // tile)
-    def _(step):
-        at = pl.ds(pl.multiple_of(step * tile, tile), tile)
-        x = jnp.concatenate([xa_ref[:, at], xb_ref[:, at]], axis=0)
-        gate_acc[...] += dot(x, wg_ref[at, :])
-        up_acc[...] += dot(x, wu_ref[at, :])
-
-    gate, up, grad_act = gate_acc[...], up_acc[...], ga_ref[...]
-    sig = jax.nn.sigmoid(gate)
-    out_ref[:, :width] = (gate * sig * up).astype(BF16)
-    out_ref[:, width : 2 * width] = (grad_act * up * sig * (1.0 + gate * (1.0 - sig))).astype(BF16)
-    out_ref[:, 2 * width :] = (grad_act * gate * sig).astype(BF16)
+def gate_up_kernel(xa_ref, xb_ref, wg_ref, wu_ref, ga_ref, out_ref):
+    width = wg_ref.shape[1]
+    x = jnp.concatenate([xa_ref[...], xb_ref[...]], axis=0)
+    tile = 256
+    for start in range(0, width, tile):
+        end = min(start + tile, width)
+        gate, up = dot(x, wg_ref[:, start:end]), dot(x, wu_ref[:, start:end])
+        grad_act = ga_ref[:, start:end]
+        sig = jax.nn.sigmoid(gate)
+        out_ref[:, start:end] = (gate * sig * up).astype(BF16)
+        grad_gate = grad_act * up * sig * (1.0 + gate * (1.0 - sig))
+        out_ref[:, width + start : width + end] = grad_gate.astype(BF16)
+        out_ref[:, 2 * width + start : 2 * width + end] = (grad_act * gate * sig).astype(BF16)
 
 
 def gate_up_call(xa, xb, w_gate, w_up, grad_act):
@@ -328,7 +322,6 @@
         out_shape=jax.ShapeDtypeStruct((rows, 3 * width), BF16),
         in_specs=[VMEM] * 5,
         out_specs=VMEM,
-        scratch_shapes=[pltpu.VMEM((rows, width), F32)] * 2,
         compiler_params=params(24),
         cost_estimate=cost(2),
         name="gate_up_and_gradients",
@@ -338,13 +331,12 @@
 def normed_grad_kernel(pay_ref, wg_ref, wu_ref, keep_ref, give_ref):
     depth, width = wg_ref.shape
     half = keep_ref.shape[0]
-    tile = 512
-
-    @pl.loop(0, depth // tile)
-    def _(step):
-        at = pl.ds(pl.multiple_of(step * tile, tile), tile)
-        out = dot(pay_ref[:, width : 2 * width], wg_ref[at, :], NT)
-        out = (out + dot(pay_ref[:, 2 * width :], wu_ref[at, :], NT)).astype(BF16)
+    grad_gate, grad_up = pay_ref[:, width : 2 * width], pay_ref[:, 2 * width :]
+    tile = 1024
+    for start in range(0, depth, tile):
+        at = slice(start, start + tile)
+        out = dot(wg_ref[at, :], grad_gate, NT) + dot(wu_ref[at, :], grad_up, NT)
+        out = out.T.astype(BF16)
         keep_ref[:, at] = out[:half]
         give_ref[:, at] = out[half:]
 
@@ -572,30 +564,45 @@
     terms = scatter_rows(total)
     cot_b = beside(after(cot_a, total))
     terms[0] = after(terms[0], cot_b)
-    hidden, normed = norm_call(resid_in, gain_row, terms)
 
     assert 2 * width == cols
-    cot_late = after(cot_a, normed)
+    cot_late = after(cot_a, cot_b)
     cot_blocks = list(column_blocks(c_ref, cot_late, n_c))
     att_blocks = [jnp.concatenate([att[:pair], att[pair:]], axis=1)]
 
-    def crossing(bit):
-        moving = [k for k in range(n_c) if k >> bit & 1]
-        return moving, jnp.concatenate([cot_blocks[k] for k in moving] + att_blocks, axis=0)
-
-    def crossed(moving, message):
-        parts = [message[i : i + pair] for i in range(0, message.shape[0], pair)]
-        for k, part in zip(moving, parts):
-            cot_blocks[k] = part
-        att_blocks.extend(parts[len(moving) :])
-
+    def split(message):
+        return [message[i : i + pair] for i in range(0, message.shape[0], pair)]
+
+    def owned(bit):
+        return [k for k in range(n_c) if k >> bit & 1 and not k & ((1 << bit) - 1)]
+
+    first_messages = [
+        exchange(
+            jnp.concatenate([cot_blocks[k] for k in owned(bit)] + att_blocks, axis=0),
+            "ctx",
+            1 << bit,
+        )
+        for bit in bits
+    ]
+    terms[0] = after(terms[0], first_messages)
+    hidden, normed = norm_call(resid_in, gain_row, terms)
     normed_a = gather_rows(normed)
     for bit in bits:
-        moving, message = crossing(bit)
+        *blocks, att_block = split(first_messages[bit])
+        for k, block in zip(owned(bit), blocks):
+            cot_blocks[k] = block
+        passed_on = [k for k in range(n_c) if k >> bit & 1 and k not in owned(bit)]
+        if bit == 0:
+            att_blocks.append(att_block)
+            continue
+        message = jnp.concatenate([cot_blocks[k] for k in passed_on] + att_blocks[1:], axis=0)
         if bit == bits[-1]:
             grad_act = dot(jnp.concatenate([cot_a, cot_b], axis=0), w_down, NT)
             normed_a = after(normed_a, grad_act, message)
-        crossed(moving, exchange(message, "ctx", 1 << bit))
+        blocks = split(exchange(message, "ctx", 1 << bit))
+        for k, block in zip(passed_on, blocks):
+            cot_blocks[k] = block
+        att_blocks.extend([att_block] + blocks[len(passed_on) :])
     normed_b = beside(normed_a)
 
     pay = gate_up_call(normed_a, normed_b, w_gate, w_up, grad_act)
@@ -652,28 +659,36 @@
 
     grad_a = gather_rows(grad_send)
     down_total = pair_sum(down[:pair], down[pair:])
-    grad_a = after(grad_a, down_total)
+    grad_a = after(grad_a, down_total, [h.arrays[-1] for h in halves])
     grad_b = beside(grad_a)
-    mixed_terms = scatter_rows(after(down_total, grad_a))
+    down_late = after(down_total, grad_a)
+    down_blocks = {m: down_late[m * share : (m + 1) * share] for m in range(half)}
+
+    def crossing_down(blocks, bit):
+        moving = [m for m in blocks if m >> bit & 1]
+        message = jnp.concatenate([blocks[m] for m in moving], axis=0)
+        return moving, exchange(message, "ffn", 2 << bit)
+
+    def added_down(blocks, bit, moving, message):
+        message = message.astype(F32)
+        parts = {m ^ 1 << bit: message[i * share : (i + 1) * share] for i, m in enumerate(moving)}
+        return {m: parts[m] + blocks[m].astype(F32) for m in parts}
+
+    moving, message = crossing_down(down_blocks, 0)
 
     grad_queries, *parts = attention_grad_call(
         f_ref, q_rel, att, lse, gain_part, grad_a, grad_b, w_out, pieces, n_f
     )
-    parts = [parts[0]] + [exchange(parts[k], "ctx", k) for k in range(1, n_c)]
-    grad_cols = to_columns(column_blocks(c_ref, after(grad_a, *parts), n_c))
-    grad_cols = jnp.concatenate(grad_cols, axis=0)
-    grad_side = beside(grad_cols)
-
-    own_chunks, beside_chunks = sum_call(f_ref, parts, rows, n_f)
-    chunks = jnp.stack([own_chunks, beside(beside_chunks)], axis=1)
-    chunks = [chunks[0]] + [exchange(chunks[m], "ffn", 2 * m) for m in range(1, half)]
-    grad_keys, grad_values, grad_gain = heads_call(f_ref, chunks, depth, n_f)
-
     normed_cols = jnp.concatenate(
         [jnp.concatenate([h.columns[k] for h in halves], axis=1) for k in range(n_c)], axis=0
     )
-    normed_cols = after(normed_cols, parts[0])
     normed_side = beside(normed_cols)
+    parts = [parts[0]] + [exchange(parts[k], "ctx", k) for k in range(1, n_c)]
+    down_blocks = added_down(down_blocks, 0, moving, after(message, parts[0]))
+    for bit in range(1, log2(half)):
+        down_blocks = {m: block.astype(BF16) for m, block in down_blocks.items()}
+        moving, message = crossing_down(down_blocks, bit)
+        down_blocks = added_down(down_blocks, bit, moving, message)
     offset = len(halves[0].arrays)
     hidden_refs = halves[0].arrays + halves[1].arrays
 
@@ -687,22 +702,30 @@
 
     columns = [(0, 0, n_c * pair, 0), (1, 0, n_c * pair, 0)]
     att_rows = [(k, 0, pair, 0) for k in range(n_c)] + [(k, 0, pair, width) for k in range(n_c)]
-    normed_pair, shape = (normed_cols, normed_side), (cols, hidden_units)
-    grad_w_gate = weight_grad_call(
-        columns, normed_pair, hidden_part(1), hidden_refs, shape, 0, "grad_w_gate"
-    )
+    normed_pair, shape = after((normed_cols, normed_side), parts[0]), (cols, hidden_units)
     grad_w_up = weight_grad_call(
         columns, normed_pair, hidden_part(2), hidden_refs, shape, 0, "grad_w_up"
     )
     grad_w_down = weight_grad_call(
         hidden_part(0), hidden_refs, columns, (cot_cols, cot_side), shape[::-1], 1, "grad_w_down"
     )
+    own_chunks, beside_chunks = sum_call(f_ref, after(parts, grad_w_up), rows, n_f)
+    grad_cols = to_columns(column_blocks(c_ref, after(grad_a, own_chunks), n_c))
+    grad_cols = jnp.concatenate(grad_cols, axis=0)
+    grad_side = beside(grad_cols)
+
+    chunks = jnp.stack([own_chunks, beside(beside_chunks)], axis=1)
+    chunks = [chunks[0]] + [exchange(chunks[m], "ffn", 2 * m) for m in range(1, half)]
+    grad_w_gate = weight_grad_call(
+        columns, after(normed_pair, own_chunks), hidden_part(1), hidden_refs, shape, 0, "grad_w_gate"
+    )
+    grad_keys, grad_values, grad_gain = heads_call(f_ref, after(chunks, grad_w_gate), depth, n_f)
+
     grad_w_out = weight_grad_call(
         att_rows, att_blocks, columns, (grad_cols, grad_side), (width, cols), 1, "grad_w_out"
     )
 
-    mixed = functools.reduce(jnp.add, [t.astype(F32) for t in mixed_terms])
-    mixed = (hidden.astype(F32) + mixed).astype(BF16)
+    mixed = (hidden.astype(F32) + down_blocks[0]).astype(BF16)
 
     return (
         mixed,

time: 145 us -> 139 us (0.959)
  Pallas kernels: 30.7 us -> 27.5 us
  waiting for transfers between devices: 53 us -> 51.1 us
  starting transfers between devices: 51.4 us -> 49.7 us
    ppermute x46, waiting for transfers between devices: 53 us -> 51.1 us  [exchange(): lax.ppermute(x, axis, [(i, i ^ k) for i in range(lax.axis_size(axis))])]
    pallas_call x1, Pallas kernels: 5.97 us -> 4.18 us  [normed_grad_call(): pl.pallas_call(normed_grad_kernel, out_shape=(out, out), in_specs=[VMEM]...]
    ppermute x46, starting transfers between devices: 51.4 us -> 49.7 us  [exchange(): lax.ppermute(x, axis, [(i, i ^ k) for i in range(lax.axis_size(axis))])]
    pallas_call x1, Pallas kernels: 4.03 us -> 2.56 us  [gate_up_call(): pl.pallas_call(gate_up_kernel, out_shape=jax.ShapeDtypeStruct((rows, 3 *...]
  transfers between devices with their start and end apart: 46 -> 46, of which waited for: 23 -> 20; matrix products, arithmetic and copies ran while one was open for 4% -> 5% of each run, Pallas kernels for 19% -> 18%
where the time goes in v5:
time: 139 us; the launch traced here: 138 us
  waiting for transfers between devices  51.1 us (37%)
  starting transfers between devices  49.7 us (36%)
  Pallas kernels  27.5 us (20%)
  matrix products  3.7 us (3%)
  other arithmetic  2.67 us (2%)
  local copies, waits for them, and re-layouts  2.13 us (2%)
  between operations  1.56 us (1%)
    ppermute x46, waiting for transfers between devices, exchange(): lax.ppermute(x, axis, [(i, i ^ k) for i in range(lax.axis_size(axis))])  51.1 us
    ppermute x46, starting transfers between devices, exchange(): lax.ppermute(x, axis, [(i, i ^ k) for i in range(lax.axis_size(axis))])  49.7 us
    pallas_call x4, Pallas kernels, weight_grad_call(): pl.pallas_call(functools.partial(weight_grad_kernel, left, right, len(lef...  9.01 us
    pallas_call x1, Pallas kernels, attention_call(): pl.pallas_call(functools.partial(attention_kernel, n_f, len(pieces)), out...  4.3 us
    pallas_call x1, Pallas kernels, normed_grad_call(): pl.pallas_call(normed_grad_kernel, out_shape=(out, out), in_specs=[VMEM]...  4.18 us
    dot_general x2, matrix products, dot(): return lax.dot_general(a, b, dims, preferred_element_type=F32)  3.7 us
    pallas_call x1, Pallas kernels, attention_grad_call(): pl.pallas_call(functools.partial(attention_grad_kernel, n_f, n_c), out_sh...  3.69 us
  transfers between devices with their start and end apart: 46, of which 20 were waited for; matrix products, arithmetic and copies ran while one was open for 5% of the time, Pallas kernels for 18%

profile of v5, /device:TPU:0, one launch (start us, length us, event | category | flops | bytes accessed | tf_op | source)
XLA Modules:
  0.0 138.4 jit_solution(7766157042499943315)
XLA Ops:
  0.7 5.1 %collective-permute-start.6 = (bf16[16,4096]{1,0:T(8,128)(2,1)}, bf16[16,4096]{1,0:T(8,128)(2,1)S(1)}, u32[]{:S(2)}, u32[]{:S(2)}) collective-permute-start(bf16[16,4096]{1,0:T(8,128)(2,1)} %cot_ref.1), channel_id=1, source_target_pairs={{0,6},{1,7},{2,4},{3,5},{4,2},{5,3},{6,0},{7,1},{8,14},{9,15},{10,... | collective-permute-start | bytes 393224 | tf_op jit(solution)/shard_map/ppermute | solution.py:521
  5.8 1.8 %prepare_attention.1 = (bf16[128,512]{1,0:T(8,128)(2,1)}, bf16[272,128]{1,0:T(8,128)(2,1)}) custom-call(s32[1]{0:T(128)} %bitcast.1.f_ref, s32[1]{0:T(128)} %bitcast.2.group_ref, bf16[128,512]{1,0:T(8,128)(2,1)} %q_hbm.1, bf16[128,1024]{1,0:T(8,128)(2,1)} %k_hbm.1, bf16[128,1024]{1,0:T(8,128)(2,1)} %v_hbm.1, s32[1,128]{1,0:T(1,128)} %bitcast.31, ...), custom_call_target="tpu_custom_call" | custom-call | flops 1000000000 | bytes 4000000 | tf_op jit(solution)/shard_map/prepare_attention/pallas_call | solution.py:122
  7.6 2.5 %collective-permute-start.2 = (bf16[272,128]{1,0:T(8,128)(2,1)}, bf16[272,128]{1,0:T(8,128)(2,1)S(1)}, u32[]{:S(2)}, u32[]{:S(2)}) collective-permute-start(bf16[272,128]{1,0:T(8,128)(2,1)} %get-tuple-element.72.refs_1_.refs_0_), channel_id=1, source_target_pairs={{0,24},{8,16},{16,8},{24,0},{1,25},{9,17},{17,9},{25,1},{2,26},{10... | collective-permute-start | bytes 208904 | tf_op jit(solution)/shard_map/ppermute | solution.py:521
  11.2 2.0 %collective-permute-done.2.refs_4_.refs_3_ = bf16[272,128]{1,0:T(8,128)(2,1)S(1)} collective-permute-done((bf16[272,128]{1,0:T(8,128)(2,1)}, bf16[272,128]{1,0:T(8,128)(2,1)S(1)}, u32[]{:S(2)}, u32[]{:S(2)}) %collective-permute-start.2) | collective-permute-done | bytes 69664 | tf_op jit(solution)/shard_map/ppermute | solution.py:521
  15.8 4.3 %attention_and_projection.1 = (bf16[64,4096]{1,0:T(8,128)(2,1)}, bf16[64,4096]{1,0:T(8,128)(2,1)}, bf16[128,512]{1,0:T(8,128)(2,1)}, f32[128,128]{1,0:T(8,128)}) custom-call(s32[1]{0:T(128)} %bitcast.1.f_ref, bf16[128,512]{1,0:T(8,128)(2,1)} %get-tuple-element.71.refs_0_.refs_4_, bf16[272,128]{1,0:T(8,128)(2,1)} %get-tuple-element.72.refs_1_.refs_0_, ...), custom_call_target="tpu_custom_call" | custom-call | flops 2000000000 | bytes 8000000 | tf_op jit(solution)/shard_map/attention_and_projection/pallas_call | solution.py:176
  22.3 1.2 add_convert_fusion.2
  23.7 2.5 %collective-permute-start.12 = (bf16[16,4096]{1,0:T(8,128)(2,1)S(1)}, bf16[16,4096]{1,0:T(8,128)(2,1)S(1)}, u32[]{:S(2)}, u32[]{:S(2)}) collective-permute-start(bf16[16,4096]{1,0:T(8,128)(2,1)S(1)} %get-tuple-element.144), channel_id=1, source_target_pairs={{0,6},{1,7},{2,4},{3,5},{4,2},{5,3},{6,0},{7,1},{8,14},{9,15},{10,... | collective-permute-start | bytes 393224 | tf_op jit(solution)/shard_map/ppermute | solution.py:521
  26.8 1.4 collective-permute-start.10
  28.2 1.6 %collective-permute-start.9 = (bf16[128,1024]{1,0:T(8,128)(2,1)S(1)}, bf16[128,1024]{1,0:T(8,128)(2,1)S(1)}, u32[]{:S(2)}, u32[]{:S(2)}) collective-permute-start(bf16[128,1024]{1,0:T(8,128)(2,1)S(1)} %maximum_maximum_fusion.2), channel_id=1, source_target_pairs={{0,16},{8,24},{16,0},{24,8},{1,17},{9,25},{17,1},{25,9},{2,18},{10... | collective-permute-start | bytes 786440 | tf_op jit(solution)/shard_map/ppermute | solution.py:521
  30.5 5.5 %collective-permute-done.9 = bf16[128,1024]{1,0:T(8,128)(2,1)S(1)} collective-permute-done((bf16[128,1024]{1,0:T(8,128)(2,1)S(1)}, bf16[128,1024]{1,0:T(8,128)(2,1)S(1)}, u32[]{:S(2)}, u32[]{:S(2)}) %collective-permute-start.9) | collective-permute-done | bytes 262176 | tf_op jit(solution)/shard_map/ppermute | solution.py:521
  36.0 4.1 %collective-permute-done.8 = bf16[192,1024]{1,0:T(8,128)(2,1)S(1)} collective-permute-done((bf16[192,1024]{1,0:T(8,128)(2,1)S(1)}, bf16[192,1024]{1,0:T(8,128)(2,1)S(1)}, u32[]{:S(2)}, u32[]{:S(2)}) %collective-permute-start.8) | collective-permute-done | bytes 393248 | tf_op jit(solution)/shard_map/ppermute | solution.py:521
  40.5 3.0 %collective-permute-start.15 = (bf16[16,4096]{1,0:T(8,128)(2,1)S(1)}, bf16[16,4096]{1,0:T(8,128)(2,1)S(1)}, u32[]{:S(2)}, u32[]{:S(2)}) collective-permute-start(bf16[16,4096]{1,0:T(8,128)(2,1)S(1)} %get-tuple-element.85), channel_id=1, source_target_pairs={{0,6},{1,7},{2,4},{3,5},{4,2},{5,3},{6,0},{7,1},{8,14},{9,15},{10,... | collective-permute-start | bytes 393224 | tf_op jit(solution)/shard_map/ppermute | solution.py:521
  43.5 1.4 %collective-permute-start.13 = (bf16[16,4096]{1,0:T(8,128)(2,1)S(1)}, bf16[16,4096]{1,0:T(8,128)(2,1)S(1)}, u32[]{:S(2)}, u32[]{:S(2)}) collective-permute-start(bf16[16,4096]{1,0:T(8,128)(2,1)S(1)} %get-tuple-element.85), channel_id=1, source_target_pairs={{0,2},{1,3},{2,0},{3,1},{4,6},{5,7},{6,4},{7,5},{8,10},{9,11},{10,... | collective-permute-start | bytes 393224 | tf_op jit(solution)/shard_map/ppermute | solution.py:521
  44.9 2.4 %fusion.25.ga_ref = f32[128,896]{1,0:T(8,128)S(1)} fusion(bf16[128,4096]{1,0:T(8,128)(2,1)S(1)} %constant_dynamic-update-slice_fusion.4, bf16[896,4096]{1,0:T(8,128)(2,1)S(1)} %bitcast.28), kind=kOutput, calls=%fused_computation.64 | convolution fusion | flops 939524096 | bytes 8847360 | tf_op jit(solution)/shard_map/dot_general | solution.py:31
  47.4 1.4 %collective-permute-done.15 = bf16[16,4096]{1,0:T(8,128)(2,1)S(1)} collective-permute-done((bf16[16,4096]{1,0:T(8,128)(2,1)S(1)}, bf16[16,4096]{1,0:T(8,128)(2,1)S(1)}, u32[]{:S(2)}, u32[]{:S(2)}) %collective-permute-start.15) | collective-permute-done | bytes 131104 | tf_op jit(solution)/shard_map/ppermute | solution.py:521
  48.8 4.7 %collective-permute-done.14 = bf16[16,4096]{1,0:T(8,128)(2,1)S(1)} collective-permute-done((bf16[16,4096]{1,0:T(8,128)(2,1)S(1)}, bf16[16,4096]{1,0:T(8,128)(2,1)S(1)}, u32[]{:S(2)}, u32[]{:S(2)}) %collective-permute-start.14) | collective-permute-done | bytes 131104 | tf_op jit(solution)/shard_map/ppermute | solution.py:521
  53.7 1.4 collective-permute-start.40
  55.5 2.6 %gate_up_and_gradients.1.pay_ref.refs_2_.refs_5_.refs_0_.refs_3_ = bf16[128,2688]{1,0:T(8,128)(2,1)S(1)} custom-call(bf16[64,4096]{1,0:T(8,128)(2,1)S(1)} %pad_maximum_fusion.2.xa_ref.a_ref, bf16[64,4096]{1,0:T(8,128)(2,1)S(1)} %collective-permute-done.16.xb_ref, bf16[4096,896]{1,0:T(8,128)(2,1)S(1)} %bitcast.21, bf16[4096,896]{1,0:T(8,128)(2,1)S(1)} %bitcast.23, ...), custom_call_target="tpu_custom_call" | custom-call | flops 1000000000 | bytes 4000000 | tf_op jit(solution)/shard_map/gate_up_and_gradients/pallas_call | solution.py:320
  58.1 4.2 %normed_gradients.1 = (bf16[64,4096]{1,0:T(8,128)(2,1)S(1)}, bf16[64,4096]{1,0:T(8,128)(2,1)S(1)}) custom-call(bf16[128,2688]{1,0:T(8,128)(2,1)S(1)} %gate_up_and_gradients.1.pay_ref.refs_2_.refs_5_.refs_0_.refs_3_, bf16[4096,896]{1,0:T(8,128)(2,1)S(1)} %bitcast.21, bf16[4096,896]{1,0:T(8,128)(2,1)S(1)} %bitcast.23), custom_call_target="tpu_custom_call" | custom-call | flops 1000000000 | bytes 4000000 | tf_op jit(solution)/shard_map/normed_gradients/pallas_call | solution.py:348
  62.6 1.7 %collective-permute-done.17 = bf16[64,4096]{1,0:T(8,128)(2,1)S(1)} collective-permute-done((bf16[64,4096]{1,0:T(8,128)(2,1)S(1)}, bf16[64,4096]{1,0:T(8,128)(2,1)S(1)}, u32[]{:S(2)}, u32[]{:S(2)}) %collective-permute-start.17) | collective-permute-done | bytes 524320 | tf_op jit(solution)/shard_map/ppermute | solution.py:521
  64.6 2.6 %collective-permute-start.23 = (bf16[16,4096]{1,0:T(8,128)(2,1)S(1)}, bf16[16,4096]{1,0:T(8,128)(2,1)S(1)}, u32[]{:S(2)}, u32[]{:S(2)}) collective-permute-start(bf16[16,4096]{1,0:T(8,128)(2,1)S(1)} %get-tuple-element.140), channel_id=1, source_target_pairs={{0,6},{1,7},{2,4},{3,5},{4,2},{5,3},{6,0},{7,1},{8,14},{9,15},{10,... | collective-permute-start | bytes 393224 | tf_op jit(solution)/shard_map/ppermute | solution.py:521
  67.2 1.9 %collective-permute-start.21 = (bf16[16,4096]{1,0:T(8,128)(2,1)S(1)}, bf16[16,4096]{1,0:T(8,128)(2,1)S(1)}, u32[]{:S(2)}, u32[]{:S(2)}) collective-permute-start(bf16[16,4096]{1,0:T(8,128)(2,1)S(1)} %get-tuple-element.142), channel_id=1, source_target_pairs={{0,2},{1,3},{2,0},{3,1},{4,6},{5,7},{6,4},{7,5},{8,10},{9,11},{10,... | collective-permute-start | bytes 393224 | tf_op jit(solution)/shard_map/ppermute | solution.py:521
  70.0 1.3 collective-permute-start.20
  71.3 1.3 convolution_convert_fusion
  72.6 9.2 %collective-permute-done.20.refs_6_.refs_4_ = bf16[64,3712]{1,0:T(8,128)(2,1)S(1)} collective-permute-done((bf16[64,3712]{1,0:T(8,128)(2,1)S(1)}, bf16[64,3712]{1,0:T(8,128)(2,1)S(1)}, u32[]{:S(2)}, u32[]{:S(2)}) %collective-permute-start.20) | collective-permute-done | bytes 475168 | tf_op jit(solution)/shard_map/ppermute | solution.py:521
  82.0 1.3 collective-permute-start.28
  83.4 1.4 collective-permute-start.27
  85.7 2.6 %collective-permute-start.26 = (bf16[16,4096]{1,0:T(8,128)(2,1)S(1)}, bf16[16,4096]{1,0:T(8,128)(2,1)S(1)}, u32[]{:S(2)}, u32[]{:S(2)}) collective-permute-start(bf16[16,4096]{1,0:T(8,128)(2,1)S(1)} %get-tuple-element.95), channel_id=1, source_target_pairs={{0,6},{1,7},{2,4},{3,5},{4,2},{5,3},{6,0},{7,1},{8,14},{9,15},{10,... | collective-permute-start | bytes 393224 | tf_op jit(solution)/shard_map/ppermute | solution.py:521
  88.3 1.8 %collective-permute-start.24 = (bf16[16,4096]{1,0:T(8,128)(2,1)S(1)}, bf16[16,4096]{1,0:T(8,128)(2,1)S(1)}, u32[]{:S(2)}, u32[]{:S(2)}) collective-permute-start(bf16[16,4096]{1,0:T(8,128)(2,1)S(1)} %get-tuple-element.95), channel_id=1, source_target_pairs={{0,2},{1,3},{2,0},{3,1},{4,6},{5,7},{6,4},{7,5},{8,10},{9,11},{10,... | collective-permute-start | bytes 393224 | tf_op jit(solution)/shard_map/ppermute | solution.py:521
  90.2 3.7 %collective-permute-done.26 = bf16[16,4096]{1,0:T(8,128)(2,1)S(1)} collective-permute-done((bf16[16,4096]{1,0:T(8,128)(2,1)S(1)}, bf16[16,4096]{1,0:T(8,128)(2,1)S(1)}, u32[]{:S(2)}, u32[]{:S(2)}) %collective-permute-start.26) | collective-permute-done | bytes 131104 | tf_op jit(solution)/shard_map/ppermute | solution.py:521
  93.9 5.5 %collective-permute-done.25 = bf16[16,4096]{1,0:T(8,128)(2,1)S(1)} collective-permute-done((bf16[16,4096]{1,0:T(8,128)(2,1)S(1)}, bf16[16,4096]{1,0:T(8,128)(2,1)S(1)}, u32[]{:S(2)}, u32[]{:S(2)}) %collective-permute-start.25) | collective-permute-done | bytes 131104 | tf_op jit(solution)/shard_map/ppermute | solution.py:521
  99.4 3.3 %collective-permute-done.28.refs_7_.refs_5_ = bf16[64,6400]{1,0:T(8,128)(2,1)S(1)} collective-permute-done((bf16[64,6400]{1,0:T(8,128)(2,1)S(1)}, bf16[64,6400]{1,0:T(8,128)(2,1)S(1)}, u32[]{:S(2)}, u32[]{:S(2)}) %collective-permute-start.28) | collective-permute-done | bytes 819232 | tf_op jit(solution)/shard_map/ppermute | solution.py:521
  102.7 1.1 collective-permute-done.27.refs_4_.refs_2_
  105.2 2.5 %grad_w_down.1 = f32[896,1024]{1,0:T(8,128)} custom-call(bf16[128,2688]{1,0:T(8,128)(2,1)S(1)} %gate_up_and_gradients.1.pay_ref.refs_2_.refs_5_.refs_0_.refs_3_, bf16[64,3712]{1,0:T(8,128)(2,1)S(1)} %collective-permute-done.19.refs_3_.refs_1_, bf16[64,6400]{1,0:T(8,128)(2,1)S(1)} %collective-permute-done.27.refs_4_.refs_2_, ...), custom_call_target="tpu_custom_call" | custom-call | flops 1500000000 | bytes 6000000 | tf_op jit(solution)/shard_map/grad_w_down/pallas_call | solution.py:407
  107.8 3.7 %attention_gradients.1 = (bf16[128,512]{1,0:T(8,128)(2,1)}, bf16[160,256]{1,0:T(8,128)(2,1)S(1)}, bf16[160,256]{1,0:T(8,128)(2,1)S(1)}, bf16[160,256]{1,0:T(8,128)(2,1)S(1)}, bf16[160,256]{1,0:T(8,128)(2,1)S(1)}) custom-call(s32[1]{0:T(128)} %bitcast.1.f_ref, bf16[272,128]{1,0:T(8,128)(2,1)S(1)} %copy-done.4, bf16[272,128]{1,0:T(8,128)(2,1)S(1)} %copy-done.10, ...), custom_call_target="tpu_custom_call" | custom-call | flops 2000000000 | bytes 8000000 | tf_op jit(solution)/shard_map/attention_gradients/pallas_call | solution.py:234
  111.5 1.4 %collective-permute-done.29 = bf16[32,4096]{1,0:T(8,128)(2,1)S(1)} collective-permute-done((bf16[32,4096]{1,0:T(8,128)(2,1)S(1)}, bf16[32,4096]{1,0:T(8,128)(2,1)S(1)}, u32[]{:S(2)}, u32[]{:S(2)}) %collective-permute-start.29) | collective-permute-done | bytes 262176 | tf_op jit(solution)/shard_map/ppermute | solution.py:521
  113.8 1.3 collective-permute-start.33
  115.0 1.4 %collective-permute-start.34 = (bf16[160,256]{1,0:T(8,128)(2,1)S(1)}, bf16[160,256]{1,0:T(8,128)(2,1)S(1)}, u32[]{:S(2)}, u32[]{:S(2)}) collective-permute-start(bf16[160,256]{1,0:T(8,128)(2,1)S(1)} %get-tuple-element.106), channel_id=1, source_target_pairs={{0,24},{8,16},{16,8},{24,0},{1,25},{9,17},{17,9},{25,1},{2,26},{10... | collective-permute-start | bytes 245768 | tf_op jit(solution)/shard_map/ppermute | solution.py:521
  116.5 1.4 %collective-permute-start.31 = (bf16[16,4096]{1,0:T(8,128)(2,1)S(1)}, bf16[16,4096]{1,0:T(8,128)(2,1)S(1)}, u32[]{:S(2)}, u32[]{:S(2)}) collective-permute-start(bf16[16,4096]{1,0:T(8,128)(2,1)S(1)} %fusion.1), channel_id=1, source_target_pairs={{0,4},{1,5},{2,6},{3,7},{4,0},{5,1},{6,2},{7,3},{8,12},{9,13},{10,... | collective-permute-start | bytes 393224 | tf_op jit(solution)/shard_map/ppermute | solution.py:521
  117.9 2.3 %grad_w_up.1 = f32[1024,896]{1,0:T(8,128)} custom-call(bf16[256,1024]{1,0:T(8,128)(2,1)S(1)} %maximum_maximum_fusion.refs_0_, bf16[256,1024]{1,0:T(8,128)(2,1)S(1)} %collective-permute-done.35.refs_1_, bf16[128,2688]{1,0:T(8,128)(2,1)S(1)} %gate_up_and_gradients.1.pay_ref.refs_2_.refs_5_.refs_0_.refs_3_, ...), custom_call_target="tpu_custom_call" | custom-call | flops 1500000000 | bytes 6000000 | tf_op jit(solution)/shard_map/grad_w_up/pallas_call | solution.py:407
  120.5 1.3 collective-permute-start.41
  122.6 1.5 %collective-permute-start.43 = (bf16[64,1024]{1,0:T(8,128)(2,1)S(1)}, bf16[64,1024]{1,0:T(8,128)(2,1)S(1)}, u32[]{:S(2)}, u32[]{:S(2)}) collective-permute-start(bf16[64,1024]{1,0:T(8,128)(2,1)S(1)} %get-tuple-element.129), channel_id=1, source_target_pairs={{0,24},{8,16},{16,8},{24,0},{1,25},{9,17},{17,9},{25,1},{2,26},{10... | collective-permute-start | bytes 393224 | tf_op jit(solution)/shard_map/ppermute | solution.py:521
  124.1 2.3 %grad_w_gate.1 = f32[1024,896]{1,0:T(8,128)} custom-call(bf16[256,1024]{1,0:T(8,128)(2,1)S(1)} %maximum_maximum_fusion.refs_0_, bf16[256,1024]{1,0:T(8,128)(2,1)S(1)} %collective-permute-done.35.refs_1_, bf16[128,2688]{1,0:T(8,128)(2,1)S(1)} %gate_up_and_gradients.1.pay_ref.refs_2_.refs_5_.refs_0_.refs_3_, ...), custom_call_target="tpu_custom_call" | custom-call | flops 1500000000 | bytes 6000000 | tf_op jit(solution)/shard_map/grad_w_gate/pallas_call | solution.py:407
  126.5 2.6 %collective-permute-start.39 = (bf16[2,48,256]{2,1,0:T(8,128)(2,1)S(1)}, bf16[2,48,256]{2,1,0:T(8,128)(2,1)S(1)}, u32[]{:S(2)}, u32[]{:S(2)}) collective-permute-start(bf16[2,48,256]{2,1,0:T(8,128)(2,1)S(1)} %get-tuple-element.158), channel_id=1, source_target_pairs={{0,6},{1,7},{2,4},{3,5},{4,2},{5,3},{6,0},{7,1},{8,14},{9,15},{10,... | collective-permute-start | bytes 147464 | tf_op jit(solution)/shard_map/ppermute | solution.py:521
  129.1 1.1 collective-permute-done.42
  130.3 1.4 %collective-permute-start.38 = (bf16[2,48,256]{2,1,0:T(8,128)(2,1)S(1)}, bf16[2,48,256]{2,1,0:T(8,128)(2,1)S(1)}, u32[]{:S(2)}, u32[]{:S(2)}) collective-permute-start(bf16[2,48,256]{2,1,0:T(8,128)(2,1)S(1)} %get-tuple-element.161), channel_id=1, source_target_pairs={{0,4},{1,5},{2,6},{3,7},{4,0},{5,1},{6,2},{7,3},{8,12},{9,13},{10,... | collective-permute-start | bytes 147464 | tf_op jit(solution)/shard_map/ppermute | solution.py:521
  133.5 2.3 %collective-permute-done.38.refs_2_ = bf16[2,48,256]{2,1,0:T(8,128)(2,1)S(1)} collective-permute-done((bf16[2,48,256]{2,1,0:T(8,128)(2,1)S(1)}, bf16[2,48,256]{2,1,0:T(8,128)(2,1)S(1)}, u32[]{:S(2)}, u32[]{:S(2)}) %collective-permute-start.38) | collective-permute-done | bytes 49184 | tf_op jit(solution)/shard_map/ppermute | solution.py:521
  136.5 1.8 %grad_w_out.1 = f32[512,1024]{1,0:T(8,128)} custom-call(bf16[64,1024]{1,0:T(8,128)(2,1)S(1)} %pad_maximum_fusion.8.refs_0_, bf16[64,1024]{1,0:T(8,128)(2,1)S(1)} %get-tuple-element.153.refs_1_, bf16[64,1024]{1,0:T(8,128)(2,1)S(1)} %get-tuple-element.155.refs_2_, bf16[64,1024]{1,0:T(8,128)(2,1)S(1)} %get-tuple-element.157.refs_3_, ...), custom_call_target="tpu_custom_call" | custom-call | flops 1500000000 | bytes 6000000 | tf_op jit(solution)/shard_map/grad_w_out/pallas_call | solution.py:407
  (152 shorter events, 16.6 us)
Async XLA Ops:
  0.7 20.5 %collective-permute-start.6 = (bf16[16,4096]{1,0:T(8,128)(2,1)}, bf16[16,4096]{1,0:T(8,128)(2,1)S(1)}, u32[]{:S(2)}, u32[]{:S(2)}) collective-permute-start(bf16[16,4096]{1,0:T(8,128)(2,1)} %cot_ref.1), channel_id=1, source_target_pairs={{0,6},{1,7},{2,4},{3,5},{4,2},{5,3},{6,0},{7,1},{8,14},{9,15},{10,... | collective-permute-start | bytes 393224 | tf_op jit(solution)/shard_map/ppermute | solution.py:521
  5.8 15.3 %collective-permute-start.5 = (bf16[16,4096]{1,0:T(8,128)(2,1)}, bf16[16,4096]{1,0:T(8,128)(2,1)S(1)}, u32[]{:S(2)}, u32[]{:S(2)}) collective-permute-start(bf16[16,4096]{1,0:T(8,128)(2,1)} %cot_ref.1), channel_id=1, source_target_pairs={{0,4},{1,5},{2,6},{3,7},{4,0},{5,1},{6,2},{7,3},{8,12},{9,13},{10,... | collective-permute-start | bytes 393224 | tf_op jit(solution)/shard_map/ppermute | solution.py:521
  7.6 5.6 %collective-permute-start.2 = (bf16[272,128]{1,0:T(8,128)(2,1)}, bf16[272,128]{1,0:T(8,128)(2,1)S(1)}, u32[]{:S(2)}, u32[]{:S(2)}) collective-permute-start(bf16[272,128]{1,0:T(8,128)(2,1)} %get-tuple-element.72.refs_1_.refs_0_), channel_id=1, source_target_pairs={{0,24},{8,16},{16,8},{24,0},{1,25},{9,17},{17,9},{25,1},{2,26},{10... | collective-permute-start | bytes 208904 | tf_op jit(solution)/shard_map/ppermute | solution.py:521
  10.1 4.5 %collective-permute-start.1 = (bf16[272,128]{1,0:T(8,128)(2,1)}, bf16[272,128]{1,0:T(8,128)(2,1)S(1)}, u32[]{:S(2)}, u32[]{:S(2)}) collective-permute-start(bf16[272,128]{1,0:T(8,128)(2,1)} %get-tuple-element.72.refs_1_.refs_0_), channel_id=1, source_target_pairs={{0,16},{8,24},{16,0},{24,8},{1,17},{9,25},{17,1},{25,9},{2,18},{10... | collective-permute-start | bytes 208904 | tf_op jit(solution)/shard_map/ppermute | solution.py:521
  10.6 4.5 %collective-permute-start = (bf16[272,128]{1,0:T(8,128)(2,1)}, bf16[272,128]{1,0:T(8,128)(2,1)S(1)}, u32[]{:S(2)}, u32[]{:S(2)}) collective-permute-start(bf16[272,128]{1,0:T(8,128)(2,1)} %get-tuple-element.72.refs_1_.refs_0_), channel_id=1, source_target_pairs={{0,8},{8,0},{16,24},{24,16},{1,9},{9,1},{17,25},{25,17},{2,10},{10... | collective-permute-start | bytes 208904 | tf_op jit(solution)/shard_map/ppermute | solution.py:521
  13.2 7.9 %collective-permute-start.4 = (bf16[16,4096]{1,0:T(8,128)(2,1)S(1)}, bf16[16,4096]{1,0:T(8,128)(2,1)S(1)}, u32[]{:S(2)}, u32[]{:S(2)}) collective-permute-start(bf16[16,4096]{1,0:T(8,128)(2,1)S(1)} %copy-done), channel_id=1, source_target_pairs={{0,2},{1,3},{2,0},{3,1},{4,6},{5,7},{6,4},{7,5},{8,10},{9,11},{10,... | collective-permute-start | bytes 393224 | tf_op jit(solution)/shard_map/ppermute | solution.py:521
  15.8 29.1 %slice-start.4 = ((s8[7340032]{0:T(1024)(128)(4,1)}), s8[3145728]{0:T(1024)(128)(4,1)S(1)}, s32[]{:S(2)}) async-start(s8[7340032]{0:T(1024)(128)(4,1)} %bitcast.27), calls=%async_computation.4 | async-start | bytes 6291456
  20.1 2.2 %collective-permute-start.3 = (bf16[64,4096]{1,0:T(8,128)(2,1)}, bf16[64,4096]{1,0:T(8,128)(2,1)S(1)}, u32[]{:S(2)}, u32[]{:S(2)}) collective-permute-start(bf16[64,4096]{1,0:T(8,128)(2,1)} %get-tuple-element.74), channel_id=1, source_target_pairs={{0,1},{1,0},{2,3},{3,2},{4,5},{5,4},{6,7},{7,6},{8,9},{9,8},{10,11... | collective-permute-start | bytes 1572872 | tf_op jit(solution)/shard_map/ppermute | solution.py:521
  23.4 4.7 %collective-permute-start.7 = (bf16[64,4096]{1,0:T(8,128)(2,1)S(1)}, bf16[64,4096]{1,0:T(8,128)(2,1)S(1)}, u32[]{:S(2)}, u32[]{:S(2)}) collective-permute-start(bf16[64,4096]{1,0:T(8,128)(2,1)S(1)} %get-tuple-element.78.a_ref), channel_id=1, source_target_pairs={{0,1},{1,0},{2,3},{3,2},{4,5},{5,4},{6,7},{7,6},{8,9},{9,8},{10,11... | collective-permute-start | bytes 1572872 | tf_op jit(solution)/shard_map/ppermute | solution.py:521
  23.7 16.5 %collective-permute-start.12 = (bf16[16,4096]{1,0:T(8,128)(2,1)S(1)}, bf16[16,4096]{1,0:T(8,128)(2,1)S(1)}, u32[]{:S(2)}, u32[]{:S(2)}) collective-permute-start(bf16[16,4096]{1,0:T(8,128)(2,1)S(1)} %get-tuple-element.144), channel_id=1, source_target_pairs={{0,6},{1,7},{2,4},{3,5},{4,2},{5,3},{6,0},{7,1},{8,14},{9,15},{10,... | collective-permute-start | bytes 393224 | tf_op jit(solution)/shard_map/ppermute | solution.py:521
  26.2 14.0 %collective-permute-start.11 = (bf16[16,4096]{1,0:T(8,128)(2,1)S(1)}, bf16[16,4096]{1,0:T(8,128)(2,1)S(1)}, u32[]{:S(2)}, u32[]{:S(2)}) collective-permute-start(bf16[16,4096]{1,0:T(8,128)(2,1)S(1)} %get-tuple-element.145), channel_id=1, source_target_pairs={{0,4},{1,5},{2,6},{3,7},{4,0},{5,1},{6,2},{7,3},{8,12},{9,13},{10,... | collective-permute-start | bytes 393224 | tf_op jit(solution)/shard_map/ppermute | solution.py:521
  26.8 13.4 %collective-permute-start.10 = (bf16[16,4096]{1,0:T(8,128)(2,1)S(1)}, bf16[16,4096]{1,0:T(8,128)(2,1)S(1)}, u32[]{:S(2)}, u32[]{:S(2)}) collective-permute-start(bf16[16,4096]{1,0:T(8,128)(2,1)S(1)} %get-tuple-element.146), channel_id=1, source_target_pairs={{0,2},{1,3},{2,0},{3,1},{4,6},{5,7},{6,4},{7,5},{8,10},{9,11},{10,... | collective-permute-start | bytes 393224 | tf_op jit(solution)/shard_map/ppermute | solution.py:521
  28.2 7.8 %collective-permute-start.9 = (bf16[128,1024]{1,0:T(8,128)(2,1)S(1)}, bf16[128,1024]{1,0:T(8,128)(2,1)S(1)}, u32[]{:S(2)}, u32[]{:S(2)}) collective-permute-start(bf16[128,1024]{1,0:T(8,128)(2,1)S(1)} %maximum_maximum_fusion.2), channel_id=1, source_target_pairs={{0,16},{8,24},{16,0},{24,8},{1,17},{9,25},{17,1},{25,9},{2,18},{10... | collective-permute-start | bytes 786440 | tf_op jit(solution)/shard_map/ppermute | solution.py:521
  29.8 10.3 %collective-permute-start.8 = (bf16[192,1024]{1,0:T(8,128)(2,1)S(1)}, bf16[192,1024]{1,0:T(8,128)(2,1)S(1)}, u32[]{:S(2)}, u32[]{:S(2)}) collective-permute-start(bf16[192,1024]{1,0:T(8,128)(2,1)S(1)} %maximum_maximum_fusion.1), channel_id=1, source_target_pairs={{0,8},{8,0},{16,24},{24,16},{1,9},{9,1},{17,25},{25,17},{2,10},{10... | collective-permute-start | bytes 1179656 | tf_op jit(solution)/shard_map/ppermute | solution.py:521
  40.2 15.3 %slice-start = ((s8[7340032]{0:T(1024)(128)(4,1)}), s8[4194304]{0:T(1024)(128)(4,1)S(1)}, s32[]{:S(2)}) async-start(s8[7340032]{0:T(1024)(128)(4,1)} %bitcast.20), calls=%async_computation | async-start | bytes 8388608
  40.5 8.3 %collective-permute-start.15 = (bf16[16,4096]{1,0:T(8,128)(2,1)S(1)}, bf16[16,4096]{1,0:T(8,128)(2,1)S(1)}, u32[]{:S(2)}, u32[]{:S(2)}) collective-permute-start(bf16[16,4096]{1,0:T(8,128)(2,1)S(1)} %get-tuple-element.85), channel_id=1, source_target_pairs={{0,6},{1,7},{2,4},{3,5},{4,2},{5,3},{6,0},{7,1},{8,14},{9,15},{10,... | collective-permute-start | bytes 393224 | tf_op jit(solution)/shard_map/ppermute | solution.py:521
  43.5 10.0 %collective-permute-start.14 = (bf16[16,4096]{1,0:T(8,128)(2,1)S(1)}, bf16[16,4096]{1,0:T(8,128)(2,1)S(1)}, u32[]{:S(2)}, u32[]{:S(2)}) collective-permute-start(bf16[16,4096]{1,0:T(8,128)(2,1)S(1)} %get-tuple-element.85), channel_id=1, source_target_pairs={{0,4},{1,5},{2,6},{3,7},{4,0},{5,1},{6,2},{7,3},{8,12},{9,13},{10,... | collective-permute-start | bytes 393224 | tf_op jit(solution)/shard_map/ppermute | solution.py:521
  43.5 10.0 %collective-permute-start.13 = (bf16[16,4096]{1,0:T(8,128)(2,1)S(1)}, bf16[16,4096]{1,0:T(8,128)(2,1)S(1)}, u32[]{:S(2)}, u32[]{:S(2)}) collective-permute-start(bf16[16,4096]{1,0:T(8,128)(2,1)S(1)} %get-tuple-element.85), channel_id=1, source_target_pairs={{0,2},{1,3},{2,0},{3,1},{4,6},{5,7},{6,4},{7,5},{8,10},{9,11},{10,... | collective-permute-start | bytes 393224 | tf_op jit(solution)/shard_map/ppermute | solution.py:521
  53.5 2.0 %collective-permute-start.16 = (bf16[64,4096]{1,0:T(8,128)(2,1)S(1)}, bf16[64,4096]{1,0:T(8,128)(2,1)S(1)}, u32[]{:S(2)}, u32[]{:S(2)}) collective-permute-start(bf16[64,4096]{1,0:T(8,128)(2,1)S(1)} %pad_maximum_fusion.2.xa_ref.a_ref), channel_id=1, source_target_pairs={{0,1},{1,0},{2,3},{3,2},{4,5},{5,4},{6,7},{7,6},{8,9},{9,8},{10,11... | collective-permute-start | bytes 1572872 | tf_op jit(solution)/shard_map/ppermute | solution.py:521
  53.7 8.9 %collective-permute-start.40 = (bf16[128,1024]{1,0:T(8,128)(2,1)S(1)}, bf16[128,1024]{1,0:T(8,128)(2,1)S(1)}, u32[]{:S(2)}, u32[]{:S(2)}) collective-permute-start(bf16[128,1024]{1,0:T(8,128)(2,1)S(1)} %concatenate.78), channel_id=1, source_target_pairs={{0,16},{8,24},{16,0},{24,8},{1,17},{9,25},{17,1},{25,9},{2,18},{10... | collective-permute-start | bytes 786440 | tf_op jit(solution)/shard_map/ppermute | solution.py:521
  62.3 2.0 %collective-permute-start.17 = (bf16[64,4096]{1,0:T(8,128)(2,1)S(1)}, bf16[64,4096]{1,0:T(8,128)(2,1)S(1)}, u32[]{:S(2)}, u32[]{:S(2)}) collective-permute-start(bf16[64,4096]{1,0:T(8,128)(2,1)S(1)} %get-tuple-element.88), channel_id=1, source_target_pairs={{0,1},{1,0},{2,3},{3,2},{4,5},{5,4},{6,7},{7,6},{8,9},{9,8},{10,11... | collective-permute-start | bytes 1572872 | tf_op jit(solution)/shard_map/ppermute | solution.py:521
  64.6 18.8 %collective-permute-start.23 = (bf16[16,4096]{1,0:T(8,128)(2,1)S(1)}, bf16[16,4096]{1,0:T(8,128)(2,1)S(1)}, u32[]{:S(2)}, u32[]{:S(2)}) collective-permute-start(bf16[16,4096]{1,0:T(8,128)(2,1)S(1)} %get-tuple-element.140), channel_id=1, source_target_pairs={{0,6},{1,7},{2,4},{3,5},{4,2},{5,3},{6,0},{7,1},{8,14},{9,15},{10,... | collective-permute-start | bytes 393224 | tf_op jit(solution)/shard_map/ppermute | solution.py:521
  67.2 17.6 %collective-permute-start.22 = (bf16[16,4096]{1,0:T(8,128)(2,1)S(1)}, bf16[16,4096]{1,0:T(8,128)(2,1)S(1)}, u32[]{:S(2)}, u32[]{:S(2)}) collective-permute-start(bf16[16,4096]{1,0:T(8,128)(2,1)S(1)} %get-tuple-element.141), channel_id=1, source_target_pairs={{0,4},{1,5},{2,6},{3,7},{4,0},{5,1},{6,2},{7,3},{8,12},{9,13},{10,... | collective-permute-start | bytes 393224 | tf_op jit(solution)/shard_map/ppermute | solution.py:521
  67.2 17.6 %collective-permute-start.21 = (bf16[16,4096]{1,0:T(8,128)(2,1)S(1)}, bf16[16,4096]{1,0:T(8,128)(2,1)S(1)}, u32[]{:S(2)}, u32[]{:S(2)}) collective-permute-start(bf16[16,4096]{1,0:T(8,128)(2,1)S(1)} %get-tuple-element.142), channel_id=1, source_target_pairs={{0,2},{1,3},{2,0},{3,1},{4,6},{5,7},{6,4},{7,5},{8,10},{9,11},{10,... | collective-permute-start | bytes 393224 | tf_op jit(solution)/shard_map/ppermute | solution.py:521
  69.1 12.9 %collective-permute-start.19 = (bf16[64,3712]{1,0:T(8,128)(2,1)S(1)}, bf16[64,3712]{1,0:T(8,128)(2,1)S(1)}, u32[]{:S(2)}, u32[]{:S(2)}) collective-permute-start(bf16[64,3712]{1,0:T(8,128)(2,1)S(1)} %pad_maximum_fusion.5), channel_id=1, source_target_pairs={{0,8},{8,0},{16,24},{24,16},{1,9},{9,1},{17,25},{25,17},{2,10},{10... | collective-permute-start | bytes 1425416 | tf_op jit(solution)/shard_map/ppermute | solution.py:521
  70.0 11.9 %collective-permute-start.20 = (bf16[64,3712]{1,0:T(8,128)(2,1)S(1)}, bf16[64,3712]{1,0:T(8,128)(2,1)S(1)}, u32[]{:S(2)}, u32[]{:S(2)}) collective-permute-start(bf16[64,3712]{1,0:T(8,128)(2,1)S(1)} %pad_maximum_fusion.6), channel_id=1, source_target_pairs={{0,16},{8,24},{16,0},{24,8},{1,17},{9,25},{17,1},{25,9},{2,18},{10... | collective-permute-start | bytes 1425416 | tf_op jit(solution)/shard_map/ppermute | solution.py:521
  81.9 6.4 %collective-permute-start.18 = (bf16[64,4096]{1,0:T(8,128)(2,1)S(1)}, bf16[64,4096]{1,0:T(8,128)(2,1)S(1)}, u32[]{:S(2)}, u32[]{:S(2)}) collective-permute-start(bf16[64,4096]{1,0:T(8,128)(2,1)S(1)} %slice.196), channel_id=1, source_target_pairs={{0,1},{1,0},{2,3},{3,2},{4,5},{5,4},{6,7},{7,6},{8,9},{9,8},{10,11... | collective-permute-start | bytes 1572872 | tf_op jit(solution)/shard_map/ppermute | solution.py:521
  82.0 20.7 %collective-permute-start.28 = (bf16[64,6400]{1,0:T(8,128)(2,1)S(1)}, bf16[64,6400]{1,0:T(8,128)(2,1)S(1)}, u32[]{:S(2)}, u32[]{:S(2)}) collective-permute-start(bf16[64,6400]{1,0:T(8,128)(2,1)S(1)} %pad_maximum_fusion.1), channel_id=1, source_target_pairs={{0,8},{8,0},{16,24},{24,16},{1,9},{9,1},{17,25},{25,17},{2,10},{10... | collective-permute-start | bytes 2457608 | tf_op jit(solution)/shard_map/ppermute | solution.py:521
  83.4 20.4 %collective-permute-start.27 = (bf16[64,6400]{1,0:T(8,128)(2,1)S(1)}, bf16[64,6400]{1,0:T(8,128)(2,1)S(1)}, u32[]{:S(2)}, u32[]{:S(2)}) collective-permute-start(bf16[64,6400]{1,0:T(8,128)(2,1)S(1)} %pad_maximum_fusion), channel_id=1, source_target_pairs={{0,16},{8,24},{16,0},{24,8},{1,17},{9,25},{17,1},{25,9},{2,18},{10... | collective-permute-start | bytes 2457608 | tf_op jit(solution)/shard_map/ppermute | solution.py:521
  85.7 8.2 %collective-permute-start.26 = (bf16[16,4096]{1,0:T(8,128)(2,1)S(1)}, bf16[16,4096]{1,0:T(8,128)(2,1)S(1)}, u32[]{:S(2)}, u32[]{:S(2)}) collective-permute-start(bf16[16,4096]{1,0:T(8,128)(2,1)S(1)} %get-tuple-element.95), channel_id=1, source_target_pairs={{0,6},{1,7},{2,4},{3,5},{4,2},{5,3},{6,0},{7,1},{8,14},{9,15},{10,... | collective-permute-start | bytes 393224 | tf_op jit(solution)/shard_map/ppermute | solution.py:521
  88.3 11.1 %collective-permute-start.25 = (bf16[16,4096]{1,0:T(8,128)(2,1)S(1)}, bf16[16,4096]{1,0:T(8,128)(2,1)S(1)}, u32[]{:S(2)}, u32[]{:S(2)}) collective-permute-start(bf16[16,4096]{1,0:T(8,128)(2,1)S(1)} %get-tuple-element.95), channel_id=1, source_target_pairs={{0,4},{1,5},{2,6},{3,7},{4,0},{5,1},{6,2},{7,3},{8,12},{9,13},{10,... | collective-permute-start | bytes 393224 | tf_op jit(solution)/shard_map/ppermute | solution.py:521
  88.3 11.1 %collective-permute-start.24 = (bf16[16,4096]{1,0:T(8,128)(2,1)S(1)}, bf16[16,4096]{1,0:T(8,128)(2,1)S(1)}, u32[]{:S(2)}, u32[]{:S(2)}) collective-permute-start(bf16[16,4096]{1,0:T(8,128)(2,1)S(1)} %get-tuple-element.95), channel_id=1, source_target_pairs={{0,2},{1,3},{2,0},{3,1},{4,6},{5,7},{6,4},{7,5},{8,10},{9,11},{10,... | collective-permute-start | bytes 393224 | tf_op jit(solution)/shard_map/ppermute | solution.py:521
  93.9 11.3 %collective-permute-start.45 = (bf16[256,1024]{1,0:T(8,128)(2,1)S(1)}, bf16[256,1024]{1,0:T(8,128)(2,1)S(1)}, u32[]{:S(2)}, u32[]{:S(2)}) collective-permute-start(bf16[256,1024]{1,0:T(8,128)(2,1)S(1)} %pad_maximum_fusion.4.refs_6_), channel_id=1, source_target_pairs={{0,1},{1,0},{2,3},{3,2},{4,5},{5,4},{6,7},{7,6},{8,9},{9,8},{10,11... | collective-permute-start | bytes 1572872 | tf_op jit(solution)/shard_map/ppermute | solution.py:521
  103.8 3.9 %collective-permute-start.30 = (bf16[64,4096]{1,0:T(8,128)(2,1)S(1)}, bf16[64,4096]{1,0:T(8,128)(2,1)S(1)}, u32[]{:S(2)}, u32[]{:S(2)}) collective-permute-start(bf16[64,4096]{1,0:T(8,128)(2,1)S(1)} %pad_maximum_fusion.3.refs_8_.a_ref), channel_id=1, source_target_pairs={{0,1},{1,0},{2,3},{3,2},{4,5},{5,4},{6,7},{7,6},{8,9},{9,8},{10,11... | collective-permute-start | bytes 1572872 | tf_op jit(solution)/shard_map/ppermute | solution.py:521
  103.9 7.6 %collective-permute-start.35 = (bf16[256,1024]{1,0:T(8,128)(2,1)S(1)}, bf16[256,1024]{1,0:T(8,128)(2,1)S(1)}, u32[]{:S(2)}, u32[]{:S(2)}) collective-permute-start(bf16[256,1024]{1,0:T(8,128)(2,1)S(1)} %maximum_maximum_fusion.refs_0_), channel_id=1, source_target_pairs={{0,1},{1,0},{2,3},{3,2},{4,5},{5,4},{6,7},{7,6},{8,9},{9,8},{10,11... | collective-permute-start | bytes 1572872 | tf_op jit(solution)/shard_map/ppermute | solution.py:521
  104.7 8.3 %collective-permute-start.29 = (bf16[32,4096]{1,0:T(8,128)(2,1)S(1)}, bf16[32,4096]{1,0:T(8,128)(2,1)S(1)}, u32[]{:S(2)}, u32[]{:S(2)}) collective-permute-start(bf16[32,4096]{1,0:T(8,128)(2,1)S(1)} %pad_maximum_fusion.7), channel_id=1, source_target_pairs={{0,2},{1,3},{2,0},{3,1},{4,6},{5,7},{6,4},{7,5},{8,10},{9,11},{10,... | collective-permute-start | bytes 786440 | tf_op jit(solution)/shard_map/ppermute | solution.py:521
  113.0 7.3 %collective-permute-start.32 = (bf16[160,256]{1,0:T(8,128)(2,1)S(1)}, bf16[160,256]{1,0:T(8,128)(2,1)S(1)}, u32[]{:S(2)}, u32[]{:S(2)}) collective-permute-start(bf16[160,256]{1,0:T(8,128)(2,1)S(1)} %get-tuple-element.104), channel_id=1, source_target_pairs={{0,8},{8,0},{16,24},{24,16},{1,9},{9,1},{17,25},{25,17},{2,10},{10... | collective-permute-start | bytes 245768 | tf_op jit(solution)/shard_map/ppermute | solution.py:521
  113.8 6.5 %collective-permute-start.33 = (bf16[160,256]{1,0:T(8,128)(2,1)S(1)}, bf16[160,256]{1,0:T(8,128)(2,1)S(1)}, u32[]{:S(2)}, u32[]{:S(2)}) collective-permute-start(bf16[160,256]{1,0:T(8,128)(2,1)S(1)} %get-tuple-element.105), channel_id=1, source_target_pairs={{0,16},{8,24},{16,0},{24,8},{1,17},{9,25},{17,1},{25,9},{2,18},{10... | collective-permute-start | bytes 245768 | tf_op jit(solution)/shard_map/ppermute | solution.py:521
  115.0 5.3 %collective-permute-start.34 = (bf16[160,256]{1,0:T(8,128)(2,1)S(1)}, bf16[160,256]{1,0:T(8,128)(2,1)S(1)}, u32[]{:S(2)}, u32[]{:S(2)}) collective-permute-start(bf16[160,256]{1,0:T(8,128)(2,1)S(1)} %get-tuple-element.106), channel_id=1, source_target_pairs={{0,24},{8,16},{16,8},{24,0},{1,25},{9,17},{17,9},{25,1},{2,26},{10... | collective-permute-start | bytes 245768 | tf_op jit(solution)/shard_map/ppermute | solution.py:521
  116.5 15.3 %collective-permute-start.31 = (bf16[16,4096]{1,0:T(8,128)(2,1)S(1)}, bf16[16,4096]{1,0:T(8,128)(2,1)S(1)}, u32[]{:S(2)}, u32[]{:S(2)}) collective-permute-start(bf16[16,4096]{1,0:T(8,128)(2,1)S(1)} %fusion.1), channel_id=1, source_target_pairs={{0,4},{1,5},{2,6},{3,7},{4,0},{5,1},{6,2},{7,3},{8,12},{9,13},{10,... | collective-permute-start | bytes 393224 | tf_op jit(solution)/shard_map/ppermute | solution.py:521
  120.5 6.0 %collective-permute-start.36 = (bf16[4,48,256]{2,1,0:T(8,128)(2,1)S(1)}, bf16[4,48,256]{2,1,0:T(8,128)(2,1)S(1)}, u32[]{:S(2)}, u32[]{:S(2)}) collective-permute-start(bf16[4,48,256]{2,1,0:T(8,128)(2,1)S(1)} %get-tuple-element.115), channel_id=1, source_target_pairs={{0,1},{1,0},{2,3},{3,2},{4,5},{5,4},{6,7},{7,6},{8,9},{9,8},{10,11... | collective-permute-start | bytes 294920 | tf_op jit(solution)/shard_map/ppermute | solution.py:521
  120.5 8.6 %collective-permute-start.41 = (bf16[64,1024]{1,0:T(8,128)(2,1)S(1)}, bf16[64,1024]{1,0:T(8,128)(2,1)S(1)}, u32[]{:S(2)}, u32[]{:S(2)}) collective-permute-start(bf16[64,1024]{1,0:T(8,128)(2,1)S(1)} %get-tuple-element.127), channel_id=1, source_target_pairs={{0,8},{8,0},{16,24},{24,16},{1,9},{9,1},{17,25},{25,17},{2,10},{10... | collective-permute-start | bytes 393224 | tf_op jit(solution)/shard_map/ppermute | solution.py:521
  121.9 8.4 %collective-permute-start.42 = (bf16[64,1024]{1,0:T(8,128)(2,1)S(1)}, bf16[64,1024]{1,0:T(8,128)(2,1)S(1)}, u32[]{:S(2)}, u32[]{:S(2)}) collective-permute-start(bf16[64,1024]{1,0:T(8,128)(2,1)S(1)} %get-tuple-element.128), channel_id=1, source_target_pairs={{0,16},{8,24},{16,0},{24,8},{1,17},{9,25},{17,1},{25,9},{2,18},{10... | collective-permute-start | bytes 393224 | tf_op jit(solution)/shard_map/ppermute | solution.py:521
  122.6 9.0 %collective-permute-start.43 = (bf16[64,1024]{1,0:T(8,128)(2,1)S(1)}, bf16[64,1024]{1,0:T(8,128)(2,1)S(1)}, u32[]{:S(2)}, u32[]{:S(2)}) collective-permute-start(bf16[64,1024]{1,0:T(8,128)(2,1)S(1)} %get-tuple-element.129), channel_id=1, source_target_pairs={{0,24},{8,16},{16,8},{24,0},{1,25},{9,17},{17,9},{25,1},{2,26},{10... | collective-permute-start | bytes 393224 | tf_op jit(solution)/shard_map/ppermute | solution.py:521
  126.5 6.0 %collective-permute-start.39 = (bf16[2,48,256]{2,1,0:T(8,128)(2,1)S(1)}, bf16[2,48,256]{2,1,0:T(8,128)(2,1)S(1)}, u32[]{:S(2)}, u32[]{:S(2)}) collective-permute-start(bf16[2,48,256]{2,1,0:T(8,128)(2,1)S(1)} %get-tuple-element.158), channel_id=1, source_target_pairs={{0,6},{1,7},{2,4},{3,5},{4,2},{5,3},{6,0},{7,1},{8,14},{9,15},{10,... | collective-permute-start | bytes 147464 | tf_op jit(solution)/shard_map/ppermute | solution.py:521
  129.1 4.4 %collective-permute-start.37 = (bf16[2,48,256]{2,1,0:T(8,128)(2,1)S(1)}, bf16[2,48,256]{2,1,0:T(8,128)(2,1)S(1)}, u32[]{:S(2)}, u32[]{:S(2)}) collective-permute-start(bf16[2,48,256]{2,1,0:T(8,128)(2,1)S(1)} %get-tuple-element.160), channel_id=1, source_target_pairs={{0,2},{1,3},{2,0},{3,1},{4,6},{5,7},{6,4},{7,5},{8,10},{9,11},{10,... | collective-permute-start | bytes 147464 | tf_op jit(solution)/shard_map/ppermute | solution.py:521
  130.3 5.5 %collective-permute-start.38 = (bf16[2,48,256]{2,1,0:T(8,128)(2,1)S(1)}, bf16[2,48,256]{2,1,0:T(8,128)(2,1)S(1)}, u32[]{:S(2)}, u32[]{:S(2)}) collective-permute-start(bf16[2,48,256]{2,1,0:T(8,128)(2,1)S(1)} %get-tuple-element.161), channel_id=1, source_target_pairs={{0,4},{1,5},{2,6},{3,7},{4,0},{5,1},{6,2},{7,3},{8,12},{9,13},{10,... | collective-permute-start | bytes 147464 | tf_op jit(solution)/shard_map/ppermute | solution.py:521
  131.7 4.8 %collective-permute-start.44 = (bf16[256,1024]{1,0:T(8,128)(2,1)S(1)}, bf16[256,1024]{1,0:T(8,128)(2,1)S(1)}, u32[]{:S(2)}, u32[]{:S(2)}) collective-permute-start(bf16[256,1024]{1,0:T(8,128)(2,1)S(1)} %constant_dynamic-update-slice_fusion.9.refs_4_), channel_id=1, source_target_pairs={{0,1},{1,0},{2,3},{3,2},{4,5},{5,4},{6,7},{7,6},{8,9},{9,8},{10,11... | collective-permute-start | bytes 1572872 | tf_op jit(solution)/shard_map/ppermute | solution.py:521
  (18 other events, 123.5 us)

commit v6 on v5

--- a/solution.py
+++ b/solution.py
@@ -242,6 +242,22 @@
     )(f, *pieces, queries, att, lse, gain, grad_a, grad_b, w_out)
 
 
+def pair_sum_kernel(keep_ref, recv_ref, out_ref):
+    out_ref[...] = (keep_ref[...].astype(F32) + recv_ref[...].astype(F32)).astype(BF16)
+
+
+def pair_sum_call(keep, received):
+    return pl.pallas_call(
+        pair_sum_kernel,
+        out_shape=jax.ShapeDtypeStruct(keep.shape, BF16),
+        in_specs=[VMEM] * 2,
+        out_specs=VMEM,
+        compiler_params=params(8),
+        cost_estimate=cost(1),
+        name="pair_sum",
+    )(keep, received)
+
+
 def norm_kernel(resid_ref, gain_ref, *refs):
     terms, (hidden_ref, normed_ref) = refs[:-2], refs[-2:]
     total = resid_ref[...].astype(F32)
@@ -560,7 +576,7 @@
     cot_a = gather_rows(cotangent)
 
     keep, give, att, lse = attention_call(f_ref, q_rel, w_out, pieces, n_f)
-    total = after(pair_sum(keep, give), cot_a)
+    total = after(pair_sum_call(keep, beside(give)), cot_a)
     terms = scatter_rows(total)
     cot_b = beside(after(cot_a, total))
     terms[0] = after(terms[0], cot_b)

time: 139 us -> 139 us (level)
  transfers between devices with their start and end apart: 46 -> 46, of which waited for: 20 -> 19; matrix products, arithmetic and copies ran while one was open for 5% -> 5% of each run, Pallas kernels for 18% -> 18%
where the time goes in v6:
time: 139 us; the launch traced here: 138 us
  waiting for transfers between devices  51.1 us (37%)
  starting transfers between devices  49.7 us (36%)
  Pallas kernels  27.7 us (20%)
  matrix products  3.69 us (3%)
  local copies, waits for them, and re-layouts  3.17 us (2%)
  between operations  1.56 us (1%)
  other arithmetic  1.5 us (1%)
    ppermute x46, waiting for transfers between devices, exchange(): lax.ppermute(x, axis, [(i, i ^ k) for i in range(lax.axis_size(axis))])  51.1 us
    ppermute x46, starting transfers between devices, exchange(): lax.ppermute(x, axis, [(i, i ^ k) for i in range(lax.axis_size(axis))])  49.7 us
    pallas_call x4, Pallas kernels, weight_grad_call(): pl.pallas_call(functools.partial(weight_grad_kernel, left, right, len(lef...  9.01 us
    pallas_call x1, Pallas kernels, attention_call(): pl.pallas_call(functools.partial(attention_kernel, n_f, len(pieces)), out...  4.3 us
    pallas_call x1, Pallas kernels, normed_grad_call(): pl.pallas_call(normed_grad_kernel, out_shape=(out, out), in_specs=[VMEM]...  4.18 us
    dot_general x2, matrix products, dot(): return lax.dot_general(a, b, dims, preferred_element_type=F32)  3.69 us
    pallas_call x1, Pallas kernels, attention_grad_call(): pl.pallas_call(functools.partial(attention_grad_kernel, n_f, n_c), out_sh...  3.69 us
  transfers between devices with their start and end apart: 46, of which 19 were waited for; matrix products, arithmetic and copies ran while one was open for 5% of the time, Pallas kernels for 18%

profile of v6, /device:TPU:0, one launch (start us, length us, event | category | flops | bytes accessed | tf_op | source)
XLA Modules:
  0.0 138.4 jit_solution(800307201103836477)
XLA Ops:
  0.7 5.1 %collective-permute-start.6 = (bf16[16,4096]{1,0:T(8,128)(2,1)}, bf16[16,4096]{1,0:T(8,128)(2,1)S(1)}, u32[]{:S(2)}, u32[]{:S(2)}) collective-permute-start(bf16[16,4096]{1,0:T(8,128)(2,1)} %cot_ref.1), channel_id=1, source_target_pairs={{0,6},{1,7},{2,4},{3,5},{4,2},{5,3},{6,0},{7,1},{8,14},{9,15},{10,... | collective-permute-start | bytes 393224 | tf_op jit(solution)/shard_map/ppermute | solution.py:537
  5.8 1.8 %prepare_attention.1 = (bf16[128,512]{1,0:T(8,128)(2,1)}, bf16[272,128]{1,0:T(8,128)(2,1)}) custom-call(s32[1]{0:T(128)} %bitcast.1.f_ref, s32[1]{0:T(128)} %bitcast.2.group_ref, bf16[128,512]{1,0:T(8,128)(2,1)} %q_hbm.1, bf16[128,1024]{1,0:T(8,128)(2,1)} %k_hbm.1, bf16[128,1024]{1,0:T(8,128)(2,1)} %v_hbm.1, s32[1,128]{1,0:T(1,128)} %bitcast.31, ...), custom_call_target="tpu_custom_call" | custom-call | flops 1000000000 | bytes 4000000 | tf_op jit(solution)/shard_map/prepare_attention/pallas_call | solution.py:122
  7.6 2.5 %collective-permute-start.2 = (bf16[272,128]{1,0:T(8,128)(2,1)}, bf16[272,128]{1,0:T(8,128)(2,1)S(1)}, u32[]{:S(2)}, u32[]{:S(2)}) collective-permute-start(bf16[272,128]{1,0:T(8,128)(2,1)} %get-tuple-element.72.refs_1_.refs_0_), channel_id=1, source_target_pairs={{0,24},{8,16},{16,8},{24,0},{1,25},{9,17},{17,9},{25,1},{2,26},{10... | collective-permute-start | bytes 208904 | tf_op jit(solution)/shard_map/ppermute | solution.py:537
  11.2 2.0 %collective-permute-done.2.refs_4_.refs_3_ = bf16[272,128]{1,0:T(8,128)(2,1)S(1)} collective-permute-done((bf16[272,128]{1,0:T(8,128)(2,1)}, bf16[272,128]{1,0:T(8,128)(2,1)S(1)}, u32[]{:S(2)}, u32[]{:S(2)}) %collective-permute-start.2) | collective-permute-done | bytes 69664 | tf_op jit(solution)/shard_map/ppermute | solution.py:537
  15.8 4.3 %attention_and_projection.1 = (bf16[64,4096]{1,0:T(8,128)(2,1)}, bf16[64,4096]{1,0:T(8,128)(2,1)}, bf16[128,512]{1,0:T(8,128)(2,1)}, f32[128,128]{1,0:T(8,128)}) custom-call(s32[1]{0:T(128)} %bitcast.1.f_ref, bf16[128,512]{1,0:T(8,128)(2,1)} %get-tuple-element.71.refs_0_.refs_4_, bf16[272,128]{1,0:T(8,128)(2,1)} %get-tuple-element.72.refs_1_.refs_0_, ...), custom_call_target="tpu_custom_call" | custom-call | flops 2000000000 | bytes 8000000 | tf_op jit(solution)/shard_map/attention_and_projection/pallas_call | solution.py:176
  21.2 1.1 collective-permute-done.3.recv_ref
  23.7 2.5 %collective-permute-start.12 = (bf16[16,4096]{1,0:T(8,128)(2,1)S(1)}, bf16[16,4096]{1,0:T(8,128)(2,1)S(1)}, u32[]{:S(2)}, u32[]{:S(2)}) collective-permute-start(bf16[16,4096]{1,0:T(8,128)(2,1)S(1)} %get-tuple-element.144), channel_id=1, source_target_pairs={{0,6},{1,7},{2,4},{3,5},{4,2},{5,3},{6,0},{7,1},{8,14},{9,15},{10,... | collective-permute-start | bytes 393224 | tf_op jit(solution)/shard_map/ppermute | solution.py:537
  26.8 1.4 collective-permute-start.10
  28.2 1.6 %collective-permute-start.9 = (bf16[128,1024]{1,0:T(8,128)(2,1)S(1)}, bf16[128,1024]{1,0:T(8,128)(2,1)S(1)}, u32[]{:S(2)}, u32[]{:S(2)}) collective-permute-start(bf16[128,1024]{1,0:T(8,128)(2,1)S(1)} %maximum_maximum_fusion.2), channel_id=1, source_target_pairs={{0,16},{8,24},{16,0},{24,8},{1,17},{9,25},{17,1},{25,9},{2,18},{10... | collective-permute-start | bytes 786440 | tf_op jit(solution)/shard_map/ppermute | solution.py:537
  30.5 5.5 %collective-permute-done.9 = bf16[128,1024]{1,0:T(8,128)(2,1)S(1)} collective-permute-done((bf16[128,1024]{1,0:T(8,128)(2,1)S(1)}, bf16[128,1024]{1,0:T(8,128)(2,1)S(1)}, u32[]{:S(2)}, u32[]{:S(2)}) %collective-permute-start.9) | collective-permute-done | bytes 262176 | tf_op jit(solution)/shard_map/ppermute | solution.py:537
  36.0 4.1 %collective-permute-done.8 = bf16[192,1024]{1,0:T(8,128)(2,1)S(1)} collective-permute-done((bf16[192,1024]{1,0:T(8,128)(2,1)S(1)}, bf16[192,1024]{1,0:T(8,128)(2,1)S(1)}, u32[]{:S(2)}, u32[]{:S(2)}) %collective-permute-start.8) | collective-permute-done | bytes 393248 | tf_op jit(solution)/shard_map/ppermute | solution.py:537
  40.5 3.0 %collective-permute-start.15 = (bf16[16,4096]{1,0:T(8,128)(2,1)S(1)}, bf16[16,4096]{1,0:T(8,128)(2,1)S(1)}, u32[]{:S(2)}, u32[]{:S(2)}) collective-permute-start(bf16[16,4096]{1,0:T(8,128)(2,1)S(1)} %get-tuple-element.85), channel_id=1, source_target_pairs={{0,6},{1,7},{2,4},{3,5},{4,2},{5,3},{6,0},{7,1},{8,14},{9,15},{10,... | collective-permute-start | bytes 393224 | tf_op jit(solution)/shard_map/ppermute | solution.py:537
  43.5 1.4 %collective-permute-start.13 = (bf16[16,4096]{1,0:T(8,128)(2,1)S(1)}, bf16[16,4096]{1,0:T(8,128)(2,1)S(1)}, u32[]{:S(2)}, u32[]{:S(2)}) collective-permute-start(bf16[16,4096]{1,0:T(8,128)(2,1)S(1)} %get-tuple-element.85), channel_id=1, source_target_pairs={{0,2},{1,3},{2,0},{3,1},{4,6},{5,7},{6,4},{7,5},{8,10},{9,11},{10,... | collective-permute-start | bytes 393224 | tf_op jit(solution)/shard_map/ppermute | solution.py:537
  44.9 2.4 %fusion.25.ga_ref = f32[128,896]{1,0:T(8,128)S(1)} fusion(bf16[128,4096]{1,0:T(8,128)(2,1)S(1)} %constant_dynamic-update-slice_fusion.4, bf16[896,4096]{1,0:T(8,128)(2,1)S(1)} %bitcast.28), kind=kOutput, calls=%fused_computation.63 | convolution fusion | flops 939524096 | bytes 8847360 | tf_op jit(solution)/shard_map/dot_general | solution.py:31
  47.4 1.4 %collective-permute-done.15 = bf16[16,4096]{1,0:T(8,128)(2,1)S(1)} collective-permute-done((bf16[16,4096]{1,0:T(8,128)(2,1)S(1)}, bf16[16,4096]{1,0:T(8,128)(2,1)S(1)}, u32[]{:S(2)}, u32[]{:S(2)}) %collective-permute-start.15) | collective-permute-done | bytes 131104 | tf_op jit(solution)/shard_map/ppermute | solution.py:537
  48.8 4.7 %collective-permute-done.14 = bf16[16,4096]{1,0:T(8,128)(2,1)S(1)} collective-permute-done((bf16[16,4096]{1,0:T(8,128)(2,1)S(1)}, bf16[16,4096]{1,0:T(8,128)(2,1)S(1)}, u32[]{:S(2)}, u32[]{:S(2)}) %collective-permute-start.14) | collective-permute-done | bytes 131104 | tf_op jit(solution)/shard_map/ppermute | solution.py:537
  53.7 1.4 collective-permute-start.40
  55.5 2.6 %gate_up_and_gradients.1.pay_ref.refs_2_.refs_5_.refs_0_.refs_3_ = bf16[128,2688]{1,0:T(8,128)(2,1)S(1)} custom-call(bf16[64,4096]{1,0:T(8,128)(2,1)S(1)} %pad_maximum_fusion.2.xa_ref.a_ref, bf16[64,4096]{1,0:T(8,128)(2,1)S(1)} %collective-permute-done.16.xb_ref, bf16[4096,896]{1,0:T(8,128)(2,1)S(1)} %bitcast.21, bf16[4096,896]{1,0:T(8,128)(2,1)S(1)} %bitcast.23, ...), custom_call_target="tpu_custom_call" | custom-call | flops 1000000000 | bytes 4000000 | tf_op jit(solution)/shard_map/gate_up_and_gradients/pallas_call | solution.py:336
  58.1 4.2 %normed_gradients.1 = (bf16[64,4096]{1,0:T(8,128)(2,1)S(1)}, bf16[64,4096]{1,0:T(8,128)(2,1)S(1)}) custom-call(bf16[128,2688]{1,0:T(8,128)(2,1)S(1)} %gate_up_and_gradients.1.pay_ref.refs_2_.refs_5_.refs_0_.refs_3_, bf16[4096,896]{1,0:T(8,128)(2,1)S(1)} %bitcast.21, bf16[4096,896]{1,0:T(8,128)(2,1)S(1)} %bitcast.23), custom_call_target="tpu_custom_call" | custom-call | flops 1000000000 | bytes 4000000 | tf_op jit(solution)/shard_map/normed_gradients/pallas_call | solution.py:364
  62.6 1.7 %collective-permute-done.17 = bf16[64,4096]{1,0:T(8,128)(2,1)S(1)} collective-permute-done((bf16[64,4096]{1,0:T(8,128)(2,1)S(1)}, bf16[64,4096]{1,0:T(8,128)(2,1)S(1)}, u32[]{:S(2)}, u32[]{:S(2)}) %collective-permute-start.17) | collective-permute-done | bytes 524320 | tf_op jit(solution)/shard_map/ppermute | solution.py:537
  64.6 2.6 %collective-permute-start.23 = (bf16[16,4096]{1,0:T(8,128)(2,1)S(1)}, bf16[16,4096]{1,0:T(8,128)(2,1)S(1)}, u32[]{:S(2)}, u32[]{:S(2)}) collective-permute-start(bf16[16,4096]{1,0:T(8,128)(2,1)S(1)} %get-tuple-element.140), channel_id=1, source_target_pairs={{0,6},{1,7},{2,4},{3,5},{4,2},{5,3},{6,0},{7,1},{8,14},{9,15},{10,... | collective-permute-start | bytes 393224 | tf_op jit(solution)/shard_map/ppermute | solution.py:537
  67.2 1.9 %collective-permute-start.21 = (bf16[16,4096]{1,0:T(8,128)(2,1)S(1)}, bf16[16,4096]{1,0:T(8,128)(2,1)S(1)}, u32[]{:S(2)}, u32[]{:S(2)}) collective-permute-start(bf16[16,4096]{1,0:T(8,128)(2,1)S(1)} %get-tuple-element.142), channel_id=1, source_target_pairs={{0,2},{1,3},{2,0},{3,1},{4,6},{5,7},{6,4},{7,5},{8,10},{9,11},{10,... | collective-permute-start | bytes 393224 | tf_op jit(solution)/shard_map/ppermute | solution.py:537
  70.0 1.3 collective-permute-start.20
  71.3 1.3 convolution_convert_fusion
  72.6 9.2 %collective-permute-done.20.refs_6_.refs_4_ = bf16[64,3712]{1,0:T(8,128)(2,1)S(1)} collective-permute-done((bf16[64,3712]{1,0:T(8,128)(2,1)S(1)}, bf16[64,3712]{1,0:T(8,128)(2,1)S(1)}, u32[]{:S(2)}, u32[]{:S(2)}) %collective-permute-start.20) | collective-permute-done | bytes 475168 | tf_op jit(solution)/shard_map/ppermute | solution.py:537
  82.0 1.3 collective-permute-start.28
  83.4 1.4 collective-permute-start.27
  85.7 2.6 %collective-permute-start.26 = (bf16[16,4096]{1,0:T(8,128)(2,1)S(1)}, bf16[16,4096]{1,0:T(8,128)(2,1)S(1)}, u32[]{:S(2)}, u32[]{:S(2)}) collective-permute-start(bf16[16,4096]{1,0:T(8,128)(2,1)S(1)} %get-tuple-element.95), channel_id=1, source_target_pairs={{0,6},{1,7},{2,4},{3,5},{4,2},{5,3},{6,0},{7,1},{8,14},{9,15},{10,... | collective-permute-start | bytes 393224 | tf_op jit(solution)/shard_map/ppermute | solution.py:537
  88.3 1.8 %collective-permute-start.24 = (bf16[16,4096]{1,0:T(8,128)(2,1)S(1)}, bf16[16,4096]{1,0:T(8,128)(2,1)S(1)}, u32[]{:S(2)}, u32[]{:S(2)}) collective-permute-start(bf16[16,4096]{1,0:T(8,128)(2,1)S(1)} %get-tuple-element.95), channel_id=1, source_target_pairs={{0,2},{1,3},{2,0},{3,1},{4,6},{5,7},{6,4},{7,5},{8,10},{9,11},{10,... | collective-permute-start | bytes 393224 | tf_op jit(solution)/shard_map/ppermute | solution.py:537
  90.2 3.7 %collective-permute-done.26 = bf16[16,4096]{1,0:T(8,128)(2,1)S(1)} collective-permute-done((bf16[16,4096]{1,0:T(8,128)(2,1)S(1)}, bf16[16,4096]{1,0:T(8,128)(2,1)S(1)}, u32[]{:S(2)}, u32[]{:S(2)}) %collective-permute-start.26) | collective-permute-done | bytes 131104 | tf_op jit(solution)/shard_map/ppermute | solution.py:537
  93.9 5.5 %collective-permute-done.25 = bf16[16,4096]{1,0:T(8,128)(2,1)S(1)} collective-permute-done((bf16[16,4096]{1,0:T(8,128)(2,1)S(1)}, bf16[16,4096]{1,0:T(8,128)(2,1)S(1)}, u32[]{:S(2)}, u32[]{:S(2)}) %collective-permute-start.25) | collective-permute-done | bytes 131104 | tf_op jit(solution)/shard_map/ppermute | solution.py:537
  99.5 3.3 %collective-permute-done.28.refs_7_.refs_5_ = bf16[64,6400]{1,0:T(8,128)(2,1)S(1)} collective-permute-done((bf16[64,6400]{1,0:T(8,128)(2,1)S(1)}, bf16[64,6400]{1,0:T(8,128)(2,1)S(1)}, u32[]{:S(2)}, u32[]{:S(2)}) %collective-permute-start.28) | collective-permute-done | bytes 819232 | tf_op jit(solution)/shard_map/ppermute | solution.py:537
  102.7 1.1 collective-permute-done.27.refs_4_.refs_2_
  105.2 2.5 %grad_w_down.1 = f32[896,1024]{1,0:T(8,128)} custom-call(bf16[128,2688]{1,0:T(8,128)(2,1)S(1)} %gate_up_and_gradients.1.pay_ref.refs_2_.refs_5_.refs_0_.refs_3_, bf16[64,3712]{1,0:T(8,128)(2,1)S(1)} %collective-permute-done.19.refs_3_.refs_1_, bf16[64,6400]{1,0:T(8,128)(2,1)S(1)} %collective-permute-done.27.refs_4_.refs_2_, ...), custom_call_target="tpu_custom_call" | custom-call | flops 1500000000 | bytes 6000000 | tf_op jit(solution)/shard_map/grad_w_down/pallas_call | solution.py:423
  107.8 3.7 %attention_gradients.1 = (bf16[128,512]{1,0:T(8,128)(2,1)}, bf16[160,256]{1,0:T(8,128)(2,1)S(1)}, bf16[160,256]{1,0:T(8,128)(2,1)S(1)}, bf16[160,256]{1,0:T(8,128)(2,1)S(1)}, bf16[160,256]{1,0:T(8,128)(2,1)S(1)}) custom-call(s32[1]{0:T(128)} %bitcast.1.f_ref, bf16[272,128]{1,0:T(8,128)(2,1)S(1)} %copy-done.4, bf16[272,128]{1,0:T(8,128)(2,1)S(1)} %copy-done.10, ...), custom_call_target="tpu_custom_call" | custom-call | flops 2000000000 | bytes 8000000 | tf_op jit(solution)/shard_map/attention_gradients/pallas_call | solution.py:234
  111.5 1.4 %collective-permute-done.29 = bf16[32,4096]{1,0:T(8,128)(2,1)S(1)} collective-permute-done((bf16[32,4096]{1,0:T(8,128)(2,1)S(1)}, bf16[32,4096]{1,0:T(8,128)(2,1)S(1)}, u32[]{:S(2)}, u32[]{:S(2)}) %collective-permute-start.29) | collective-permute-done | bytes 262176 | tf_op jit(solution)/shard_map/ppermute | solution.py:537
  113.8 1.3 collective-permute-start.33
  115.0 1.4 %collective-permute-start.34 = (bf16[160,256]{1,0:T(8,128)(2,1)S(1)}, bf16[160,256]{1,0:T(8,128)(2,1)S(1)}, u32[]{:S(2)}, u32[]{:S(2)}) collective-permute-start(bf16[160,256]{1,0:T(8,128)(2,1)S(1)} %get-tuple-element.106), channel_id=1, source_target_pairs={{0,24},{8,16},{16,8},{24,0},{1,25},{9,17},{17,9},{25,1},{2,26},{10... | collective-permute-start | bytes 245768 | tf_op jit(solution)/shard_map/ppermute | solution.py:537
  116.5 1.4 %collective-permute-start.31 = (bf16[16,4096]{1,0:T(8,128)(2,1)S(1)}, bf16[16,4096]{1,0:T(8,128)(2,1)S(1)}, u32[]{:S(2)}, u32[]{:S(2)}) collective-permute-start(bf16[16,4096]{1,0:T(8,128)(2,1)S(1)} %fusion.1), channel_id=1, source_target_pairs={{0,4},{1,5},{2,6},{3,7},{4,0},{5,1},{6,2},{7,3},{8,12},{9,13},{10,... | collective-permute-start | bytes 393224 | tf_op jit(solution)/shard_map/ppermute | solution.py:537
  117.9 2.3 %grad_w_up.1 = f32[1024,896]{1,0:T(8,128)} custom-call(bf16[256,1024]{1,0:T(8,128)(2,1)S(1)} %maximum_maximum_fusion.refs_0_, bf16[256,1024]{1,0:T(8,128)(2,1)S(1)} %collective-permute-done.35.refs_1_, bf16[128,2688]{1,0:T(8,128)(2,1)S(1)} %gate_up_and_gradients.1.pay_ref.refs_2_.refs_5_.refs_0_.refs_3_, ...), custom_call_target="tpu_custom_call" | custom-call | flops 1500000000 | bytes 6000000 | tf_op jit(solution)/shard_map/grad_w_up/pallas_call | solution.py:423
  120.5 1.4 collective-permute-start.41
  122.6 1.5 %collective-permute-start.43 = (bf16[64,1024]{1,0:T(8,128)(2,1)S(1)}, bf16[64,1024]{1,0:T(8,128)(2,1)S(1)}, u32[]{:S(2)}, u32[]{:S(2)}) collective-permute-start(bf16[64,1024]{1,0:T(8,128)(2,1)S(1)} %get-tuple-element.129), channel_id=1, source_target_pairs={{0,24},{8,16},{16,8},{24,0},{1,25},{9,17},{17,9},{25,1},{2,26},{10... | collective-permute-start | bytes 393224 | tf_op jit(solution)/shard_map/ppermute | solution.py:537
  124.1 2.3 %grad_w_gate.1 = f32[1024,896]{1,0:T(8,128)} custom-call(bf16[256,1024]{1,0:T(8,128)(2,1)S(1)} %maximum_maximum_fusion.refs_0_, bf16[256,1024]{1,0:T(8,128)(2,1)S(1)} %collective-permute-done.35.refs_1_, bf16[128,2688]{1,0:T(8,128)(2,1)S(1)} %gate_up_and_gradients.1.pay_ref.refs_2_.refs_5_.refs_0_.refs_3_, ...), custom_call_target="tpu_custom_call" | custom-call | flops 1500000000 | bytes 6000000 | tf_op jit(solution)/shard_map/grad_w_gate/pallas_call | solution.py:423
  126.5 2.6 %collective-permute-start.39 = (bf16[2,48,256]{2,1,0:T(8,128)(2,1)S(1)}, bf16[2,48,256]{2,1,0:T(8,128)(2,1)S(1)}, u32[]{:S(2)}, u32[]{:S(2)}) collective-permute-start(bf16[2,48,256]{2,1,0:T(8,128)(2,1)S(1)} %get-tuple-element.158), channel_id=1, source_target_pairs={{0,6},{1,7},{2,4},{3,5},{4,2},{5,3},{6,0},{7,1},{8,14},{9,15},{10,... | collective-permute-start | bytes 147464 | tf_op jit(solution)/shard_map/ppermute | solution.py:537
  129.1 1.2 collective-permute-done.42
  130.3 1.4 collective-permute-start.38
  133.5 2.3 %collective-permute-done.38.refs_2_ = bf16[2,48,256]{2,1,0:T(8,128)(2,1)S(1)} collective-permute-done((bf16[2,48,256]{2,1,0:T(8,128)(2,1)S(1)}, bf16[2,48,256]{2,1,0:T(8,128)(2,1)S(1)}, u32[]{:S(2)}, u32[]{:S(2)}) %collective-permute-start.38) | collective-permute-done | bytes 49184 | tf_op jit(solution)/shard_map/ppermute | solution.py:537
  136.5 1.8 %grad_w_out.1 = f32[512,1024]{1,0:T(8,128)} custom-call(bf16[64,1024]{1,0:T(8,128)(2,1)S(1)} %pad_maximum_fusion.8.refs_0_, bf16[64,1024]{1,0:T(8,128)(2,1)S(1)} %get-tuple-element.153.refs_1_, bf16[64,1024]{1,0:T(8,128)(2,1)S(1)} %get-tuple-element.155.refs_2_, bf16[64,1024]{1,0:T(8,128)(2,1)S(1)} %get-tuple-element.157.refs_3_, ...), custom_call_target="tpu_custom_call" | custom-call | flops 1500000000 | bytes 6000000 | tf_op jit(solution)/shard_map/grad_w_out/pallas_call | solution.py:423
  (154 shorter events, 16.6 us)
Async XLA Ops:
  0.7 20.5 %collective-permute-start.6 = (bf16[16,4096]{1,0:T(8,128)(2,1)}, bf16[16,4096]{1,0:T(8,128)(2,1)S(1)}, u32[]{:S(2)}, u32[]{:S(2)}) collective-permute-start(bf16[16,4096]{1,0:T(8,128)(2,1)} %cot_ref.1), channel_id=1, source_target_pairs={{0,6},{1,7},{2,4},{3,5},{4,2},{5,3},{6,0},{7,1},{8,14},{9,15},{10,... | collective-permute-start | bytes 393224 | tf_op jit(solution)/shard_map/ppermute | solution.py:537
  5.8 15.3 %collective-permute-start.5 = (bf16[16,4096]{1,0:T(8,128)(2,1)}, bf16[16,4096]{1,0:T(8,128)(2,1)S(1)}, u32[]{:S(2)}, u32[]{:S(2)}) collective-permute-start(bf16[16,4096]{1,0:T(8,128)(2,1)} %cot_ref.1), channel_id=1, source_target_pairs={{0,4},{1,5},{2,6},{3,7},{4,0},{5,1},{6,2},{7,3},{8,12},{9,13},{10,... | collective-permute-start | bytes 393224 | tf_op jit(solution)/shard_map/ppermute | solution.py:537
  7.6 5.6 %collective-permute-start.2 = (bf16[272,128]{1,0:T(8,128)(2,1)}, bf16[272,128]{1,0:T(8,128)(2,1)S(1)}, u32[]{:S(2)}, u32[]{:S(2)}) collective-permute-start(bf16[272,128]{1,0:T(8,128)(2,1)} %get-tuple-element.72.refs_1_.refs_0_), channel_id=1, source_target_pairs={{0,24},{8,16},{16,8},{24,0},{1,25},{9,17},{17,9},{25,1},{2,26},{10... | collective-permute-start | bytes 208904 | tf_op jit(solution)/shard_map/ppermute | solution.py:537
  10.1 4.5 %collective-permute-start.1 = (bf16[272,128]{1,0:T(8,128)(2,1)}, bf16[272,128]{1,0:T(8,128)(2,1)S(1)}, u32[]{:S(2)}, u32[]{:S(2)}) collective-permute-start(bf16[272,128]{1,0:T(8,128)(2,1)} %get-tuple-element.72.refs_1_.refs_0_), channel_id=1, source_target_pairs={{0,16},{8,24},{16,0},{24,8},{1,17},{9,25},{17,1},{25,9},{2,18},{10... | collective-permute-start | bytes 208904 | tf_op jit(solution)/shard_map/ppermute | solution.py:537
  10.6 4.5 %collective-permute-start = (bf16[272,128]{1,0:T(8,128)(2,1)}, bf16[272,128]{1,0:T(8,128)(2,1)S(1)}, u32[]{:S(2)}, u32[]{:S(2)}) collective-permute-start(bf16[272,128]{1,0:T(8,128)(2,1)} %get-tuple-element.72.refs_1_.refs_0_), channel_id=1, source_target_pairs={{0,8},{8,0},{16,24},{24,16},{1,9},{9,1},{17,25},{25,17},{2,10},{10... | collective-permute-start | bytes 208904 | tf_op jit(solution)/shard_map/ppermute | solution.py:537
  13.2 7.9 %collective-permute-start.4 = (bf16[16,4096]{1,0:T(8,128)(2,1)S(1)}, bf16[16,4096]{1,0:T(8,128)(2,1)S(1)}, u32[]{:S(2)}, u32[]{:S(2)}) collective-permute-start(bf16[16,4096]{1,0:T(8,128)(2,1)S(1)} %copy-done), channel_id=1, source_target_pairs={{0,2},{1,3},{2,0},{3,1},{4,6},{5,7},{6,4},{7,5},{8,10},{9,11},{10,... | collective-permute-start | bytes 393224 | tf_op jit(solution)/shard_map/ppermute | solution.py:537
  15.8 29.1 %slice-start.4 = ((s8[7340032]{0:T(1024)(128)(4,1)}), s8[3145728]{0:T(1024)(128)(4,1)S(1)}, s32[]{:S(2)}) async-start(s8[7340032]{0:T(1024)(128)(4,1)} %bitcast.27), calls=%async_computation.4 | async-start | bytes 6291456
  20.1 2.2 %collective-permute-start.3 = (bf16[64,4096]{1,0:T(8,128)(2,1)}, bf16[64,4096]{1,0:T(8,128)(2,1)S(1)}, u32[]{:S(2)}, u32[]{:S(2)}) collective-permute-start(bf16[64,4096]{1,0:T(8,128)(2,1)} %get-tuple-element.74), channel_id=1, source_target_pairs={{0,1},{1,0},{2,3},{3,2},{4,5},{5,4},{6,7},{7,6},{8,9},{9,8},{10,11... | collective-permute-start | bytes 1572872 | tf_op jit(solution)/shard_map/ppermute | solution.py:537
  23.4 4.7 %collective-permute-start.7 = (bf16[64,4096]{1,0:T(8,128)(2,1)S(1)}, bf16[64,4096]{1,0:T(8,128)(2,1)S(1)}, u32[]{:S(2)}, u32[]{:S(2)}) collective-permute-start(bf16[64,4096]{1,0:T(8,128)(2,1)S(1)} %get-tuple-element.78.a_ref), channel_id=1, source_target_pairs={{0,1},{1,0},{2,3},{3,2},{4,5},{5,4},{6,7},{7,6},{8,9},{9,8},{10,11... | collective-permute-start | bytes 1572872 | tf_op jit(solution)/shard_map/ppermute | solution.py:537
  23.7 16.5 %collective-permute-start.12 = (bf16[16,4096]{1,0:T(8,128)(2,1)S(1)}, bf16[16,4096]{1,0:T(8,128)(2,1)S(1)}, u32[]{:S(2)}, u32[]{:S(2)}) collective-permute-start(bf16[16,4096]{1,0:T(8,128)(2,1)S(1)} %get-tuple-element.144), channel_id=1, source_target_pairs={{0,6},{1,7},{2,4},{3,5},{4,2},{5,3},{6,0},{7,1},{8,14},{9,15},{10,... | collective-permute-start | bytes 393224 | tf_op jit(solution)/shard_map/ppermute | solution.py:537
  26.2 14.0 %collective-permute-start.11 = (bf16[16,4096]{1,0:T(8,128)(2,1)S(1)}, bf16[16,4096]{1,0:T(8,128)(2,1)S(1)}, u32[]{:S(2)}, u32[]{:S(2)}) collective-permute-start(bf16[16,4096]{1,0:T(8,128)(2,1)S(1)} %get-tuple-element.145), channel_id=1, source_target_pairs={{0,4},{1,5},{2,6},{3,7},{4,0},{5,1},{6,2},{7,3},{8,12},{9,13},{10,... | collective-permute-start | bytes 393224 | tf_op jit(solution)/shard_map/ppermute | solution.py:537
  26.8 13.4 %collective-permute-start.10 = (bf16[16,4096]{1,0:T(8,128)(2,1)S(1)}, bf16[16,4096]{1,0:T(8,128)(2,1)S(1)}, u32[]{:S(2)}, u32[]{:S(2)}) collective-permute-start(bf16[16,4096]{1,0:T(8,128)(2,1)S(1)} %get-tuple-element.146), channel_id=1, source_target_pairs={{0,2},{1,3},{2,0},{3,1},{4,6},{5,7},{6,4},{7,5},{8,10},{9,11},{10,... | collective-permute-start | bytes 393224 | tf_op jit(solution)/shard_map/ppermute | solution.py:537
  28.2 7.8 %collective-permute-start.9 = (bf16[128,1024]{1,0:T(8,128)(2,1)S(1)}, bf16[128,1024]{1,0:T(8,128)(2,1)S(1)}, u32[]{:S(2)}, u32[]{:S(2)}) collective-permute-start(bf16[128,1024]{1,0:T(8,128)(2,1)S(1)} %maximum_maximum_fusion.2), channel_id=1, source_target_pairs={{0,16},{8,24},{16,0},{24,8},{1,17},{9,25},{17,1},{25,9},{2,18},{10... | collective-permute-start | bytes 786440 | tf_op jit(solution)/shard_map/ppermute | solution.py:537
  29.9 10.3 %collective-permute-start.8 = (bf16[192,1024]{1,0:T(8,128)(2,1)S(1)}, bf16[192,1024]{1,0:T(8,128)(2,1)S(1)}, u32[]{:S(2)}, u32[]{:S(2)}) collective-permute-start(bf16[192,1024]{1,0:T(8,128)(2,1)S(1)} %maximum_maximum_fusion.1), channel_id=1, source_target_pairs={{0,8},{8,0},{16,24},{24,16},{1,9},{9,1},{17,25},{25,17},{2,10},{10... | collective-permute-start | bytes 1179656 | tf_op jit(solution)/shard_map/ppermute | solution.py:537
  40.2 15.3 %slice-start = ((s8[7340032]{0:T(1024)(128)(4,1)}), s8[4194304]{0:T(1024)(128)(4,1)S(1)}, s32[]{:S(2)}) async-start(s8[7340032]{0:T(1024)(128)(4,1)} %bitcast.20), calls=%async_computation | async-start | bytes 8388608
  40.5 8.3 %collective-permute-start.15 = (bf16[16,4096]{1,0:T(8,128)(2,1)S(1)}, bf16[16,4096]{1,0:T(8,128)(2,1)S(1)}, u32[]{:S(2)}, u32[]{:S(2)}) collective-permute-start(bf16[16,4096]{1,0:T(8,128)(2,1)S(1)} %get-tuple-element.85), channel_id=1, source_target_pairs={{0,6},{1,7},{2,4},{3,5},{4,2},{5,3},{6,0},{7,1},{8,14},{9,15},{10,... | collective-permute-start | bytes 393224 | tf_op jit(solution)/shard_map/ppermute | solution.py:537
  43.5 10.0 %collective-permute-start.14 = (bf16[16,4096]{1,0:T(8,128)(2,1)S(1)}, bf16[16,4096]{1,0:T(8,128)(2,1)S(1)}, u32[]{:S(2)}, u32[]{:S(2)}) collective-permute-start(bf16[16,4096]{1,0:T(8,128)(2,1)S(1)} %get-tuple-element.85), channel_id=1, source_target_pairs={{0,4},{1,5},{2,6},{3,7},{4,0},{5,1},{6,2},{7,3},{8,12},{9,13},{10,... | collective-permute-start | bytes 393224 | tf_op jit(solution)/shard_map/ppermute | solution.py:537
  43.5 10.0 %collective-permute-start.13 = (bf16[16,4096]{1,0:T(8,128)(2,1)S(1)}, bf16[16,4096]{1,0:T(8,128)(2,1)S(1)}, u32[]{:S(2)}, u32[]{:S(2)}) collective-permute-start(bf16[16,4096]{1,0:T(8,128)(2,1)S(1)} %get-tuple-element.85), channel_id=1, source_target_pairs={{0,2},{1,3},{2,0},{3,1},{4,6},{5,7},{6,4},{7,5},{8,10},{9,11},{10,... | collective-permute-start | bytes 393224 | tf_op jit(solution)/shard_map/ppermute | solution.py:537
  53.5 2.0 %collective-permute-start.16 = (bf16[64,4096]{1,0:T(8,128)(2,1)S(1)}, bf16[64,4096]{1,0:T(8,128)(2,1)S(1)}, u32[]{:S(2)}, u32[]{:S(2)}) collective-permute-start(bf16[64,4096]{1,0:T(8,128)(2,1)S(1)} %pad_maximum_fusion.2.xa_ref.a_ref), channel_id=1, source_target_pairs={{0,1},{1,0},{2,3},{3,2},{4,5},{5,4},{6,7},{7,6},{8,9},{9,8},{10,11... | collective-permute-start | bytes 1572872 | tf_op jit(solution)/shard_map/ppermute | solution.py:537
  53.7 8.9 %collective-permute-start.40 = (bf16[128,1024]{1,0:T(8,128)(2,1)S(1)}, bf16[128,1024]{1,0:T(8,128)(2,1)S(1)}, u32[]{:S(2)}, u32[]{:S(2)}) collective-permute-start(bf16[128,1024]{1,0:T(8,128)(2,1)S(1)} %concatenate.78), channel_id=1, source_target_pairs={{0,16},{8,24},{16,0},{24,8},{1,17},{9,25},{17,1},{25,9},{2,18},{10... | collective-permute-start | bytes 786440 | tf_op jit(solution)/shard_map/ppermute | solution.py:537
  62.3 2.0 %collective-permute-start.17 = (bf16[64,4096]{1,0:T(8,128)(2,1)S(1)}, bf16[64,4096]{1,0:T(8,128)(2,1)S(1)}, u32[]{:S(2)}, u32[]{:S(2)}) collective-permute-start(bf16[64,4096]{1,0:T(8,128)(2,1)S(1)} %get-tuple-element.88), channel_id=1, source_target_pairs={{0,1},{1,0},{2,3},{3,2},{4,5},{5,4},{6,7},{7,6},{8,9},{9,8},{10,11... | collective-permute-start | bytes 1572872 | tf_op jit(solution)/shard_map/ppermute | solution.py:537
  64.6 18.8 %collective-permute-start.23 = (bf16[16,4096]{1,0:T(8,128)(2,1)S(1)}, bf16[16,4096]{1,0:T(8,128)(2,1)S(1)}, u32[]{:S(2)}, u32[]{:S(2)}) collective-permute-start(bf16[16,4096]{1,0:T(8,128)(2,1)S(1)} %get-tuple-element.140), channel_id=1, source_target_pairs={{0,6},{1,7},{2,4},{3,5},{4,2},{5,3},{6,0},{7,1},{8,14},{9,15},{10,... | collective-permute-start | bytes 393224 | tf_op jit(solution)/shard_map/ppermute | solution.py:537
  67.2 17.6 %collective-permute-start.22 = (bf16[16,4096]{1,0:T(8,128)(2,1)S(1)}, bf16[16,4096]{1,0:T(8,128)(2,1)S(1)}, u32[]{:S(2)}, u32[]{:S(2)}) collective-permute-start(bf16[16,4096]{1,0:T(8,128)(2,1)S(1)} %get-tuple-element.141), channel_id=1, source_target_pairs={{0,4},{1,5},{2,6},{3,7},{4,0},{5,1},{6,2},{7,3},{8,12},{9,13},{10,... | collective-permute-start | bytes 393224 | tf_op jit(solution)/shard_map/ppermute | solution.py:537
  67.2 17.6 %collective-permute-start.21 = (bf16[16,4096]{1,0:T(8,128)(2,1)S(1)}, bf16[16,4096]{1,0:T(8,128)(2,1)S(1)}, u32[]{:S(2)}, u32[]{:S(2)}) collective-permute-start(bf16[16,4096]{1,0:T(8,128)(2,1)S(1)} %get-tuple-element.142), channel_id=1, source_target_pairs={{0,2},{1,3},{2,0},{3,1},{4,6},{5,7},{6,4},{7,5},{8,10},{9,11},{10,... | collective-permute-start | bytes 393224 | tf_op jit(solution)/shard_map/ppermute | solution.py:537
  69.1 12.9 %collective-permute-start.19 = (bf16[64,3712]{1,0:T(8,128)(2,1)S(1)}, bf16[64,3712]{1,0:T(8,128)(2,1)S(1)}, u32[]{:S(2)}, u32[]{:S(2)}) collective-permute-start(bf16[64,3712]{1,0:T(8,128)(2,1)S(1)} %pad_maximum_fusion.5), channel_id=1, source_target_pairs={{0,8},{8,0},{16,24},{24,16},{1,9},{9,1},{17,25},{25,17},{2,10},{10... | collective-permute-start | bytes 1425416 | tf_op jit(solution)/shard_map/ppermute | solution.py:537
  70.0 11.9 %collective-permute-start.20 = (bf16[64,3712]{1,0:T(8,128)(2,1)S(1)}, bf16[64,3712]{1,0:T(8,128)(2,1)S(1)}, u32[]{:S(2)}, u32[]{:S(2)}) collective-permute-start(bf16[64,3712]{1,0:T(8,128)(2,1)S(1)} %pad_maximum_fusion.6), channel_id=1, source_target_pairs={{0,16},{8,24},{16,0},{24,8},{1,17},{9,25},{17,1},{25,9},{2,18},{10... | collective-permute-start | bytes 1425416 | tf_op jit(solution)/shard_map/ppermute | solution.py:537
  81.9 6.4 %collective-permute-start.18 = (bf16[64,4096]{1,0:T(8,128)(2,1)S(1)}, bf16[64,4096]{1,0:T(8,128)(2,1)S(1)}, u32[]{:S(2)}, u32[]{:S(2)}) collective-permute-start(bf16[64,4096]{1,0:T(8,128)(2,1)S(1)} %slice.196), channel_id=1, source_target_pairs={{0,1},{1,0},{2,3},{3,2},{4,5},{5,4},{6,7},{7,6},{8,9},{9,8},{10,11... | collective-permute-start | bytes 1572872 | tf_op jit(solution)/shard_map/ppermute | solution.py:537
  82.0 20.7 %collective-permute-start.28 = (bf16[64,6400]{1,0:T(8,128)(2,1)S(1)}, bf16[64,6400]{1,0:T(8,128)(2,1)S(1)}, u32[]{:S(2)}, u32[]{:S(2)}) collective-permute-start(bf16[64,6400]{1,0:T(8,128)(2,1)S(1)} %pad_maximum_fusion.1), channel_id=1, source_target_pairs={{0,8},{8,0},{16,24},{24,16},{1,9},{9,1},{17,25},{25,17},{2,10},{10... | collective-permute-start | bytes 2457608 | tf_op jit(solution)/shard_map/ppermute | solution.py:537
  83.4 20.4 %collective-permute-start.27 = (bf16[64,6400]{1,0:T(8,128)(2,1)S(1)}, bf16[64,6400]{1,0:T(8,128)(2,1)S(1)}, u32[]{:S(2)}, u32[]{:S(2)}) collective-permute-start(bf16[64,6400]{1,0:T(8,128)(2,1)S(1)} %pad_maximum_fusion), channel_id=1, source_target_pairs={{0,16},{8,24},{16,0},{24,8},{1,17},{9,25},{17,1},{25,9},{2,18},{10... | collective-permute-start | bytes 2457608 | tf_op jit(solution)/shard_map/ppermute | solution.py:537
  85.7 8.2 %collective-permute-start.26 = (bf16[16,4096]{1,0:T(8,128)(2,1)S(1)}, bf16[16,4096]{1,0:T(8,128)(2,1)S(1)}, u32[]{:S(2)}, u32[]{:S(2)}) collective-permute-start(bf16[16,4096]{1,0:T(8,128)(2,1)S(1)} %get-tuple-element.95), channel_id=1, source_target_pairs={{0,6},{1,7},{2,4},{3,5},{4,2},{5,3},{6,0},{7,1},{8,14},{9,15},{10,... | collective-permute-start | bytes 393224 | tf_op jit(solution)/shard_map/ppermute | solution.py:537
  88.3 11.1 %collective-permute-start.25 = (bf16[16,4096]{1,0:T(8,128)(2,1)S(1)}, bf16[16,4096]{1,0:T(8,128)(2,1)S(1)}, u32[]{:S(2)}, u32[]{:S(2)}) collective-permute-start(bf16[16,4096]{1,0:T(8,128)(2,1)S(1)} %get-tuple-element.95), channel_id=1, source_target_pairs={{0,4},{1,5},{2,6},{3,7},{4,0},{5,1},{6,2},{7,3},{8,12},{9,13},{10,... | collective-permute-start | bytes 393224 | tf_op jit(solution)/shard_map/ppermute | solution.py:537
  88.3 11.1 %collective-permute-start.24 = (bf16[16,4096]{1,0:T(8,128)(2,1)S(1)}, bf16[16,4096]{1,0:T(8,128)(2,1)S(1)}, u32[]{:S(2)}, u32[]{:S(2)}) collective-permute-start(bf16[16,4096]{1,0:T(8,128)(2,1)S(1)} %get-tuple-element.95), channel_id=1, source_target_pairs={{0,2},{1,3},{2,0},{3,1},{4,6},{5,7},{6,4},{7,5},{8,10},{9,11},{10,... | collective-permute-start | bytes 393224 | tf_op jit(solution)/shard_map/ppermute | solution.py:537
  93.9 11.3 %collective-permute-start.45 = (bf16[256,1024]{1,0:T(8,128)(2,1)S(1)}, bf16[256,1024]{1,0:T(8,128)(2,1)S(1)}, u32[]{:S(2)}, u32[]{:S(2)}) collective-permute-start(bf16[256,1024]{1,0:T(8,128)(2,1)S(1)} %pad_maximum_fusion.4.refs_6_), channel_id=1, source_target_pairs={{0,1},{1,0},{2,3},{3,2},{4,5},{5,4},{6,7},{7,6},{8,9},{9,8},{10,11... | collective-permute-start | bytes 1572872 | tf_op jit(solution)/shard_map/ppermute | solution.py:537
  103.9 3.9 %collective-permute-start.30 = (bf16[64,4096]{1,0:T(8,128)(2,1)S(1)}, bf16[64,4096]{1,0:T(8,128)(2,1)S(1)}, u32[]{:S(2)}, u32[]{:S(2)}) collective-permute-start(bf16[64,4096]{1,0:T(8,128)(2,1)S(1)} %pad_maximum_fusion.3.refs_8_.a_ref), channel_id=1, source_target_pairs={{0,1},{1,0},{2,3},{3,2},{4,5},{5,4},{6,7},{7,6},{8,9},{9,8},{10,11... | collective-permute-start | bytes 1572872 | tf_op jit(solution)/shard_map/ppermute | solution.py:537
  104.0 7.6 %collective-permute-start.35 = (bf16[256,1024]{1,0:T(8,128)(2,1)S(1)}, bf16[256,1024]{1,0:T(8,128)(2,1)S(1)}, u32[]{:S(2)}, u32[]{:S(2)}) collective-permute-start(bf16[256,1024]{1,0:T(8,128)(2,1)S(1)} %maximum_maximum_fusion.refs_0_), channel_id=1, source_target_pairs={{0,1},{1,0},{2,3},{3,2},{4,5},{5,4},{6,7},{7,6},{8,9},{9,8},{10,11... | collective-permute-start | bytes 1572872 | tf_op jit(solution)/shard_map/ppermute | solution.py:537
  104.7 8.3 %collective-permute-start.29 = (bf16[32,4096]{1,0:T(8,128)(2,1)S(1)}, bf16[32,4096]{1,0:T(8,128)(2,1)S(1)}, u32[]{:S(2)}, u32[]{:S(2)}) collective-permute-start(bf16[32,4096]{1,0:T(8,128)(2,1)S(1)} %pad_maximum_fusion.7), channel_id=1, source_target_pairs={{0,2},{1,3},{2,0},{3,1},{4,6},{5,7},{6,4},{7,5},{8,10},{9,11},{10,... | collective-permute-start | bytes 786440 | tf_op jit(solution)/shard_map/ppermute | solution.py:537
  113.0 7.3 %collective-permute-start.32 = (bf16[160,256]{1,0:T(8,128)(2,1)S(1)}, bf16[160,256]{1,0:T(8,128)(2,1)S(1)}, u32[]{:S(2)}, u32[]{:S(2)}) collective-permute-start(bf16[160,256]{1,0:T(8,128)(2,1)S(1)} %get-tuple-element.104), channel_id=1, source_target_pairs={{0,8},{8,0},{16,24},{24,16},{1,9},{9,1},{17,25},{25,17},{2,10},{10... | collective-permute-start | bytes 245768 | tf_op jit(solution)/shard_map/ppermute | solution.py:537
  113.8 6.5 %collective-permute-start.33 = (bf16[160,256]{1,0:T(8,128)(2,1)S(1)}, bf16[160,256]{1,0:T(8,128)(2,1)S(1)}, u32[]{:S(2)}, u32[]{:S(2)}) collective-permute-start(bf16[160,256]{1,0:T(8,128)(2,1)S(1)} %get-tuple-element.105), channel_id=1, source_target_pairs={{0,16},{8,24},{16,0},{24,8},{1,17},{9,25},{17,1},{25,9},{2,18},{10... | collective-permute-start | bytes 245768 | tf_op jit(solution)/shard_map/ppermute | solution.py:537
  115.0 5.3 %collective-permute-start.34 = (bf16[160,256]{1,0:T(8,128)(2,1)S(1)}, bf16[160,256]{1,0:T(8,128)(2,1)S(1)}, u32[]{:S(2)}, u32[]{:S(2)}) collective-permute-start(bf16[160,256]{1,0:T(8,128)(2,1)S(1)} %get-tuple-element.106), channel_id=1, source_target_pairs={{0,24},{8,16},{16,8},{24,0},{1,25},{9,17},{17,9},{25,1},{2,26},{10... | collective-permute-start | bytes 245768 | tf_op jit(solution)/shard_map/ppermute | solution.py:537
  116.5 15.3 %collective-permute-start.31 = (bf16[16,4096]{1,0:T(8,128)(2,1)S(1)}, bf16[16,4096]{1,0:T(8,128)(2,1)S(1)}, u32[]{:S(2)}, u32[]{:S(2)}) collective-permute-start(bf16[16,4096]{1,0:T(8,128)(2,1)S(1)} %fusion.1), channel_id=1, source_target_pairs={{0,4},{1,5},{2,6},{3,7},{4,0},{5,1},{6,2},{7,3},{8,12},{9,13},{10,... | collective-permute-start | bytes 393224 | tf_op jit(solution)/shard_map/ppermute | solution.py:537
  120.5 6.0 %collective-permute-start.36 = (bf16[4,48,256]{2,1,0:T(8,128)(2,1)S(1)}, bf16[4,48,256]{2,1,0:T(8,128)(2,1)S(1)}, u32[]{:S(2)}, u32[]{:S(2)}) collective-permute-start(bf16[4,48,256]{2,1,0:T(8,128)(2,1)S(1)} %get-tuple-element.115), channel_id=1, source_target_pairs={{0,1},{1,0},{2,3},{3,2},{4,5},{5,4},{6,7},{7,6},{8,9},{9,8},{10,11... | collective-permute-start | bytes 294920 | tf_op jit(solution)/shard_map/ppermute | solution.py:537
  120.5 8.6 %collective-permute-start.41 = (bf16[64,1024]{1,0:T(8,128)(2,1)S(1)}, bf16[64,1024]{1,0:T(8,128)(2,1)S(1)}, u32[]{:S(2)}, u32[]{:S(2)}) collective-permute-start(bf16[64,1024]{1,0:T(8,128)(2,1)S(1)} %get-tuple-element.127), channel_id=1, source_target_pairs={{0,8},{8,0},{16,24},{24,16},{1,9},{9,1},{17,25},{25,17},{2,10},{10... | collective-permute-start | bytes 393224 | tf_op jit(solution)/shard_map/ppermute | solution.py:537
  121.9 8.4 %collective-permute-start.42 = (bf16[64,1024]{1,0:T(8,128)(2,1)S(1)}, bf16[64,1024]{1,0:T(8,128)(2,1)S(1)}, u32[]{:S(2)}, u32[]{:S(2)}) collective-permute-start(bf16[64,1024]{1,0:T(8,128)(2,1)S(1)} %get-tuple-element.128), channel_id=1, source_target_pairs={{0,16},{8,24},{16,0},{24,8},{1,17},{9,25},{17,1},{25,9},{2,18},{10... | collective-permute-start | bytes 393224 | tf_op jit(solution)/shard_map/ppermute | solution.py:537
  122.6 9.0 %collective-permute-start.43 = (bf16[64,1024]{1,0:T(8,128)(2,1)S(1)}, bf16[64,1024]{1,0:T(8,128)(2,1)S(1)}, u32[]{:S(2)}, u32[]{:S(2)}) collective-permute-start(bf16[64,1024]{1,0:T(8,128)(2,1)S(1)} %get-tuple-element.129), channel_id=1, source_target_pairs={{0,24},{8,16},{16,8},{24,0},{1,25},{9,17},{17,9},{25,1},{2,26},{10... | collective-permute-start | bytes 393224 | tf_op jit(solution)/shard_map/ppermute | solution.py:537
  126.5 6.0 %collective-permute-start.39 = (bf16[2,48,256]{2,1,0:T(8,128)(2,1)S(1)}, bf16[2,48,256]{2,1,0:T(8,128)(2,1)S(1)}, u32[]{:S(2)}, u32[]{:S(2)}) collective-permute-start(bf16[2,48,256]{2,1,0:T(8,128)(2,1)S(1)} %get-tuple-element.158), channel_id=1, source_target_pairs={{0,6},{1,7},{2,4},{3,5},{4,2},{5,3},{6,0},{7,1},{8,14},{9,15},{10,... | collective-permute-start | bytes 147464 | tf_op jit(solution)/shard_map/ppermute | solution.py:537
  129.1 4.4 %collective-permute-start.37 = (bf16[2,48,256]{2,1,0:T(8,128)(2,1)S(1)}, bf16[2,48,256]{2,1,0:T(8,128)(2,1)S(1)}, u32[]{:S(2)}, u32[]{:S(2)}) collective-permute-start(bf16[2,48,256]{2,1,0:T(8,128)(2,1)S(1)} %get-tuple-element.160), channel_id=1, source_target_pairs={{0,2},{1,3},{2,0},{3,1},{4,6},{5,7},{6,4},{7,5},{8,10},{9,11},{10,... | collective-permute-start | bytes 147464 | tf_op jit(solution)/shard_map/ppermute | solution.py:537
  130.3 5.5 %collective-permute-start.38 = (bf16[2,48,256]{2,1,0:T(8,128)(2,1)S(1)}, bf16[2,48,256]{2,1,0:T(8,128)(2,1)S(1)}, u32[]{:S(2)}, u32[]{:S(2)}) collective-permute-start(bf16[2,48,256]{2,1,0:T(8,128)(2,1)S(1)} %get-tuple-element.161), channel_id=1, source_target_pairs={{0,4},{1,5},{2,6},{3,7},{4,0},{5,1},{6,2},{7,3},{8,12},{9,13},{10,... | collective-permute-start | bytes 147464 | tf_op jit(solution)/shard_map/ppermute | solution.py:537
  131.7 4.8 %collective-permute-start.44 = (bf16[256,1024]{1,0:T(8,128)(2,1)S(1)}, bf16[256,1024]{1,0:T(8,128)(2,1)S(1)}, u32[]{:S(2)}, u32[]{:S(2)}) collective-permute-start(bf16[256,1024]{1,0:T(8,128)(2,1)S(1)} %constant_dynamic-update-slice_fusion.9.refs_4_), channel_id=1, source_target_pairs={{0,1},{1,0},{2,3},{3,2},{4,5},{5,4},{6,7},{7,6},{8,9},{9,8},{10,11... | collective-permute-start | bytes 1572872 | tf_op jit(solution)/shard_map/ppermute | solution.py:537
  (19 other events, 124.5 us)
